TPU v7x, 32 devices: a whole 2x2x4 slice. The times are simulated.
32 devices in a mesh: seq: 16 (over z, y, x), head: 2 (over core).
Axes of the slice: x: 2, y: 2, z: 4, core: 2. Of those that a mesh axis runs over, the one named last changes fastest.
Arguments:
- queries: bfloat16 [8192, 2048], P('seq', 'head'), may hold values from -60 to 60
- keys: bfloat16 [8192, 2048], P('seq', 'head'), may hold values from -6 to 6
- values: bfloat16 [8192, 2048], P('seq', 'head'), may hold values from -6 to 6
- out_grad: bfloat16 [8192, 2048], P('seq', 'head'), may hold values from -6 to 6
- rand_ids: int32 [16, 64, 3], replicated, may hold values from 0 to 63, as said below
- glob_ids: int32 [2], replicated, may hold values from 0 to 63, as said below
Outputs:
- out: bfloat16 [8192, 2048], P('seq', 'head')
- query_gradient: bfloat16 [8192, 2048], P('seq', 'head')
- key_grad: bfloat16 [8192, 2048], P('seq', 'head')
- value_grad: bfloat16 [8192, 2048], P('seq', 'head')
Inputs may be any that keep to these rules, and one draw needn't show every extreme that they name: `rand_ids`: group the heads into runs of 8 and the query blocks into runs of 4; within one head run and one query run, the entries name key blocks of any one aligned run of 4 blocks (blocks 4j to 4j + 3, those of one index of seq) at most 8 times, and exactly 8 times for some such run. `glob_ids`: the ids are distinct, and one of them is the last block, 63.
All inputs are finite; a program needn't handle non-finite values.
Results may differ from a plain program's by a relative error of at most 0.014.
Values may be sent and summed in bfloat16 or wider, within the bound.
No kernel may reach another device: no remote copies, remote signals or barrier semaphores. Data moves between devices by JAX's collectives and lax.ppermute only.
A program may use at most 128 MiB of HBM per device.

v0:
```python
import math

import jax
import jax.numpy as jnp
from jax import lax
from jax.sharding import PartitionSpec as P

BLOCK = 128
DH = 128
RAND = 3
GLOB = 2
WMAX = 1


masked_value = -1e30


def with_halo(block, sides, width):
    for axis, dim in sides:
        count = lax.axis_size(axis)
        forward = [(i, i + 1) for i in range(count - 1)]
        backward = [(target, source) for source, target in forward]
        low = lax.ppermute(
            lax.slice_in_dim(block, block.shape[dim] - width, None, axis=dim), axis, forward
        )
        high = lax.ppermute(lax.slice_in_dim(block, 0, width, axis=dim), axis, backward)
        block = jnp.concatenate([low, block, high], axis=dim)
    return block


def spread_2(array, axis, root):
    mine = lax.axis_index(axis) == root
    return lax.psum(jnp.where(mine, array, jnp.zeros_like(array)), axis)


def from_behind(value, axis, steps):
    count = lax.axis_size(axis)
    initial, last = (max(0, -steps), min(count, count - steps))
    return lax.ppermute(value, axis, [(source, source + steps) for source in range(initial, last)])


def body(queries, keys, values, out_grad, rand_ids, glob_ids):
    block_size = BLOCK
    head_size = DH
    half_width = WMAX
    rand_count = RAND
    glob_count = GLOB
    window_span = 2 * half_width + 1
    rows_here = queries.shape[0]
    heads_here = queries.shape[1] // head_size
    blocks_here = rows_here // block_size
    shards = lax.axis_size("seq")
    place = lax.axis_index("seq")
    group = lax.axis_index("head")
    all_blocks = blocks_here * shards
    score_scale = 1.0 / math.sqrt(head_size)

    def to_heads(array):
        return array.reshape(blocks_here, block_size, heads_here, head_size).transpose(2, 0, 1, 3)

    def from_heads(array):
        return array.transpose(1, 2, 0, 3).reshape(rows_here, heads_here * head_size)

    kv_pair = jnp.stack([keys, values])
    banded = with_halo(kv_pair, (("seq", 1),), half_width * block_size)
    band_pair = banded.reshape(
        2, blocks_here + 2 * half_width, block_size, heads_here, head_size
    ).transpose(3, 0, 1, 2, 4)
    pieces = []
    for glob_number in range(glob_count):
        owner_index = glob_ids[glob_number] // blocks_here
        local_block = glob_ids[glob_number] - owner_index * blocks_here
        piece = lax.dynamic_slice_in_dim(kv_pair, local_block * block_size, block_size, 1)
        pieces.append(spread_2(piece, "seq", owner_index))
    glob_pair = (
        jnp.stack(pieces)
        .reshape(glob_count, 2, block_size, heads_here, head_size)
        .transpose(3, 1, 0, 2, 4)
    )
    rows_per = heads_here * blocks_here * rand_count
    cap = max(2, (5 * rows_per + 4 * shards - 1) // (4 * shards))
    ids_mine = lax.dynamic_slice_in_dim(rand_ids, group * heads_here, heads_here, 0)
    requests = (
        ids_mine.reshape(heads_here, shards, blocks_here, rand_count)
        .transpose(1, 0, 2, 3)
        .reshape(shards, rows_per)
    )
    source = requests // blocks_here
    source_hits = (source[:, :, None] == jnp.arange(shards, dtype=jnp.int32)[None, None, :]).astype(
        jnp.int32
    )
    earlier = jnp.cumsum(source_hits, axis=1) - source_hits
    slot_index = jnp.sum(earlier * source_hits, axis=2)
    own_source = lax.dynamic_index_in_dim(source, place, 0, False)
    own_slot = lax.dynamic_index_in_dim(slot_index, place, 0, False)
    pick_index = own_source * cap + own_slot
    head_of = jnp.arange(rows_per, dtype=jnp.int32) // (blocks_here * rand_count)
    flat_index = (requests - place * blocks_here) * heads_here + head_of[None, :]
    slot_match = (source == place)[:, :, None] & (
        slot_index[:, :, None] == jnp.arange(cap, dtype=jnp.int32)[None, None, :]
    )
    send_index = jnp.sum(jnp.where(slot_match, flat_index[:, :, None], 0), axis=1)
    send_live = jnp.any(slot_match, axis=1)
    block_table = kv_pair.reshape(2, blocks_here, block_size, heads_here, head_size).transpose(
        1, 3, 0, 2, 4
    )
    block_table = block_table.reshape(blocks_here * heads_here, 2, block_size, head_size)
    payload = block_table[send_index]
    chosen = lax.all_to_all(payload, "seq", split_axis=0, concat_axis=0, tiled=True).reshape(
        shards * cap, 2, block_size, head_size
    )[pick_index]
    chosen = chosen.reshape(heads_here, blocks_here, rand_count, 2, block_size, head_size)
    fetched = chosen.transpose(0, 3, 1, 2, 4, 5)
    offsets = jnp.arange(window_span, dtype=jnp.int32) - half_width
    positions = (
        place * blocks_here + jnp.arange(blocks_here, dtype=jnp.int32)[:, None] + offsets[None, :]
    )
    inside = (positions >= 0) & (positions < all_blocks)
    live_window = jnp.broadcast_to(inside[None], (heads_here, blocks_here, window_span))
    live_mask = jnp.concatenate(
        [live_window, jnp.ones((heads_here, blocks_here, rand_count + glob_count), bool)], axis=2
    )

    def gathered_key_blocks(band_head, rand_head, glob_head):
        windowed = jnp.stack(
            [band_head[:, offset : offset + blocks_here] for offset in range(window_span)], axis=2
        )
        spread = jnp.broadcast_to(
            glob_head[:, None], (2, blocks_here, glob_count, block_size, head_size)
        )
        return jnp.concatenate([windowed, rand_head, spread], axis=2)

    def softmax_weights(query_per_head, listed_blocks, live_head):
        unscaled_scores = (
            jnp.einsum(
                "zjs,zcls->zjcl",
                query_per_head,
                listed_blocks[0],
                preferred_element_type=jnp.float32,
            )
            * score_scale
        )
        unscaled_scores = jnp.where(live_head[:, None, :, None], unscaled_scores, masked_value)
        peak = jnp.max(unscaled_scores, axis=(2, 3), keepdims=True)
        exponent = jnp.exp(unscaled_scores - peak)
        return exponent / jnp.sum(exponent, axis=(2, 3), keepdims=True)

    def forward_head(operands):
        query_per_head, band_head, rand_head, glob_head, live_head = operands
        listed_blocks = gathered_key_blocks(band_head, rand_head, glob_head)
        weights_narrow_float = softmax_weights(query_per_head, listed_blocks, live_head).astype(
            jnp.bfloat16
        )
        result = jnp.einsum(
            "qhgf,qgfm->qhm",
            weights_narrow_float,
            listed_blocks[1],
            preferred_element_type=jnp.float32,
        )
        return result.astype(jnp.bfloat16)

    query_heads = to_heads(queries)
    grad_heads = to_heads(out_grad)
    out_heads = lax.map(forward_head, (query_heads, band_pair, fetched, glob_pair, live_mask))

    def backward_head(operands):
        (
            query_per_head,
            band_head,
            rand_head,
            glob_head,
            live_head,
            gradient_per_head,
            output_per_head,
        ) = operands
        listed_blocks = gathered_key_blocks(band_head, rand_head, glob_head)
        weights = softmax_weights(query_per_head, listed_blocks, live_head)
        weights_narrow_float = weights.astype(jnp.bfloat16)
        row_delta = jnp.sum(
            gradient_per_head.astype(jnp.float32) * output_per_head.astype(jnp.float32), axis=-1
        )
        probability_gradient = jnp.einsum(
            "zjs,zcls->zjcl",
            gradient_per_head,
            listed_blocks[1],
            preferred_element_type=jnp.float32,
        )
        score_narrow_float = (
            weights * (probability_gradient - row_delta[:, :, None, None])
        ).astype(jnp.bfloat16)
        query_gradient = (
            jnp.einsum(
                "qhgf,qgfm->qhm",
                score_narrow_float,
                listed_blocks[0],
                preferred_element_type=jnp.float32,
            )
            * score_scale
        )
        key_gradient_parts = (
            jnp.einsum(
                "yelt,yev->yltv",
                score_narrow_float,
                query_per_head,
                preferred_element_type=jnp.float32,
            )
            * score_scale
        )
        value_gradient_parts = jnp.einsum(
            "yelt,yev->yltv",
            weights_narrow_float,
            gradient_per_head,
            preferred_element_type=jnp.float32,
        )
        terms = jnp.stack([key_gradient_parts, value_gradient_parts])
        band_sum = jnp.zeros((2, blocks_here + 2 * half_width, block_size, head_size), jnp.float32)
        for offset in range(window_span):
            band_sum = band_sum + jnp.pad(
                terms[:, :, offset], ((0, 0), (offset, window_span - 1 - offset), (0, 0), (0, 0))
            )
        rand_part = terms[:, :, window_span : window_span + rand_count].astype(jnp.bfloat16)
        glob_part = jnp.sum(terms[:, :, window_span + rand_count :], axis=1)
        return (query_gradient.astype(jnp.bfloat16), band_sum, rand_part, glob_part)

    query_grads, band_sums, rand_terms, glob_terms = lax.map(
        backward_head,
        (query_heads, band_pair, fetched, glob_pair, live_mask, grad_heads, out_heads),
    )
    center = band_sums[:, :, half_width : half_width + blocks_here]
    for shift_by in (1, -1):
        if shift_by == 1:
            rim_terms = band_sums[:, :, blocks_here + half_width :]
        else:
            rim_terms = band_sums[:, :, :half_width]
        moved_rim = from_behind(rim_terms, "seq", shift_by)
        if shift_by == 1:
            center = center.at[:, :, :half_width].add(moved_rim)
        else:
            center = center.at[:, :, blocks_here - half_width :].add(moved_rim)
    glob_total = lax.psum(glob_terms, "seq")
    owned_mask = (
        glob_ids[:, None] == place * blocks_here + jnp.arange(blocks_here, dtype=jnp.int32)[None, :]
    ).astype(jnp.float32)
    center = center + jnp.einsum(
        "gi,hcgbd->hcibd", owned_mask, glob_total, precision=lax.Precision.HIGHEST
    )
    outgoing_terms = rand_terms.transpose(0, 2, 3, 1, 4, 5).reshape(
        rows_per, 2, block_size, head_size
    )
    outgoing = (
        jnp.zeros((shards * cap, 2, block_size, head_size), jnp.bfloat16)
        .at[pick_index]
        .set(outgoing_terms)
    )
    outgoing = outgoing.reshape(shards, cap, 2, block_size, head_size)
    returned = lax.all_to_all(outgoing, "seq", split_axis=0, concat_axis=0, tiled=True)
    target = jnp.where(send_live, send_index, blocks_here * heads_here).reshape(-1)
    gathered = (
        jnp.zeros((blocks_here * heads_here, 2, block_size, head_size), jnp.float32)
        .at[target]
        .add(
            returned.reshape(shards * cap, 2, block_size, head_size).astype(jnp.float32),
            mode="drop",
        )
    )
    center = center + gathered.reshape(blocks_here, heads_here, 2, block_size, head_size).transpose(
        1, 2, 0, 3, 4
    )
    key_grad = from_heads(center[:, 0].astype(jnp.bfloat16))
    value_grad = from_heads(center[:, 1].astype(jnp.bfloat16))
    return (from_heads(out_heads), from_heads(query_grads), key_grad, value_grad)


def solution(mesh):
    return jax.shard_map(
        body,
        mesh=mesh,
        in_specs=(P("seq", "head"), P("seq", "head"), P("seq", "head"), P("seq", "head"), P(), P()),
        out_specs=(P("seq", "head"), P("seq", "head"), P("seq", "head"), P("seq", "head")),
        check_vma=False,
    )
```

profile of v0, /device:TPU:16, one launch (start us, length us, event | category | flops | bytes accessed | tf_op | source)
XLA Modules:
  0.0 890.5 jit_solution(7985396716135853531)
XLA Ops:
  8.4 2.1 select_reduce_fusion
  13.7 6.5 gather_fusion
  20.2 7.2 all-to-all-start
  37.4 3.5 collective-permute-start
  40.9 4.3 collective-permute-start.1
  49.1 193.4 %collective-permute-done = bf16[2,128,1024]{1,2,0:T(8,128)(2,1)} collective-permute-done((bf16[2,128,1024]{1,2,0:T(8,128)(2,1)}, bf16[2,128,1024]{1,2,0:T(8,128)(2,1)}, u32[]{:S(2)}, u32[]{:S(2)}) %collective-permute-start) | collective-permute-done | bytes 524320 | tf_op jit(solution)/shard_map/ppermute | solution.py:23
  242.5 2.2 pad_maximum_fusion.1
  244.7 2.9 copy.202
  247.6 2.7 copy.252
  251.1 52.7 %all-reduce.10.cloned.1.call-done = (bf16[1,2,128,8,128]{2,4,3,1,0:T(8,128)(2,1)}, bf16[1,2,128,8,128]{2,4,3,1,0:T(8,128)(2,1)}) async-done(((bf16[1,2,128,8,128]{2,4,3,1,0:T(8,128)(2,1)}, bf16[1,2,128,8,128]{2,4,3,1,0:T(8,128)(2,1)}), (bf16[1,2,128,8,128]{2,4,3,1,0:T(8,128)(2,1)}, bf16[1,2,128,8,128]{2,4,3,1,0:T(8,128)(2,1)})) %all-reduce.10.cloned.1.call-update) | async-done | bytes 1048592 | tf_op jit(solution)/shard_map/psum | solution.py:33
  303.8 2.3 maximum_bitcast_fusion.1
  306.1 2.3 copy.219
  308.3 9.4 %gather_fusion.1 = bf16[96,2,128,128]{3,2,1,0:T(8,128)(2,1)} fusion(bf16[128,2,128,128]{3,2,1,0:T(8,128)(2,1)} %bitcast.58, s32[1024]{0:T(1024)S(1)} %pad_clamp_fusion), kind=kCustom, calls=%fused_computation.1 | custom fusion | bytes 12583296 | tf_op jit(solution)/shard_map/gather | solution.py:109
  317.8 8.1 copy.218
  327.1 47.6 %while.30 = (s32[]{:T(128)}, bf16[8,4,128,128]{3,2,1,0:T(8,128)(2,1)}, pred[8,4,8]{2,1,0:T(4,128)(4,1)S(1)}, bf16[8,4,128,128]{3,2,1,0:T(8,128)(2,1)}, bf16[8,2,...) while((s32[]{:T(128)}, ...), condition=%wide.region_8.9_spmd, body=%wide.region_5.8_spmd.sunk | while | flops 274791424 | bytes 13512901 | solution.py:164
  375.9 116.5 %while.31 = (s32[]{:T(128)}, bf16[8,4,128,128]{3,2,1,0:T(8,128)(2,1)}, f32[8,2,6,128,128]{4,3,2,1,0:T(8,128)}, bf16[8,2,4,3,128,128]{5,4,1,3,2,0:T(8,128)(2,1)},...) while((s32[]{:T(128)}, ...), condition=%wide.region_14.15_spmd, body=%wide.region_9.14_spmd.sunk | while | flops 683604480 | bytes 42753296 | solution.py:225
  380.4 1.6 convolution_bitcast_fusion.4
  383.1 1.7 multiply_convert_fusion.2
  395.0 1.6 convolution_bitcast_fusion.4
  397.7 1.7 multiply_convert_fusion.2
  412.2 1.7 multiply_convert_fusion.2
  426.7 1.7 multiply_convert_fusion.2
  441.2 1.7 multiply_convert_fusion.2
  455.7 1.7 multiply_convert_fusion.2
  470.2 1.7 multiply_convert_fusion.2
  482.0 1.6 convolution_bitcast_fusion.4
  484.7 1.7 multiply_convert_fusion.2
  492.5 5.3 broadcast_in_dim.151
  497.8 17.6 %scatter_fusion = bf16[128,2,128,128]{3,2,1,0:T(8,128)(2,1)} fusion(bf16[128,2,128,128]{3,2,1,0:T(8,128)(2,1)} %broadcast_in_dim.151, s32[96]{0:T(128)S(1)} %fusion.75, bf16[96,2,128,128]{3,2,1,0:T(8,128)(2,1)} %bitcast.341), kind=kCustom, calls=%fused_computation.2 | custom fusion | bytes 18874752 | tf_op jit(solution)/shard_map/scatter | solution.py:253
  515.4 6.4 all-to-all-start.1
  521.9 3.5 fusion.79
  525.3 3.4 collective-permute-start.2
  528.7 4.3 collective-permute-start.3
  533.5 7.4 copy.227
  540.8 3.1 slice.214
  543.9 1.9 copy.226
  545.8 1.9 copy.220
  547.8 1.8 copy_bitcast_fusion.2
  549.6 202.9 %collective-permute-done.2 = f32[8,2,1,128,128]{4,2,3,1,0:T(1,128)S(1)} collective-permute-done((f32[8,2,1,128,128]{4,2,3,1,0:T(1,128)}, f32[8,2,1,128,128]{4,2,3,1,0:T(1,128)S(1)}, u32[]{:S(2)}, u32[]{:S(2)}) %collective-permute-start.2) | collective-permute-done | bytes 1048608 | tf_op jit(solution)/shard_map/ppermute | solution.py:39
  753.4 3.4 add.204
  756.8 28.4 %scatter-add.14 = f32[8,2,4,128,128]{4,2,3,1,0:T(4,128)} dynamic-update-slice(f32[8,2,4,128,128]{4,2,3,1,0:T(4,128)} %slice.214, f32[8,2,1,128,128]{4,2,3,1,0:T(1,128)S(1)} %add.204, s32[]{:T(128)} %constant.208.clone.1, s32[]{:T(128)} %constant.208.clone.1, s32[]{:T(128)} %constant.208.clone.1, s32[]{:T(128)} %constant.208.clone.1, s32[]{:T(128)} %constant.208.clone.1) | dynamic-update-slice | bytes 2097156 | tf_op jit(solution)/shard_map/scatter-add | solution.py:237
  785.2 3.9 slice_add_fusion
  789.1 28.2 %scatter-add.18 = f32[8,2,4,128,128]{4,2,3,1,0:T(4,128)} dynamic-update-slice(f32[8,2,4,128,128]{4,2,3,1,0:T(4,128)} %scatter-add.14, f32[8,2,1,128,128]{4,2,3,1,0:T(1,128)S(1)} %slice_add_fusion, s32[]{:T(128)} %constant.208.clone.1, s32[]{:T(128)} %constant.208.clone.1, s32[]{:T(128)} %constant.214.clone.1, s32[]{:T(128)} %constant.208.clone.1, s32[]{:T(128)} %constant.208.clone.1) | dynamic-update-slice | bytes 2097156 | tf_op jit(solution)/shard_map/scatter-add | solution.py:239
  817.3 11.2 %bitcast_convert_fusion = f32[128,2,128,128]{3,2,1,0:T(8,128)} fusion(bf16[16,8,2,128,128]{4,3,2,1,0:T(8,128)(2,1)} %all-to-all-done.1), kind=kLoop, calls=%fused_computation.100 | loop fusion | flops 4194304 | bytes 25165824 | tf_op jit(solution)/shard_map/convert_element_type | solution.py:262
  828.5 2.4 broadcast_in_dim.150
  831.0 37.2 %scatter_fusion.1 = f32[32,2,128,128]{3,2,1,0:T(8,128)} fusion(f32[32,2,128,128]{3,2,1,0:T(8,128)} %broadcast_in_dim.150, s32[128]{0:T(128)S(1)} %fusion.76, f32[128,2,128,128]{3,2,1,0:T(8,128)} %bitcast_convert_fusion), kind=kCustom, calls=%fused_computation.3 | custom fusion | flops 4194304 | bytes 50332160 | tf_op jit(solution)/shard_map/scatter-add | solution.py:261
  868.2 11.2 %fusion.54 = bf16[8,2,4,128,128]{4,2,3,1,0:T(4,128)(2,1)S(1)} fusion(f32[8,2,4,128,128]{4,2,3,1,0:T(4,128)} %scatter-add.18, f32[4,8,2,128,128]{4,3,2,1,0:T(8,128)} %bitcast.329, f32[8,2,2,128,128]{4,2,3,1,0:T(2,128)} %all-reduce.8.cloned.1.call-done, s32[4]{0:T(128)S(1)} %copy-done.16, s32[2]{0:T(128)S(1)} %copy-done.14), kind=kOutput, calls=%fused_computation.102 | convolution fusion | flops 28311560 | bytes 12582936 | tf_op jit(solution)/shard_map/gi,hcgbd->hcibd/dot_general | solution.py:244
  881.6 1.8 copy_bitcast_fusion
  (330 shorter events, 162.9 us)
Async XLA Ops:
  7.2 0.7 copy-start
  7.2 5.5 copy-start.5
  8.3 4.7 copy-start.11
  10.9 2.1 copy-start.9
  20.2 7.3 copy-start.13
  20.2 14.4 %copy-start.4 = (bf16[512,1024]{1,0:T(8,128)(2,1)S(1)}, bf16[512,1024]{1,0:T(8,128)(2,1)}, u32[]{:S(2)}) copy-start(bf16[512,1024]{1,0:T(8,128)(2,1)} %param.15) | copy-start | bytes 3145732
  20.2 288.1 %all-to-all-start = ((bf16[16,8,2,128,128]{4,3,2,1,0:T(8,128)(2,1)}), bf16[16,8,2,128,128]{4,3,2,1,0:T(8,128)(2,1)}, u32[]{:S(2)}, u32[]{:S(2)}) async-start(bf16[16,8,2,128,128]{4,3,2,1,0:T(8,128)(2,1)} %bitcast.332), calls=%async_computation | async-start | bytes 16777216 | tf_op jit(solution)/shard_map/all_to_all | solution.py:109
  27.5 276.3 %all-reduce.10.cloned.1.call-start = ((), (), s32[]{:S(2)}) async-start(), calls=%async_computation.3 | async-start | bytes 2097152 | tf_op jit(solution)/shard_map/psum | solution.py:33
  35.2 2.0 copy-start.2
  35.7 1.7 copy-start.3
  35.8 9.4 %copy-start.7 = (bf16[512,1024]{1,0:T(8,128)(2,1)S(1)}, bf16[512,1024]{1,0:T(8,128)(2,1)}, u32[]{:S(2)}) copy-start(bf16[512,1024]{1,0:T(8,128)(2,1)} %param.14) | copy-start | bytes 3145732
  37.4 8.1 copy-start.8
  37.4 205.1 %collective-permute-start = (bf16[2,128,1024]{1,2,0:T(8,128)(2,1)}, bf16[2,128,1024]{1,2,0:T(8,128)(2,1)}, u32[]{:S(2)}, u32[]{:S(2)}) collective-permute-start(bf16[2,128,1024]{1,2,0:T(8,128)(2,1)} %get-tuple-element.372), channel_id=1, source_target_pairs={{0,2},{2,4},{4,6},{6,8},{8,10},{10,12},{12,14},{14,16},{16,18},{18... | collective-permute-start | bytes 1572872 | tf_op jit(solution)/shard_map/ppermute | solution.py:23
  40.9 201.6 %collective-permute-start.1 = (bf16[2,128,1024]{1,2,0:T(8,128)(2,1)}, bf16[2,128,1024]{1,2,0:T(8,128)(2,1)}, u32[]{:S(2)}, u32[]{:S(2)}) collective-permute-start(bf16[2,128,1024]{1,2,0:T(8,128)(2,1)} %get-tuple-element.373), channel_id=1, source_target_pairs={{2,0},{4,2},{6,4},{8,6},{10,8},{12,10},{14,12},{16,14},{18,16},{20... | collective-permute-start | bytes 1572872 | tf_op jit(solution)/shard_map/ppermute | solution.py:26
  48.4 0.6 copy-start.15
  515.4 301.9 %all-to-all-start.1 = ((bf16[16,8,2,128,128]{4,3,2,1,0:T(8,128)(2,1)}), bf16[16,8,2,128,128]{4,3,2,1,0:T(8,128)(2,1)}, u32[]{:S(2)}, u32[]{:S(2)}) async-start(bf16[16,8,2,128,128]{4,3,2,1,0:T(8,128)(2,1)} %bitcast.330), calls=%async_computation.1 | async-start | bytes 16777216 | tf_op jit(solution)/shard_map/all_to_all | solution.py:256
  521.8 346.4 %all-reduce.8.cloned.1.call-start = ((), (), s32[]{:S(2)}) async-start(), calls=%async_computation.2 | async-start | bytes 4194304 | tf_op jit(solution)/shard_map/psum | solution.py:240
  521.8 11.2 %copy-start.12 = (pred[16,96]{1,0:T(8,128)(4,1)S(1)}, pred[16,96]{1,0:T(8,128)(4,1)}, u32[]{:S(2)}) copy-start(pred[16,96]{1,0:T(8,128)(4,1)} %copy-done.11) | copy-start | bytes 4612
  521.8 11.5 %copy-start.10 = (s32[16,8]{1,0:T(8,128)S(1)}, s32[16,8]{1,0:T(8,128)}, u32[]{:S(2)}) copy-start(s32[16,8]{1,0:T(8,128)} %copy-done.9) | copy-start | bytes 1540
  525.3 227.1 %collective-permute-start.2 = (f32[8,2,1,128,128]{4,2,3,1,0:T(1,128)}, f32[8,2,1,128,128]{4,2,3,1,0:T(1,128)S(1)}, u32[]{:S(2)}, u32[]{:S(2)}) collective-permute-start(f32[8,2,1,128,128]{4,2,3,1,0:T(1,128)} %bitcast.73), channel_id=1, source_target_pairs={{0,2},{2,4},{4,6},{6,8},{8,10},{10,12},{12,14},{14,16},{16,18},{18... | collective-permute-start | bytes 3145736 | tf_op jit(solution)/shard_map/ppermute | solution.py:39
  528.7 256.5 %collective-permute-start.3 = (f32[8,2,1,128,128]{4,2,3,1,0:T(1,128)}, f32[8,2,1,128,128]{4,2,3,1,0:T(1,128)S(1)}, u32[]{:S(2)}, u32[]{:S(2)}) collective-permute-start(f32[8,2,1,128,128]{4,2,3,1,0:T(1,128)} %bitcast.74), channel_id=1, source_target_pairs={{2,0},{4,2},{6,4},{8,6},{10,8},{12,10},{14,12},{16,14},{18,16},{20... | collective-permute-start | bytes 3145736 | tf_op jit(solution)/shard_map/ppermute | solution.py:39
  752.5 1.0 copy-start.6
  831.0 37.2 %copy-start.14 = (s32[2]{0:T(128)S(1)}, s32[2]{0:T(128)}, u32[]{:S(2)}) copy-start(s32[2]{0:T(128)} %param.19) | copy-start | bytes 28
  831.0 37.2 %copy-start.16 = (s32[4]{0:T(128)S(1)}, s32[4]{0:T(128)}, u32[]{:S(2)}) copy-start(s32[4]{0:T(128)} %copy-done.15) | copy-start | bytes 52
  881.6 1.9 copy-start.1
Sparse Core Ops, SparseCore 0:
  45.3 258.4 all-reduce.9
  544.1 257.2 all-reduce.7
where the time goes:
time: 900 us; the launch traced here: 890 us
  waiting for transfers between devices  449 us (50%)
  local copies, waits for them, and re-layouts  198 us (22%)
  other arithmetic  102 us (11%)
  matrix products  90.4 us (10%)
  starting transfers between devices  29.1 us (3%)
  between operations  21.2 us (2%)
    ppermute x2, waiting for transfers between devices, from_behind(): lax.ppermute(value, axis, [(source, source + steps) for source in range(i...  203 us
    ppermute x1, waiting for transfers between devices, with_halo(): lax.ppermute(lax.slice_in_dim(block, block.shape[dim] - width, None, axis...  193 us
    psum x1, waiting for transfers between devices, spread_2(): return lax.psum(jnp.where(mine, array, jnp.zeros_like(array)), axis)  52.7 us
    scatter-add x1, other arithmetic, body(): gathered = jnp.zeros((blocks_here * heads_here, 2, block_size, head_size)...  37.2 us
    scatter-add x1, local copies, waits for them, and re-layouts, body(): center = center.at[:, :, :half_width].add(moved_rim)  28.4 us
    scatter-add x1, local copies, waits for them, and re-layouts, body(): center = center.at[:, :, blocks_here - half_width:].add(moved_rim)  28.2 us
    dot_general x16, matrix products, softmax_weights(): jnp.einsum('zjs,zcls->zjcl', query_per_head, listed_blocks[0], preferred_...  21.9 us
    while x64, local copies, waits for them, and re-layouts  21.7 us
  transfers between devices with their start and end apart: 8, of which 3 were waited for; matrix products, arithmetic and copies ran while one was open for 17% of the time, Pallas kernels for 0%

commit v1 on v0

v1 whole, which is shorter than its diff:
```python
import math

import jax
import jax.numpy as jnp
from jax import lax
from jax.experimental import pallas as pl
from jax.experimental.pallas import tpu as pltpu
from jax.sharding import PartitionSpec as P

BLOCK = 128
DH = 128
RAND = 3
GLOB = 2
WMAX = 1
SPAN = 2 * WMAX + 1
LISTED = SPAN + RAND + GLOB
PLANES = 4
PARTS = 2
ROWS = BLOCK // PARTS
SCALE = 1.0 / math.sqrt(DH)
MASKED = -1e30
VMEM_BYTES = 48 * 1024 * 1024

NT = (((1,), (1,)), ((), ()))
NN = (((1,), (0,)), ((), ()))
TN = (((0,), (0,)), ((), ()))

SMEM = pltpu.SMEM
ANY = pl.ANY


def dot(a, b, dims):
    return lax.dot_general(a, b, dims, preferred_element_type=jnp.float32)


def params():
    return pltpu.CompilerParams(vmem_limit_bytes=VMEM_BYTES)


def smem_spec():
    return pl.BlockSpec(memory_space=SMEM)


def any_spec():
    return pl.BlockSpec(memory_space=ANY)


def pick_blocks(column, table, glob_info, heads, lanes, slots):
    rows = column.shape[1]

    def kernel(table_ref, info_ref, column_ref, *outs):
        for partner in range(lanes):

            def step(slot, carry, partner=partner):
                index = jnp.maximum(table_ref[partner * slots + slot], 0)
                lane = pl.multiple_of((index % heads) * DH, DH)
                outs[partner][slot] = column_ref[index // heads, :, pl.ds(lane, DH)]
                return carry

            lax.fori_loop(0, slots, step, 0)
        for glob in range(GLOB):
            block = column_ref[info_ref[2 * glob]]
            mine = info_ref[2 * glob + 1] > 0
            outs[lanes][glob] = jnp.where(mine, block, jnp.zeros_like(block))

    vmem = pl.BlockSpec(memory_space=pltpu.VMEM)
    return pl.pallas_call(
        kernel,
        out_shape=[jax.ShapeDtypeStruct((slots, rows, DH), column.dtype)] * lanes
        + [jax.ShapeDtypeStruct((GLOB, rows, column.shape[2]), column.dtype)],
        in_specs=[smem_spec(), smem_spec(), vmem],
        out_specs=[vmem] * (lanes + 1),
        compiler_params=params(),
        cost_estimate=pl.CostEstimate(flops=0, bytes_accessed=4 * column.size, transcendentals=0),
    )(table, glob_info, column)


def sum_blocks(returned, glob_sum, table, glob_info, part, blocks, heads, slots):
    lanes = len(returned)
    rows = returned[0].shape[1]
    width = glob_sum.shape[2]

    def kernel(table_ref, info_ref, glob_ref, *rest):
        refs, out_ref, total = rest[:lanes], rest[lanes], rest[lanes + 1]
        total[...] = jnp.zeros_like(total)
        for partner in range(lanes):

            def step(slot, carry, partner=partner):
                index = table_ref[partner * slots + slot]

                @pl.when(index >= 0)
                def _():
                    lane = pl.multiple_of((index % heads) * DH, DH)
                    row = index // heads
                    total[row, :, pl.ds(lane, DH)] += refs[partner][slot].astype(jnp.float32)

                return carry

            lax.fori_loop(0, slots, step, 0)
        for glob in range(GLOB):

            @pl.when(info_ref[2 * glob + 1] > 0)
            def _(glob=glob):
                total[info_ref[2 * glob]] += glob_ref[glob].astype(jnp.float32)

        out_ref[...] = total[...].astype(out_ref.dtype)

    vmem = pl.BlockSpec(memory_space=pltpu.VMEM)
    shape = (blocks, rows, width)
    return pl.pallas_call(
        kernel,
        grid=(1,),
        out_shape=jax.ShapeDtypeStruct(shape, jnp.bfloat16),
        in_specs=[
            smem_spec(),
            smem_spec(),
            pl.BlockSpec((GLOB, rows, width), lambda g: (0, part, 0)),
        ]
        + [vmem] * lanes,
        out_specs=vmem,
        scratch_shapes=[pltpu.VMEM(shape, jnp.float32)],
        compiler_params=params(),
        cost_estimate=pl.CostEstimate(
            flops=0, bytes_accessed=8 * blocks * rows * width, transcendentals=0
        ),
    )(table, glob_info, glob_sum, *returned)


def copy_parts(refs, buffer, sems, lanes, slots, outward):
    copies = []
    for partner in range(lanes):
        for part in range(PARTS):
            number = partner * PARTS + part
            inside = buffer.at[pl.ds(partner * slots, slots), pl.ds(part * ROWS, ROWS)]
            pair = (inside, refs[number]) if outward else (refs[number], inside)
            copies.append(pltpu.make_async_copy(*pair, sems.at[number]))
    return copies


def run_copies(copies):
    for copy in copies:
        copy.start()
    for copy in copies:
        copy.wait()


def weights_kernel(lanes, slots, heads, blocks):
    count = lanes * PARTS

    def kernel(pick, ends, q_ref, g_ref, k_ref, kl_ref, kh_ref, kg_ref, *rest):
        kr_refs, rest = rest[:count], rest[count:]
        p_ref, own_ref, low_ref, high_ref, glob_ref = rest[:5]
        pay_refs, rest = rest[5 : 5 + count], rest[5 + count :]
        rand, pay, band, band_sum, glob_sum, sems = rest
        head = pl.program_id(0)

        @pl.when(head == 0)
        def _():
            run_copies(copy_parts(kr_refs, rand, sems, lanes, slots, False))

        band[:BLOCK] = kl_ref[...]
        band[BLOCK : BLOCK * (blocks + 1)] = k_ref[...]
        band[BLOCK * (blocks + 1) :] = kh_ref[...]
        band_sum[...] = jnp.zeros_like(band_sum)
        for block in range(blocks):
            here = slice(block * BLOCK, (block + 1) * BLOCK)
            near = slice(block * BLOCK, (block + SPAN) * BLOCK)
            query = q_ref[here]
            grad = g_ref[here]
            entry = (head * blocks + block) * RAND
            places = [pick[entry + r] for r in range(RAND)]
            window = dot(band[near], query, NT)
            scores = [window[o * BLOCK : (o + 1) * BLOCK] for o in range(SPAN)]
            if block == 0:
                scores[0] = jnp.where(ends[0] > 0, MASKED, scores[0])
            if block == blocks - 1:
                scores[-1] = jnp.where(ends[1] > 0, MASKED, scores[-1])
            scores += [dot(rand[at], query, NT) for at in places]
            scores += [dot(kg_ref[g], query, NT) for g in range(GLOB)]
            peak = scores[0]
            for score in scores[1:]:
                peak = jnp.maximum(peak, score)
            peak = jnp.max(peak, axis=0, keepdims=True)
            powers = [jnp.exp((score - peak) * SCALE) for score in scores]
            total = powers[0]
            for power in powers[1:]:
                total = total + power
            inverse = 1.0 / jnp.sum(total, axis=0, keepdims=True)
            for number, power in enumerate(powers):
                weights = (power * inverse).astype(jnp.bfloat16)
                p_ref[0, block, number * BLOCK : (number + 1) * BLOCK] = weights
            band_sum[near] += dot(p_ref[0, block, : SPAN * BLOCK], grad, NN)
            for r, at in enumerate(places):
                start = (SPAN + r) * BLOCK
                term = dot(p_ref[0, block, start : start + BLOCK], grad, NN)
                pay[at] = term.astype(jnp.bfloat16)
            term = dot(p_ref[0, block, (SPAN + RAND) * BLOCK :], grad, NN)
            if block == 0:
                glob_sum[...] = term
            else:
                glob_sum[...] += term
        own_ref[...] = band_sum[BLOCK : BLOCK * (blocks + 1)]
        low_ref[...] = band_sum[:BLOCK].astype(jnp.bfloat16)
        high_ref[...] = band_sum[BLOCK * (blocks + 1) :].astype(jnp.bfloat16)
        for g in range(GLOB):
            glob_ref[g] = glob_sum[g * BLOCK : (g + 1) * BLOCK].astype(jnp.bfloat16)

        @pl.when(head == heads - 1)
        def _():
            run_copies(copy_parts(pay_refs, pay, sems, lanes, slots, True))

    return kernel


def gradient_kernel(lanes, slots, heads, blocks):
    count = lanes * PARTS

    def kernel(pick, q_ref, g_ref, p_ref, k_ref, kl_ref, kh_ref, kg_ref, *rest):
        v_ref, vl_ref, vh_ref, vg_ref = rest[:4]
        kr_refs, vr_refs = rest[4 : 4 + count], rest[4 + count : 4 + 2 * count]
        rest = rest[4 + 2 * count :]
        out_ref, dq_ref, own_ref, low_ref, high_ref, glob_ref = rest[:6]
        pay_refs, rest = rest[6 : 6 + count], rest[6 + count :]
        k_rand, v_rand, pay, k_band, v_band, band_sum, glob_sum, sems, more = rest
        head = pl.program_id(0)

        @pl.when(head == 0)
        def _():
            run_copies(
                copy_parts(kr_refs, k_rand, sems, lanes, slots, False)
                + copy_parts(vr_refs, v_rand, more, lanes, slots, False)
            )

        for band, low, own, high in (
            (k_band, kl_ref, k_ref, kh_ref),
            (v_band, vl_ref, v_ref, vh_ref),
        ):
            band[:BLOCK] = low[...]
            band[BLOCK : BLOCK * (blocks + 1)] = own[...]
            band[BLOCK * (blocks + 1) :] = high[...]
        band_sum[...] = jnp.zeros_like(band_sum)
        for block in range(blocks):
            here = slice(block * BLOCK, (block + 1) * BLOCK)
            near = slice(block * BLOCK, (block + SPAN) * BLOCK)
            query = q_ref[here]
            grad = g_ref[here]
            entry = (head * blocks + block) * RAND
            places = [pick[entry + r] for r in range(RAND)]
            value_blocks = [v_band[near]] + [v_rand[at] for at in places]
            key_blocks = [k_band[near]] + [k_rand[at] for at in places]
            value_blocks += [vg_ref[g] for g in range(GLOB)]
            key_blocks += [kg_ref[g] for g in range(GLOB)]
            starts = [0] + [(SPAN + n) * BLOCK for n in range(RAND + GLOB + 1)]
            weights = [p_ref[0, block, a:b] for a, b in zip(starts[:-1], starts[1:])]
            result = dot(weights[0], value_blocks[0], TN)
            for weight, value in zip(weights[1:], value_blocks[1:]):
                result = result + dot(weight, value, TN)
            out_ref[here] = result.astype(jnp.bfloat16)
            slopes = [dot(value, grad, NT) for value in value_blocks]
            wide = [weight.astype(jnp.float32) for weight in weights]
            delta = 0.0
            for weight, slope in zip(wide, slopes):
                delta = delta + jnp.sum(weight * slope, axis=0, keepdims=True)
            narrow = [
                (weight * (slope - delta)).astype(jnp.bfloat16)
                for weight, slope in zip(wide, slopes)
            ]
            for r, at in enumerate(places):
                pay[at] = (dot(narrow[1 + r], query, NN) * SCALE).astype(jnp.bfloat16)
            result = dot(narrow[0], key_blocks[0], TN)
            for slope, key in zip(narrow[1:], key_blocks[1:]):
                result = result + dot(slope, key, TN)
            dq_ref[here] = (result * SCALE).astype(jnp.bfloat16)
            band_sum[near] += dot(narrow[0], query, NN)
            for g in range(GLOB):
                term = dot(narrow[1 + RAND + g], query, NN)
                if block == 0:
                    glob_sum[g] = term
                else:
                    glob_sum[g] += term
        own_ref[...] = band_sum[BLOCK : BLOCK * (blocks + 1)] * SCALE
        low_ref[...] = (band_sum[:BLOCK] * SCALE).astype(jnp.bfloat16)
        high_ref[...] = (band_sum[BLOCK * (blocks + 1) :] * SCALE).astype(jnp.bfloat16)
        glob_ref[...] = (glob_sum[...] * SCALE).astype(jnp.bfloat16)

        @pl.when(head == heads - 1)
        def _():
            run_copies(copy_parts(pay_refs, pay, sems, lanes, slots, True))

    return kernel


def body(queries, keys, values, out_grad, rand_ids, glob_ids):
    rows_here, width = queries.shape
    heads = width // DH
    blocks = rows_here // BLOCK
    shards = lax.axis_size("seq")
    planes = PLANES
    lanes = shards // planes
    place = lax.axis_index("seq")
    group = lax.axis_index("head")
    plane, lane = place // lanes, place % lanes
    columns = [[z * lanes + c for z in range(planes)] for c in range(lanes)]
    entries = heads * blocks * RAND
    cap = max(2, (5 * entries + 4 * shards - 1) // (4 * shards))
    slots = planes * cap
    total_slots = lanes * slots
    forward = [(i, i + 1) for i in range(shards - 1)]
    backward = [(i + 1, i) for i in range(shards - 1)]

    def swap(array, bits):
        return lax.ppermute(array, "seq", [(i, i ^ bits) for i in range(shards)])

    def to_partners(arrays):
        return [arrays[0]] + [swap(arrays[k], k) for k in range(1, lanes)]

    def plane_sum(array):
        bits = 1
        while bits < lanes:
            other = swap(array, bits)
            wide = array.astype(jnp.float32) + other.astype(jnp.float32)
            array = wide.astype(jnp.bfloat16)
            bits *= 2
        return array

    tail = jnp.stack([keys[-BLOCK:], values[-BLOCK:]])
    front = jnp.stack([keys[:BLOCK], values[:BLOCK]])
    low_pair = lax.ppermute(tail, "seq", forward)
    high_pair = lax.ppermute(front, "seq", backward)

    ids_mine = lax.dynamic_slice_in_dim(rand_ids, group * heads, heads, 0)
    ids_plane = lax.dynamic_slice_in_dim(ids_mine, plane * lanes * blocks, lanes * blocks, 1)
    wanted = (
        ids_plane.reshape(heads, lanes, blocks, RAND).transpose(1, 0, 2, 3).reshape(lanes, entries)
    )
    source = wanted // blocks
    same = source[:, :, None] == source[:, None, :]
    before = jnp.tril(jnp.ones((entries, entries), bool), -1)
    slot = jnp.sum((same & before[None]).astype(jnp.int32), axis=2)
    source_plane, source_lane = source // lanes, source % lanes
    spot = source_plane * cap + slot
    pick = ((source_lane ^ lane) * slots + spot)[lane]
    head_of = jnp.arange(entries, dtype=jnp.int32) // (blocks * RAND)
    inside = (source_plane * blocks + wanted % blocks) * heads + head_of[None, :]
    hit = (source_lane == lane)[:, :, None] & (
        spot[:, :, None] == jnp.arange(slots, dtype=jnp.int32)[None, None, :]
    )
    table = jnp.sum(jnp.where(hit, inside[:, :, None] + 1, 0), axis=1) - 1
    partners = jnp.arange(lanes, dtype=jnp.int32) ^ lane
    table = table[partners].reshape(-1)
    glob_place = glob_ids // blocks
    glob_info = jnp.stack(
        [
            (glob_place // lanes) * blocks + glob_ids % blocks,
            (glob_place % lanes == lane).astype(jnp.int32),
        ],
        axis=1,
    ).reshape(-1)
    ends = jnp.stack([place == 0, place == shards - 1]).astype(jnp.int32)

    def fetch(array, after):
        received = []
        globals_here = []
        cut = array.reshape(blocks, BLOCK, width)
        for part in range(PARTS):
            piece = cut[:, part * ROWS : (part + 1) * ROWS]
            if after is not None:
                piece, after = lax.optimization_barrier((piece, after))
            column = lax.all_gather(piece, "seq", axis_index_groups=columns)
            after = column
            column = column.reshape(planes * blocks, ROWS, width)
            outs = pick_blocks(column, table, glob_info, heads, lanes, slots)
            received.append(to_partners(outs[:lanes]))
            globals_here.append(plane_sum(outs[lanes]))
        flat = [received[part][k] for k in range(lanes) for part in range(PARTS)]
        return flat, jnp.concatenate(globals_here, axis=1), after

    key_rand, key_glob, after = fetch(keys, None)
    value_rand, value_glob, after = fetch(values, after)

    head_block = pl.BlockSpec((rows_here, DH), lambda h: (0, h))
    rim_block = pl.BlockSpec((BLOCK, DH), lambda h: (0, h))
    glob_block = pl.BlockSpec((GLOB, BLOCK, DH), lambda h: (0, 0, h))
    weight_block = pl.BlockSpec((1, blocks, LISTED * BLOCK, BLOCK), lambda h: (h, 0, 0, 0))
    count = lanes * PARTS
    pay_shape = jax.ShapeDtypeStruct((slots, ROWS, DH), jnp.bfloat16)
    pool = pltpu.VMEM((total_slots, BLOCK, DH), jnp.bfloat16)
    band = pltpu.VMEM(((blocks + 2 * WMAX) * BLOCK, DH), jnp.bfloat16)
    band_sum = pltpu.VMEM(((blocks + 2 * WMAX) * BLOCK, DH), jnp.float32)
    like = jax.ShapeDtypeStruct((rows_here, width), jnp.bfloat16)
    wide_like = jax.ShapeDtypeStruct((rows_here, width), jnp.float32)
    rim_like = jax.ShapeDtypeStruct((BLOCK, width), jnp.bfloat16)
    glob_like = jax.ShapeDtypeStruct((GLOB, BLOCK, width), jnp.bfloat16)
    product = 2 * heads * blocks * LISTED * BLOCK * BLOCK * DH

    outs = pl.pallas_call(
        weights_kernel(lanes, slots, heads, blocks),
        grid=(heads,),
        out_shape=[
            jax.ShapeDtypeStruct((heads, blocks, LISTED * BLOCK, BLOCK), jnp.bfloat16),
            wide_like,
            rim_like,
            rim_like,
            glob_like,
        ]
        + [pay_shape] * count,
        in_specs=[smem_spec(), smem_spec(), head_block, head_block, head_block]
        + [rim_block, rim_block, glob_block]
        + [any_spec()] * count,
        out_specs=[weight_block, head_block, rim_block, rim_block, glob_block]
        + [any_spec()] * count,
        scratch_shapes=[
            pool,
            pool,
            band,
            band_sum,
            pltpu.VMEM((GLOB * BLOCK, DH), jnp.float32),
            pltpu.SemaphoreType.DMA((count,)),
        ],
        compiler_params=params(),
        cost_estimate=pl.CostEstimate(
            flops=8 * product, bytes_accessed=2**24, transcendentals=product // 256
        ),
    )(pick, ends, queries, out_grad, keys, low_pair[0], high_pair[0], key_glob, *key_rand)
    weights, value_own, value_low, value_high, value_globs = outs[:5]
    value_terms = outs[5:]

    def give_back(terms, own, low, high, globs):
        low_in = lax.ppermute(high, "seq", forward)
        high_in = lax.ppermute(low, "seq", backward)
        glob_sum = plane_sum(globs)
        sums = []
        for part in range(PARTS):
            returned = to_partners([terms[k * PARTS + part] for k in range(lanes)])
            dense = sum_blocks(
                returned, glob_sum, table, glob_info, part, planes * blocks, heads, slots
            )
            sums.append(
                lax.psum_scatter(
                    dense, "seq", scatter_dimension=0, axis_index_groups=columns, tiled=True
                )
            )
        total = own.reshape(blocks, BLOCK, width) + jnp.concatenate(sums, axis=1).astype(
            jnp.float32
        )
        total = total.at[0].add(low_in.astype(jnp.float32))
        total = total.at[-1].add(high_in.astype(jnp.float32))
        return total.astype(jnp.bfloat16).reshape(rows_here, width)

    value_grad = give_back(value_terms, value_own, value_low, value_high, value_globs)

    outs = pl.pallas_call(
        gradient_kernel(lanes, slots, heads, blocks),
        grid=(heads,),
        out_shape=[like, like, wide_like, rim_like, rim_like, glob_like] + [pay_shape] * count,
        in_specs=[smem_spec(), head_block, head_block, weight_block]
        + [head_block, rim_block, rim_block, glob_block] * 2
        + [any_spec()] * (2 * count),
        out_specs=[head_block, head_block, head_block, rim_block, rim_block, glob_block]
        + [any_spec()] * count,
        scratch_shapes=[
            pool,
            pool,
            pool,
            band,
            band,
            band_sum,
            pltpu.VMEM((GLOB, BLOCK, DH), jnp.float32),
            pltpu.SemaphoreType.DMA((count,)),
            pltpu.SemaphoreType.DMA((count,)),
        ],
        compiler_params=params(),
        cost_estimate=pl.CostEstimate(
            flops=16 * product, bytes_accessed=2**25, transcendentals=0
        ),
    )(
        pick,
        queries,
        out_grad,
        weights,
        keys,
        low_pair[0],
        high_pair[0],
        key_glob,
        values,
        low_pair[1],
        high_pair[1],
        value_glob,
        *key_rand,
        *value_rand,
    )
    out, query_grad, key_own, key_low, key_high, key_globs = outs[:6]
    key_grad = give_back(outs[6:], key_own, key_low, key_high, key_globs)
    return out, query_grad, key_grad, value_grad


def solution(mesh):
    return jax.shard_map(
        body,
        mesh=mesh,
        in_specs=(P("seq", "head"), P("seq", "head"), P("seq", "head"), P("seq", "head"), P(), P()),
        out_specs=(P("seq", "head"), P("seq", "head"), P("seq", "head"), P("seq", "head")),
        check_vma=False,
    )
```

time: 900 us -> 548 us (0.61)
  local copies, waits for them, and re-layouts: 198 us -> 21.8 us
  waiting for transfers between devices: 449 us -> 323 us
  matrix products: 90.4 us -> 0 us
  Pallas kernels: 0 us -> 82.7 us
  other arithmetic: 102 us -> 20.4 us
  starting transfers between devices: 29.1 us -> 82.3 us
    ppermute x4 -> x42, waiting for transfers between devices: 396 us -> 184 us  [the longest x36 184 us: swap(): return lax.ppermute(array, 'seq', [(i, i ^ bits) for i in range(shards)])]
    dot_general x57 -> x0, matrix products: 90.4 us -> none  [the longest x16 21.9 us: softmax_weights(): jnp.einsum('zjs,zcls->zjcl', query_per_head, listed_blocks[0], preferred_...]
    pallas_call x0 -> x10, Pallas kernels: none -> 82.7 us  [the longest x1 27.2 us: body(): pl.pallas_call(gradient_kernel(lanes, slots, heads, blocks), grid=(heads,...]
    all_gather x0 -> x4, waiting for transfers between devices: none -> 80.8 us  [fetch(): column = lax.all_gather(piece, 'seq', axis_index_groups=columns)]
    ppermute x4 -> x42, starting transfers between devices: 15.4 us -> 81.8 us  [the longest x36 58.4 us: swap(): return lax.ppermute(array, 'seq', [(i, i ^ bits) for i in range(shards)])]
    reduce_scatter x0 -> x4, waiting for transfers between devices: none -> 57.3 us  [give_back(): lax.psum_scatter(dense, 'seq', scatter_dimension=0, axis_index_groups=col...]
    scatter-add x2 -> x0, local copies, waits for them, and re-layouts: 56.5 us -> none  [the longest x1 28.4 us: body(): center = center.at[:, :, :half_width].add(moved_rim)]
    psum x2 -> x0, waiting for transfers between devices: 52.7 us -> none  [the longest x1 52.7 us: spread_2(): return lax.psum(jnp.where(mine, array, jnp.zeros_like(array)), axis)]
  transfers between devices with their start and end apart: 8 -> 50, of which waited for: 3 -> 22; matrix products, arithmetic and copies ran while one was open for 17% -> 4% of each run, Pallas kernels for 0% -> 15%
where the time goes in v1:
time: 548 us; the launch traced here: 545 us
  waiting for transfers between devices  323 us (59%)
  Pallas kernels  82.7 us (15%)
  starting transfers between devices  82.3 us (15%)
  local copies, waits for them, and re-layouts  21.8 us (4%)
  other arithmetic  20.4 us (4%)
  between operations  14.8 us (3%)
    ppermute x36, waiting for transfers between devices, swap(): return lax.ppermute(array, 'seq', [(i, i ^ bits) for i in range(shards)])  184 us
    all_gather x4, waiting for transfers between devices, fetch(): column = lax.all_gather(piece, 'seq', axis_index_groups=columns)  80.8 us
    ppermute x36, starting transfers between devices, swap(): return lax.ppermute(array, 'seq', [(i, i ^ bits) for i in range(shards)])  58.4 us
    reduce_scatter x4, waiting for transfers between devices, give_back(): lax.psum_scatter(dense, 'seq', scatter_dimension=0, axis_index_groups=col...  57.3 us
    pallas_call x1, Pallas kernels, body(): pl.pallas_call(gradient_kernel(lanes, slots, heads, blocks), grid=(heads,...  27.2 us
    pallas_call x1, Pallas kernels, body(): pl.pallas_call(weights_kernel(lanes, slots, heads, blocks), grid=(heads,)...  23.4 us
    pallas_call x4, Pallas kernels, sum_blocks(): pl.pallas_call(kernel, grid=(1,), out_shape=jax.ShapeDtypeStruct(shape, j...  21.2 us
    unnamed x91, local copies, waits for them, and re-layouts  15.2 us
  transfers between devices with their start and end apart: 50, of which 22 were waited for; matrix products, arithmetic and copies ran while one was open for 4% of the time, Pallas kernels for 15%

profile of v1, /device:TPU:16, one launch (start us, length us, event | category | flops | bytes accessed | tf_op | source)
XLA Modules:
  0.0 545.2 jit_solution(16043886425851924014)
XLA Ops:
  7.2 2.3 fusion.17
  11.7 4.2 collective-permute-start.1
  18.0 45.7 %all-gather.9.cloned.1.call-done.column_ref = bf16[16,64,1024]{2,1,0:T(8,128)(2,1)} async-done(((bf16[4,64,1024]{2,1,0:T(8,128)(2,1)}), bf16[16,64,1024]{2,1,0:T(8,128)(2,1)}) %all-gather.9.cloned.1.call-update) | async-done | bytes 2097168 | tf_op jit(solution)/shard_map/all_gather | solution.py:369
  65.2 2.5 shard_map.93
  69.4 3.9 collective-permute-start
  73.4 35.1 %all-gather.11.cloned.1.call-done.column_ref = bf16[16,64,1024]{2,1,0:T(8,128)(2,1)} async-done(((bf16[4,64,1024]{2,1,0:T(8,128)(2,1)}), bf16[16,64,1024]{2,1,0:T(8,128)(2,1)}) %all-gather.11.cloned.1.call-update) | async-done | bytes 2097168 | tf_op jit(solution)/shard_map/all_gather | solution.py:369
  110.1 2.5 shard_map.94
  114.3 10.1 %collective-permute-start.11 = (bf16[32,64,128]{2,1,0:T(8,128)(2,1)S(1)}, bf16[32,64,128]{2,1,0:T(8,128)(2,1)S(1)}, u32[]{:S(2)}, u32[]{:S(2)}) collective-permute-start(bf16[32,64,128]{2,1,0:T(8,128)(2,1)S(1)} %get-tuple-element.112), channel_id=1, source_target_pairs={{0,6},{2,4},{4,2},{6,0},{8,14},{10,12},{12,10},{14,8},{16,22},{18,... | collective-permute-start | bytes 1572872 | tf_op jit(solution)/shard_map/ppermute | solution.py:312
  126.1 6.0 %collective-permute-start.5 = (bf16[2,64,1024]{2,1,0:T(8,128)(2,1)S(1)}, bf16[2,64,1024]{2,1,0:T(8,128)(2,1)S(1)}, u32[]{:S(2)}, u32[]{:S(2)}) collective-permute-start(bf16[2,64,1024]{2,1,0:T(8,128)(2,1)S(1)} %add_convert_fusion.9), channel_id=1, source_target_pairs={{0,4},{2,6},{4,0},{6,2},{8,12},{10,14},{12,8},{14,10},{16,20},{18,... | collective-permute-start | bytes 786440 | tf_op jit(solution)/shard_map/ppermute | solution.py:312
  132.2 1.9 slice_bitcast_fusion.1
  134.0 2.1 collective-permute-start.7
  136.1 9.8 %collective-permute-done.3 = bf16[2,64,1024]{2,1,0:T(8,128)(2,1)S(1)} collective-permute-done((bf16[2,64,1024]{2,1,0:T(8,128)(2,1)S(1)}, bf16[2,64,1024]{2,1,0:T(8,128)(2,1)S(1)}, u32[]{:S(2)}, u32[]{:S(2)}) %collective-permute-start.3) | collective-permute-done | bytes 262176 | tf_op jit(solution)/shard_map/ppermute | solution.py:312
  147.0 4.6 collective-permute-done.5
  151.6 2.0 collective-permute-start.6
  154.6 19.4 %collective-permute-done.9.rest_5_.rest_9_ = bf16[32,64,128]{2,1,0:T(8,128)(2,1)S(1)} collective-permute-done((bf16[32,64,128]{2,1,0:T(8,128)(2,1)S(1)}, bf16[32,64,128]{2,1,0:T(8,128)(2,1)S(1)}, u32[]{:S(2)}, u32[]{:S(2)}) %collective-permute-start.9) | collective-permute-done | bytes 524320 | tf_op jit(solution)/shard_map/ppermute | solution.py:312
  174.1 9.9 %collective-permute-done.8.rest_4_.rest_8_ = bf16[32,64,128]{2,1,0:T(8,128)(2,1)S(1)} collective-permute-done((bf16[32,64,128]{2,1,0:T(8,128)(2,1)S(1)}, bf16[32,64,128]{2,1,0:T(8,128)(2,1)S(1)}, u32[]{:S(2)}, u32[]{:S(2)}) %collective-permute-start.8) | collective-permute-done | bytes 524320 | tf_op jit(solution)/shard_map/ppermute | solution.py:312
  184.7 23.4 %shard_map.95 = (bf16[8,4,1024,128]{3,2,1,0:T(8,128)(2,1)}, f32[512,1024]{1,0:T(8,128)}, bf16[128,1024]{1,0:T(8,128)(2,1)S(1)}, bf16[128,1024]{1,0:T(8,128)(2,1)...) custom-call(s32[96]{0:T(128)S(1)} %fusion.12.pick, ...), custom_call_target="tpu_custom_call" | custom-call | flops 8589934592 | bytes 16777216 | tf_op jit(solution)/shard_map/pallas_call | solution.py:396
  209.9 11.0 %collective-permute-done.32 = bf16[2,128,1024]{2,1,0:T(8,128)(2,1)S(1)} collective-permute-done((bf16[2,128,1024]{2,1,0:T(8,128)(2,1)S(1)}, bf16[2,128,1024]{2,1,0:T(8,128)(2,1)S(1)}, u32[]{:S(2)}, u32[]{:S(2)}) %collective-permute-start.32) | collective-permute-done | bytes 524320 | tf_op jit(solution)/shard_map/ppermute | solution.py:312
  226.2 21.0 %collective-permute-done.33 = bf16[2,128,1024]{2,1,0:T(8,128)(2,1)S(1)} collective-permute-done((bf16[2,128,1024]{2,1,0:T(8,128)(2,1)S(1)}, bf16[2,128,1024]{2,1,0:T(8,128)(2,1)S(1)}, u32[]{:S(2)}, u32[]{:S(2)}) %collective-permute-start.33) | collective-permute-done | bytes 524320 | tf_op jit(solution)/shard_map/ppermute | solution.py:312
  247.5 9.1 %collective-permute-done.35.rest_2_ = bf16[32,64,128]{2,1,0:T(8,128)(2,1)S(1)} collective-permute-done((bf16[32,64,128]{2,1,0:T(8,128)(2,1)S(1)}, bf16[32,64,128]{2,1,0:T(8,128)(2,1)S(1)}, u32[]{:S(2)}, u32[]{:S(2)}) %collective-permute-start.35) | collective-permute-done | bytes 524320 | tf_op jit(solution)/shard_map/ppermute | solution.py:312
  256.6 5.3 shard_map.101
  267.1 2.5 shard_map.97
  274.8 3.3 shard_map.96
  281.5 12.6 %collective-permute-done.14 = bf16[2,64,1024]{2,1,0:T(8,128)(2,1)} collective-permute-done((bf16[2,64,1024]{2,1,0:T(8,128)(2,1)S(1)}, bf16[2,64,1024]{2,1,0:T(8,128)(2,1)}, u32[]{:S(2)}, u32[]{:S(2)}) %collective-permute-start.14) | collective-permute-done | bytes 262176 | tf_op jit(solution)/shard_map/ppermute | solution.py:312
  297.7 5.3 shard_map.102
  304.8 2.0 collective-permute-start.17
  308.8 4.9 collective-permute-done.13
  318.8 3.3 collective-permute-done.17.rest_15_
  322.1 25.3 %collective-permute-done.18.rest_16_ = bf16[32,64,128]{2,1,0:T(8,128)(2,1)S(1)} collective-permute-done((bf16[32,64,128]{2,1,0:T(8,128)(2,1)}, bf16[32,64,128]{2,1,0:T(8,128)(2,1)S(1)}, u32[]{:S(2)}, u32[]{:S(2)}) %collective-permute-start.18) | collective-permute-done | bytes 524320 | tf_op jit(solution)/shard_map/ppermute | solution.py:312
  347.4 5.6 %collective-permute-done.19.rest_17_ = bf16[32,64,128]{2,1,0:T(8,128)(2,1)S(1)} collective-permute-done((bf16[32,64,128]{2,1,0:T(8,128)(2,1)S(1)}, bf16[32,64,128]{2,1,0:T(8,128)(2,1)S(1)}, u32[]{:S(2)}, u32[]{:S(2)}) %collective-permute-start.19) | collective-permute-done | bytes 524320 | tf_op jit(solution)/shard_map/ppermute | solution.py:312
  354.2 27.2 %shard_map.98 = (bf16[512,1024]{1,0:T(8,128)(2,1)}, bf16[512,1024]{1,0:T(8,128)(2,1)}, f32[512,1024]{1,0:T(8,128)}, bf16[128,1024]{1,0:T(8,128)(2,1)S(1)}, bf16[...) custom-call(s32[96]{0:T(128)S(1)} %fusion.12.pick, ...), custom_call_target="tpu_custom_call" | custom-call | flops 17179869184 | bytes 33554432 | tf_op jit(solution)/shard_map/pallas_call | solution.py:452
  381.4 2.1 collective-permute-start.22
  383.5 7.3 %collective-permute-done.22 = bf16[2,128,1024]{2,1,0:T(8,128)(2,1)S(1)} collective-permute-done((bf16[2,128,1024]{2,1,0:T(8,128)(2,1)S(1)}, bf16[2,128,1024]{2,1,0:T(8,128)(2,1)S(1)}, u32[]{:S(2)}, u32[]{:S(2)}) %collective-permute-start.22) | collective-permute-done | bytes 524320 | tf_op jit(solution)/shard_map/ppermute | solution.py:312
  391.0 4.3 collective-permute-start.23
  395.3 2.0 collective-permute-start.24
  398.8 18.9 %collective-permute-done.23 = bf16[2,128,1024]{2,1,0:T(8,128)(2,1)S(1)} collective-permute-done((bf16[2,128,1024]{2,1,0:T(8,128)(2,1)S(1)}, bf16[2,128,1024]{2,1,0:T(8,128)(2,1)S(1)}, u32[]{:S(2)}, u32[]{:S(2)}) %collective-permute-start.23) | collective-permute-done | bytes 524320 | tf_op jit(solution)/shard_map/ppermute | solution.py:312
  417.9 5.4 collective-permute-done.25.rest_2_
  423.3 5.3 shard_map.99
  432.3 8.8 %collective-permute-done.27.rest_1_ = bf16[32,64,128]{2,1,0:T(8,128)(2,1)S(1)} collective-permute-done((bf16[32,64,128]{2,1,0:T(8,128)(2,1)S(1)}, bf16[32,64,128]{2,1,0:T(8,128)(2,1)S(1)}, u32[]{:S(2)}, u32[]{:S(2)}) %collective-permute-start.27) | collective-permute-done | bytes 524320 | tf_op jit(solution)/shard_map/ppermute | solution.py:312
  441.1 6.3 %collective-permute-done.28.rest_2_ = bf16[32,64,128]{2,1,0:T(8,128)(2,1)S(1)} collective-permute-done((bf16[32,64,128]{2,1,0:T(8,128)(2,1)S(1)}, bf16[32,64,128]{2,1,0:T(8,128)(2,1)S(1)}, u32[]{:S(2)}, u32[]{:S(2)}) %collective-permute-start.28) | collective-permute-done | bytes 524320 | tf_op jit(solution)/shard_map/ppermute | solution.py:312
  448.2 5.3 shard_map.100
  454.4 3.2 collective-permute-start.40
  457.6 4.5 collective-permute-start.41
  462.1 1.9 collective-permute-start.30
  464.0 5.7 %collective-permute-start.31 = (bf16[128,1024]{1,0:T(8,128)(2,1)S(1)}, bf16[128,1024]{1,0:T(8,128)(2,1)S(1)}, u32[]{:S(2)}, u32[]{:S(2)}) collective-permute-start(bf16[128,1024]{1,0:T(8,128)(2,1)S(1)} %get-tuple-element.139), channel_id=1, source_target_pairs={{2,0},{4,2},{6,4},{8,6},{10,8},{12,10},{14,12},{16,14},{18,16},{20... | collective-permute-start | bytes 786440 | tf_op jit(solution)/shard_map/ppermute | solution.py:430
  469.8 3.8 convert_add_fusion
  473.6 11.1 %reduce-scatter.5.cloned.1.call-done = bf16[4,64,1024]{2,1,0:T(8,128)(2,1)} async-done(((bf16[16,64,1024]{2,1,0:T(8,128)(2,1)}), bf16[4,64,1024]{2,1,0:T(8,128)(2,1)}) %reduce-scatter.5.cloned.1.call-update) | async-done | bytes 524304 | tf_op jit(solution)/shard_map/reduce_scatter | solution.py:439
  484.7 46.2 %reduce-scatter.7.cloned.1.call-done = bf16[4,64,1024]{2,1,0:T(8,128)(2,1)} async-done(((bf16[16,64,1024]{2,1,0:T(8,128)(2,1)}), bf16[4,64,1024]{2,1,0:T(8,128)(2,1)}) %reduce-scatter.7.cloned.1.call-update) | async-done | bytes 524304 | tf_op jit(solution)/shard_map/reduce_scatter | solution.py:439
  (213 shorter events, 64.5 us)
Async XLA Ops:
  7.2 56.4 %all-gather.9.cloned.1.call-start = ((), (), s32[]{:S(2)}) async-start(), calls=%async_computation.8 | async-start | bytes 2621440 | tf_op jit(solution)/shard_map/all_gather | solution.py:369
  9.6 99.0 %all-gather.11.cloned.1.call-start = ((), (), s32[]{:S(2)}) async-start(), calls=%async_computation.9 | async-start | bytes 2621440 | tf_op jit(solution)/shard_map/all_gather | solution.py:369
  10.3 255.2 %all-gather.15.cloned.1.call-start = ((), (), s32[]{:S(2)}) async-start(), calls=%async_computation.11 | async-start | bytes 2621440 | tf_op jit(solution)/shard_map/all_gather | solution.py:369
  11.5 261.7 %all-gather.13.cloned.1.call-start = ((), (), s32[]{:S(2)}) async-start(), calls=%async_computation.10 | async-start | bytes 2621440 | tf_op jit(solution)/shard_map/all_gather | solution.py:369
  11.7 120.4 %collective-permute-start.1 = (bf16[2,128,1024]{2,1,0:T(8,128)(2,1)S(1)}, bf16[2,128,1024]{2,1,0:T(8,128)(2,1)S(1)}, u32[]{:S(2)}, u32[]{:S(2)}) collective-permute-start(bf16[2,128,1024]{2,1,0:T(8,128)(2,1)S(1)} %pad_maximum_fusion.1), channel_id=1, source_target_pairs={{2,0},{4,2},{6,4},{8,6},{10,8},{12,10},{14,12},{16,14},{18,16},{20... | collective-permute-start | bytes 1572872 | tf_op jit(solution)/shard_map/ppermute | solution.py:329
  68.6 55.8 %collective-permute-start.2 = (bf16[2,64,1024]{2,1,0:T(8,128)(2,1)S(1)}, bf16[2,64,1024]{2,1,0:T(8,128)(2,1)}, u32[]{:S(2)}, u32[]{:S(2)}) collective-permute-start(bf16[2,64,1024]{2,1,0:T(8,128)(2,1)S(1)} %get-tuple-element.102), channel_id=1, source_target_pairs={{0,2},{2,0},{4,6},{6,4},{8,10},{10,8},{12,14},{14,12},{16,18},{18,... | collective-permute-start | bytes 786440 | tf_op jit(solution)/shard_map/ppermute | solution.py:312
  69.4 62.8 %collective-permute-start = (bf16[2,128,1024]{2,1,0:T(8,128)(2,1)}, bf16[2,128,1024]{2,1,0:T(8,128)(2,1)}, u32[]{:S(2)}, u32[]{:S(2)}) collective-permute-start(bf16[2,128,1024]{2,1,0:T(8,128)(2,1)} %pad_maximum_fusion), channel_id=1, source_target_pairs={{0,2},{2,4},{4,6},{6,8},{8,10},{10,12},{12,14},{14,16},{16,18},{18... | collective-permute-start | bytes 1572872 | tf_op jit(solution)/shard_map/ppermute | solution.py:328
  73.3 396.4 %reduce-scatter.9.cloned.1.call-start = ((), (), s32[]{:S(2)}) async-start(), calls=%async_computation.6 | async-start | bytes 2621440 | tf_op jit(solution)/shard_map/reduce_scatter | solution.py:439
  112.7 13.4 %collective-permute-start.4 = (bf16[2,64,1024]{2,1,0:T(8,128)(2,1)S(1)}, bf16[2,64,1024]{2,1,0:T(8,128)(2,1)S(1)}, u32[]{:S(2)}, u32[]{:S(2)}) collective-permute-start(bf16[2,64,1024]{2,1,0:T(8,128)(2,1)S(1)} %get-tuple-element.104), channel_id=1, source_target_pairs={{0,2},{2,0},{4,6},{6,4},{8,10},{10,8},{12,14},{14,12},{16,18},{18,... | collective-permute-start | bytes 786440 | tf_op jit(solution)/shard_map/ppermute | solution.py:312
  114.3 39.3 %collective-permute-start.11 = (bf16[32,64,128]{2,1,0:T(8,128)(2,1)S(1)}, bf16[32,64,128]{2,1,0:T(8,128)(2,1)S(1)}, u32[]{:S(2)}, u32[]{:S(2)}) collective-permute-start(bf16[32,64,128]{2,1,0:T(8,128)(2,1)S(1)} %get-tuple-element.112), channel_id=1, source_target_pairs={{0,6},{2,4},{4,2},{6,0},{8,14},{10,12},{12,10},{14,8},{16,22},{18,... | collective-permute-start | bytes 1572872 | tf_op jit(solution)/shard_map/ppermute | solution.py:312
  125.4 20.5 %collective-permute-start.3 = (bf16[2,64,1024]{2,1,0:T(8,128)(2,1)S(1)}, bf16[2,64,1024]{2,1,0:T(8,128)(2,1)S(1)}, u32[]{:S(2)}, u32[]{:S(2)}) collective-permute-start(bf16[2,64,1024]{2,1,0:T(8,128)(2,1)S(1)} %add_convert_fusion.11), channel_id=1, source_target_pairs={{0,4},{2,6},{4,0},{6,2},{8,12},{10,14},{12,8},{14,10},{16,20},{18,... | collective-permute-start | bytes 786440 | tf_op jit(solution)/shard_map/ppermute | solution.py:312
  126.1 25.4 %collective-permute-start.5 = (bf16[2,64,1024]{2,1,0:T(8,128)(2,1)S(1)}, bf16[2,64,1024]{2,1,0:T(8,128)(2,1)S(1)}, u32[]{:S(2)}, u32[]{:S(2)}) collective-permute-start(bf16[2,64,1024]{2,1,0:T(8,128)(2,1)S(1)} %add_convert_fusion.9), channel_id=1, source_target_pairs={{0,4},{2,6},{4,0},{6,2},{8,12},{10,14},{12,8},{14,10},{16,20},{18,... | collective-permute-start | bytes 786440 | tf_op jit(solution)/shard_map/ppermute | solution.py:312
  134.0 20.6 %collective-permute-start.7 = (bf16[32,64,128]{2,1,0:T(8,128)(2,1)S(1)}, bf16[32,64,128]{2,1,0:T(8,128)(2,1)S(1)}, u32[]{:S(2)}, u32[]{:S(2)}) collective-permute-start(bf16[32,64,128]{2,1,0:T(8,128)(2,1)S(1)} %get-tuple-element.108), channel_id=1, source_target_pairs={{0,2},{2,0},{4,6},{6,4},{8,10},{10,8},{12,14},{14,12},{16,18},{18,... | collective-permute-start | bytes 1572872 | tf_op jit(solution)/shard_map/ppermute | solution.py:312
  136.1 37.9 %collective-permute-start.9 = (bf16[32,64,128]{2,1,0:T(8,128)(2,1)S(1)}, bf16[32,64,128]{2,1,0:T(8,128)(2,1)S(1)}, u32[]{:S(2)}, u32[]{:S(2)}) collective-permute-start(bf16[32,64,128]{2,1,0:T(8,128)(2,1)S(1)} %get-tuple-element.110), channel_id=1, source_target_pairs={{0,4},{2,6},{4,0},{6,2},{8,12},{10,14},{12,8},{14,10},{16,20},{18,... | collective-permute-start | bytes 1572872 | tf_op jit(solution)/shard_map/ppermute | solution.py:312
  145.9 28.1 %collective-permute-start.10 = (bf16[32,64,128]{2,1,0:T(8,128)(2,1)S(1)}, bf16[32,64,128]{2,1,0:T(8,128)(2,1)S(1)}, u32[]{:S(2)}, u32[]{:S(2)}) collective-permute-start(bf16[32,64,128]{2,1,0:T(8,128)(2,1)S(1)} %get-tuple-element.111), channel_id=1, source_target_pairs={{0,6},{2,4},{4,2},{6,0},{8,14},{10,12},{12,10},{14,8},{16,22},{18,... | collective-permute-start | bytes 1572872 | tf_op jit(solution)/shard_map/ppermute | solution.py:312
  151.6 22.5 %collective-permute-start.6 = (bf16[32,64,128]{2,1,0:T(8,128)(2,1)S(1)}, bf16[32,64,128]{2,1,0:T(8,128)(2,1)S(1)}, u32[]{:S(2)}, u32[]{:S(2)}) collective-permute-start(bf16[32,64,128]{2,1,0:T(8,128)(2,1)S(1)} %get-tuple-element.107), channel_id=1, source_target_pairs={{0,2},{2,0},{4,6},{6,4},{8,10},{10,8},{12,14},{14,12},{16,18},{18,... | collective-permute-start | bytes 1572872 | tf_op jit(solution)/shard_map/ppermute | solution.py:312
  153.6 30.3 %collective-permute-start.8 = (bf16[32,64,128]{2,1,0:T(8,128)(2,1)S(1)}, bf16[32,64,128]{2,1,0:T(8,128)(2,1)S(1)}, u32[]{:S(2)}, u32[]{:S(2)}) collective-permute-start(bf16[32,64,128]{2,1,0:T(8,128)(2,1)S(1)} %get-tuple-element.109), channel_id=1, source_target_pairs={{0,4},{2,6},{4,0},{6,2},{8,12},{10,14},{12,8},{14,10},{16,20},{18,... | collective-permute-start | bytes 1572872 | tf_op jit(solution)/shard_map/ppermute | solution.py:312
  208.1 12.8 %collective-permute-start.32 = (bf16[2,128,1024]{2,1,0:T(8,128)(2,1)S(1)}, bf16[2,128,1024]{2,1,0:T(8,128)(2,1)S(1)}, u32[]{:S(2)}, u32[]{:S(2)}) collective-permute-start(bf16[2,128,1024]{2,1,0:T(8,128)(2,1)S(1)} %get-tuple-element.141), channel_id=1, source_target_pairs={{0,2},{2,0},{4,6},{6,4},{8,10},{10,8},{12,14},{14,12},{16,18},{18,... | collective-permute-start | bytes 1572872 | tf_op jit(solution)/shard_map/ppermute | solution.py:312
  221.1 26.2 %collective-permute-start.33 = (bf16[2,128,1024]{2,1,0:T(8,128)(2,1)S(1)}, bf16[2,128,1024]{2,1,0:T(8,128)(2,1)S(1)}, u32[]{:S(2)}, u32[]{:S(2)}) collective-permute-start(bf16[2,128,1024]{2,1,0:T(8,128)(2,1)S(1)} %add_convert_fusion.1), channel_id=1, source_target_pairs={{0,4},{2,6},{4,0},{6,2},{8,12},{10,14},{12,8},{14,10},{16,20},{18,... | collective-permute-start | bytes 1572872 | tf_op jit(solution)/shard_map/ppermute | solution.py:312
  222.8 24.7 %collective-permute-start.34 = (bf16[32,64,128]{2,1,0:T(8,128)(2,1)S(1)}, bf16[32,64,128]{2,1,0:T(8,128)(2,1)S(1)}, u32[]{:S(2)}, u32[]{:S(2)}) collective-permute-start(bf16[32,64,128]{2,1,0:T(8,128)(2,1)S(1)} %get-tuple-element.143), channel_id=1, source_target_pairs={{0,2},{2,0},{4,6},{6,4},{8,10},{10,8},{12,14},{14,12},{16,18},{18,... | collective-permute-start | bytes 1572872 | tf_op jit(solution)/shard_map/ppermute | solution.py:312
  223.0 33.5 %collective-permute-start.35 = (bf16[32,64,128]{2,1,0:T(8,128)(2,1)S(1)}, bf16[32,64,128]{2,1,0:T(8,128)(2,1)S(1)}, u32[]{:S(2)}, u32[]{:S(2)}) collective-permute-start(bf16[32,64,128]{2,1,0:T(8,128)(2,1)S(1)} %get-tuple-element.144), channel_id=1, source_target_pairs={{0,4},{2,6},{4,0},{6,2},{8,12},{10,14},{12,8},{14,10},{16,20},{18,... | collective-permute-start | bytes 1572872 | tf_op jit(solution)/shard_map/ppermute | solution.py:312
  224.6 32.0 %collective-permute-start.36 = (bf16[32,64,128]{2,1,0:T(8,128)(2,1)S(1)}, bf16[32,64,128]{2,1,0:T(8,128)(2,1)S(1)}, u32[]{:S(2)}, u32[]{:S(2)}) collective-permute-start(bf16[32,64,128]{2,1,0:T(8,128)(2,1)S(1)} %get-tuple-element.145), channel_id=1, source_target_pairs={{0,6},{2,4},{4,2},{6,0},{8,14},{10,12},{12,10},{14,8},{16,22},{18,... | collective-permute-start | bytes 1572872 | tf_op jit(solution)/shard_map/ppermute | solution.py:312
  261.9 207.9 %reduce-scatter.11.cloned.1.call-start = ((), (), s32[]{:S(2)}) async-start(), calls=%async_computation.7 | async-start | bytes 2621440 | tf_op jit(solution)/shard_map/reduce_scatter | solution.py:439
  262.0 33.9 %collective-permute-start.37 = (bf16[32,64,128]{2,1,0:T(8,128)(2,1)}, bf16[32,64,128]{2,1,0:T(8,128)(2,1)S(1)}, u32[]{:S(2)}, u32[]{:S(2)}) collective-permute-start(bf16[32,64,128]{2,1,0:T(8,128)(2,1)} %get-tuple-element.147), channel_id=1, source_target_pairs={{0,2},{2,0},{4,6},{6,4},{8,10},{10,8},{12,14},{14,12},{16,18},{18,... | collective-permute-start | bytes 1572872 | tf_op jit(solution)/shard_map/ppermute | solution.py:312
  262.1 35.6 %collective-permute-start.38 = (bf16[32,64,128]{2,1,0:T(8,128)(2,1)}, bf16[32,64,128]{2,1,0:T(8,128)(2,1)S(1)}, u32[]{:S(2)}, u32[]{:S(2)}) collective-permute-start(bf16[32,64,128]{2,1,0:T(8,128)(2,1)} %get-tuple-element.148), channel_id=1, source_target_pairs={{0,4},{2,6},{4,0},{6,2},{8,12},{10,14},{12,8},{14,10},{16,20},{18,... | collective-permute-start | bytes 1572872 | tf_op jit(solution)/shard_map/ppermute | solution.py:312
  263.9 33.8 %collective-permute-start.39 = (bf16[32,64,128]{2,1,0:T(8,128)(2,1)}, bf16[32,64,128]{2,1,0:T(8,128)(2,1)S(1)}, u32[]{:S(2)}, u32[]{:S(2)}) collective-permute-start(bf16[32,64,128]{2,1,0:T(8,128)(2,1)} %get-tuple-element.149), channel_id=1, source_target_pairs={{0,6},{2,4},{4,2},{6,0},{8,14},{10,12},{12,10},{14,8},{16,22},{18,... | collective-permute-start | bytes 1572872 | tf_op jit(solution)/shard_map/ppermute | solution.py:312
  272.9 21.2 %collective-permute-start.14 = (bf16[2,64,1024]{2,1,0:T(8,128)(2,1)S(1)}, bf16[2,64,1024]{2,1,0:T(8,128)(2,1)}, u32[]{:S(2)}, u32[]{:S(2)}) collective-permute-start(bf16[2,64,1024]{2,1,0:T(8,128)(2,1)S(1)} %get-tuple-element.117), channel_id=1, source_target_pairs={{0,2},{2,0},{4,6},{6,4},{8,10},{10,8},{12,14},{14,12},{16,18},{18,... | collective-permute-start | bytes 786440 | tf_op jit(solution)/shard_map/ppermute | solution.py:312
  279.8 23.5 %collective-permute-start.12 = (bf16[2,64,1024]{2,1,0:T(8,128)(2,1)S(1)}, bf16[2,64,1024]{2,1,0:T(8,128)(2,1)}, u32[]{:S(2)}, u32[]{:S(2)}) collective-permute-start(bf16[2,64,1024]{2,1,0:T(8,128)(2,1)S(1)} %get-tuple-element.115), channel_id=1, source_target_pairs={{0,2},{2,0},{4,6},{6,4},{8,10},{10,8},{12,14},{14,12},{16,18},{18,... | collective-permute-start | bytes 786440 | tf_op jit(solution)/shard_map/ppermute | solution.py:312
  294.1 21.4 %collective-permute-start.16 = (bf16[32,64,128]{2,1,0:T(8,128)(2,1)}, bf16[32,64,128]{2,1,0:T(8,128)(2,1)}, u32[]{:S(2)}, u32[]{:S(2)}) collective-permute-start(bf16[32,64,128]{2,1,0:T(8,128)(2,1)} %get-tuple-element.120), channel_id=1, source_target_pairs={{0,2},{2,0},{4,6},{6,4},{8,10},{10,8},{12,14},{14,12},{16,18},{18,... | collective-permute-start | bytes 1572872 | tf_op jit(solution)/shard_map/ppermute | solution.py:312
  295.9 12.7 %collective-permute-start.15 = (bf16[2,64,1024]{2,1,0:T(8,128)(2,1)}, bf16[2,64,1024]{2,1,0:T(8,128)(2,1)}, u32[]{:S(2)}, u32[]{:S(2)}) collective-permute-start(bf16[2,64,1024]{2,1,0:T(8,128)(2,1)} %add_convert_fusion.5), channel_id=1, source_target_pairs={{0,4},{2,6},{4,0},{6,2},{8,12},{10,14},{12,8},{14,10},{16,20},{18,... | collective-permute-start | bytes 786440 | tf_op jit(solution)/shard_map/ppermute | solution.py:312
  303.0 181.7 %reduce-scatter.5.cloned.1.call-start = ((), (), s32[]{:S(2)}) async-start(), calls=%async_computation.4 | async-start | bytes 2621440 | tf_op jit(solution)/shard_map/reduce_scatter | solution.py:439
  304.8 17.3 %collective-permute-start.17 = (bf16[32,64,128]{2,1,0:T(8,128)(2,1)S(1)}, bf16[32,64,128]{2,1,0:T(8,128)(2,1)S(1)}, u32[]{:S(2)}, u32[]{:S(2)}) collective-permute-start(bf16[32,64,128]{2,1,0:T(8,128)(2,1)S(1)} %copy-done.20), channel_id=1, source_target_pairs={{0,2},{2,0},{4,6},{6,4},{8,10},{10,8},{12,14},{14,12},{16,18},{18,... | collective-permute-start | bytes 1572872 | tf_op jit(solution)/shard_map/ppermute | solution.py:312
  306.8 40.6 %collective-permute-start.18 = (bf16[32,64,128]{2,1,0:T(8,128)(2,1)}, bf16[32,64,128]{2,1,0:T(8,128)(2,1)S(1)}, u32[]{:S(2)}, u32[]{:S(2)}) collective-permute-start(bf16[32,64,128]{2,1,0:T(8,128)(2,1)} %copy-done.23), channel_id=1, source_target_pairs={{0,4},{2,6},{4,0},{6,2},{8,12},{10,14},{12,8},{14,10},{16,20},{18,... | collective-permute-start | bytes 1572872 | tf_op jit(solution)/shard_map/ppermute | solution.py:312
  308.6 44.5 %collective-permute-start.19 = (bf16[32,64,128]{2,1,0:T(8,128)(2,1)S(1)}, bf16[32,64,128]{2,1,0:T(8,128)(2,1)S(1)}, u32[]{:S(2)}, u32[]{:S(2)}) collective-permute-start(bf16[32,64,128]{2,1,0:T(8,128)(2,1)S(1)} %copy-done.18), channel_id=1, source_target_pairs={{0,4},{2,6},{4,0},{6,2},{8,12},{10,14},{12,8},{14,10},{16,20},{18,... | collective-permute-start | bytes 1572872 | tf_op jit(solution)/shard_map/ppermute | solution.py:312
  313.8 39.2 %collective-permute-start.20 = (bf16[32,64,128]{2,1,0:T(8,128)(2,1)S(1)}, bf16[32,64,128]{2,1,0:T(8,128)(2,1)S(1)}, u32[]{:S(2)}, u32[]{:S(2)}) collective-permute-start(bf16[32,64,128]{2,1,0:T(8,128)(2,1)S(1)} %copy-done.22), channel_id=1, source_target_pairs={{0,6},{2,4},{4,2},{6,0},{8,14},{10,12},{12,10},{14,8},{16,22},{18,... | collective-permute-start | bytes 1572872 | tf_op jit(solution)/shard_map/ppermute | solution.py:312
  315.5 37.5 %collective-permute-start.21 = (bf16[32,64,128]{2,1,0:T(8,128)(2,1)S(1)}, bf16[32,64,128]{2,1,0:T(8,128)(2,1)S(1)}, u32[]{:S(2)}, u32[]{:S(2)}) collective-permute-start(bf16[32,64,128]{2,1,0:T(8,128)(2,1)S(1)} %copy-done.16), channel_id=1, source_target_pairs={{0,6},{2,4},{4,2},{6,0},{8,14},{10,12},{12,10},{14,8},{16,22},{18,... | collective-permute-start | bytes 1572872 | tf_op jit(solution)/shard_map/ppermute | solution.py:312
  391.0 26.7 %collective-permute-start.23 = (bf16[2,128,1024]{2,1,0:T(8,128)(2,1)S(1)}, bf16[2,128,1024]{2,1,0:T(8,128)(2,1)S(1)}, u32[]{:S(2)}, u32[]{:S(2)}) collective-permute-start(bf16[2,128,1024]{2,1,0:T(8,128)(2,1)S(1)} %add_convert_fusion.3), channel_id=1, source_target_pairs={{0,4},{2,6},{4,0},{6,2},{8,12},{10,14},{12,8},{14,10},{16,20},{18,... | collective-permute-start | bytes 1572872 | tf_op jit(solution)/shard_map/ppermute | solution.py:312
  395.3 22.6 %collective-permute-start.24 = (bf16[32,64,128]{2,1,0:T(8,128)(2,1)S(1)}, bf16[32,64,128]{2,1,0:T(8,128)(2,1)S(1)}, u32[]{:S(2)}, u32[]{:S(2)}) collective-permute-start(bf16[32,64,128]{2,1,0:T(8,128)(2,1)S(1)} %get-tuple-element.131), channel_id=1, source_target_pairs={{0,2},{2,0},{4,6},{6,4},{8,10},{10,8},{12,14},{14,12},{16,18},{18,... | collective-permute-start | bytes 1572872 | tf_op jit(solution)/shard_map/ppermute | solution.py:312
  397.2 26.1 %collective-permute-start.25 = (bf16[32,64,128]{2,1,0:T(8,128)(2,1)S(1)}, bf16[32,64,128]{2,1,0:T(8,128)(2,1)S(1)}, u32[]{:S(2)}, u32[]{:S(2)}) collective-permute-start(bf16[32,64,128]{2,1,0:T(8,128)(2,1)S(1)} %get-tuple-element.132), channel_id=1, source_target_pairs={{0,4},{2,6},{4,0},{6,2},{8,12},{10,14},{12,8},{14,10},{16,20},{18,... | collective-permute-start | bytes 1572872 | tf_op jit(solution)/shard_map/ppermute | solution.py:312
  397.3 26.0 %collective-permute-start.26 = (bf16[32,64,128]{2,1,0:T(8,128)(2,1)S(1)}, bf16[32,64,128]{2,1,0:T(8,128)(2,1)S(1)}, u32[]{:S(2)}, u32[]{:S(2)}) collective-permute-start(bf16[32,64,128]{2,1,0:T(8,128)(2,1)S(1)} %get-tuple-element.133), channel_id=1, source_target_pairs={{0,6},{2,4},{4,2},{6,0},{8,14},{10,12},{12,10},{14,8},{16,22},{18,... | collective-permute-start | bytes 1572872 | tf_op jit(solution)/shard_map/ppermute | solution.py:312
  428.6 102.3 %reduce-scatter.7.cloned.1.call-start = ((), (), s32[]{:S(2)}) async-start(), calls=%async_computation.5 | async-start | bytes 2621440 | tf_op jit(solution)/shard_map/reduce_scatter | solution.py:439
  428.7 12.4 %collective-permute-start.27 = (bf16[32,64,128]{2,1,0:T(8,128)(2,1)S(1)}, bf16[32,64,128]{2,1,0:T(8,128)(2,1)S(1)}, u32[]{:S(2)}, u32[]{:S(2)}) collective-permute-start(bf16[32,64,128]{2,1,0:T(8,128)(2,1)S(1)} %get-tuple-element.135), channel_id=1, source_target_pairs={{0,2},{2,0},{4,6},{6,4},{8,10},{10,8},{12,14},{14,12},{16,18},{18,... | collective-permute-start | bytes 1572872 | tf_op jit(solution)/shard_map/ppermute | solution.py:312
  430.2 17.1 %collective-permute-start.28 = (bf16[32,64,128]{2,1,0:T(8,128)(2,1)S(1)}, bf16[32,64,128]{2,1,0:T(8,128)(2,1)S(1)}, u32[]{:S(2)}, u32[]{:S(2)}) collective-permute-start(bf16[32,64,128]{2,1,0:T(8,128)(2,1)S(1)} %get-tuple-element.136), channel_id=1, source_target_pairs={{0,4},{2,6},{4,0},{6,2},{8,12},{10,14},{12,8},{14,10},{16,20},{18,... | collective-permute-start | bytes 1572872 | tf_op jit(solution)/shard_map/ppermute | solution.py:312
  432.0 16.2 %collective-permute-start.29 = (bf16[32,64,128]{2,1,0:T(8,128)(2,1)S(1)}, bf16[32,64,128]{2,1,0:T(8,128)(2,1)S(1)}, u32[]{:S(2)}, u32[]{:S(2)}) collective-permute-start(bf16[32,64,128]{2,1,0:T(8,128)(2,1)S(1)} %copy-done.38), channel_id=1, source_target_pairs={{0,6},{2,4},{4,2},{6,0},{8,14},{10,12},{12,10},{14,8},{16,22},{18,... | collective-permute-start | bytes 1572872 | tf_op jit(solution)/shard_map/ppermute | solution.py:312
  454.4 78.2 %collective-permute-start.40 = (bf16[128,1024]{1,0:T(8,128)(2,1)S(1)}, bf16[128,1024]{1,0:T(8,128)(2,1)}, u32[]{:S(2)}, u32[]{:S(2)}) collective-permute-start(bf16[128,1024]{1,0:T(8,128)(2,1)S(1)} %copy-done.27), channel_id=1, source_target_pairs={{0,2},{2,4},{4,6},{6,8},{8,10},{10,12},{12,14},{14,16},{16,18},{18... | collective-permute-start | bytes 786440 | tf_op jit(solution)/shard_map/ppermute | solution.py:429
  457.6 76.2 %collective-permute-start.41 = (bf16[128,1024]{1,0:T(8,128)(2,1)S(1)}, bf16[128,1024]{1,0:T(8,128)(2,1)}, u32[]{:S(2)}, u32[]{:S(2)}) collective-permute-start(bf16[128,1024]{1,0:T(8,128)(2,1)S(1)} %copy-done.25), channel_id=1, source_target_pairs={{2,0},{4,2},{6,4},{8,6},{10,8},{12,10},{14,12},{16,14},{18,16},{20... | collective-permute-start | bytes 786440 | tf_op jit(solution)/shard_map/ppermute | solution.py:430
  462.1 74.0 %collective-permute-start.30 = (bf16[128,1024]{1,0:T(8,128)(2,1)S(1)}, bf16[128,1024]{1,0:T(8,128)(2,1)}, u32[]{:S(2)}, u32[]{:S(2)}) collective-permute-start(bf16[128,1024]{1,0:T(8,128)(2,1)S(1)} %get-tuple-element.138), channel_id=1, source_target_pairs={{0,2},{2,4},{4,6},{6,8},{8,10},{10,12},{12,14},{14,16},{16,18},{18... | collective-permute-start | bytes 786440 | tf_op jit(solution)/shard_map/ppermute | solution.py:429
  464.0 73.1 %collective-permute-start.31 = (bf16[128,1024]{1,0:T(8,128)(2,1)S(1)}, bf16[128,1024]{1,0:T(8,128)(2,1)S(1)}, u32[]{:S(2)}, u32[]{:S(2)}) collective-permute-start(bf16[128,1024]{1,0:T(8,128)(2,1)S(1)} %get-tuple-element.139), channel_id=1, source_target_pairs={{2,0},{4,2},{6,4},{8,6},{10,8},{12,10},{14,12},{16,14},{18,16},{20... | collective-permute-start | bytes 786440 | tf_op jit(solution)/shard_map/ppermute | solution.py:430
  (47 other events, 744.7 us)
Sparse Core Ops, SparseCore 0:
  10.2 53.3 all-gather.8
  65.8 42.7 all-gather.10
  110.1 55.8 all-gather.14
  167.4 44.6 all-gather.12
  262.1 44.7 reduce-scatter.8
  309.1 43.1 reduce-scatter.10
  428.7 55.9 reduce-scatter.4
  487.1 43.7 reduce-scatter.6

commit v2 on v1

v2 whole, which is shorter than its diff:
```python
import math

import jax
import jax.numpy as jnp
from jax import lax
from jax.experimental import pallas as pl
from jax.experimental.pallas import tpu as pltpu
from jax.sharding import PartitionSpec as P

BLOCK = 128
DH = 128
RAND = 3
GLOB = 2
WMAX = 1
SPAN = 2 * WMAX + 1
LISTED = SPAN + RAND + GLOB
PLANES = 4
PARTS = 2
ROWS = BLOCK // PARTS
SCALE = 1.0 / math.sqrt(DH)
POWER = SCALE / math.log(2.0)
MASKED = -1e30
VMEM_BYTES = 48 * 1024 * 1024

NT = (((1,), (1,)), ((), ()))
NN = (((1,), (0,)), ((), ()))
TN = (((0,), (0,)), ((), ()))

SMEM = pltpu.SMEM
ANY = pl.ANY


def dot(a, b, dims):
    return lax.dot_general(a, b, dims, preferred_element_type=jnp.float32)


def cost(micros):
    return pl.CostEstimate(flops=0, bytes_accessed=int(micros * 3.5e6), transcendentals=0)


def tie(*values):
    return lax.optimization_barrier(values)


def params():
    return pltpu.CompilerParams(vmem_limit_bytes=VMEM_BYTES)


def smem_spec():
    return pl.BlockSpec(memory_space=SMEM)


def any_spec():
    return pl.BlockSpec(memory_space=ANY)


def vmem_spec():
    return pl.BlockSpec(memory_space=pltpu.VMEM)


def call(kernel, out_shape, in_specs, micros, scratch=()):
    return pl.pallas_call(
        kernel,
        out_shape=out_shape,
        in_specs=in_specs,
        out_specs=jax.tree.map(lambda _: vmem_spec(), out_shape),
        scratch_shapes=list(scratch),
        compiler_params=params(),
        cost_estimate=cost(micros),
    )


def lanes_of(index, heads):
    return pl.ds(pl.multiple_of((index % heads) * DH, DH), DH)


def pick_own(keys, values, table, heads, lanes, slots, cap):
    blocks = keys.shape[0]

    def kernel(table_ref, *rest):
        sources, outs = rest[:2], rest[2:]
        for partner in range(lanes):

            def step(slot, carry, partner=partner):
                index = jnp.maximum(table_ref[partner * slots + slot], 0)
                row, lane = (index // heads) % blocks, lanes_of(index, heads)
                for number, source in enumerate(sources):
                    outs[partner][number, slot] = source[row, :, lane]
                return carry

            lax.fori_loop(0, cap, step, 0)

    shape = jax.ShapeDtypeStruct((2, cap, BLOCK, DH), keys.dtype)
    specs = [smem_spec(), vmem_spec(), vmem_spec()]
    return call(kernel, [shape] * lanes, specs, 3)(table, keys, values)


def pick_blocks(column, table, info, heads, lanes, slots, cap):
    rows, width = column.shape[1:]

    def kernel(table_ref, info_ref, column_ref, *outs):
        for partner in range(lanes):

            def step(slot, carry, partner=partner):
                index = jnp.maximum(table_ref[partner * slots + cap + slot], 0)
                outs[partner][slot] = column_ref[index // heads, :, lanes_of(index, heads)]
                return carry

            lax.fori_loop(0, slots - cap, step, 0)
        for glob in range(GLOB):
            block = column_ref[info_ref[2 * glob]]
            mine = info_ref[2 * glob + 1] > 0
            outs[lanes][glob] = jnp.where(mine, block, jnp.zeros_like(block))
        for side in range(2):
            outs[lanes + 1 + side][...] = column_ref[info_ref[2 * GLOB + side]]

    shapes = [jax.ShapeDtypeStruct((slots - cap, rows, DH), column.dtype)] * lanes
    shapes += [jax.ShapeDtypeStruct((GLOB, rows, width), column.dtype)]
    shapes += [jax.ShapeDtypeStruct((rows, width), column.dtype)] * 2
    specs = [smem_spec(), smem_spec(), vmem_spec()]
    return call(kernel, shapes, specs, 3)(table, info, column)


def sum_blocks(returned, glob_sum, rims, table, info, blocks, heads, slots, cap):
    lanes = len(returned)
    rows = returned[0].shape[1]
    width = glob_sum.shape[2]

    def kernel(table_ref, info_ref, glob_ref, low_ref, high_ref, *rest):
        refs, out_ref, total = rest[:lanes], rest[lanes], rest[lanes + 1]
        total[...] = jnp.zeros_like(total)
        for partner in range(lanes):

            def step(slot, carry, partner=partner):
                index = table_ref[partner * slots + cap + slot]

                @pl.when(index >= 0)
                def _():
                    term = refs[partner][slot].astype(jnp.float32)
                    total[index // heads, :, lanes_of(index, heads)] += term

                return carry

            lax.fori_loop(0, slots - cap, step, 0)
        for glob in range(GLOB):

            @pl.when(info_ref[2 * glob + 1] > 0)
            def _(glob=glob):
                total[info_ref[2 * glob]] += glob_ref[glob].astype(jnp.float32)

        for side, rim_ref in enumerate((low_ref, high_ref)):
            row = info_ref[2 * GLOB + 2 + side]

            @pl.when(row >= 0)
            def _(row=row, rim_ref=rim_ref):
                total[row] += rim_ref[...].astype(jnp.float32)

        out_ref[...] = total[...].astype(out_ref.dtype)

    shape = (blocks, rows, width)
    specs = [smem_spec()] * 2 + [vmem_spec()] * (3 + lanes)
    return call(
        kernel,
        jax.ShapeDtypeStruct(shape, jnp.bfloat16),
        specs,
        6,
        [pltpu.VMEM(shape, jnp.float32)],
    )(table, info, glob_sum, *rims, *returned)


def final_sum(own, sums, returned, table, heads, slots, cap):
    blocks, _, width = own.shape
    lanes = len(returned)

    def kernel(table_ref, own_ref, *rest):
        sum_refs, refs = rest[:PARTS], rest[PARTS : PARTS + lanes]
        out_ref, total = rest[PARTS + lanes :]
        for part, sum_ref in enumerate(sum_refs):
            here = slice(part * ROWS, (part + 1) * ROWS)
            total[:, here] = own_ref[:, here] + sum_ref[...].astype(jnp.float32)
        for partner in range(lanes):

            def step(slot, carry, partner=partner):
                index = table_ref[partner * slots + slot]

                @pl.when(index >= 0)
                def _():
                    term = refs[partner][slot].astype(jnp.float32)
                    total[(index // heads) % blocks, :, lanes_of(index, heads)] += term

                return carry

            lax.fori_loop(0, cap, step, 0)
        out_ref[...] = total[...].astype(out_ref.dtype)

    specs = [smem_spec()] + [vmem_spec()] * (1 + PARTS + lanes)
    return call(
        kernel,
        jax.ShapeDtypeStruct(own.shape, jnp.bfloat16),
        specs,
        5,
        [pltpu.VMEM(own.shape, jnp.float32)],
    )(table, own, *sums, *returned)


def copy_parts(refs, buffer, sems, lanes, slots, cap, outward, which=None):
    copies = []
    for partner in range(lanes):
        first = partner * slots
        for part in range(PARTS + 1):
            number = partner * (PARTS + 1) + part
            ref = refs[number]
            if part == 0:
                inside = buffer.at[pl.ds(first, cap)]
                ref = ref if which is None else ref.at[which]
            else:
                rows = pl.ds((part - 1) * ROWS, ROWS)
                inside = buffer.at[pl.ds(first + cap, slots - cap), rows]
            pair = (inside, ref) if outward else (ref, inside)
            copies.append(pltpu.make_async_copy(*pair, sems.at[number]))
    return copies


def run_copies(copies):
    for copy in copies:
        copy.start()
    for copy in copies:
        copy.wait()


def fill(refs, band, glob, blocks):
    own, lows, highs, globs = refs[0], refs[1 : 1 + PARTS], refs[1 + PARTS : 1 + 2 * PARTS], None
    globs = refs[1 + 2 * PARTS :]
    end = BLOCK * (blocks + 1)
    band[BLOCK:end] = own[...]
    for part in range(PARTS):
        start = part * ROWS
        band[start : start + ROWS] = lows[part][...]
        band[end + start : end + start + ROWS] = highs[part][...]
        for g in range(GLOB):
            glob[g * BLOCK + start : g * BLOCK + start + ROWS] = globs[part][g]


def pieces():
    starts = [0] + [(SPAN + n) * BLOCK for n in range(RAND + 1)] + [LISTED * BLOCK]
    return list(zip(starts[:-1], starts[1:]))


def store_sums(refs, band_sum, glob_sum, blocks, scale):
    own_ref, lows = refs[0], refs[1 : 1 + PARTS]
    highs, globs = refs[1 + PARTS : 1 + 2 * PARTS], refs[1 + 2 * PARTS :]
    end = BLOCK * (blocks + 1)
    own_ref[...] = band_sum[BLOCK:end] * scale
    for part in range(PARTS):
        here = slice(part * ROWS, (part + 1) * ROWS)
        there = slice(end + part * ROWS, end + (part + 1) * ROWS)
        lows[part][...] = (band_sum[here] * scale).astype(jnp.bfloat16)
        highs[part][...] = (band_sum[there] * scale).astype(jnp.bfloat16)
        for g in range(GLOB):
            rows = slice(g * BLOCK + part * ROWS, g * BLOCK + (part + 1) * ROWS)
            globs[part][g] = (glob_sum[rows] * scale).astype(jnp.bfloat16)


LISTS = 1 + 3 * PARTS


def weights_kernel(lanes, slots, cap, heads, blocks):
    count = lanes * (PARTS + 1)

    def kernel(pick, ends, q_ref, g_ref, *rest):
        k_refs, kr_refs = rest[:LISTS], rest[LISTS : LISTS + count]
        rest = rest[LISTS + count :]
        p_ref, sum_refs = rest[0], rest[1 : 1 + LISTS]
        pay_refs, rest = rest[1 + LISTS : 1 + LISTS + count], rest[1 + LISTS + count :]
        rand, pay, band, glob, band_sum, glob_sum, sems = rest
        head = pl.program_id(0)

        @pl.when(head == 0)
        def _():
            run_copies(copy_parts(kr_refs, rand, sems, lanes, slots, cap, False, 0))

        fill(k_refs, band, glob, blocks)
        band_sum[...] = jnp.zeros_like(band_sum)
        for block in range(blocks):
            here = slice(block * BLOCK, (block + 1) * BLOCK)
            near = slice(block * BLOCK, (block + SPAN) * BLOCK)
            query = q_ref[here]
            grad = g_ref[here]
            entry = (head * blocks + block) * RAND
            places = [pick[entry + r] for r in range(RAND)]
            window = dot(band[near], query, NT)
            scores = [window[o * BLOCK : (o + 1) * BLOCK] for o in range(SPAN)]
            if block == 0:
                scores[0] = jnp.where(ends[0] > 0, MASKED, scores[0])
            if block == blocks - 1:
                scores[-1] = jnp.where(ends[1] > 0, MASKED, scores[-1])
            scores += [dot(rand[at], query, NT) for at in places]
            far = dot(glob[...], query, NT)
            scores += [far[g * BLOCK : (g + 1) * BLOCK] for g in range(GLOB)]
            peak = scores[0]
            for score in scores[1:]:
                peak = jnp.maximum(peak, score)
            peak = jnp.max(peak, axis=0, keepdims=True)
            powers = [jnp.exp2((score - peak) * POWER) for score in scores]
            total = powers[0]
            for power in powers[1:]:
                total = total + power
            inverse = 1.0 / jnp.sum(total, axis=0, keepdims=True)
            for number, power in enumerate(powers):
                weights = (power * inverse).astype(jnp.bfloat16)
                p_ref[0, block, number * BLOCK : (number + 1) * BLOCK] = weights
            cuts = pieces()
            for at, (a, b) in zip(places, cuts[1:]):
                pay[at] = dot(p_ref[0, block, a:b], grad, NN).astype(jnp.bfloat16)
            a, b = cuts[0]
            band_sum[near] += dot(p_ref[0, block, a:b], grad, NN)
            a, b = cuts[-1]
            term = dot(p_ref[0, block, a:b], grad, NN)
            if block == 0:
                glob_sum[...] = term
            else:
                glob_sum[...] += term
        store_sums(sum_refs, band_sum, glob_sum, blocks, 1.0)

        @pl.when(head == heads - 1)
        def _():
            run_copies(copy_parts(pay_refs, pay, sems, lanes, slots, cap, True))

    return kernel


def slope_kernel(lanes, slots, cap, heads, blocks):
    count = lanes * (PARTS + 1)

    def kernel(pick, q_ref, g_ref, p_ref, *rest):
        v_refs, vr_refs = rest[:LISTS], rest[LISTS : LISTS + count]
        rest = rest[LISTS + count :]
        ds_ref, sum_refs = rest[0], rest[1 : 1 + LISTS]
        pay_refs, rest = rest[1 + LISTS : 1 + LISTS + count], rest[1 + LISTS + count :]
        rand, pay, band, glob, band_sum, glob_sum, sems = rest
        head = pl.program_id(0)

        @pl.when(head == 0)
        def _():
            run_copies(copy_parts(vr_refs, rand, sems, lanes, slots, cap, False, 1))

        fill(v_refs, band, glob, blocks)
        band_sum[...] = jnp.zeros_like(band_sum)
        cuts = pieces()
        for block in range(blocks):
            here = slice(block * BLOCK, (block + 1) * BLOCK)
            near = slice(block * BLOCK, (block + SPAN) * BLOCK)
            query = q_ref[here]
            grad = g_ref[here]
            entry = (head * blocks + block) * RAND
            places = [pick[entry + r] for r in range(RAND)]
            listed = [band[near]] + [rand[at] for at in places] + [glob[...]]
            slopes = [dot(value, grad, NT) for value in listed]
            wide = [p_ref[0, block, a:b].astype(jnp.float32) for a, b in cuts]
            delta = 0.0
            for weight, slope in zip(wide, slopes):
                delta = delta + jnp.sum(weight * slope, axis=0, keepdims=True)
            for (a, b), weight, slope in zip(cuts, wide, slopes):
                ds_ref[0, block, a:b] = (weight * (slope - delta)).astype(jnp.bfloat16)
            for at, (a, b) in zip(places, cuts[1:]):
                term = dot(ds_ref[0, block, a:b], query, NN) * SCALE
                pay[at] = term.astype(jnp.bfloat16)
            a, b = cuts[0]
            band_sum[near] += dot(ds_ref[0, block, a:b], query, NN)
            a, b = cuts[-1]
            term = dot(ds_ref[0, block, a:b], query, NN)
            if block == 0:
                glob_sum[...] = term
            else:
                glob_sum[...] += term
        store_sums(sum_refs, band_sum, glob_sum, blocks, SCALE)

        @pl.when(head == heads - 1)
        def _():
            run_copies(copy_parts(pay_refs, pay, sems, lanes, slots, cap, True))

    return kernel


def output_kernel(lanes, slots, cap, heads, blocks):
    count = lanes * (PARTS + 1)

    def kernel(pick, p_ref, ds_ref, *rest):
        k_refs, v_refs, rest = rest[:LISTS], rest[LISTS : 2 * LISTS], rest[2 * LISTS :]
        kr_refs, vr_refs, rest = rest[:count], rest[count : 2 * count], rest[2 * count :]
        out_ref, dq_ref, k_rand, v_rand, k_band, v_band, k_glob, v_glob, sems, more = rest
        head = pl.program_id(0)

        @pl.when(head == 0)
        def _():
            run_copies(
                copy_parts(kr_refs, k_rand, sems, lanes, slots, cap, False, 0)
                + copy_parts(vr_refs, v_rand, more, lanes, slots, cap, False, 1)
            )

        fill(k_refs, k_band, k_glob, blocks)
        fill(v_refs, v_band, v_glob, blocks)
        for block in range(blocks):
            here = slice(block * BLOCK, (block + 1) * BLOCK)
            near = slice(block * BLOCK, (block + SPAN) * BLOCK)
            entry = (head * blocks + block) * RAND
            places = [pick[entry + r] for r in range(RAND)]
            for left, band, pool, glob, scale, to_ref in (
                (p_ref, v_band, v_rand, v_glob, 1.0, out_ref),
                (ds_ref, k_band, k_rand, k_glob, SCALE, dq_ref),
            ):
                listed = [band[near]] + [pool[at] for at in places] + [glob[...]]
                result = 0.0
                for (a, b), item in zip(pieces(), listed):
                    result = result + dot(left[0, block, a:b], item, TN)
                to_ref[here] = (result * scale).astype(jnp.bfloat16)

    return kernel


def body(queries, keys, values, out_grad, rand_ids, glob_ids):
    rows_here, width = queries.shape
    heads = width // DH
    blocks = rows_here // BLOCK
    shards = lax.axis_size("seq")
    planes = PLANES
    lanes = shards // planes
    place = lax.axis_index("seq")
    group = lax.axis_index("head")
    plane, lane = place // lanes, place % lanes
    columns = [[z * lanes + c for z in range(planes)] for c in range(lanes)]
    entries = heads * blocks * RAND
    cap = max(2, (5 * entries + 4 * shards - 1) // (4 * shards))
    slots = planes * cap
    total_slots = lanes * slots
    turn = [(i, i // lanes * lanes + (i + 1) % lanes) for i in range(shards)]
    back = [(target, source) for source, target in turn]
    sizes = (heads, lanes, slots, cap)

    def swap(array, bits):
        return lax.ppermute(array, "seq", [(i, i ^ bits) for i in range(shards)])

    def to_partners(arrays):
        return [arrays[0]] + [swap(arrays[k], k) for k in range(1, lanes)]

    def plane_sum(array):
        bits = 1
        while bits < lanes:
            other = swap(array, bits)
            wide = array.astype(jnp.float32) + other.astype(jnp.float32)
            array = wide.astype(jnp.bfloat16)
            bits *= 2
        return array

    ids_mine = lax.dynamic_slice_in_dim(rand_ids, group * heads, heads, 0)
    ids_plane = lax.dynamic_slice_in_dim(ids_mine, plane * lanes * blocks, lanes * blocks, 1)
    wanted = (
        ids_plane.reshape(heads, lanes, blocks, RAND).transpose(1, 0, 2, 3).reshape(lanes, entries)
    )
    source = wanted // blocks
    same = source[:, :, None] == source[:, None, :]
    before = jnp.tril(jnp.ones((entries, entries), bool), -1)
    slot = jnp.sum((same & before[None]).astype(jnp.int32), axis=2)
    source_plane, source_lane = source // lanes, source % lanes
    spot = ((source_plane - plane + planes) % planes) * cap + slot
    pick = ((source_lane ^ lane) * slots + spot)[lane]
    head_of = jnp.arange(entries, dtype=jnp.int32) // (blocks * RAND)
    inside = (source_plane * blocks + wanted % blocks) * heads + head_of[None, :]
    hit = (source_lane == lane)[:, :, None] & (
        spot[:, :, None] == jnp.arange(slots, dtype=jnp.int32)[None, None, :]
    )
    table = jnp.sum(jnp.where(hit, inside[:, :, None] + 1, 0), axis=1) - 1
    partners = jnp.arange(lanes, dtype=jnp.int32) ^ lane
    table = table[partners].reshape(-1)
    glob_place = glob_ids // blocks
    first, last = lane == 0, lane == lanes - 1
    own_first, own_last = plane * blocks, plane * blocks + blocks - 1
    rims = [
        jnp.where(last, jnp.maximum(own_first - 1, 0), own_last),
        jnp.where(first, jnp.minimum(own_last + 1, planes * blocks - 1), own_first),
        jnp.where(first, jnp.where(plane < planes - 1, own_last + 1, -1), own_first),
        jnp.where(last, own_first - 1, own_last),
    ]
    info = jnp.stack(
        [
            (glob_place // lanes) * blocks + glob_ids % blocks,
            (glob_place % lanes == lane).astype(jnp.int32),
        ],
        axis=1,
    )
    info = jnp.concatenate([info.reshape(-1), jnp.stack(rims)]).astype(jnp.int32)
    ends = jnp.stack([place == 0, place == shards - 1]).astype(jnp.int32)

    def cut(array, part):
        return array.reshape(blocks, BLOCK, width)[:, part * ROWS : (part + 1) * ROWS]

    def gather(piece):
        column = lax.all_gather(piece, "seq", axis_index_groups=columns)
        return column.reshape(planes * blocks, ROWS, width)

    def choose(column, table):
        return pick_blocks(column, table, info, *sizes)

    def exchange(outs):
        spread = plane_sum(outs[lanes])
        received = to_partners(outs[:lanes])
        low = lax.ppermute(outs[lanes + 1], "seq", turn)
        high = lax.ppermute(outs[lanes + 2], "seq", back)
        return received, spread, low, high

    def listed(own, parts):
        return [own] + [part[n] for n in (2, 3, 1) for part in parts]

    def requested(own, parts):
        return [array for k in range(lanes) for array in [own[k]] + [part[0][k] for part in parts]]

    def dense(returned, edges):
        glob_sum, low_in, high_in = edges
        return sum_blocks(
            returned, glob_sum, (low_in, high_in), table, info, planes * blocks, *sizes_back
        )

    def terms_of(outs, part):
        return [outs[1 + LISTS + k * (PARTS + 1) + part] for k in range(lanes)]

    def rims_of(outs, part):
        low, high = outs[2 + part], outs[2 + PARTS + part]
        low_in = lax.ppermute(high, "seq", turn)
        high_in = lax.ppermute(low, "seq", back)
        return plane_sum(outs[2 + 2 * PARTS + part]), low_in, high_in

    def scatter(array):
        return lax.psum_scatter(
            array, "seq", scatter_dimension=0, axis_index_groups=columns, tiled=True
        )

    def finish(own, sums, returned):
        own = own.reshape(blocks, BLOCK, width)
        total = final_sum(own, sums, returned, table, heads, slots, cap)
        return total.reshape(rows_here, width)

    sizes_back = (heads, slots, cap)
    head_block = pl.BlockSpec((rows_here, DH), lambda h: (0, h))
    rim_block = pl.BlockSpec((ROWS, DH), lambda h: (0, h))
    glob_block = pl.BlockSpec((GLOB, ROWS, DH), lambda h: (0, 0, h))
    weight_block = pl.BlockSpec((1, blocks, LISTED * BLOCK, BLOCK), lambda h: (h, 0, 0, 0))
    list_blocks = [head_block] + [rim_block] * (2 * PARTS) + [glob_block] * PARTS
    like = jax.ShapeDtypeStruct((rows_here, width), jnp.bfloat16)
    weights_like = jax.ShapeDtypeStruct((heads, blocks, LISTED * BLOCK, BLOCK), jnp.bfloat16)
    sums_like = [jax.ShapeDtypeStruct((rows_here, width), jnp.float32)]
    sums_like += [jax.ShapeDtypeStruct((ROWS, width), jnp.bfloat16)] * (2 * PARTS)
    sums_like += [jax.ShapeDtypeStruct((GLOB, ROWS, width), jnp.bfloat16)] * PARTS
    own_like = jax.ShapeDtypeStruct((cap, BLOCK, DH), jnp.bfloat16)
    part_like = jax.ShapeDtypeStruct((slots - cap, ROWS, DH), jnp.bfloat16)
    pay_like = ([own_like] + [part_like] * PARTS) * lanes
    count = len(pay_like)
    pool = pltpu.VMEM((total_slots, BLOCK, DH), jnp.bfloat16)
    band = pltpu.VMEM(((blocks + 2 * WMAX) * BLOCK, DH), jnp.bfloat16)
    glob = pltpu.VMEM((GLOB * BLOCK, DH), jnp.bfloat16)
    band_sum = pltpu.VMEM(((blocks + 2 * WMAX) * BLOCK, DH), jnp.float32)
    glob_sum = pltpu.VMEM((GLOB * BLOCK, DH), jnp.float32)
    sems = pltpu.SemaphoreType.DMA((count,))

    def per_head(kernel, out_shape, in_specs, out_specs, scratch, micros):
        return pl.pallas_call(
            kernel(lanes, slots, cap, heads, blocks),
            grid=(heads,),
            out_shape=out_shape,
            in_specs=in_specs,
            out_specs=out_specs,
            scratch_shapes=scratch,
            compiler_params=params(),
            cost_estimate=cost(micros),
        )

    column_0 = gather(cut(keys, 0))
    piece, table = tie(cut(keys, 1), table)
    column_1 = gather(piece)
    blocks_of = (blocks, BLOCK, width)
    own = pick_own(keys.reshape(blocks_of), values.reshape(blocks_of), table, *sizes)
    own = to_partners(own)
    column_0, own = tie(column_0, own)
    chosen_0 = choose(column_0, table)
    piece, chosen_0 = tie(cut(values, 0), chosen_0)
    column_2 = gather(piece)
    key_0 = exchange(chosen_0)
    column_1, key_0 = tie(column_1, key_0)
    chosen_1 = choose(column_1, table)
    piece, chosen_1 = tie(cut(values, 1), chosen_1)
    column_3 = gather(piece)
    key_1 = exchange(chosen_1)
    key_list, key_rand = listed(keys, [key_0, key_1]), requested(own, [key_0, key_1])

    outs = per_head(
        weights_kernel,
        [weights_like] + sums_like + pay_like,
        [smem_spec()] * 2 + [head_block] * 2 + list_blocks + [any_spec()] * count,
        [weight_block] + list_blocks + [any_spec()] * count,
        [pool, pool, band, glob, band_sum, glob_sum, sems],
        24,
    )(pick, ends, queries, out_grad, *key_list, *key_rand)
    weights, value_own = outs[:2]

    edges = rims_of(outs, 0)
    returned = to_partners(terms_of(outs, 1))
    column_2, value_own = tie(column_2, value_own)
    value_0 = exchange(choose(column_2, table))
    column_3, value_0 = tie(column_3, value_0)
    chosen_3 = choose(column_3, table)
    chosen_3, returned = tie(chosen_3, returned)
    value_1 = exchange(chosen_3)
    later = [outs[n] for n in range(len(outs))]
    later, value_1 = tie(later, value_1)
    total, weights = tie(dense(returned, edges), weights)
    value_sums = [scatter(total)]
    edges = rims_of(later, 1)
    returned = to_partners(terms_of(later, 2))
    value_list = listed(values, [value_0, value_1])
    value_rand = requested(own, [value_0, value_1])

    outs = per_head(
        slope_kernel,
        [weights_like] + sums_like + pay_like,
        [smem_spec()] + [head_block] * 2 + [weight_block] + list_blocks + [any_spec()] * count,
        [weight_block] + list_blocks + [any_spec()] * count,
        [pool, pool, band, glob, band_sum, glob_sum, sems],
        20,
    )(pick, queries, out_grad, weights, *value_list, *value_rand)
    slopes, key_own = outs[:2]

    returned, key_own = tie(returned, key_own)
    value_sums.append(scatter(dense(returned, edges)))
    edges = rims_of(outs, 0)
    returned = to_partners(terms_of(outs, 1))
    more = [outs[n] for n in range(len(outs))]
    more, returned = tie(more, returned)
    key_sums = [scatter(dense(returned, edges))]
    edges = rims_of(more, 1)
    returned = to_partners(terms_of(more, 2))
    value_mine, key_mine, returned = tie(terms_of(later, 0), terms_of(more, 0), returned)
    total, slopes = tie(dense(returned, edges), slopes)
    key_sums.append(scatter(total))
    value_mine, key_mine = to_partners(value_mine), to_partners(key_mine)

    out, query_grad = per_head(
        output_kernel,
        [like, like],
        [smem_spec()] + [weight_block] * 2 + list_blocks * 2 + [any_spec()] * (2 * count),
        [head_block] * 2,
        [pool, pool, band, band, glob, glob, sems, sems],
        15,
    )(pick, weights, slopes, *key_list, *value_list, *key_rand, *value_rand)
    value_grad = finish(value_own, value_sums, value_mine)
    key_grad = finish(key_own, key_sums, key_mine)
    return out, query_grad, key_grad, value_grad


def solution(mesh):
    return jax.shard_map(
        body,
        mesh=mesh,
        in_specs=(P("seq", "head"), P("seq", "head"), P("seq", "head"), P("seq", "head"), P(), P()),
        out_specs=(P("seq", "head"), P("seq", "head"), P("seq", "head"), P("seq", "head")),
        check_vma=False,
    )
```

time: 548 us -> 477 us (0.87)
  waiting for transfers between devices: 323 us -> 211 us
  local copies, waits for them, and re-layouts: 21.8 us -> 59.3 us
  other arithmetic: 20.4 us -> 4.94 us
  Pallas kernels: 82.7 us -> 96.7 us
    ppermute x36 -> x49, waiting for transfers between devices: 184 us -> 103 us  [swap(): return lax.ppermute(array, 'seq', [(i, i ^ bits) for i in range(shards)])]
    ppermute x6 -> x16, waiting for transfers between devices: 0.02 us -> 49.4 us  [the longest x4 31.4 us: exchange(): low = lax.ppermute(outs[lanes + 1], 'seq', turn)]
    all_gather x4, waiting for transfers between devices: 80.8 us -> 36.4 us  [gather(): column = lax.all_gather(piece, 'seq', axis_index_groups=columns)]
    unnamed x91 -> x223, local copies, waits for them, and re-layouts: 15.2 us -> 53.9 us
    reduce_scatter x4, waiting for transfers between devices: 57.3 us -> 21.7 us  [scatter(): lax.psum_scatter(array, 'seq', scatter_dimension=0, axis_index_groups=col...]
    pallas_call x10 -> x14, Pallas kernels: 82.7 us -> 96.7 us  [the longest x1 23.8 us: body(): per_head(weights_kernel, [weights_like] + sums_like + pay_like, [smem_spe...]
    add x2 -> x0, other arithmetic: 5.48 us -> none  [give_back(): own.reshape(blocks, BLOCK, width)]
    ppermute x36 -> x49, starting transfers between devices: 58.4 us -> 62.5 us  [swap(): return lax.ppermute(array, 'seq', [(i, i ^ bits) for i in range(shards)])]
  transfers between devices with their start and end apart: 50 -> 73, of which waited for: 22 -> 37; matrix products, arithmetic and copies ran while one was open for 4% -> 2% of each run, Pallas kernels for 15% -> 19%
where the time goes in v2:
time: 477 us; the launch traced here: 474 us
  waiting for transfers between devices  211 us (44%)
  Pallas kernels  96.7 us (20%)
  starting transfers between devices  87.3 us (18%)
  local copies, waits for them, and re-layouts  59.3 us (12%)
  between operations  14.9 us (3%)
  other arithmetic  4.94 us (1%)
    ppermute x49, waiting for transfers between devices, swap(): return lax.ppermute(array, 'seq', [(i, i ^ bits) for i in range(shards)])  103 us
    ppermute x49, starting transfers between devices, swap(): return lax.ppermute(array, 'seq', [(i, i ^ bits) for i in range(shards)])  62.5 us
    unnamed x223, local copies, waits for them, and re-layouts  53.9 us
    all_gather x4, waiting for transfers between devices, gather(): column = lax.all_gather(piece, 'seq', axis_index_groups=columns)  36.4 us
    ppermute x4, waiting for transfers between devices, exchange(): low = lax.ppermute(outs[lanes + 1], 'seq', turn)  31.4 us
    pallas_call x1, Pallas kernels, body(): per_head(weights_kernel, [weights_like] + sums_like + pay_like, [smem_spe...  23.8 us
    reduce_scatter x4, waiting for transfers between devices, scatter(): lax.psum_scatter(array, 'seq', scatter_dimension=0, axis_index_groups=col...  21.7 us
    pallas_call x1, Pallas kernels, body(): per_head(slope_kernel, [weights_like] + sums_like + pay_like, [smem_spec(...  20.9 us
  transfers between devices with their start and end apart: 73, of which 37 were waited for; matrix products, arithmetic and copies ran while one was open for 2% of the time, Pallas kernels for 19%

profile of v2, /device:TPU:16, one launch (start us, length us, event | category | flops | bytes accessed | tf_op | source)
XLA Modules:
  0.0 473.7 jit_solution(5023304712923074802)
XLA Ops:
  7.3 2.4 fusion.16
  20.1 10.2 %collective-permute-done.rest_10_.rest_17_.rest_29_ = bf16[2,8,128,128]{3,2,1,0:T(8,128)(2,1)S(1)} collective-permute-done((bf16[2,8,128,128]{3,2,1,0:T(8,128)(2,1)}, bf16[2,8,128,128]{3,2,1,0:T(8,128)(2,1)S(1)}, u32[]{:S(2)}, u32[]{:S(2)}) %collective-permute-start) | collective-permute-done | bytes 524320 | tf_op jit(solution)/shard_map/ppermute | solution.py:441
  30.2 10.1 %collective-permute-done.1.rest_13_.rest_20_.rest_32_ = bf16[2,8,128,128]{3,2,1,0:T(8,128)(2,1)S(1)} collective-permute-done((bf16[2,8,128,128]{3,2,1,0:T(8,128)(2,1)S(1)}, bf16[2,8,128,128]{3,2,1,0:T(8,128)(2,1)S(1)}, u32[]{:S(2)}, u32[]{:S(2)}) %collective-permute-start.1) | collective-permute-done | bytes 524320 | tf_op jit(solution)/shard_map/ppermute | solution.py:441
  41.4 14.4 %all-gather.11.cloned.1.call-done.column_ref = bf16[16,64,1024]{2,1,0:T(8,128)(2,1)} async-done(((bf16[4,64,1024]{2,1,0:T(8,128)(2,1)}), bf16[16,64,1024]{2,1,0:T(8,128)(2,1)}) %all-gather.11.cloned.1.call-update) | async-done | bytes 2097168 | tf_op jit(solution)/shard_map/all_gather | solution.py:498
  61.9 6.6 %collective-permute-done.6 = bf16[2,64,1024]{2,1,0:T(8,128)(2,1)S(1)} collective-permute-done((bf16[2,64,1024]{2,1,0:T(8,128)(2,1)S(1)}, bf16[2,64,1024]{2,1,0:T(8,128)(2,1)S(1)}, u32[]{:S(2)}, u32[]{:S(2)}) %collective-permute-start.6) | collective-permute-done | bytes 262176 | tf_op jit(solution)/shard_map/ppermute | solution.py:441
  75.0 3.3 collective-permute-done.7
  78.3 2.4 collective-permute-start.9
  80.7 22.0 %all-gather.9.cloned.1.call-done.column_ref = bf16[16,64,1024]{2,1,0:T(8,128)(2,1)} async-done(((bf16[4,64,1024]{2,1,0:T(8,128)(2,1)}), bf16[16,64,1024]{2,1,0:T(8,128)(2,1)}) %all-gather.9.cloned.1.call-update) | async-done | bytes 2097168 | tf_op jit(solution)/shard_map/all_gather | solution.py:498
  104.7 3.0 shard_map.95
  110.6 6.6 %collective-permute-done.12 = bf16[2,64,1024]{2,1,0:T(8,128)(2,1)S(1)} collective-permute-done((bf16[2,64,1024]{2,1,0:T(8,128)(2,1)S(1)}, bf16[2,64,1024]{2,1,0:T(8,128)(2,1)S(1)}, u32[]{:S(2)}, u32[]{:S(2)}) %collective-permute-start.12) | collective-permute-done | bytes 262176 | tf_op jit(solution)/shard_map/ppermute | solution.py:441
  125.1 2.7 collective-permute-done.13
  128.6 2.4 collective-permute-start.11
  132.1 10.0 %collective-permute-done.10.rest_2_ = bf16[64,1024]{1,0:T(8,128)(2,1)S(1)} collective-permute-done((bf16[64,1024]{1,0:T(8,128)(2,1)}, bf16[64,1024]{1,0:T(8,128)(2,1)S(1)}, u32[]{:S(2)}, u32[]{:S(2)}) %collective-permute-start.10) | collective-permute-done | bytes 131104 | tf_op jit(solution)/shard_map/ppermute | solution.py:507
  146.5 23.8 %shard_map.96 = (bf16[8,4,1024,128]{3,2,1,0:T(8,128)(2,1)}, f32[512,1024]{1,0:T(8,128)}, bf16[64,1024]{1,0:T(8,128)(2,1)}, bf16[64,1024]{1,0:T(8,128)(2,1)S(1)},...) custom-call(s32[96]{0:T(128)S(1)} %dynamic-slice_bitcast_fusion.pick, ...), custom_call_target="tpu_custom_call" | custom-call | bytes 84000000 | tf_op jit(solution)/shard_map/pallas_call | solution.py:594
  174.6 4.9 %collective-permute-done.17 = bf16[2,64,1024]{2,1,0:T(8,128)(2,1)S(1)} collective-permute-done((bf16[2,64,1024]{2,1,0:T(8,128)(2,1)S(1)}, bf16[2,64,1024]{2,1,0:T(8,128)(2,1)S(1)}, u32[]{:S(2)}, u32[]{:S(2)}) %collective-permute-start.17) | collective-permute-done | bytes 262176 | tf_op jit(solution)/shard_map/ppermute | solution.py:441
  190.6 3.6 collective-permute-done.24
  195.7 9.8 %collective-permute-done.26.rest_1_.rest_8_ = bf16[64,1024]{1,0:T(8,128)(2,1)S(1)} collective-permute-done((bf16[64,1024]{1,0:T(8,128)(2,1)S(1)}, bf16[64,1024]{1,0:T(8,128)(2,1)S(1)}, u32[]{:S(2)}, u32[]{:S(2)}) %collective-permute-start.26) | collective-permute-done | bytes 131104 | tf_op jit(solution)/shard_map/ppermute | solution.py:507
  214.3 2.4 collective-permute-done.23.rest_17_.rest_36_
  218.2 2.4 collective-permute-done.25
  223.7 2.7 shard_map.98
  229.3 5.0 %collective-permute-done.29.rest_2_ = bf16[24,64,128]{2,1,0:T(8,128)(2,1)S(1)} collective-permute-done((bf16[24,64,128]{2,1,0:T(8,128)(2,1)}, bf16[24,64,128]{2,1,0:T(8,128)(2,1)S(1)}, u32[]{:S(2)}, u32[]{:S(2)}) %collective-permute-start.29) | collective-permute-done | bytes 393248 | tf_op jit(solution)/shard_map/ppermute | solution.py:441
  235.0 5.1 %shard_map.99 = bf16[16,64,1024]{2,1,0:T(8,128)(2,1)} custom-call(s32[128]{0:T(128)S(1)} %reshape.264.table_ref, s32[8]{0:T(128)S(1)} %concatenate.3.info_ref, bf16[2,64,1024]{2,1,0:T(8,128)(2,1)S(1)} %add_convert_fusion.10.glob_ref, bf16[64,1024]{1,0:T(8,128)(2,1)} %collective-permute-done.19.low_ref, bf16[64,1024]{1,0:T(8,128)(2,1)} %collective-permute-done.20.high_ref, ...), custom_call_target="tpu_custom_call" | custom-call | bytes 21000000 | tf_op jit(solution)/shard_map/pallas_call | solution.py:162
  241.0 7.9 %collective-permute-done.34 = bf16[2,64,1024]{2,1,0:T(8,128)(2,1)S(1)} collective-permute-done((bf16[2,64,1024]{2,1,0:T(8,128)(2,1)S(1)}, bf16[2,64,1024]{2,1,0:T(8,128)(2,1)S(1)}, u32[]{:S(2)}, u32[]{:S(2)}) %collective-permute-start.34) | collective-permute-done | bytes 262176 | tf_op jit(solution)/shard_map/ppermute | solution.py:441
  249.1 2.5 collective-permute-start.31
  255.1 4.3 collective-permute-done.35
  259.6 11.6 %collective-permute-done.36.rest_2_.rest_9_ = bf16[64,1024]{1,0:T(8,128)(2,1)S(1)} collective-permute-done((bf16[64,1024]{1,0:T(8,128)(2,1)}, bf16[64,1024]{1,0:T(8,128)(2,1)S(1)}, u32[]{:S(2)}, u32[]{:S(2)}) %collective-permute-start.36) | collective-permute-done | bytes 131104 | tf_op jit(solution)/shard_map/ppermute | solution.py:507
  273.1 3.3 collective-permute-start.58
  276.6 3.2 collective-permute-start.50
  279.9 3.7 collective-permute-done.58
  285.8 20.9 %shard_map.100 = (bf16[8,4,1024,128]{3,2,1,0:T(8,128)(2,1)}, f32[512,1024]{1,0:T(8,128)}, bf16[64,1024]{1,0:T(8,128)(2,1)S(1)}, bf16[64,1024]{1,0:T(8,128)(2,1)S...) custom-call(s32[96]{0:T(128)S(1)} %dynamic-slice_bitcast_fusion.pick, ...), custom_call_target="tpu_custom_call" | custom-call | bytes 70000000 | tf_op jit(solution)/shard_map/pallas_call | solution.py:621
  315.1 5.1 %collective-permute-done.61.high_ref = bf16[64,1024]{1,0:T(8,128)(2,1)S(1)} collective-permute-done((bf16[64,1024]{1,0:T(8,128)(2,1)S(1)}, bf16[64,1024]{1,0:T(8,128)(2,1)S(1)}, u32[]{:S(2)}, u32[]{:S(2)}) %collective-permute-start.61) | collective-permute-done | bytes 131104 | tf_op jit(solution)/shard_map/ppermute | solution.py:529
  320.2 4.7 %shard_map.105 = bf16[16,64,1024]{2,1,0:T(8,128)(2,1)} custom-call(s32[128]{0:T(128)S(1)} %reshape.264.table_ref, s32[8]{0:T(128)S(1)} %concatenate.3.info_ref, bf16[2,64,1024]{2,1,0:T(8,128)(2,1)S(1)} %add_convert_fusion.glob_ref, bf16[64,1024]{1,0:T(8,128)(2,1)S(1)} %collective-permute-done.60.low_ref, ...), custom_call_target="tpu_custom_call" | custom-call | bytes 21000000 | tf_op jit(solution)/shard_map/pallas_call | solution.py:162
  325.0 2.4 collective-permute-start.51
  336.4 2.4 collective-permute-start.53
  338.8 6.8 %collective-permute-done.40.rest_3_ = bf16[24,64,128]{2,1,0:T(8,128)(2,1)S(1)} collective-permute-done((bf16[24,64,128]{2,1,0:T(8,128)(2,1)S(1)}, bf16[24,64,128]{2,1,0:T(8,128)(2,1)S(1)}, u32[]{:S(2)}, u32[]{:S(2)}) %collective-permute-start.40) | collective-permute-done | bytes 393248 | tf_op jit(solution)/shard_map/ppermute | solution.py:441
  347.6 3.8 collective-permute-done.53.low_ref
  351.4 4.6 shard_map.103
  358.5 2.6 collective-permute-start.47
  364.2 4.4 collective-permute-done.45.rest_1_
  368.6 7.5 %collective-permute-done.47.rest_3_ = bf16[24,64,128]{2,1,0:T(8,128)(2,1)S(1)} collective-permute-done((bf16[24,64,128]{2,1,0:T(8,128)(2,1)S(1)}, bf16[24,64,128]{2,1,0:T(8,128)(2,1)S(1)}, u32[]{:S(2)}, u32[]{:S(2)}) %collective-permute-start.47) | collective-permute-done | bytes 393248 | tf_op jit(solution)/shard_map/ppermute | solution.py:441
  376.1 4.4 collective-permute-done.42
  382.7 4.6 shard_map.101
  387.4 3.0 collective-permute-start.63
  394.7 2.5 collective-permute-start.57
  413.4 14.7 %shard_map.102 = (bf16[512,1024]{1,0:T(8,128)(2,1)}, bf16[512,1024]{1,0:T(8,128)(2,1)}) custom-call(s32[96]{0:T(128)S(1)} %dynamic-slice_bitcast_fusion.pick, bf16[8,4,1024,128]{3,2,1,0:T(8,128)(2,1)} %get-tuple-element.262.p_ref, bf16[8,4,1024,128]{3,2,1,0:T(8,128)(2,1)} %get-tuple-element.334.ds_ref, bf16[512,1024]{1,0:T(8,128)(2,1)} %rest_0_.5, ...), custom_call_target="tpu_custom_call" | custom-call | bytes 52500000 | tf_op jit(solution)/shard_map/pallas_call | solution.py:645
  435.5 2.7 shard_map.106
  438.2 21.7 %reduce-scatter.7.cloned.1.call-done.rest_1_ = bf16[4,64,1024]{2,1,0:T(8,128)(2,1)} async-done(((bf16[16,64,1024]{2,1,0:T(8,128)(2,1)}), bf16[4,64,1024]{2,1,0:T(8,128)(2,1)}) %reduce-scatter.7.cloned.1.call-update) | async-done | bytes 524304 | tf_op jit(solution)/shard_map/reduce_scatter | solution.py:533
  463.6 3.3 shard_map.104
  (384 shorter events, 144.2 us)
Async XLA Ops:
  7.2 48.7 %all-gather.11.cloned.1.call-start = ((), (), s32[]{:S(2)}) async-start(), calls=%async_computation.9 | async-start | bytes 2621440 | tf_op jit(solution)/shard_map/all_gather | solution.py:498
  9.7 93.0 %all-gather.9.cloned.1.call-start = ((), (), s32[]{:S(2)}) async-start(), calls=%async_computation.8 | async-start | bytes 2621440 | tf_op jit(solution)/shard_map/all_gather | solution.py:498
  12.0 169.2 %all-gather.15.cloned.1.call-start = ((), (), s32[]{:S(2)}) async-start(), calls=%async_computation.11 | async-start | bytes 2621440 | tf_op jit(solution)/shard_map/all_gather | solution.py:498
  15.2 15.0 %collective-permute-start = (bf16[2,8,128,128]{3,2,1,0:T(8,128)(2,1)}, bf16[2,8,128,128]{3,2,1,0:T(8,128)(2,1)S(1)}, u32[]{:S(2)}, u32[]{:S(2)}) collective-permute-start(bf16[2,8,128,128]{3,2,1,0:T(8,128)(2,1)} %get-tuple-element.187), channel_id=1, source_target_pairs={{0,2},{2,0},{4,6},{6,4},{8,10},{10,8},{12,14},{14,12},{16,18},{18,... | collective-permute-start | bytes 1572872 | tf_op jit(solution)/shard_map/ppermute | solution.py:441
  16.7 23.7 %collective-permute-start.1 = (bf16[2,8,128,128]{3,2,1,0:T(8,128)(2,1)S(1)}, bf16[2,8,128,128]{3,2,1,0:T(8,128)(2,1)S(1)}, u32[]{:S(2)}, u32[]{:S(2)}) collective-permute-start(bf16[2,8,128,128]{3,2,1,0:T(8,128)(2,1)S(1)} %get-tuple-element.188), channel_id=1, source_target_pairs={{0,4},{2,6},{4,0},{6,2},{8,12},{10,14},{12,8},{14,10},{16,20},{18,... | collective-permute-start | bytes 1572872 | tf_op jit(solution)/shard_map/ppermute | solution.py:441
  18.2 23.2 %collective-permute-start.2 = (bf16[2,8,128,128]{3,2,1,0:T(8,128)(2,1)S(1)}, bf16[2,8,128,128]{3,2,1,0:T(8,128)(2,1)}, u32[]{:S(2)}, u32[]{:S(2)}) collective-permute-start(bf16[2,8,128,128]{3,2,1,0:T(8,128)(2,1)S(1)} %get-tuple-element.189), channel_id=1, source_target_pairs={{0,6},{2,4},{4,2},{6,0},{8,14},{10,12},{12,10},{14,8},{16,22},{18,... | collective-permute-start | bytes 1572872 | tf_op jit(solution)/shard_map/ppermute | solution.py:441
  60.3 161.7 %all-gather.13.cloned.1.call-start = ((), (), s32[]{:S(2)}) async-start(), calls=%async_computation.10 | async-start | bytes 2621440 | tf_op jit(solution)/shard_map/all_gather | solution.py:498
  70.1 32.6 %collective-permute-start.3 = (bf16[24,64,128]{2,1,0:T(8,128)(2,1)S(1)}, bf16[24,64,128]{2,1,0:T(8,128)(2,1)S(1)}, u32[]{:S(2)}, u32[]{:S(2)}) collective-permute-start(bf16[24,64,128]{2,1,0:T(8,128)(2,1)S(1)} %get-tuple-element.199), channel_id=1, source_target_pairs={{0,2},{2,0},{4,6},{6,4},{8,10},{10,8},{12,14},{14,12},{16,18},{18,... | collective-permute-start | bytes 1179656 | tf_op jit(solution)/shard_map/ppermute | solution.py:441
  71.5 31.2 %collective-permute-start.4 = (bf16[24,64,128]{2,1,0:T(8,128)(2,1)S(1)}, bf16[24,64,128]{2,1,0:T(8,128)(2,1)S(1)}, u32[]{:S(2)}, u32[]{:S(2)}) collective-permute-start(bf16[24,64,128]{2,1,0:T(8,128)(2,1)S(1)} %get-tuple-element.200), channel_id=1, source_target_pairs={{0,4},{2,6},{4,0},{6,2},{8,12},{10,14},{12,8},{14,10},{16,20},{18,... | collective-permute-start | bytes 1179656 | tf_op jit(solution)/shard_map/ppermute | solution.py:441
  72.1 30.6 %collective-permute-start.5 = (bf16[24,64,128]{2,1,0:T(8,128)(2,1)S(1)}, bf16[24,64,128]{2,1,0:T(8,128)(2,1)S(1)}, u32[]{:S(2)}, u32[]{:S(2)}) collective-permute-start(bf16[24,64,128]{2,1,0:T(8,128)(2,1)S(1)} %get-tuple-element.201), channel_id=1, source_target_pairs={{0,6},{2,4},{4,2},{6,0},{8,14},{10,12},{12,10},{14,8},{16,22},{18,... | collective-permute-start | bytes 1179656 | tf_op jit(solution)/shard_map/ppermute | solution.py:441
  73.6 29.1 %collective-permute-start.8 = (bf16[64,1024]{1,0:T(8,128)(2,1)S(1)}, bf16[64,1024]{1,0:T(8,128)(2,1)S(1)}, u32[]{:S(2)}, u32[]{:S(2)}) collective-permute-start(bf16[64,1024]{1,0:T(8,128)(2,1)S(1)} %get-tuple-element.203), channel_id=1, source_target_pairs={{0,2},{2,4},{4,6},{6,0},{8,10},{10,12},{12,14},{14,8},{16,18},{18,... | collective-permute-start | bytes 393224 | tf_op jit(solution)/shard_map/ppermute | solution.py:507
  78.3 24.4 %collective-permute-start.9 = (bf16[64,1024]{1,0:T(8,128)(2,1)S(1)}, bf16[64,1024]{1,0:T(8,128)(2,1)S(1)}, u32[]{:S(2)}, u32[]{:S(2)}) collective-permute-start(bf16[64,1024]{1,0:T(8,128)(2,1)S(1)} %get-tuple-element.204), channel_id=1, source_target_pairs={{2,0},{4,2},{6,4},{0,6},{10,8},{12,10},{14,12},{8,14},{18,16},{20,... | collective-permute-start | bytes 393224 | tf_op jit(solution)/shard_map/ppermute | solution.py:508
  109.1 320.5 %reduce-scatter.9.cloned.1.call-start = ((), (), s32[]{:S(2)}) async-start(), calls=%async_computation.6 | async-start | bytes 2621440 | tf_op jit(solution)/shard_map/reduce_scatter | solution.py:533
  119.5 24.0 %collective-permute-start.14 = (bf16[24,64,128]{2,1,0:T(8,128)(2,1)}, bf16[24,64,128]{2,1,0:T(8,128)(2,1)S(1)}, u32[]{:S(2)}, u32[]{:S(2)}) collective-permute-start(bf16[24,64,128]{2,1,0:T(8,128)(2,1)} %get-tuple-element.224), channel_id=1, source_target_pairs={{0,2},{2,0},{4,6},{6,4},{8,10},{10,8},{12,14},{14,12},{16,18},{18,... | collective-permute-start | bytes 1179656 | tf_op jit(solution)/shard_map/ppermute | solution.py:441
  120.9 24.1 %collective-permute-start.15 = (bf16[24,64,128]{2,1,0:T(8,128)(2,1)}, bf16[24,64,128]{2,1,0:T(8,128)(2,1)S(1)}, u32[]{:S(2)}, u32[]{:S(2)}) collective-permute-start(bf16[24,64,128]{2,1,0:T(8,128)(2,1)} %get-tuple-element.227), channel_id=1, source_target_pairs={{0,4},{2,6},{4,0},{6,2},{8,12},{10,14},{12,8},{14,10},{16,20},{18,... | collective-permute-start | bytes 1179656 | tf_op jit(solution)/shard_map/ppermute | solution.py:441
  121.5 23.6 %collective-permute-start.16 = (bf16[24,64,128]{2,1,0:T(8,128)(2,1)S(1)}, bf16[24,64,128]{2,1,0:T(8,128)(2,1)S(1)}, u32[]{:S(2)}, u32[]{:S(2)}) collective-permute-start(bf16[24,64,128]{2,1,0:T(8,128)(2,1)S(1)} %get-tuple-element.230), channel_id=1, source_target_pairs={{0,6},{2,4},{4,2},{6,0},{8,14},{10,12},{12,10},{14,8},{16,22},{18,... | collective-permute-start | bytes 1179656 | tf_op jit(solution)/shard_map/ppermute | solution.py:441
  123.7 18.5 %collective-permute-start.10 = (bf16[64,1024]{1,0:T(8,128)(2,1)}, bf16[64,1024]{1,0:T(8,128)(2,1)S(1)}, u32[]{:S(2)}, u32[]{:S(2)}) collective-permute-start(bf16[64,1024]{1,0:T(8,128)(2,1)} %copy-done.98), channel_id=1, source_target_pairs={{0,2},{2,4},{4,6},{6,0},{8,10},{10,12},{12,14},{14,8},{16,18},{18,... | collective-permute-start | bytes 393224 | tf_op jit(solution)/shard_map/ppermute | solution.py:507
  186.4 23.3 %collective-permute-start.21 = (bf16[24,64,128]{2,1,0:T(8,128)(2,1)S(1)}, bf16[24,64,128]{2,1,0:T(8,128)(2,1)S(1)}, u32[]{:S(2)}, u32[]{:S(2)}) collective-permute-start(bf16[24,64,128]{2,1,0:T(8,128)(2,1)S(1)} %get-tuple-element.239), channel_id=1, source_target_pairs={{0,2},{2,0},{4,6},{6,4},{8,10},{10,8},{12,14},{14,12},{16,18},{18,... | collective-permute-start | bytes 1179656 | tf_op jit(solution)/shard_map/ppermute | solution.py:441
  187.0 25.0 %collective-permute-start.22 = (bf16[24,64,128]{2,1,0:T(8,128)(2,1)S(1)}, bf16[24,64,128]{2,1,0:T(8,128)(2,1)S(1)}, u32[]{:S(2)}, u32[]{:S(2)}) collective-permute-start(bf16[24,64,128]{2,1,0:T(8,128)(2,1)S(1)} %get-tuple-element.240), channel_id=1, source_target_pairs={{0,4},{2,6},{4,0},{6,2},{8,12},{10,14},{12,8},{14,10},{16,20},{18,... | collective-permute-start | bytes 1179656 | tf_op jit(solution)/shard_map/ppermute | solution.py:441
  187.5 18.0 %collective-permute-start.26 = (bf16[64,1024]{1,0:T(8,128)(2,1)S(1)}, bf16[64,1024]{1,0:T(8,128)(2,1)S(1)}, u32[]{:S(2)}, u32[]{:S(2)}) collective-permute-start(bf16[64,1024]{1,0:T(8,128)(2,1)S(1)} %get-tuple-element.243), channel_id=1, source_target_pairs={{0,2},{2,4},{4,6},{6,0},{8,10},{10,12},{12,14},{14,8},{16,18},{18,... | collective-permute-start | bytes 393224 | tf_op jit(solution)/shard_map/ppermute | solution.py:507
  189.0 19.3 %collective-permute-start.27 = (bf16[64,1024]{1,0:T(8,128)(2,1)S(1)}, bf16[64,1024]{1,0:T(8,128)(2,1)S(1)}, u32[]{:S(2)}, u32[]{:S(2)}) collective-permute-start(bf16[64,1024]{1,0:T(8,128)(2,1)S(1)} %get-tuple-element.244), channel_id=1, source_target_pairs={{2,0},{4,2},{6,4},{0,6},{10,8},{12,10},{14,12},{8,14},{18,16},{20,... | collective-permute-start | bytes 393224 | tf_op jit(solution)/shard_map/ppermute | solution.py:508
  194.2 22.5 %collective-permute-start.23 = (bf16[24,64,128]{2,1,0:T(8,128)(2,1)S(1)}, bf16[24,64,128]{2,1,0:T(8,128)(2,1)S(1)}, u32[]{:S(2)}, u32[]{:S(2)}) collective-permute-start(bf16[24,64,128]{2,1,0:T(8,128)(2,1)S(1)} %get-tuple-element.241), channel_id=1, source_target_pairs={{0,6},{2,4},{4,2},{6,0},{8,14},{10,12},{12,10},{14,8},{16,22},{18,... | collective-permute-start | bytes 1179656 | tf_op jit(solution)/shard_map/ppermute | solution.py:441
  205.5 15.1 %collective-permute-start.25 = (bf16[2,64,1024]{2,1,0:T(8,128)(2,1)S(1)}, bf16[2,64,1024]{2,1,0:T(8,128)(2,1)S(1)}, u32[]{:S(2)}, u32[]{:S(2)}) collective-permute-start(bf16[2,64,1024]{2,1,0:T(8,128)(2,1)S(1)} %add_convert_fusion.9), channel_id=1, source_target_pairs={{0,4},{2,6},{4,0},{6,2},{8,12},{10,14},{12,8},{14,10},{16,20},{18,... | collective-permute-start | bytes 786440 | tf_op jit(solution)/shard_map/ppermute | solution.py:441
  208.3 21.0 %collective-permute-start.28 = (bf16[24,64,128]{2,1,0:T(8,128)(2,1)}, bf16[24,64,128]{2,1,0:T(8,128)(2,1)S(1)}, u32[]{:S(2)}, u32[]{:S(2)}) collective-permute-start(bf16[24,64,128]{2,1,0:T(8,128)(2,1)} %get-tuple-element.254), channel_id=1, source_target_pairs={{0,2},{2,0},{4,6},{6,4},{8,10},{10,8},{12,14},{14,12},{16,18},{18,... | collective-permute-start | bytes 1179656 | tf_op jit(solution)/shard_map/ppermute | solution.py:441
  210.5 23.8 %collective-permute-start.29 = (bf16[24,64,128]{2,1,0:T(8,128)(2,1)}, bf16[24,64,128]{2,1,0:T(8,128)(2,1)S(1)}, u32[]{:S(2)}, u32[]{:S(2)}) collective-permute-start(bf16[24,64,128]{2,1,0:T(8,128)(2,1)} %get-tuple-element.255), channel_id=1, source_target_pairs={{0,4},{2,6},{4,0},{6,2},{8,12},{10,14},{12,8},{14,10},{16,20},{18,... | collective-permute-start | bytes 1179656 | tf_op jit(solution)/shard_map/ppermute | solution.py:441
  212.7 21.6 %collective-permute-start.30 = (bf16[24,64,128]{2,1,0:T(8,128)(2,1)}, bf16[24,64,128]{2,1,0:T(8,128)(2,1)S(1)}, u32[]{:S(2)}, u32[]{:S(2)}) collective-permute-start(bf16[24,64,128]{2,1,0:T(8,128)(2,1)} %get-tuple-element.256), channel_id=1, source_target_pairs={{0,6},{2,4},{4,2},{6,0},{8,14},{10,12},{12,10},{14,8},{16,22},{18,... | collective-permute-start | bytes 1179656 | tf_op jit(solution)/shard_map/ppermute | solution.py:441
  216.7 17.6 %collective-permute-start.19 = (bf16[64,1024]{1,0:T(8,128)(2,1)}, bf16[64,1024]{1,0:T(8,128)(2,1)}, u32[]{:S(2)}, u32[]{:S(2)}) collective-permute-start(bf16[64,1024]{1,0:T(8,128)(2,1)} %get-tuple-element.232), channel_id=1, source_target_pairs={{0,2},{2,4},{4,6},{6,0},{8,10},{10,12},{12,14},{14,8},{16,18},{18,... | collective-permute-start | bytes 393224 | tf_op jit(solution)/shard_map/ppermute | solution.py:528
  240.1 189.4 %reduce-scatter.11.cloned.1.call-start = ((), (), s32[]{:S(2)}) async-start(), calls=%async_computation.7 | async-start | bytes 2621440 | tf_op jit(solution)/shard_map/reduce_scatter | solution.py:533
  249.1 23.9 %collective-permute-start.31 = (bf16[24,64,128]{2,1,0:T(8,128)(2,1)}, bf16[24,64,128]{2,1,0:T(8,128)(2,1)S(1)}, u32[]{:S(2)}, u32[]{:S(2)}) collective-permute-start(bf16[24,64,128]{2,1,0:T(8,128)(2,1)} %copy-done.78), channel_id=1, source_target_pairs={{0,2},{2,0},{4,6},{6,4},{8,10},{10,8},{12,14},{14,12},{16,18},{18,... | collective-permute-start | bytes 1179656 | tf_op jit(solution)/shard_map/ppermute | solution.py:441
  251.6 21.4 %collective-permute-start.32 = (bf16[24,64,128]{2,1,0:T(8,128)(2,1)S(1)}, bf16[24,64,128]{2,1,0:T(8,128)(2,1)S(1)}, u32[]{:S(2)}, u32[]{:S(2)}) collective-permute-start(bf16[24,64,128]{2,1,0:T(8,128)(2,1)S(1)} %copy-done.77), channel_id=1, source_target_pairs={{0,4},{2,6},{4,0},{6,2},{8,12},{10,14},{12,8},{14,10},{16,20},{18,... | collective-permute-start | bytes 1179656 | tf_op jit(solution)/shard_map/ppermute | solution.py:441
  251.7 21.3 %collective-permute-start.33 = (bf16[24,64,128]{2,1,0:T(8,128)(2,1)S(1)}, bf16[24,64,128]{2,1,0:T(8,128)(2,1)S(1)}, u32[]{:S(2)}, u32[]{:S(2)}) collective-permute-start(bf16[24,64,128]{2,1,0:T(8,128)(2,1)S(1)} %copy-done.74), channel_id=1, source_target_pairs={{0,6},{2,4},{4,2},{6,0},{8,14},{10,12},{12,10},{14,8},{16,22},{18,... | collective-permute-start | bytes 1179656 | tf_op jit(solution)/shard_map/ppermute | solution.py:441
  253.1 18.0 %collective-permute-start.36 = (bf16[64,1024]{1,0:T(8,128)(2,1)}, bf16[64,1024]{1,0:T(8,128)(2,1)S(1)}, u32[]{:S(2)}, u32[]{:S(2)}) collective-permute-start(bf16[64,1024]{1,0:T(8,128)(2,1)} %get-tuple-element.280), channel_id=1, source_target_pairs={{0,2},{2,4},{4,6},{6,0},{8,10},{10,12},{12,14},{14,8},{16,18},{18,... | collective-permute-start | bytes 393224 | tf_op jit(solution)/shard_map/ppermute | solution.py:507
  276.4 37.3 %collective-permute-start.48 = (bf16[24,64,128]{2,1,0:T(8,128)(2,1)}, bf16[24,64,128]{2,1,0:T(8,128)(2,1)S(1)}, u32[]{:S(2)}, u32[]{:S(2)}) collective-permute-start(bf16[24,64,128]{2,1,0:T(8,128)(2,1)} %get-tuple-element.338), channel_id=1, source_target_pairs={{0,2},{2,0},{4,6},{6,4},{8,10},{10,8},{12,14},{14,12},{16,18},{18,... | collective-permute-start | bytes 1179656 | tf_op jit(solution)/shard_map/ppermute | solution.py:441
  276.5 38.5 %collective-permute-start.49 = (bf16[24,64,128]{2,1,0:T(8,128)(2,1)S(1)}, bf16[24,64,128]{2,1,0:T(8,128)(2,1)S(1)}, u32[]{:S(2)}, u32[]{:S(2)}) collective-permute-start(bf16[24,64,128]{2,1,0:T(8,128)(2,1)S(1)} %copy-done.64), channel_id=1, source_target_pairs={{0,4},{2,6},{4,0},{6,2},{8,12},{10,14},{12,8},{14,10},{16,20},{18,... | collective-permute-start | bytes 1179656 | tf_op jit(solution)/shard_map/ppermute | solution.py:441
  276.6 38.3 %collective-permute-start.50 = (bf16[24,64,128]{2,1,0:T(8,128)(2,1)}, bf16[24,64,128]{2,1,0:T(8,128)(2,1)S(1)}, u32[]{:S(2)}, u32[]{:S(2)}) collective-permute-start(bf16[24,64,128]{2,1,0:T(8,128)(2,1)} %get-tuple-element.340), channel_id=1, source_target_pairs={{0,6},{2,4},{4,2},{6,0},{8,14},{10,12},{12,10},{14,8},{16,22},{18,... | collective-permute-start | bytes 1179656 | tf_op jit(solution)/shard_map/ppermute | solution.py:441
  283.7 31.3 %collective-permute-start.59 = (bf16[2,64,1024]{2,1,0:T(8,128)(2,1)S(1)}, bf16[2,64,1024]{2,1,0:T(8,128)(2,1)S(1)}, u32[]{:S(2)}, u32[]{:S(2)}) collective-permute-start(bf16[2,64,1024]{2,1,0:T(8,128)(2,1)S(1)} %add_convert_fusion.1), channel_id=1, source_target_pairs={{0,4},{2,6},{4,0},{6,2},{8,12},{10,14},{12,8},{14,10},{16,20},{18,... | collective-permute-start | bytes 786440 | tf_op jit(solution)/shard_map/ppermute | solution.py:441
  284.0 31.1 %collective-permute-start.60 = (bf16[64,1024]{1,0:T(8,128)(2,1)}, bf16[64,1024]{1,0:T(8,128)(2,1)S(1)}, u32[]{:S(2)}, u32[]{:S(2)}) collective-permute-start(bf16[64,1024]{1,0:T(8,128)(2,1)} %get-tuple-element.354), channel_id=1, source_target_pairs={{0,2},{2,4},{4,6},{6,0},{8,10},{10,12},{12,14},{14,8},{16,18},{18,... | collective-permute-start | bytes 393224 | tf_op jit(solution)/shard_map/ppermute | solution.py:528
  324.9 113.3 %reduce-scatter.5.cloned.1.call-start = ((), (), s32[]{:S(2)}) async-start(), calls=%async_computation.4 | async-start | bytes 2621440 | tf_op jit(solution)/shard_map/reduce_scatter | solution.py:533
  328.8 16.9 %collective-permute-start.40 = (bf16[24,64,128]{2,1,0:T(8,128)(2,1)S(1)}, bf16[24,64,128]{2,1,0:T(8,128)(2,1)S(1)}, u32[]{:S(2)}, u32[]{:S(2)}) collective-permute-start(bf16[24,64,128]{2,1,0:T(8,128)(2,1)S(1)} %copy-done.70), channel_id=1, source_target_pairs={{0,6},{2,4},{4,2},{6,0},{8,14},{10,12},{12,10},{14,8},{16,22},{18,... | collective-permute-start | bytes 1179656 | tf_op jit(solution)/shard_map/ppermute | solution.py:441
  356.0 103.9 %reduce-scatter.7.cloned.1.call-start = ((), (), s32[]{:S(2)}) async-start(), calls=%async_computation.5 | async-start | bytes 2621440 | tf_op jit(solution)/shard_map/reduce_scatter | solution.py:533
  358.5 17.6 %collective-permute-start.47 = (bf16[24,64,128]{2,1,0:T(8,128)(2,1)S(1)}, bf16[24,64,128]{2,1,0:T(8,128)(2,1)S(1)}, u32[]{:S(2)}, u32[]{:S(2)}) collective-permute-start(bf16[24,64,128]{2,1,0:T(8,128)(2,1)S(1)} %copy-done.109), channel_id=1, source_target_pairs={{0,6},{2,4},{4,2},{6,0},{8,14},{10,12},{12,10},{14,8},{16,22},{18,... | collective-permute-start | bytes 1179656 | tf_op jit(solution)/shard_map/ppermute | solution.py:441
  362.6 17.9 %collective-permute-start.42 = (bf16[2,64,1024]{2,1,0:T(8,128)(2,1)S(1)}, bf16[2,64,1024]{2,1,0:T(8,128)(2,1)S(1)}, u32[]{:S(2)}, u32[]{:S(2)}) collective-permute-start(bf16[2,64,1024]{2,1,0:T(8,128)(2,1)S(1)} %add_convert_fusion.5), channel_id=1, source_target_pairs={{0,4},{2,6},{4,0},{6,2},{8,12},{10,14},{12,8},{14,10},{16,20},{18,... | collective-permute-start | bytes 786440 | tf_op jit(solution)/shard_map/ppermute | solution.py:441
  363.0 17.6 %collective-permute-start.43 = (bf16[64,1024]{1,0:T(8,128)(2,1)S(1)}, bf16[64,1024]{1,0:T(8,128)(2,1)S(1)}, u32[]{:S(2)}, u32[]{:S(2)}) collective-permute-start(bf16[64,1024]{1,0:T(8,128)(2,1)S(1)} %copy-done.90), channel_id=1, source_target_pairs={{0,2},{2,4},{4,6},{6,0},{8,10},{10,12},{12,14},{14,8},{16,18},{18,... | collective-permute-start | bytes 393224 | tf_op jit(solution)/shard_map/ppermute | solution.py:528
  387.4 40.7 %collective-permute-start.63 = (bf16[8,128,128]{2,1,0:T(8,128)(2,1)}, bf16[8,128,128]{2,1,0:T(8,128)(2,1)S(1)}, u32[]{:S(2)}, u32[]{:S(2)}) collective-permute-start(bf16[8,128,128]{2,1,0:T(8,128)(2,1)} %copy-done.80), channel_id=1, source_target_pairs={{0,4},{2,6},{4,0},{6,2},{8,12},{10,14},{12,8},{14,10},{16,20},{18,... | collective-permute-start | bytes 786440 | tf_op jit(solution)/shard_map/ppermute | solution.py:441
  390.5 38.4 %collective-permute-start.64 = (bf16[8,128,128]{2,1,0:T(8,128)(2,1)}, bf16[8,128,128]{2,1,0:T(8,128)(2,1)S(1)}, u32[]{:S(2)}, u32[]{:S(2)}) collective-permute-start(bf16[8,128,128]{2,1,0:T(8,128)(2,1)} %copy-done.79), channel_id=1, source_target_pairs={{0,6},{2,4},{4,2},{6,0},{8,14},{10,12},{12,10},{14,8},{16,22},{18,... | collective-permute-start | bytes 786440 | tf_op jit(solution)/shard_map/ppermute | solution.py:441
  390.9 47.3 %collective-permute-start.55 = (bf16[8,128,128]{2,1,0:T(8,128)(2,1)}, bf16[8,128,128]{2,1,0:T(8,128)(2,1)}, u32[]{:S(2)}, u32[]{:S(2)}) collective-permute-start(bf16[8,128,128]{2,1,0:T(8,128)(2,1)} %copy-done.84), channel_id=1, source_target_pairs={{0,2},{2,0},{4,6},{6,4},{8,10},{10,8},{12,14},{14,12},{16,18},{18,... | collective-permute-start | bytes 786440 | tf_op jit(solution)/shard_map/ppermute | solution.py:441
  391.9 46.2 %collective-permute-start.56 = (bf16[8,128,128]{2,1,0:T(8,128)(2,1)}, bf16[8,128,128]{2,1,0:T(8,128)(2,1)}, u32[]{:S(2)}, u32[]{:S(2)}) collective-permute-start(bf16[8,128,128]{2,1,0:T(8,128)(2,1)} %copy-done.83), channel_id=1, source_target_pairs={{0,4},{2,6},{4,0},{6,2},{8,12},{10,14},{12,8},{14,10},{16,20},{18,... | collective-permute-start | bytes 786440 | tf_op jit(solution)/shard_map/ppermute | solution.py:441
  394.7 43.5 %collective-permute-start.57 = (bf16[8,128,128]{2,1,0:T(8,128)(2,1)}, bf16[8,128,128]{2,1,0:T(8,128)(2,1)}, u32[]{:S(2)}, u32[]{:S(2)}) collective-permute-start(bf16[8,128,128]{2,1,0:T(8,128)(2,1)} %copy-done.82), channel_id=1, source_target_pairs={{0,6},{2,4},{4,2},{6,0},{8,14},{10,12},{12,10},{14,8},{16,22},{18,... | collective-permute-start | bytes 786440 | tf_op jit(solution)/shard_map/ppermute | solution.py:441
  (136 other events, 1220.5 us)
Sparse Core Ops, SparseCore 0:
  10.2 45.6 all-gather.10
  58.0 44.6 all-gather.8
  104.3 44.6 all-gather.14
  151.0 44.6 all-gather.12
  240.2 43.9 reduce-scatter.8
  325.1 43.6 reduce-scatter.10
  371.1 43.1 reduce-scatter.4
  416.7 43.1 reduce-scatter.6

commit v3 on v2

v3 whole, which is shorter than its diff:
```python
import math

import jax
import jax.numpy as jnp
from jax import lax
from jax.experimental import pallas as pl
from jax.experimental.pallas import tpu as pltpu
from jax.sharding import PartitionSpec as P

BLOCK = 128
DH = 128
RAND = 3
GLOB = 2
WMAX = 1
SPAN = 2 * WMAX + 1
LISTED = SPAN + RAND + GLOB
PLANES = 4
PARTS = 2
ROWS = BLOCK // PARTS
SCALE = 1.0 / math.sqrt(DH)
POWER = SCALE / math.log(2.0)
MASKED = -1e30
VMEM_BYTES = 48 * 1024 * 1024

NT = (((1,), (1,)), ((), ()))
NN = (((1,), (0,)), ((), ()))
TN = (((0,), (0,)), ((), ()))

SMEM = pltpu.SMEM
ANY = pltpu.HBM


def dot(a, b, dims):
    return lax.dot_general(a, b, dims, preferred_element_type=jnp.float32)


def cost(micros):
    return pl.CostEstimate(flops=int(micros * 1e9), bytes_accessed=int(micros * 3.5e6), transcendentals=0)


def tie(*values):
    return lax.optimization_barrier(values)


def params():
    return pltpu.CompilerParams(vmem_limit_bytes=VMEM_BYTES)


def smem_spec():
    return pl.BlockSpec(memory_space=SMEM)


def any_spec():
    return pl.BlockSpec(memory_space=ANY)


def vmem_spec():
    return pl.BlockSpec(memory_space=pltpu.VMEM)


def call(kernel, out_shape, in_specs, micros, scratch=()):
    return pl.pallas_call(
        kernel,
        out_shape=out_shape,
        in_specs=in_specs,
        out_specs=jax.tree.map(lambda _: vmem_spec(), out_shape),
        scratch_shapes=list(scratch),
        compiler_params=params(),
        cost_estimate=cost(micros),
    )


def lanes_of(index, heads):
    return pl.ds(pl.multiple_of((index % heads) * DH, DH), DH)


def pick_own(keys, values, table, heads, lanes, slots, cap):
    blocks = keys.shape[0]

    def kernel(table_ref, *rest):
        sources, outs = rest[:2], rest[2:]
        for partner in range(lanes):

            def step(slot, carry, partner=partner):
                index = jnp.maximum(table_ref[partner * slots + slot], 0)
                row, lane = (index // heads) % blocks, lanes_of(index, heads)
                for number, source in enumerate(sources):
                    outs[partner][number, slot] = source[row, :, lane]
                return carry

            lax.fori_loop(0, cap, step, 0)

    shape = jax.ShapeDtypeStruct((2, cap, BLOCK, DH), keys.dtype)
    specs = [smem_spec(), vmem_spec(), vmem_spec()]
    return call(kernel, [shape] * lanes, specs, 3)(table, keys, values)


def has_rim(partner, lanes):
    return partner in (1, lanes - 1)


def part_slots(partner, heads, lanes, slots, cap):
    return slots - cap + (GLOB + has_rim(partner, lanes)) * heads


def pick_blocks(column, table, info, heads, lanes, slots, cap):
    rows = column.shape[1]
    main = slots - cap

    def kernel(table_ref, info_ref, column_ref, *outs):
        for partner in range(lanes):

            def step(slot, carry, partner=partner):
                index = jnp.maximum(table_ref[partner * slots + cap + slot], 0)
                outs[partner][slot] = column_ref[index // heads, :, lanes_of(index, heads)]
                return carry

            lax.fori_loop(0, main, step, 0)
            listed = [info_ref[2 * g] for g in range(GLOB)]
            if has_rim(partner, lanes):
                listed.append(info_ref[2 * GLOB + (0 if partner == 1 else 1)])
            for number, row in enumerate(listed):
                for head in range(heads):
                    block = column_ref[row, :, head * DH : (head + 1) * DH]
                    outs[partner][main + number * heads + head] = block

    shapes = [
        jax.ShapeDtypeStruct((part_slots(k, heads, lanes, slots, cap), rows, DH), column.dtype)
        for k in range(lanes)
    ]
    specs = [smem_spec(), smem_spec(), vmem_spec()]
    return call(kernel, shapes, specs, 3)(table, info, column)


def sum_blocks(returned, table, info, blocks, heads, slots, cap):
    lanes = len(returned)
    rows = returned[0].shape[1]
    main = slots - cap

    def kernel(table_ref, info_ref, *rest):
        refs, out_ref, total = rest[:lanes], rest[lanes], rest[lanes + 1]
        total[...] = jnp.zeros_like(total)
        for partner in range(lanes):

            def step(slot, carry, partner=partner):
                index = table_ref[partner * slots + cap + slot]

                @pl.when(index >= 0)
                def _():
                    term = refs[partner][slot].astype(jnp.float32)
                    total[index // heads, :, lanes_of(index, heads)] += term

                return carry

            lax.fori_loop(0, main, step, 0)

        def add_row(row, sources, first):
            for head in range(heads):
                term = sources[0][first + head].astype(jnp.float32)
                for source in sources[1:]:
                    term = term + source[first + head].astype(jnp.float32)
                total[row, :, head * DH : (head + 1) * DH] += term

        for g in range(GLOB):

            @pl.when(info_ref[2 * g + 1] > 0)
            def _(g=g):
                add_row(info_ref[2 * g], refs, main + g * heads)

        for side, partner in enumerate((lanes - 1, 1)):
            row = info_ref[2 * GLOB + 2 + side]

            @pl.when(row >= 0)
            def _(row=row, partner=partner):
                add_row(row, [refs[partner]], main + GLOB * heads)

        out_ref[...] = total[...].astype(out_ref.dtype)

    shape = (blocks, rows, heads * DH)
    specs = [smem_spec()] * 2 + [vmem_spec()] * lanes
    return call(
        kernel,
        jax.ShapeDtypeStruct(shape, jnp.bfloat16),
        specs,
        6,
        [pltpu.VMEM(shape, jnp.float32)],
    )(table, info, *returned)


def final_sum(own, sums, returned, table, heads, slots, cap):
    blocks, _, width = own.shape
    lanes = len(returned)

    def kernel(table_ref, own_ref, *rest):
        sum_refs, refs = rest[:PARTS], rest[PARTS : PARTS + lanes]
        out_ref, total = rest[PARTS + lanes :]
        for part, sum_ref in enumerate(sum_refs):
            here = slice(part * ROWS, (part + 1) * ROWS)
            total[:, here] = own_ref[:, here] + sum_ref[...].astype(jnp.float32)
        for partner in range(lanes):

            def step(slot, carry, partner=partner):
                index = table_ref[partner * slots + slot]

                @pl.when(index >= 0)
                def _():
                    term = refs[partner][slot].astype(jnp.float32)
                    total[(index // heads) % blocks, :, lanes_of(index, heads)] += term

                return carry

            lax.fori_loop(0, cap, step, 0)
        out_ref[...] = total[...].astype(out_ref.dtype)

    specs = [smem_spec()] + [vmem_spec()] * (1 + PARTS + lanes)
    return call(
        kernel,
        jax.ShapeDtypeStruct(own.shape, jnp.bfloat16),
        specs,
        5,
        [pltpu.VMEM(own.shape, jnp.float32)],
    )(table, own, *sums, *returned)


def load_parts(refs, pool, sems, which, heads, lanes, slots, cap):
    stride = slots + (GLOB + 1) * heads
    copies = []
    for partner in range(lanes):
        first = partner * stride
        length = part_slots(partner, heads, lanes, slots, cap)
        for part in range(PARTS + 1):
            number = partner * (PARTS + 1) + part
            ref = refs[number]
            if part == 0:
                pair = (ref.at[which], pool.at[pl.ds(first, cap)])
            else:
                rows = pl.ds((part - 1) * ROWS, ROWS)
                pair = (ref, pool.at[pl.ds(first + cap, length), rows])
            copies.append(pltpu.make_async_copy(*pair, sems.at[number]))
    for copy in copies:
        copy.start()
    for copy in copies:
        copy.wait()


def store_parts(refs, pay, glob_pay, rim_pay, sems, heads, lanes, slots, cap):
    main = slots - cap
    pairs = []
    for partner in range(lanes):
        first = partner * slots
        number = partner * (PARTS + 1)
        pairs.append((pay.at[pl.ds(first, cap)], refs[number]))
        for part in range(PARTS):
            ref = refs[number + 1 + part]
            rows = pl.ds(part * ROWS, ROWS)
            pairs.append((pay.at[pl.ds(first + cap, main), rows], ref.at[pl.ds(0, main)]))
            there = ref.at[pl.ds(main, GLOB * heads)]
            pairs.append((glob_pay.at[pl.ds(0, GLOB * heads), rows], there))
            if has_rim(partner, lanes):
                side = 0 if partner == 1 else 1
                there = ref.at[pl.ds(main + GLOB * heads, heads)]
                pairs.append((rim_pay.at[pl.ds(side * heads, heads), rows], there))
    copies = [pltpu.make_async_copy(*pair, sems.at[n]) for n, pair in enumerate(pairs)]
    for copy in copies:
        copy.start()
    for copy in copies:
        copy.wait()


def out_copies(lanes):
    return lanes * (1 + 2 * PARTS) + sum(has_rim(k, lanes) for k in range(lanes)) * PARTS


def fill(own, pool, band, head, heads, lanes, slots, blocks):
    stride = slots + (GLOB + 1) * heads
    rim = slots + GLOB * heads + head
    end = BLOCK * (blocks + 1)
    band[:BLOCK] = pool[stride + rim]
    band[BLOCK:end] = own[...]
    band[end:] = pool[(lanes - 1) * stride + rim]


def far_blocks(pick, pool, head, block, heads, blocks):
    entry = (head * blocks + block) * RAND
    places = [pick[entry + r] for r in range(RAND)]
    places += [pick[heads * blocks * RAND + g] + head for g in range(GLOB)]
    return [pool[at] for at in places]


def pieces():
    starts = [0] + [(SPAN + n) * BLOCK for n in range(RAND + GLOB + 1)]
    return list(zip(starts[:-1], starts[1:]))


def add_terms(left, right, block, cuts, band_sum, glob_sum):
    near = slice(block * BLOCK, (block + SPAN) * BLOCK)
    a, b = cuts[0]
    band_sum[near] += dot(left[0, block, a:b], right, NN)
    start = (SPAN + RAND) * BLOCK
    term = dot(left[0, block, start:], right, NN)
    if block == 0:
        glob_sum[...] = term
    else:
        glob_sum[...] += term


def store_random(left, right, block, cuts, pay, pick, head, heads, blocks, scale):
    entry = (head * blocks + block) * RAND
    for r in range(RAND):
        a, b = cuts[1 + r]
        term = dot(left[0, block, a:b], right, NN) * scale
        pay[pick[heads * blocks * RAND + GLOB + entry + r]] = term.astype(jnp.bfloat16)


def store_sums(own_ref, band_sum, glob_sum, glob_pay, rim_pay, head, heads, blocks, scale):
    end = BLOCK * (blocks + 1)
    own_ref[...] = band_sum[BLOCK:end] * scale
    rim_pay[head] = (band_sum[:BLOCK] * scale).astype(jnp.bfloat16)
    rim_pay[heads + head] = (band_sum[end:] * scale).astype(jnp.bfloat16)
    for g in range(GLOB):
        rows = slice(g * BLOCK, (g + 1) * BLOCK)
        glob_pay[g * heads + head] = (glob_sum[rows] * scale).astype(jnp.bfloat16)


def weights_kernel(lanes, slots, cap, heads, blocks):
    count = lanes * (PARTS + 1)
    sizes = (heads, lanes, slots, cap)

    def kernel(pick, ends, q_ref, g_ref, k_ref, *rest):
        kr_refs, (p_ref, own_ref), rest = rest[:count], rest[count : count + 2], rest[count + 2 :]
        pay_refs, rest = rest[:count], rest[count:]
        pool, pay, glob_pay, rim_pay, band, band_sum, glob_sum, sems, out_sems = rest
        head = pl.program_id(0)

        @pl.when(head == 0)
        def _():
            load_parts(kr_refs, pool, sems, 0, *sizes)

        fill(k_ref, pool, band, head, heads, lanes, slots, blocks)
        band_sum[...] = jnp.zeros_like(band_sum)
        cuts = pieces()
        for block in range(blocks):
            here = slice(block * BLOCK, (block + 1) * BLOCK)
            near = slice(block * BLOCK, (block + SPAN) * BLOCK)
            query = q_ref[here]
            grad = g_ref[here]
            window = dot(band[near], query, NT)
            scores = [window[o * BLOCK : (o + 1) * BLOCK] for o in range(SPAN)]
            if block == 0:
                scores[0] = jnp.where(ends[0] > 0, MASKED, scores[0])
            if block == blocks - 1:
                scores[-1] = jnp.where(ends[1] > 0, MASKED, scores[-1])
            far = far_blocks(pick, pool, head, block, heads, blocks)
            scores += [dot(item, query, NT) for item in far]
            peak = scores[0]
            for score in scores[1:]:
                peak = jnp.maximum(peak, score)
            peak = jnp.max(peak, axis=0, keepdims=True)
            powers = [jnp.exp2((score - peak) * POWER) for score in scores]
            total = powers[0]
            for power in powers[1:]:
                total = total + power
            inverse = 1.0 / jnp.sum(total, axis=0, keepdims=True)
            for number, power in enumerate(powers):
                weights = (power * inverse).astype(jnp.bfloat16)
                p_ref[0, block, number * BLOCK : (number + 1) * BLOCK] = weights
            store_random(p_ref, grad, block, cuts, pay, pick, head, heads, blocks, 1.0)
            add_terms(p_ref, grad, block, cuts, band_sum, glob_sum)
        store_sums(own_ref, band_sum, glob_sum, glob_pay, rim_pay, head, heads, blocks, 1.0)

        @pl.when(head == heads - 1)
        def _():
            store_parts(pay_refs, pay, glob_pay, rim_pay, out_sems, *sizes)

    return kernel


def slope_kernel(lanes, slots, cap, heads, blocks):
    count = lanes * (PARTS + 1)
    sizes = (heads, lanes, slots, cap)

    def kernel(pick, q_ref, g_ref, p_ref, v_ref, *rest):
        vr_refs, (ds_ref, own_ref), rest = rest[:count], rest[count : count + 2], rest[count + 2 :]
        pay_refs, rest = rest[:count], rest[count:]
        pool, pay, glob_pay, rim_pay, band, band_sum, glob_sum, sems, out_sems = rest
        head = pl.program_id(0)

        @pl.when(head == 0)
        def _():
            load_parts(vr_refs, pool, sems, 1, *sizes)

        fill(v_ref, pool, band, head, heads, lanes, slots, blocks)
        band_sum[...] = jnp.zeros_like(band_sum)
        cuts = pieces()
        for block in range(blocks):
            here = slice(block * BLOCK, (block + 1) * BLOCK)
            near = slice(block * BLOCK, (block + SPAN) * BLOCK)
            query = q_ref[here]
            grad = g_ref[here]
            listed = [band[near]] + far_blocks(pick, pool, head, block, heads, blocks)
            slopes = [dot(value, grad, NT) for value in listed]
            wide = [p_ref[0, block, a:b].astype(jnp.float32) for a, b in cuts]
            delta = 0.0
            for weight, slope in zip(wide, slopes):
                delta = delta + jnp.sum(weight * slope, axis=0, keepdims=True)
            for (a, b), weight, slope in zip(cuts, wide, slopes):
                ds_ref[0, block, a:b] = (weight * (slope - delta)).astype(jnp.bfloat16)
            store_random(ds_ref, query, block, cuts, pay, pick, head, heads, blocks, SCALE)
            add_terms(ds_ref, query, block, cuts, band_sum, glob_sum)
        store_sums(own_ref, band_sum, glob_sum, glob_pay, rim_pay, head, heads, blocks, SCALE)

        @pl.when(head == heads - 1)
        def _():
            store_parts(pay_refs, pay, glob_pay, rim_pay, out_sems, *sizes)

    return kernel


def output_kernel(lanes, slots, cap, heads, blocks):
    count = lanes * (PARTS + 1)
    sizes = (heads, lanes, slots, cap)

    def kernel(pick, p_ref, ds_ref, k_ref, v_ref, *rest):
        kr_refs, vr_refs, rest = rest[:count], rest[count : 2 * count], rest[2 * count :]
        out_ref, dq_ref, k_pool, v_pool, k_band, v_band, sems, more = rest
        head = pl.program_id(0)

        @pl.when(head == 0)
        def _():
            load_parts(kr_refs, k_pool, sems, 0, *sizes)
            load_parts(vr_refs, v_pool, more, 1, *sizes)

        fill(k_ref, k_pool, k_band, head, heads, lanes, slots, blocks)
        fill(v_ref, v_pool, v_band, head, heads, lanes, slots, blocks)
        for block in range(blocks):
            here = slice(block * BLOCK, (block + 1) * BLOCK)
            near = slice(block * BLOCK, (block + SPAN) * BLOCK)
            for left, band, pool, scale, to_ref in (
                (p_ref, v_band, v_pool, 1.0, out_ref),
                (ds_ref, k_band, k_pool, SCALE, dq_ref),
            ):
                listed = [band[near]] + far_blocks(pick, pool, head, block, heads, blocks)
                result = 0.0
                for (a, b), item in zip(pieces(), listed):
                    result = result + dot(left[0, block, a:b], item, TN)
                to_ref[here] = (result * scale).astype(jnp.bfloat16)

    return kernel


def body(queries, keys, values, out_grad, rand_ids, glob_ids):
    rows_here, width = queries.shape
    heads = width // DH
    blocks = rows_here // BLOCK
    shards = lax.axis_size("seq")
    planes = PLANES
    lanes = shards // planes
    place = lax.axis_index("seq")
    group = lax.axis_index("head")
    plane, lane = place // lanes, place % lanes
    columns = [[z * lanes + c for z in range(planes)] for c in range(lanes)]
    entries = heads * blocks * RAND
    cap = max(2, (5 * entries + 4 * shards - 1) // (4 * shards))
    slots = planes * cap
    stride = slots + (GLOB + 1) * heads
    sizes = (heads, lanes, slots, cap)

    def rotate(array, steps):
        moves = [(i, i // lanes * lanes + (i + steps) % lanes) for i in range(shards)]
        return lax.ppermute(array, "seq", moves)

    def out_to_partners(arrays):
        return [arrays[0]] + [rotate(arrays[k], k) for k in range(1, lanes)]

    def back_to_partners(arrays):
        return [arrays[0]] + [rotate(arrays[k], -k) for k in range(1, lanes)]

    ids_mine = lax.dynamic_slice_in_dim(rand_ids, group * heads, heads, 0)
    ids_plane = lax.dynamic_slice_in_dim(ids_mine, plane * lanes * blocks, lanes * blocks, 1)
    wanted = (
        ids_plane.reshape(heads, lanes, blocks, RAND).transpose(1, 0, 2, 3).reshape(lanes, entries)
    )
    source = wanted // blocks
    same = source[:, :, None] == source[:, None, :]
    before = jnp.tril(jnp.ones((entries, entries), bool), -1)
    slot = jnp.sum((same & before[None]).astype(jnp.int32), axis=2)
    source_plane, source_lane = source // lanes, source % lanes
    spot = ((source_plane - plane + planes) % planes) * cap + slot
    distance = (lane - source_lane[lane] + lanes) % lanes
    glob_place = glob_ids // blocks
    glob_distance = (lane - glob_place % lanes + lanes) % lanes
    pick = jnp.concatenate(
        [
            distance * stride + spot[lane],
            glob_distance * stride + slots + jnp.arange(GLOB, dtype=jnp.int32) * heads,
            distance * slots + spot[lane],
        ]
    )
    head_of = jnp.arange(entries, dtype=jnp.int32) // (blocks * RAND)
    inside = (source_plane * blocks + wanted % blocks) * heads + head_of[None, :]
    hit = (source_lane == lane)[:, :, None] & (
        spot[:, :, None] == jnp.arange(slots, dtype=jnp.int32)[None, None, :]
    )
    table = jnp.sum(jnp.where(hit, inside[:, :, None] + 1, 0), axis=1) - 1
    partners = (jnp.arange(lanes, dtype=jnp.int32) + lane) % lanes
    table = table[partners].reshape(-1)
    first, last = lane == 0, lane == lanes - 1
    own_first, own_last = plane * blocks, plane * blocks + blocks - 1
    rims = [
        jnp.where(last, jnp.maximum(own_first - 1, 0), own_last),
        jnp.where(first, jnp.minimum(own_last + 1, planes * blocks - 1), own_first),
        jnp.where(first, jnp.where(plane < planes - 1, own_last + 1, -1), own_first),
        jnp.where(last, own_first - 1, own_last),
    ]
    info = jnp.stack(
        [
            (glob_place // lanes) * blocks + glob_ids % blocks,
            (glob_place % lanes == lane).astype(jnp.int32),
        ],
        axis=1,
    )
    info = jnp.concatenate([info.reshape(-1), jnp.stack(rims)]).astype(jnp.int32)
    ends = jnp.stack([place == 0, place == shards - 1]).astype(jnp.int32)

    def cut(array, part):
        return array.reshape(blocks, BLOCK, width)[:, part * ROWS : (part + 1) * ROWS]

    def gather(piece):
        column = lax.all_gather(piece, "seq", axis_index_groups=columns)
        return column.reshape(planes * blocks, ROWS, width)

    def choose(column, table):
        return list(pick_blocks(column, table, info, *sizes))

    def exchange(outs):
        return out_to_partners(outs)

    def requested(own, parts):
        return [array for k in range(lanes) for array in [own[k]] + [part[k] for part in parts]]

    def dense(returned):
        return sum_blocks(returned, table, info, planes * blocks, heads, slots, cap)

    def terms_of(outs, part):
        return [outs[2 + k * (PARTS + 1) + part] for k in range(lanes)]

    def scatter(array):
        return lax.psum_scatter(
            array, "seq", scatter_dimension=0, axis_index_groups=columns, tiled=True
        )

    def finish(own, sums, returned):
        own = own.reshape(blocks, BLOCK, width)
        total = final_sum(own, sums, returned, table, heads, slots, cap)
        return total.reshape(rows_here, width)

    head_block = pl.BlockSpec((rows_here, DH), lambda h: (0, h))
    weight_block = pl.BlockSpec((1, blocks, LISTED * BLOCK, BLOCK), lambda h: (h, 0, 0, 0))
    like = jax.ShapeDtypeStruct((rows_here, width), jnp.bfloat16)
    wide_like = jax.ShapeDtypeStruct((rows_here, width), jnp.float32)
    weights_like = jax.ShapeDtypeStruct((heads, blocks, LISTED * BLOCK, BLOCK), jnp.bfloat16)
    pay_like = []
    for partner in range(lanes):
        pay_like.append(jax.ShapeDtypeStruct((cap, BLOCK, DH), jnp.bfloat16))
        length = part_slots(partner, *sizes)
        pay_like += [jax.ShapeDtypeStruct((length, ROWS, DH), jnp.bfloat16)] * PARTS
    count = len(pay_like)

    def many(*shape):
        return pltpu.VMEM(shape + (BLOCK, DH), jnp.bfloat16)

    pool = many(lanes * stride)
    band = pltpu.VMEM(((blocks + 2 * WMAX) * BLOCK, DH), jnp.bfloat16)
    sems = pltpu.SemaphoreType.DMA((count,))
    term_scratch = [
        pool,
        many(lanes * slots),
        many(GLOB * heads),
        many(2 * heads),
        band,
        pltpu.VMEM(((blocks + 2 * WMAX) * BLOCK, DH), jnp.float32),
        pltpu.VMEM((GLOB * BLOCK, DH), jnp.float32),
        sems,
        pltpu.SemaphoreType.DMA((out_copies(lanes),)),
    ]
    anywhere = [any_spec()] * count

    def per_head(kernel, out_shape, in_specs, out_specs, scratch, micros):
        return pl.pallas_call(
            kernel(lanes, slots, cap, heads, blocks),
            grid=(heads,),
            out_shape=out_shape,
            in_specs=in_specs,
            out_specs=out_specs,
            scratch_shapes=scratch,
            compiler_params=params(),
            cost_estimate=cost(micros),
        )

    column_0 = gather(cut(keys, 0))
    piece, table = tie(cut(keys, 1), table)
    column_1 = gather(piece)
    blocks_of = (blocks, BLOCK, width)
    own = pick_own(keys.reshape(blocks_of), values.reshape(blocks_of), table, *sizes)
    own = out_to_partners(own)
    column_0, own = tie(column_0, own)
    chosen_0 = choose(column_0, table)
    piece, chosen_0 = tie(cut(values, 0), chosen_0)
    column_2 = gather(piece)
    key_0 = exchange(chosen_0)
    column_1, key_0 = tie(column_1, key_0)
    chosen_1 = choose(column_1, table)
    piece, chosen_1 = tie(cut(values, 1), chosen_1)
    column_3 = gather(piece)
    key_1 = exchange(chosen_1)
    column_2, key_1 = tie(column_2, key_1)
    chosen_2 = choose(column_2, table)
    key_1, chosen_2 = tie(key_1, chosen_2)
    value_0 = exchange(chosen_2)
    key_rand = requested(own, [key_0, key_1])

    outs = per_head(
        weights_kernel,
        [weights_like, wide_like] + pay_like,
        [smem_spec()] * 2 + [head_block] * 3 + anywhere,
        [weight_block, head_block] + anywhere,
        term_scratch,
        24,
    )(pick, ends, queries, out_grad, keys, *key_rand)
    outs, value_0 = tie(outs, value_0)
    weights, value_own = outs[:2]

    returned = back_to_partners(terms_of(outs, 1))
    column_3, value_own = tie(column_3, value_own)
    chosen_3 = choose(column_3, table)
    chosen_3[0], returned = tie(chosen_3[0], returned)
    value_1 = exchange(chosen_3)
    total, weights = tie(dense(returned), weights)
    value_sums = [scatter(total)]
    later, value_1[lanes // 2] = tie(outs, value_1[lanes // 2])
    returned = back_to_partners(terms_of(later, 2))
    value_rand = requested(own, [value_0, value_1])

    outs = per_head(
        slope_kernel,
        [weights_like, wide_like] + pay_like,
        [smem_spec()] + [head_block] * 2 + [weight_block, head_block] + anywhere,
        [weight_block, head_block] + anywhere,
        term_scratch,
        20,
    )(pick, queries, out_grad, weights, values, *value_rand)
    slopes, key_own = outs[:2]
    returned, key_own = tie(returned, key_own)
    value_sums.append(scatter(dense(returned)))
    returned = back_to_partners(terms_of(outs, 1))
    more, returned[lanes // 2] = tie(outs, returned[lanes // 2])
    key_sums = [scatter(dense(returned))]
    returned = back_to_partners(terms_of(more, 2))
    value_mine, key_mine, returned = tie(terms_of(later, 0), terms_of(more, 0), returned)
    total, slopes = tie(dense(returned), slopes)
    key_sums.append(scatter(total))
    value_mine, key_mine = back_to_partners(value_mine), back_to_partners(key_mine)

    out, query_grad = per_head(
        output_kernel,
        [like, like],
        [smem_spec()] + [weight_block] * 2 + [head_block] * 2 + anywhere * 2,
        [head_block] * 2,
        [pool, pool, band, band, sems, sems],
        15,
    )(pick, weights, slopes, keys, values, *key_rand, *value_rand)
    value_grad = finish(value_own, value_sums, value_mine)
    key_grad = finish(key_own, key_sums, key_mine)
    return out, query_grad, key_grad, value_grad


def solution(mesh):
    return jax.shard_map(
        body,
        mesh=mesh,
        in_specs=(P("seq", "head"), P("seq", "head"), P("seq", "head"), P("seq", "head"), P(), P()),
        out_specs=(P("seq", "head"), P("seq", "head"), P("seq", "head"), P("seq", "head")),
        check_vma=False,
    )
```

time: 477 us -> 457 us (0.958)
  starting transfers between devices: 87.3 us -> 40.8 us
  waiting for transfers between devices: 211 us -> 250 us
  local copies, waits for them, and re-layouts: 59.3 us -> 48.1 us
    ppermute x65 -> x33, starting transfers between devices: 86.9 us -> 40.5 us  [rotate(): return lax.ppermute(array, 'seq', moves)]
    ppermute x65 -> x33, waiting for transfers between devices: 152 us -> 184 us  [rotate(): return lax.ppermute(array, 'seq', moves)]
    all_gather x4, waiting for transfers between devices: 36.4 us -> 56 us  [gather(): column = lax.all_gather(piece, 'seq', axis_index_groups=columns)]
    reduce_scatter x4, waiting for transfers between devices: 21.7 us -> 10.2 us  [scatter(): lax.psum_scatter(array, 'seq', scatter_dimension=0, axis_index_groups=col...]
    unnamed x223 -> x155, local copies, waits for them, and re-layouts: 53.9 us -> 43.3 us
  transfers between devices with their start and end apart: 73 -> 41, of which waited for: 37 -> 22; matrix products, arithmetic and copies ran while one was open for 2% -> 1% of each run, Pallas kernels for 19% -> 20%
where the time goes in v3:
time: 457 us; the launch traced here: 454 us
  waiting for transfers between devices  250 us (55%)
  Pallas kernels  99.3 us (22%)
  local copies, waits for them, and re-layouts  48.1 us (11%)
  starting transfers between devices  40.8 us (9%)
  between operations  14.6 us (3%)
    ppermute x33, waiting for transfers between devices, rotate(): return lax.ppermute(array, 'seq', moves)  184 us
    all_gather x4, waiting for transfers between devices, gather(): column = lax.all_gather(piece, 'seq', axis_index_groups=columns)  56 us
    unnamed x155, local copies, waits for them, and re-layouts  43.3 us
    ppermute x33, starting transfers between devices, rotate(): return lax.ppermute(array, 'seq', moves)  40.5 us
    pallas_call x1, Pallas kernels, body(): per_head(weights_kernel, [weights_like, wide_like] + pay_like, [smem_spec...  24.1 us
    pallas_call x1, Pallas kernels, body(): per_head(slope_kernel, [weights_like, wide_like] + pay_like, [smem_spec()...  21.3 us
    pallas_call x4, Pallas kernels, sum_blocks(): call(kernel, jax.ShapeDtypeStruct(shape, jnp.bfloat16), specs, 6, [pltpu....  19.6 us
    pallas_call x1, Pallas kernels, body(): per_head(output_kernel, [like, like], [smem_spec()] + [weight_block] * 2...  16.7 us
  transfers between devices with their start and end apart: 41, of which 22 were waited for; matrix products, arithmetic and copies ran while one was open for 1% of the time, Pallas kernels for 20%

profile of v3, /device:TPU:16, one launch (start us, length us, event | category | flops | bytes accessed | tf_op | source)
XLA Modules:
  0.0 453.5 jit_solution(496064009655078358)
XLA Ops:
  7.3 2.4 fusion.23
  11.6 2.5 shard_map.93
  20.7 10.1 %collective-permute-done.rest_3_.rest_15_ = bf16[2,8,128,128]{3,2,1,0:T(8,128)(2,1)S(1)} collective-permute-done((bf16[2,8,128,128]{3,2,1,0:T(8,128)(2,1)}, bf16[2,8,128,128]{3,2,1,0:T(8,128)(2,1)S(1)}, u32[]{:S(2)}, u32[]{:S(2)}) %collective-permute-start) | collective-permute-done | bytes 524320 | tf_op jit(solution)/shard_map/ppermute | solution.py:470
  31.7 9.2 %collective-permute-done.1.rest_6_.rest_18_ = bf16[2,8,128,128]{3,2,1,0:T(8,128)(2,1)S(1)} collective-permute-done((bf16[2,8,128,128]{3,2,1,0:T(8,128)(2,1)}, bf16[2,8,128,128]{3,2,1,0:T(8,128)(2,1)S(1)}, u32[]{:S(2)}, u32[]{:S(2)}) %collective-permute-start.1) | collective-permute-done | bytes 524320 | tf_op jit(solution)/shard_map/ppermute | solution.py:470
  41.7 14.2 %all-gather.11.cloned.1.call-done.column_ref = bf16[16,64,1024]{2,1,0:T(8,128)(2,1)} async-done(((bf16[4,64,1024]{2,1,0:T(8,128)(2,1)}), bf16[16,64,1024]{2,1,0:T(8,128)(2,1)}) %all-gather.11.cloned.1.call-update) | async-done | bytes 2097168 | tf_op jit(solution)/shard_map/all_gather | solution.py:529
  55.9 1.6 copy-done.4
  57.5 2.3 shard_map.94
  65.2 37.5 %all-gather.9.cloned.1.call-done.column_ref = bf16[16,64,1024]{2,1,0:T(8,128)(2,1)} async-done(((bf16[4,64,1024]{2,1,0:T(8,128)(2,1)}), bf16[16,64,1024]{2,1,0:T(8,128)(2,1)}) %all-gather.9.cloned.1.call-update) | async-done | bytes 2097168 | tf_op jit(solution)/shard_map/all_gather | solution.py:529
  102.7 1.8 copy-done.5
  104.5 2.3 shard_map.95
  110.6 1.5 collective-permute-start.7
  112.4 29.5 %collective-permute-done.7.rest_8_ = bf16[40,64,128]{2,1,0:T(8,128)(2,1)S(1)} collective-permute-done((bf16[40,64,128]{2,1,0:T(8,128)(2,1)S(1)}, bf16[40,64,128]{2,1,0:T(8,128)(2,1)S(1)}, u32[]{:S(2)}, u32[]{:S(2)}) %collective-permute-start.7) | collective-permute-done | bytes 655392 | tf_op jit(solution)/shard_map/ppermute | solution.py:470
  141.9 3.0 collective-permute-done.8.rest_11_
  144.9 4.1 all-gather.15.cloned.1.call-done.column_ref
  149.0 1.6 copy-done.6
  150.6 2.3 shard_map.96
  158.1 24.1 %shard_map.97 = (bf16[8,4,1024,128]{3,2,1,0:T(8,128)(2,1)}, f32[512,1024]{1,0:T(8,128)}, bf16[8,128,128]{2,1,0:T(8,128)(2,1)S(1)}, bf16[40,64,128]{2,1,0:T(8,128...) custom-call(s32[194]{0:T(256)S(1)} %pad_add_fusion.pick, ...), custom_call_target="tpu_custom_call" | custom-call | flops 24000000000 | bytes 84000000 | tf_op jit(solution)/shard_map/pallas_call | solution.py:622
  187.0 4.0 collective-permute-done.11.rest_10_.rest_22_
  191.1 2.4 collective-permute-start.12
  195.1 1.6 copy-done.7
  196.7 2.3 shard_map.98
  200.7 8.9 %collective-permute-done.13.rest_2_ = bf16[40,64,128]{2,1,0:T(8,128)(2,1)} collective-permute-done((bf16[40,64,128]{2,1,0:T(8,128)(2,1)}, bf16[40,64,128]{2,1,0:T(8,128)(2,1)}, u32[]{:S(2)}, u32[]{:S(2)}) %collective-permute-start.13) | collective-permute-done | bytes 655392 | tf_op jit(solution)/shard_map/ppermute | solution.py:470
  209.6 2.3 collective-permute-done.12.rest_1_
  211.8 15.6 %collective-permute-done.14.rest_3_ = bf16[48,64,128]{2,1,0:T(8,128)(2,1)} collective-permute-done((bf16[48,64,128]{2,1,0:T(8,128)(2,1)}, bf16[48,64,128]{2,1,0:T(8,128)(2,1)}, u32[]{:S(2)}, u32[]{:S(2)}) %collective-permute-start.14) | collective-permute-done | bytes 786464 | tf_op jit(solution)/shard_map/ppermute | solution.py:470
  227.4 5.4 %shard_map.99 = bf16[16,64,1024]{2,1,0:T(8,128)(2,1)} custom-call(s32[128]{0:T(128)S(1)} %reshape.301.table_ref, s32[8]{0:T(128)S(1)} %concatenate.7.info_ref, bf16[40,64,128]{2,1,0:T(8,128)(2,1)S(1)} %copy-done.64, bf16[48,64,128]{2,1,0:T(8,128)(2,1)S(1)} %collective-permute-done.12.rest_1_, bf16[40,64,128]{2,1,0:T(8,128)(2,1)} %collective-permute-done.13.rest_2_, ...), custom_call_target="tpu_custom_call" | custom-call | flops 6000000000 | bytes 21000000 | tf_op jit(solution)/shard_map/pallas_call | solution.py:181
  234.4 1.5 collective-permute-start.17
  236.5 28.9 %collective-permute-done.15.rest_8_.rest_20_ = bf16[40,64,128]{2,1,0:T(8,128)(2,1)S(1)} collective-permute-done((bf16[40,64,128]{2,1,0:T(8,128)(2,1)S(1)}, bf16[40,64,128]{2,1,0:T(8,128)(2,1)S(1)}, u32[]{:S(2)}, u32[]{:S(2)}) %collective-permute-start.15) | collective-permute-done | bytes 655392 | tf_op jit(solution)/shard_map/ppermute | solution.py:470
  265.7 2.0 collective-permute-start.24
  273.7 21.3 %shard_map.100 = (bf16[8,4,1024,128]{3,2,1,0:T(8,128)(2,1)}, f32[512,1024]{1,0:T(8,128)}, bf16[8,128,128]{2,1,0:T(8,128)(2,1)S(1)}, bf16[40,64,128]{2,1,0:T(8,12...) custom-call(s32[194]{0:T(256)S(1)} %pad_add_fusion.pick, ...), custom_call_target="tpu_custom_call" | custom-call | flops 20000000000 | bytes 70000000 | tf_op jit(solution)/shard_map/pallas_call | solution.py:644
  295.9 7.3 %collective-permute-done.24.rest_3_ = bf16[48,64,128]{2,1,0:T(8,128)(2,1)S(1)} collective-permute-done((bf16[48,64,128]{2,1,0:T(8,128)(2,1)}, bf16[48,64,128]{2,1,0:T(8,128)(2,1)S(1)}, u32[]{:S(2)}, u32[]{:S(2)}) %collective-permute-start.24) | collective-permute-done | bytes 786464 | tf_op jit(solution)/shard_map/ppermute | solution.py:470
  303.2 4.7 %shard_map.105 = bf16[16,64,1024]{2,1,0:T(8,128)(2,1)} custom-call(s32[128]{0:T(128)S(1)} %reshape.301.table_ref, s32[8]{0:T(128)S(1)} %concatenate.7.info_ref, bf16[40,64,128]{2,1,0:T(8,128)(2,1)S(1)} %copy-done.60, bf16[48,64,128]{2,1,0:T(8,128)(2,1)S(1)} %collective-permute-done.22.rest_1_, bf16[40,64,128]{2,1,0:T(8,128)(2,1)S(1)} %collective-permute-done.23.rest_2_, ...), custom_call_target="tpu_custom_call" | custom-call | flops 6000000000 | bytes 21000000 | tf_op jit(solution)/shard_map/pallas_call | solution.py:181
  308.4 1.6 collective-permute-start.26
  310.4 15.7 %collective-permute-done.18.rest_2_ = bf16[40,64,128]{2,1,0:T(8,128)(2,1)S(1)} collective-permute-done((bf16[40,64,128]{2,1,0:T(8,128)(2,1)S(1)}, bf16[40,64,128]{2,1,0:T(8,128)(2,1)S(1)}, u32[]{:S(2)}, u32[]{:S(2)}) %collective-permute-start.18) | collective-permute-done | bytes 655392 | tf_op jit(solution)/shard_map/ppermute | solution.py:470
  326.0 2.6 collective-permute-done.25.rest_1_
  328.7 14.5 %collective-permute-done.26.rest_3_ = bf16[48,64,128]{2,1,0:T(8,128)(2,1)S(1)} collective-permute-done((bf16[48,64,128]{2,1,0:T(8,128)(2,1)}, bf16[48,64,128]{2,1,0:T(8,128)(2,1)S(1)}, u32[]{:S(2)}, u32[]{:S(2)}) %collective-permute-start.26) | collective-permute-done | bytes 786464 | tf_op jit(solution)/shard_map/ppermute | solution.py:470
  343.2 4.9 %shard_map.103 = bf16[16,64,1024]{2,1,0:T(8,128)(2,1)} custom-call(s32[128]{0:T(128)S(1)} %reshape.301.table_ref, s32[8]{0:T(128)S(1)} %concatenate.7.info_ref, bf16[40,64,128]{2,1,0:T(8,128)(2,1)S(1)} %get-tuple-element.255.rest_0_, bf16[48,64,128]{2,1,0:T(8,128)(2,1)S(1)} %collective-permute-done.25.rest_1_, ...), custom_call_target="tpu_custom_call" | custom-call | flops 6000000000 | bytes 21000000 | tf_op jit(solution)/shard_map/pallas_call | solution.py:181
  350.2 1.8 collective-permute-start.20
  352.0 13.5 %collective-permute-done.20.rest_2_ = bf16[40,64,128]{2,1,0:T(8,128)(2,1)S(1)} collective-permute-done((bf16[40,64,128]{2,1,0:T(8,128)(2,1)S(1)}, bf16[40,64,128]{2,1,0:T(8,128)(2,1)S(1)}, u32[]{:S(2)}, u32[]{:S(2)}) %collective-permute-start.20) | collective-permute-done | bytes 655392 | tf_op jit(solution)/shard_map/ppermute | solution.py:470
  365.5 3.4 collective-permute-done.19.rest_1_
  368.9 15.1 %collective-permute-done.21.rest_3_ = bf16[48,64,128]{2,1,0:T(8,128)(2,1)S(1)} collective-permute-done((bf16[48,64,128]{2,1,0:T(8,128)(2,1)S(1)}, bf16[48,64,128]{2,1,0:T(8,128)(2,1)S(1)}, u32[]{:S(2)}, u32[]{:S(2)}) %collective-permute-start.21) | collective-permute-done | bytes 786464 | tf_op jit(solution)/shard_map/ppermute | solution.py:470
  385.0 4.6 %shard_map.101 = bf16[16,64,1024]{2,1,0:T(8,128)(2,1)} custom-call(s32[128]{0:T(128)S(1)} %reshape.301.table_ref, s32[8]{0:T(128)S(1)} %concatenate.7.info_ref, bf16[40,64,128]{2,1,0:T(8,128)(2,1)S(1)} %copy-done.62, bf16[48,64,128]{2,1,0:T(8,128)(2,1)S(1)} %collective-permute-done.19.rest_1_, bf16[40,64,128]{2,1,0:T(8,128)(2,1)S(1)} %collective-permute-done.20.rest_2_, ...), custom_call_target="tpu_custom_call" | custom-call | flops 6000000000 | bytes 21000000 | tf_op jit(solution)/shard_map/pallas_call | solution.py:181
  391.1 2.1 collective-permute-start.30
  400.3 16.7 %shard_map.102 = (bf16[512,1024]{1,0:T(8,128)(2,1)}, bf16[512,1024]{1,0:T(8,128)(2,1)}) custom-call(s32[194]{0:T(256)S(1)} %pad_add_fusion.pick, bf16[8,4,1024,128]{3,2,1,0:T(8,128)(2,1)} %get-tuple-element.230.p_ref, bf16[8,4,1024,128]{3,2,1,0:T(8,128)(2,1)} %get-tuple-element.278.ds_ref, bf16[512,1024]{1,0:T(8,128)(2,1)} %k_ref.3, ...), custom_call_target="tpu_custom_call" | custom-call | flops 15000000512 | bytes 52500000 | tf_op jit(solution)/shard_map/pallas_call | solution.py:664
  417.7 1.8 collective-permute-start.29
  425.9 1.6 copy-done.45
  428.4 2.7 shard_map.106
  431.2 10.2 %reduce-scatter.7.cloned.1.call-done.rest_1_ = bf16[4,64,1024]{2,1,0:T(8,128)(2,1)} async-done(((bf16[16,64,1024]{2,1,0:T(8,128)(2,1)}), bf16[4,64,1024]{2,1,0:T(8,128)(2,1)}) %reduce-scatter.7.cloned.1.call-update) | async-done | bytes 524304 | tf_op jit(solution)/shard_map/reduce_scatter | solution.py:548
  443.4 3.3 shard_map.104
  (239 shorter events, 64.9 us)
Async XLA Ops:
  7.2 48.7 %all-gather.11.cloned.1.call-start = ((), (), s32[]{:S(2)}) async-start(), calls=%async_computation.9 | async-start | bytes 2621440 | tf_op jit(solution)/shard_map/all_gather | solution.py:529
  9.7 93.0 %all-gather.9.cloned.1.call-start = ((), (), s32[]{:S(2)}) async-start(), calls=%async_computation.8 | async-start | bytes 2621440 | tf_op jit(solution)/shard_map/all_gather | solution.py:529
  11.5 137.5 %all-gather.15.cloned.1.call-start = ((), (), s32[]{:S(2)}) async-start(), calls=%async_computation.11 | async-start | bytes 2621440 | tf_op jit(solution)/shard_map/all_gather | solution.py:529
  14.9 16.0 %collective-permute-start = (bf16[2,8,128,128]{3,2,1,0:T(8,128)(2,1)}, bf16[2,8,128,128]{3,2,1,0:T(8,128)(2,1)S(1)}, u32[]{:S(2)}, u32[]{:S(2)}) collective-permute-start(bf16[2,8,128,128]{3,2,1,0:T(8,128)(2,1)} %get-tuple-element.156), channel_id=1, source_target_pairs={{0,2},{2,4},{4,6},{6,0},{8,10},{10,12},{12,14},{14,8},{16,18},{18,... | collective-permute-start | bytes 1572872 | tf_op jit(solution)/shard_map/ppermute | solution.py:470
  16.4 24.5 %collective-permute-start.1 = (bf16[2,8,128,128]{3,2,1,0:T(8,128)(2,1)}, bf16[2,8,128,128]{3,2,1,0:T(8,128)(2,1)S(1)}, u32[]{:S(2)}, u32[]{:S(2)}) collective-permute-start(bf16[2,8,128,128]{3,2,1,0:T(8,128)(2,1)} %get-tuple-element.157), channel_id=1, source_target_pairs={{0,4},{2,6},{4,0},{6,2},{8,12},{10,14},{12,8},{14,10},{16,20},{18,... | collective-permute-start | bytes 1572872 | tf_op jit(solution)/shard_map/ppermute | solution.py:470
  17.9 23.8 %collective-permute-start.2 = (bf16[2,8,128,128]{3,2,1,0:T(8,128)(2,1)S(1)}, bf16[2,8,128,128]{3,2,1,0:T(8,128)(2,1)S(1)}, u32[]{:S(2)}, u32[]{:S(2)}) collective-permute-start(bf16[2,8,128,128]{3,2,1,0:T(8,128)(2,1)S(1)} %get-tuple-element.158), channel_id=1, source_target_pairs={{0,6},{2,0},{4,2},{6,4},{8,14},{10,8},{12,10},{14,12},{16,22},{18,... | collective-permute-start | bytes 1572872 | tf_op jit(solution)/shard_map/ppermute | solution.py:470
  41.7 18.0 %copy-start.24 = (bf16[2,8,128,128]{3,2,1,0:T(8,128)(2,1)}, bf16[2,8,128,128]{3,2,1,0:T(8,128)(2,1)S(1)}, u32[]{:S(2)}) copy-start(bf16[2,8,128,128]{3,2,1,0:T(8,128)(2,1)S(1)} %collective-permute-done.2.rest_9_.rest_21_) | copy-start | bytes 1572868
  60.7 134.4 %all-gather.13.cloned.1.call-start = ((), (), s32[]{:S(2)}) async-start(), calls=%async_computation.10 | async-start | bytes 2621440 | tf_op jit(solution)/shard_map/all_gather | solution.py:529
  60.7 42.0 %collective-permute-start.3 = (bf16[48,64,128]{2,1,0:T(8,128)(2,1)S(1)}, bf16[48,64,128]{2,1,0:T(8,128)(2,1)}, u32[]{:S(2)}, u32[]{:S(2)}) collective-permute-start(bf16[48,64,128]{2,1,0:T(8,128)(2,1)S(1)} %get-tuple-element.165), channel_id=1, source_target_pairs={{0,2},{2,4},{4,6},{6,0},{8,10},{10,12},{12,14},{14,8},{16,18},{18,... | collective-permute-start | bytes 2359304 | tf_op jit(solution)/shard_map/ppermute | solution.py:470
  62.2 40.5 %collective-permute-start.5 = (bf16[48,64,128]{2,1,0:T(8,128)(2,1)S(1)}, bf16[48,64,128]{2,1,0:T(8,128)(2,1)}, u32[]{:S(2)}, u32[]{:S(2)}) collective-permute-start(bf16[48,64,128]{2,1,0:T(8,128)(2,1)S(1)} %get-tuple-element.167), channel_id=1, source_target_pairs={{0,6},{2,0},{4,2},{6,4},{8,14},{10,8},{12,10},{14,12},{16,22},{18,... | collective-permute-start | bytes 2359304 | tf_op jit(solution)/shard_map/ppermute | solution.py:470
  63.7 39.0 %collective-permute-start.4 = (bf16[40,64,128]{2,1,0:T(8,128)(2,1)S(1)}, bf16[40,64,128]{2,1,0:T(8,128)(2,1)S(1)}, u32[]{:S(2)}, u32[]{:S(2)}) collective-permute-start(bf16[40,64,128]{2,1,0:T(8,128)(2,1)S(1)} %get-tuple-element.166), channel_id=1, source_target_pairs={{0,4},{2,6},{4,0},{6,2},{8,12},{10,14},{12,8},{14,10},{16,20},{18,... | collective-permute-start | bytes 1966088 | tf_op jit(solution)/shard_map/ppermute | solution.py:470
  107.7 34.2 %collective-permute-start.6 = (bf16[48,64,128]{2,1,0:T(8,128)(2,1)S(1)}, bf16[48,64,128]{2,1,0:T(8,128)(2,1)}, u32[]{:S(2)}, u32[]{:S(2)}) collective-permute-start(bf16[48,64,128]{2,1,0:T(8,128)(2,1)S(1)} %get-tuple-element.178), channel_id=1, source_target_pairs={{0,2},{2,4},{4,6},{6,0},{8,10},{10,12},{12,14},{14,8},{16,18},{18,... | collective-permute-start | bytes 2359304 | tf_op jit(solution)/shard_map/ppermute | solution.py:470
  109.1 35.7 %collective-permute-start.8 = (bf16[48,64,128]{2,1,0:T(8,128)(2,1)S(1)}, bf16[48,64,128]{2,1,0:T(8,128)(2,1)}, u32[]{:S(2)}, u32[]{:S(2)}) collective-permute-start(bf16[48,64,128]{2,1,0:T(8,128)(2,1)S(1)} %get-tuple-element.180), channel_id=1, source_target_pairs={{0,6},{2,0},{4,2},{6,4},{8,14},{10,8},{12,10},{14,12},{16,22},{18,... | collective-permute-start | bytes 2359304 | tf_op jit(solution)/shard_map/ppermute | solution.py:470
  110.6 31.3 %collective-permute-start.7 = (bf16[40,64,128]{2,1,0:T(8,128)(2,1)S(1)}, bf16[40,64,128]{2,1,0:T(8,128)(2,1)S(1)}, u32[]{:S(2)}, u32[]{:S(2)}) collective-permute-start(bf16[40,64,128]{2,1,0:T(8,128)(2,1)S(1)} %get-tuple-element.179), channel_id=1, source_target_pairs={{0,4},{2,6},{4,0},{6,2},{8,12},{10,14},{12,8},{14,10},{16,20},{18,... | collective-permute-start | bytes 1966088 | tf_op jit(solution)/shard_map/ppermute | solution.py:470
  112.3 308.6 %reduce-scatter.9.cloned.1.call-start = ((), (), s32[]{:S(2)}) async-start(), calls=%async_computation.6 | async-start | bytes 2621440 | tf_op jit(solution)/shard_map/reduce_scatter | solution.py:548
  153.7 33.3 %collective-permute-start.10 = (bf16[40,64,128]{2,1,0:T(8,128)(2,1)S(1)}, bf16[40,64,128]{2,1,0:T(8,128)(2,1)S(1)}, u32[]{:S(2)}, u32[]{:S(2)}) collective-permute-start(bf16[40,64,128]{2,1,0:T(8,128)(2,1)S(1)} %get-tuple-element.216), channel_id=1, source_target_pairs={{0,4},{2,6},{4,0},{6,2},{8,12},{10,14},{12,8},{14,10},{16,20},{18,... | collective-permute-start | bytes 1966088 | tf_op jit(solution)/shard_map/ppermute | solution.py:470
  155.2 31.9 %collective-permute-start.9 = (bf16[48,64,128]{2,1,0:T(8,128)(2,1)S(1)}, bf16[48,64,128]{2,1,0:T(8,128)(2,1)S(1)}, u32[]{:S(2)}, u32[]{:S(2)}) collective-permute-start(bf16[48,64,128]{2,1,0:T(8,128)(2,1)S(1)} %get-tuple-element.215), channel_id=1, source_target_pairs={{0,2},{2,4},{4,6},{6,0},{8,10},{10,12},{12,14},{14,8},{16,18},{18,... | collective-permute-start | bytes 2359304 | tf_op jit(solution)/shard_map/ppermute | solution.py:470
  156.6 34.4 %collective-permute-start.11 = (bf16[48,64,128]{2,1,0:T(8,128)(2,1)S(1)}, bf16[48,64,128]{2,1,0:T(8,128)(2,1)S(1)}, u32[]{:S(2)}, u32[]{:S(2)}) collective-permute-start(bf16[48,64,128]{2,1,0:T(8,128)(2,1)S(1)} %get-tuple-element.217), channel_id=1, source_target_pairs={{0,6},{2,0},{4,2},{6,4},{8,14},{10,8},{12,10},{14,12},{16,22},{18,... | collective-permute-start | bytes 2359304 | tf_op jit(solution)/shard_map/ppermute | solution.py:470
  191.1 20.7 %collective-permute-start.12 = (bf16[48,64,128]{2,1,0:T(8,128)(2,1)}, bf16[48,64,128]{2,1,0:T(8,128)(2,1)S(1)}, u32[]{:S(2)}, u32[]{:S(2)}) collective-permute-start(bf16[48,64,128]{2,1,0:T(8,128)(2,1)} %get-tuple-element.222), channel_id=1, source_target_pairs={{0,6},{2,0},{4,2},{6,4},{8,14},{10,8},{12,10},{14,12},{16,22},{18,... | collective-permute-start | bytes 2359304 | tf_op jit(solution)/shard_map/ppermute | solution.py:470
  193.5 34.0 %collective-permute-start.14 = (bf16[48,64,128]{2,1,0:T(8,128)(2,1)}, bf16[48,64,128]{2,1,0:T(8,128)(2,1)}, u32[]{:S(2)}, u32[]{:S(2)}) collective-permute-start(bf16[48,64,128]{2,1,0:T(8,128)(2,1)} %get-tuple-element.224), channel_id=1, source_target_pairs={{0,2},{2,4},{4,6},{6,0},{8,10},{10,12},{12,14},{14,8},{16,18},{18,... | collective-permute-start | bytes 2359304 | tf_op jit(solution)/shard_map/ppermute | solution.py:470
  193.5 16.1 %collective-permute-start.13 = (bf16[40,64,128]{2,1,0:T(8,128)(2,1)}, bf16[40,64,128]{2,1,0:T(8,128)(2,1)}, u32[]{:S(2)}, u32[]{:S(2)}) collective-permute-start(bf16[40,64,128]{2,1,0:T(8,128)(2,1)} %get-tuple-element.223), channel_id=1, source_target_pairs={{0,4},{2,6},{4,0},{6,2},{8,12},{10,14},{12,8},{14,10},{16,20},{18,... | collective-permute-start | bytes 1966088 | tf_op jit(solution)/shard_map/ppermute | solution.py:470
  196.7 30.8 %copy-start.64 = (bf16[40,64,128]{2,1,0:T(8,128)(2,1)S(1)}, bf16[40,64,128]{2,1,0:T(8,128)(2,1)}, u32[]{:S(2)}) copy-start(bf16[40,64,128]{2,1,0:T(8,128)(2,1)} %copy-done.63) | copy-start | bytes 1966084
  232.9 32.5 %copy-start.13 = (bf16[40,64,128]{2,1,0:T(8,128)(2,1)S(1)}, bf16[40,64,128]{2,1,0:T(8,128)(2,1)}, u32[]{:S(2)}) copy-start(bf16[40,64,128]{2,1,0:T(8,128)(2,1)} %copy-done.12) | copy-start | bytes 1966084
  232.9 188.0 %reduce-scatter.11.cloned.1.call-start = ((), (), s32[]{:S(2)}) async-start(), calls=%async_computation.7 | async-start | bytes 2621440 | tf_op jit(solution)/shard_map/reduce_scatter | solution.py:548
  233.0 34.8 %collective-permute-start.16 = (bf16[48,64,128]{2,1,0:T(8,128)(2,1)S(1)}, bf16[48,64,128]{2,1,0:T(8,128)(2,1)S(1)}, u32[]{:S(2)}, u32[]{:S(2)}) collective-permute-start(bf16[48,64,128]{2,1,0:T(8,128)(2,1)S(1)} %get-tuple-element.247), channel_id=1, source_target_pairs={{0,2},{2,4},{4,6},{6,0},{8,10},{10,12},{12,14},{14,8},{16,18},{18,... | collective-permute-start | bytes 2359304 | tf_op jit(solution)/shard_map/ppermute | solution.py:470
  234.4 33.4 %collective-permute-start.17 = (bf16[48,64,128]{2,1,0:T(8,128)(2,1)S(1)}, bf16[48,64,128]{2,1,0:T(8,128)(2,1)S(1)}, u32[]{:S(2)}, u32[]{:S(2)}) collective-permute-start(bf16[48,64,128]{2,1,0:T(8,128)(2,1)S(1)} %get-tuple-element.251), channel_id=1, source_target_pairs={{0,6},{2,0},{4,2},{6,4},{8,14},{10,8},{12,10},{14,12},{16,22},{18,... | collective-permute-start | bytes 2359304 | tf_op jit(solution)/shard_map/ppermute | solution.py:470
  235.9 29.4 %collective-permute-start.15 = (bf16[40,64,128]{2,1,0:T(8,128)(2,1)S(1)}, bf16[40,64,128]{2,1,0:T(8,128)(2,1)S(1)}, u32[]{:S(2)}, u32[]{:S(2)}) collective-permute-start(bf16[40,64,128]{2,1,0:T(8,128)(2,1)S(1)} %copy-done.15), channel_id=1, source_target_pairs={{0,4},{2,6},{4,0},{6,2},{8,12},{10,14},{12,8},{14,10},{16,20},{18,... | collective-permute-start | bytes 1966088 | tf_op jit(solution)/shard_map/ppermute | solution.py:470
  265.3 30.5 %collective-permute-start.23 = (bf16[40,64,128]{2,1,0:T(8,128)(2,1)S(1)}, bf16[40,64,128]{2,1,0:T(8,128)(2,1)S(1)}, u32[]{:S(2)}, u32[]{:S(2)}) collective-permute-start(bf16[40,64,128]{2,1,0:T(8,128)(2,1)S(1)} %copy-done.13), channel_id=1, source_target_pairs={{0,4},{2,6},{4,0},{6,2},{8,12},{10,14},{12,8},{14,10},{16,20},{18,... | collective-permute-start | bytes 1966088 | tf_op jit(solution)/shard_map/ppermute | solution.py:470
  265.7 30.2 %collective-permute-start.22 = (bf16[48,64,128]{2,1,0:T(8,128)(2,1)}, bf16[48,64,128]{2,1,0:T(8,128)(2,1)S(1)}, u32[]{:S(2)}, u32[]{:S(2)}) collective-permute-start(bf16[48,64,128]{2,1,0:T(8,128)(2,1)} %get-tuple-element.282), channel_id=1, source_target_pairs={{0,6},{2,0},{4,2},{6,4},{8,14},{10,8},{12,10},{14,12},{16,22},{18,... | collective-permute-start | bytes 2359304 | tf_op jit(solution)/shard_map/ppermute | solution.py:470
  265.7 37.4 %collective-permute-start.24 = (bf16[48,64,128]{2,1,0:T(8,128)(2,1)}, bf16[48,64,128]{2,1,0:T(8,128)(2,1)S(1)}, u32[]{:S(2)}, u32[]{:S(2)}) collective-permute-start(bf16[48,64,128]{2,1,0:T(8,128)(2,1)} %get-tuple-element.284), channel_id=1, source_target_pairs={{0,2},{2,4},{4,6},{6,0},{8,10},{10,12},{12,14},{14,8},{16,18},{18,... | collective-permute-start | bytes 2359304 | tf_op jit(solution)/shard_map/ppermute | solution.py:470
  273.7 29.4 %copy-start.60 = (bf16[40,64,128]{2,1,0:T(8,128)(2,1)S(1)}, bf16[40,64,128]{2,1,0:T(8,128)(2,1)}, u32[]{:S(2)}) copy-start(bf16[40,64,128]{2,1,0:T(8,128)(2,1)} %copy-done.59) | copy-start | bytes 1966084
  295.9 12.0 %copy-start.67 = (bf16[8,128,128]{2,1,0:T(8,128)(2,1)}, bf16[8,128,128]{2,1,0:T(8,128)(2,1)S(1)}, u32[]{:S(2)}) copy-start(bf16[8,128,128]{2,1,0:T(8,128)(2,1)S(1)} %get-tuple-element.288.rest_2_) | copy-start | bytes 786436
  307.9 123.3 %reduce-scatter.5.cloned.1.call-start = ((), (), s32[]{:S(2)}) async-start(), calls=%async_computation.4 | async-start | bytes 2621440 | tf_op jit(solution)/shard_map/reduce_scatter | solution.py:548
  307.9 20.7 %collective-permute-start.25 = (bf16[48,64,128]{2,1,0:T(8,128)(2,1)}, bf16[48,64,128]{2,1,0:T(8,128)(2,1)S(1)}, u32[]{:S(2)}, u32[]{:S(2)}) collective-permute-start(bf16[48,64,128]{2,1,0:T(8,128)(2,1)} %get-tuple-element.258), channel_id=1, source_target_pairs={{0,6},{2,0},{4,2},{6,4},{8,14},{10,8},{12,10},{14,12},{16,22},{18,... | collective-permute-start | bytes 2359304 | tf_op jit(solution)/shard_map/ppermute | solution.py:470
  308.4 34.8 %collective-permute-start.26 = (bf16[48,64,128]{2,1,0:T(8,128)(2,1)}, bf16[48,64,128]{2,1,0:T(8,128)(2,1)S(1)}, u32[]{:S(2)}, u32[]{:S(2)}) collective-permute-start(bf16[48,64,128]{2,1,0:T(8,128)(2,1)} %get-tuple-element.264), channel_id=1, source_target_pairs={{0,2},{2,4},{4,6},{6,0},{8,10},{10,12},{12,14},{14,8},{16,18},{18,... | collective-permute-start | bytes 2359304 | tf_op jit(solution)/shard_map/ppermute | solution.py:470
  310.0 16.0 %collective-permute-start.18 = (bf16[40,64,128]{2,1,0:T(8,128)(2,1)S(1)}, bf16[40,64,128]{2,1,0:T(8,128)(2,1)S(1)}, u32[]{:S(2)}, u32[]{:S(2)}) collective-permute-start(bf16[40,64,128]{2,1,0:T(8,128)(2,1)S(1)} %get-tuple-element.261), channel_id=1, source_target_pairs={{0,4},{2,6},{4,0},{6,2},{8,12},{10,14},{12,8},{14,10},{16,20},{18,... | collective-permute-start | bytes 1966088 | tf_op jit(solution)/shard_map/ppermute | solution.py:470
  348.1 93.3 %reduce-scatter.7.cloned.1.call-start = ((), (), s32[]{:S(2)}) async-start(), calls=%async_computation.5 | async-start | bytes 2621440 | tf_op jit(solution)/shard_map/reduce_scatter | solution.py:548
  348.1 20.7 %collective-permute-start.19 = (bf16[48,64,128]{2,1,0:T(8,128)(2,1)}, bf16[48,64,128]{2,1,0:T(8,128)(2,1)S(1)}, u32[]{:S(2)}, u32[]{:S(2)}) collective-permute-start(bf16[48,64,128]{2,1,0:T(8,128)(2,1)} %get-tuple-element.271), channel_id=1, source_target_pairs={{0,6},{2,0},{4,2},{6,4},{8,14},{10,8},{12,10},{14,12},{16,22},{18,... | collective-permute-start | bytes 2359304 | tf_op jit(solution)/shard_map/ppermute | solution.py:470
  349.2 34.8 %collective-permute-start.21 = (bf16[48,64,128]{2,1,0:T(8,128)(2,1)S(1)}, bf16[48,64,128]{2,1,0:T(8,128)(2,1)S(1)}, u32[]{:S(2)}, u32[]{:S(2)}) collective-permute-start(bf16[48,64,128]{2,1,0:T(8,128)(2,1)S(1)} %copy-done.73), channel_id=1, source_target_pairs={{0,2},{2,4},{4,6},{6,0},{8,10},{10,12},{12,14},{14,8},{16,18},{18,... | collective-permute-start | bytes 2359304 | tf_op jit(solution)/shard_map/ppermute | solution.py:470
  350.2 15.3 %collective-permute-start.20 = (bf16[40,64,128]{2,1,0:T(8,128)(2,1)S(1)}, bf16[40,64,128]{2,1,0:T(8,128)(2,1)S(1)}, u32[]{:S(2)}, u32[]{:S(2)}) collective-permute-start(bf16[40,64,128]{2,1,0:T(8,128)(2,1)S(1)} %get-tuple-element.272), channel_id=1, source_target_pairs={{0,4},{2,6},{4,0},{6,2},{8,12},{10,14},{12,8},{14,10},{16,20},{18,... | collective-permute-start | bytes 1966088 | tf_op jit(solution)/shard_map/ppermute | solution.py:470
  389.7 41.4 %collective-permute-start.27 = (bf16[8,128,128]{2,1,0:T(8,128)(2,1)}, bf16[8,128,128]{2,1,0:T(8,128)(2,1)}, u32[]{:S(2)}, u32[]{:S(2)}) collective-permute-start(bf16[8,128,128]{2,1,0:T(8,128)(2,1)} %copy-done.38), channel_id=1, source_target_pairs={{0,6},{2,0},{4,2},{6,4},{8,14},{10,8},{12,10},{14,12},{16,22},{18,... | collective-permute-start | bytes 786440 | tf_op jit(solution)/shard_map/ppermute | solution.py:470
  390.8 40.3 %collective-permute-start.28 = (bf16[8,128,128]{2,1,0:T(8,128)(2,1)}, bf16[8,128,128]{2,1,0:T(8,128)(2,1)}, u32[]{:S(2)}, u32[]{:S(2)}) collective-permute-start(bf16[8,128,128]{2,1,0:T(8,128)(2,1)} %copy-done.37), channel_id=1, source_target_pairs={{0,4},{2,6},{4,0},{6,2},{8,12},{10,14},{12,8},{14,10},{16,20},{18,... | collective-permute-start | bytes 786440 | tf_op jit(solution)/shard_map/ppermute | solution.py:470
  391.1 25.8 %collective-permute-start.30 = (bf16[8,128,128]{2,1,0:T(8,128)(2,1)}, bf16[8,128,128]{2,1,0:T(8,128)(2,1)S(1)}, u32[]{:S(2)}, u32[]{:S(2)}) collective-permute-start(bf16[8,128,128]{2,1,0:T(8,128)(2,1)} %copy-done.36), channel_id=1, source_target_pairs={{0,6},{2,0},{4,2},{6,4},{8,14},{10,8},{12,10},{14,12},{16,22},{18,... | collective-permute-start | bytes 786440 | tf_op jit(solution)/shard_map/ppermute | solution.py:470
  393.3 26.2 %collective-permute-start.31 = (bf16[8,128,128]{2,1,0:T(8,128)(2,1)S(1)}, bf16[8,128,128]{2,1,0:T(8,128)(2,1)S(1)}, u32[]{:S(2)}, u32[]{:S(2)}) collective-permute-start(bf16[8,128,128]{2,1,0:T(8,128)(2,1)S(1)} %copy-done.35), channel_id=1, source_target_pairs={{0,4},{2,6},{4,0},{6,2},{8,12},{10,14},{12,8},{14,10},{16,20},{18,... | collective-permute-start | bytes 786440 | tf_op jit(solution)/shard_map/ppermute | solution.py:470
  393.5 26.7 %collective-permute-start.32 = (bf16[8,128,128]{2,1,0:T(8,128)(2,1)S(1)}, bf16[8,128,128]{2,1,0:T(8,128)(2,1)S(1)}, u32[]{:S(2)}, u32[]{:S(2)}) collective-permute-start(bf16[8,128,128]{2,1,0:T(8,128)(2,1)S(1)} %copy-done.33), channel_id=1, source_target_pairs={{0,2},{2,4},{4,6},{6,0},{8,10},{10,12},{12,14},{14,8},{16,18},{18,... | collective-permute-start | bytes 786440 | tf_op jit(solution)/shard_map/ppermute | solution.py:470
  417.7 13.4 %collective-permute-start.29 = (bf16[8,128,128]{2,1,0:T(8,128)(2,1)}, bf16[8,128,128]{2,1,0:T(8,128)(2,1)S(1)}, u32[]{:S(2)}, u32[]{:S(2)}) collective-permute-start(bf16[8,128,128]{2,1,0:T(8,128)(2,1)} %get-tuple-element.291), channel_id=1, source_target_pairs={{0,2},{2,4},{4,6},{6,0},{8,10},{10,12},{12,14},{14,8},{16,18},{18,... | collective-permute-start | bytes 786440 | tf_op jit(solution)/shard_map/ppermute | solution.py:470
  428.4 12.9 %copy-start.46 = (f32[512,1024]{1,0:T(8,128)S(1)}, f32[512,1024]{1,0:T(8,128)}, u32[]{:S(2)}) copy-start(f32[512,1024]{1,0:T(8,128)} %get-tuple-element.285) | copy-start | bytes 6291460
  428.4 12.9 %copy-start.68 = (bf16[8,128,128]{2,1,0:T(8,128)(2,1)S(1)}, bf16[8,128,128]{2,1,0:T(8,128)(2,1)}, u32[]{:S(2)}) copy-start(bf16[8,128,128]{2,1,0:T(8,128)(2,1)} %copy-done.67) | copy-start | bytes 786436
  (70 other events, 205.4 us)
Sparse Core Ops, SparseCore 0:
  10.2 45.6 all-gather.10
  58.0 44.6 all-gather.8
  104.3 44.6 all-gather.14
  150.4 44.6 all-gather.12
  233.0 42.7 reduce-scatter.8
  308.0 42.1 reduce-scatter.10
  352.5 43.1 reduce-scatter.4
  398.1 43.1 reduce-scatter.6

commit v4 on v3

--- a/solution.py
+++ b/solution.py
@@ -17,9 +17,12 @@
 PLANES = 4
 PARTS = 2
 ROWS = BLOCK // PARTS
+KEY_CUTS = (0, 64, BLOCK)
+VALUE_CUTS = (0, 48, BLOCK)
 SCALE = 1.0 / math.sqrt(DH)
 POWER = SCALE / math.log(2.0)
 MASKED = -1e30
+THIN = 16
 VMEM_BYTES = 48 * 1024 * 1024
 
 NT = (((1,), (1,)), ((), ()))
@@ -58,14 +61,14 @@
     return pl.BlockSpec(memory_space=pltpu.VMEM)
 
 
-def call(kernel, out_shape, in_specs, micros, scratch=()):
+def call(kernel, out_shape, in_specs, micros, scratch=(), limit=VMEM_BYTES):
     return pl.pallas_call(
         kernel,
         out_shape=out_shape,
         in_specs=in_specs,
         out_specs=jax.tree.map(lambda _: vmem_spec(), out_shape),
         scratch_shapes=list(scratch),
-        compiler_params=params(),
+        compiler_params=pltpu.CompilerParams(vmem_limit_bytes=limit),
         cost_estimate=cost(micros),
     )
 
@@ -101,6 +104,17 @@
 
 def part_slots(partner, heads, lanes, slots, cap):
     return slots - cap + (GLOB + has_rim(partner, lanes)) * heads
+
+
+def back_globs(part, shared, heads, lanes):
+    if shared:
+        return GLOB * heads // lanes * PARTS if part == 0 else 0
+    return GLOB * heads
+
+
+def back_slots(partner, part, shared, heads, lanes, slots, cap):
+    globs = back_globs(part, shared, heads, lanes)
+    return slots - cap + globs + has_rim(partner, lanes) * heads
 
 
 def pick_blocks(column, table, info, heads, lanes, slots, cap):
@@ -132,10 +146,12 @@
     return call(kernel, shapes, specs, 3)(table, info, column)
 
 
-def sum_blocks(returned, table, info, blocks, heads, slots, cap):
+def sum_blocks(returned, part, shared, table, info, planes, blocks, heads, slots, cap):
     lanes = len(returned)
     rows = returned[0].shape[1]
     main = slots - cap
+    pairs = GLOB * heads // lanes if shared and part == 0 else 0
+    segment = blocks * rows + (THIN if pairs else 0)
 
     def kernel(table_ref, info_ref, *rest):
         refs, out_ref, total = rest[:lanes], rest[lanes], rest[lanes + 1]
@@ -153,50 +169,87 @@
                 return carry
 
             lax.fori_loop(0, main, step, 0)
-
-        def add_row(row, sources, first):
-            for head in range(heads):
-                term = sources[0][first + head].astype(jnp.float32)
-                for source in sources[1:]:
-                    term = term + source[first + head].astype(jnp.float32)
-                total[row, :, head * DH : (head + 1) * DH] += term
-
-        for g in range(GLOB):
+        for side, partner in enumerate((lanes - 1, 1)):
+            row = info_ref[2 * GLOB + 2 + side]
+
+            @pl.when(row >= 0)
+            def _(row=row, partner=partner):
+                first = main + back_globs(part, shared, heads, lanes)
+                for head in range(heads):
+                    term = refs[partner][first + head].astype(jnp.float32)
+                    total[row, :, head * DH : (head + 1) * DH] += term
+
+        for g in range(0 if shared else GLOB):
 
             @pl.when(info_ref[2 * g + 1] > 0)
             def _(g=g):
-                add_row(info_ref[2 * g], refs, main + g * heads)
-
-        for side, partner in enumerate((lanes - 1, 1)):
-            row = info_ref[2 * GLOB + 2 + side]
-
-            @pl.when(row >= 0)
-            def _(row=row, partner=partner):
-                add_row(row, [refs[partner]], main + GLOB * heads)
-
-        out_ref[...] = total[...].astype(out_ref.dtype)
-
-    shape = (blocks, rows, heads * DH)
+                for head in range(heads):
+                    slot = main + g * heads + head
+                    term = refs[0][slot].astype(jnp.float32)
+                    for ref in refs[1:]:
+                        term = term + ref[slot].astype(jnp.float32)
+                    total[info_ref[2 * g], :, head * DH : (head + 1) * DH] += term
+
+        for plane in range(planes):
+            for block in range(blocks):
+                start = plane * segment + block * rows
+                whole = total[plane * blocks + block]
+                out_ref[start : start + rows] = whole.astype(out_ref.dtype)
+        if pairs:
+            shares = []
+            for slot in range(main, main + pairs * PARTS):
+                term = refs[0][slot].astype(jnp.float32)
+                for ref in refs[1:]:
+                    term = term + ref[slot].astype(jnp.float32)
+                shares.append(term.astype(out_ref.dtype))
+            per_plane = pairs * BLOCK // THIN // planes
+            per_half = rows // THIN
+            for plane in range(planes):
+                start = plane * segment + blocks * rows
+                for number in range(heads):
+                    piece = plane * per_plane + number
+                    pair, inner = piece // (PARTS * per_half), piece % (PARTS * per_half)
+                    if number < per_plane:
+                        half, at = inner // per_half, inner % per_half * THIN
+                        value = shares[half * pairs + pair][at : at + THIN]
+                    else:
+                        value = jnp.zeros((THIN, DH), out_ref.dtype)
+                    out_ref[start : start + THIN, number * DH : (number + 1) * DH] = value
+
+    shape = (planes * blocks, rows, heads * DH)
     specs = [smem_spec()] * 2 + [vmem_spec()] * lanes
     return call(
         kernel,
-        jax.ShapeDtypeStruct(shape, jnp.bfloat16),
+        jax.ShapeDtypeStruct((planes * segment, heads * DH), jnp.bfloat16),
         specs,
         6,
         [pltpu.VMEM(shape, jnp.float32)],
     )(table, info, *returned)
 
 
-def final_sum(own, sums, returned, table, heads, slots, cap):
+def final_sum(own, sums, returned, thins, table, final_info, heads, slots, cap):
     blocks, _, width = own.shape
     lanes = len(returned)
-
-    def kernel(table_ref, own_ref, *rest):
-        sum_refs, refs = rest[:PARTS], rest[PARTS : PARTS + lanes]
-        out_ref, total = rest[PARTS + lanes :]
+    pairs = GLOB * heads // lanes
+
+    arrays = [own, *sums, *returned, *thins]
+    number = len(arrays)
+
+    def kernel(table_ref, info_ref, *rest):
+        far, out_ref, total = rest[:number], rest[number], rest[number + 1]
+        near, sems = rest[number + 2 : 2 * number + 2], rest[2 * number + 2]
+        copies = [pltpu.make_async_copy(*pair, sems.at[n]) for n, pair in enumerate(zip(far, near))]
+        for copy in copies:
+            copy.start()
+        for copy in copies:
+            copy.wait()
+        own_ref, rest = near[0], near[1:]
+        sum_refs, refs, thin_refs = rest[:PARTS], rest[PARTS : PARTS + lanes], rest[PARTS + lanes :]
         for part, sum_ref in enumerate(sum_refs):
             here = slice(part * ROWS, (part + 1) * ROWS)
-            total[:, here] = own_ref[:, here] + sum_ref[...].astype(jnp.float32)
+            for block in range(blocks):
+                rows = slice(block * ROWS, (block + 1) * ROWS)
+                total[block, here] = own_ref[block, here] + sum_ref[rows].astype(jnp.float32)
         for partner in range(lanes):
 
             def step(slot, carry, partner=partner):
@@ -210,20 +263,46 @@
                 return carry
 
             lax.fori_loop(0, cap, step, 0)
+        plane, lane = info_ref[GLOB], info_ref[GLOB + 1]
+        for g in range(GLOB if thin_refs else 0):
+            thin_ref = thin_refs[0]
+            planes = thin_ref.shape[0]
+            per_plane = pairs * BLOCK // THIN // planes
+            row = info_ref[g]
+
+            @pl.when(row >= 0)
+            def _(g=g, row=row, thin_ref=thin_ref, planes=planes, per_plane=per_plane):
+                for head in range(heads):
+                    pair = g * heads + head
+                    steps = (lane - pair // pairs + lanes) % lanes
+                    first = pl.multiple_of(steps * THIN, THIN)
+                    for inner in range(BLOCK // THIN):
+                        piece = pair % pairs * (BLOCK // THIN) + inner
+                        hops = (plane - piece // per_plane + planes) % planes
+                        at = piece % per_plane * DH
+                        value = thin_ref[hops, pl.ds(first, THIN), at : at + DH]
+                        here = slice(inner * THIN, (inner + 1) * THIN)
+                        columns = slice(head * DH, (head + 1) * DH)
+                        total[row, here, columns] += value.astype(jnp.float32)
+
         out_ref[...] = total[...].astype(out_ref.dtype)
 
-    specs = [smem_spec()] + [vmem_spec()] * (1 + PARTS + lanes)
+    specs = [smem_spec()] * 2 + [any_spec()] * number
     return call(
         kernel,
         jax.ShapeDtypeStruct(own.shape, jnp.bfloat16),
         specs,
         5,
-        [pltpu.VMEM(own.shape, jnp.float32)],
-    )(table, own, *sums, *returned)
+        [pltpu.VMEM(own.shape, jnp.float32)]
+        + [pltpu.VMEM(array.shape, array.dtype) for array in arrays]
+        + [pltpu.SemaphoreType.DMA((number,))],
+        62 * 1024 * 1024,
+    )(table, final_info, *arrays)
 
 
 def load_parts(refs, pool, sems, which, heads, lanes, slots, cap):
     stride = slots + (GLOB + 1) * heads
+    cuts = (KEY_CUTS, VALUE_CUTS)[which]
     copies = []
     for partner in range(lanes):
         first = partner * stride
@@ -234,7 +313,7 @@
             if part == 0:
                 pair = (ref.at[which], pool.at[pl.ds(first, cap)])
             else:
-                rows = pl.ds((part - 1) * ROWS, ROWS)
+                rows = pl.ds(cuts[part - 1], cuts[part] - cuts[part - 1])
                 pair = (ref, pool.at[pl.ds(first + cap, length), rows])
             copies.append(pltpu.make_async_copy(*pair, sems.at[number]))
     for copy in copies:
@@ -243,24 +322,33 @@
         copy.wait()
 
 
-def store_parts(refs, pay, glob_pay, rim_pay, sems, heads, lanes, slots, cap):
+def store_parts(refs, shared, pick, pay, glob_pay, rim_pay, sems, sizes, blocks):
+    heads, lanes, slots, cap = sizes
     main = slots - cap
-    pairs = []
+    pairs = GLOB * heads // lanes
+    share_at = 2 * heads * blocks * RAND + GLOB
+    moves = []
     for partner in range(lanes):
         first = partner * slots
         number = partner * (PARTS + 1)
-        pairs.append((pay.at[pl.ds(first, cap)], refs[number]))
+        share = pick[share_at + partner]
+        moves.append((pay.at[pl.ds(first, cap)], refs[number]))
         for part in range(PARTS):
             ref = refs[number + 1 + part]
             rows = pl.ds(part * ROWS, ROWS)
-            pairs.append((pay.at[pl.ds(first + cap, main), rows], ref.at[pl.ds(0, main)]))
-            there = ref.at[pl.ds(main, GLOB * heads)]
-            pairs.append((glob_pay.at[pl.ds(0, GLOB * heads), rows], there))
+            moves.append((pay.at[pl.ds(first + cap, main), rows], ref.at[pl.ds(0, main)]))
+            if shared:
+                there = refs[number + 1].at[pl.ds(main + part * pairs, pairs)]
+                moves.append((glob_pay.at[pl.ds(share, pairs), rows], there))
+            else:
+                there = ref.at[pl.ds(main, GLOB * heads)]
+                moves.append((glob_pay.at[pl.ds(0, GLOB * heads), rows], there))
             if has_rim(partner, lanes):
                 side = 0 if partner == 1 else 1
-                there = ref.at[pl.ds(main + GLOB * heads, heads)]
-                pairs.append((rim_pay.at[pl.ds(side * heads, heads), rows], there))
-    copies = [pltpu.make_async_copy(*pair, sems.at[n]) for n, pair in enumerate(pairs)]
+                after = main + back_globs(part, shared, heads, lanes)
+                there = ref.at[pl.ds(after, heads)]
+                moves.append((rim_pay.at[pl.ds(side * heads, heads), rows], there))
+    copies = [pltpu.make_async_copy(*move, sems.at[n]) for n, move in enumerate(moves)]
     for copy in copies:
         copy.start()
     for copy in copies:
@@ -287,29 +375,31 @@
     return [pool[at] for at in places]
 
 
-def pieces():
-    starts = [0] + [(SPAN + n) * BLOCK for n in range(RAND + GLOB + 1)]
-    return list(zip(starts[:-1], starts[1:]))
-
-
-def add_terms(left, right, block, cuts, band_sum, glob_sum):
-    near = slice(block * BLOCK, (block + SPAN) * BLOCK)
-    a, b = cuts[0]
-    band_sum[near] += dot(left[0, block, a:b], right, NN)
-    start = (SPAN + RAND) * BLOCK
-    term = dot(left[0, block, start:], right, NN)
+def lay_out(target, pick, pool, band, head, block, heads, blocks):
+    target[: SPAN * BLOCK] = band[block * BLOCK : (block + SPAN) * BLOCK]
+    for n, item in enumerate(far_blocks(pick, pool, head, block, heads, blocks)):
+        target[(SPAN + n) * BLOCK : (SPAN + n + 1) * BLOCK] = item
+
+
+def share_terms(terms, block, band_sum, glob_sum, pay, pick, head, heads, blocks, scale):
+    band_sum[block * BLOCK : (block + SPAN) * BLOCK] += terms[: SPAN * BLOCK]
+    entry = heads * blocks * RAND + GLOB + (head * blocks + block) * RAND
+    for r in range(RAND):
+        term = terms[(SPAN + r) * BLOCK : (SPAN + r + 1) * BLOCK] * scale
+        pay[pick[entry + r]] = term.astype(jnp.bfloat16)
     if block == 0:
-        glob_sum[...] = term
+        glob_sum[...] = terms[(SPAN + RAND) * BLOCK :]
     else:
-        glob_sum[...] += term
-
-
-def store_random(left, right, block, cuts, pay, pick, head, heads, blocks, scale):
-    entry = (head * blocks + block) * RAND
-    for r in range(RAND):
-        a, b = cuts[1 + r]
-        term = dot(left[0, block, a:b], right, NN) * scale
-        pay[pick[heads * blocks * RAND + GLOB + entry + r]] = term.astype(jnp.bfloat16)
+        glob_sum[...] += terms[(SPAN + RAND) * BLOCK :]
+
+
+def in_turn(blocks, front, middle, back):
+    begun = front(0)
+    for block in range(blocks):
+        done = middle(block, begun)
+        if block + 1 < blocks:
+            begun = front(block + 1)
+        back(block, done)
 
 
 def store_sums(own_ref, band_sum, glob_sum, glob_pay, rim_pay, head, heads, blocks, scale):
@@ -329,7 +419,7 @@
     def kernel(pick, ends, q_ref, g_ref, k_ref, *rest):
         kr_refs, (p_ref, own_ref), rest = rest[:count], rest[count : count + 2], rest[count + 2 :]
         pay_refs, rest = rest[:count], rest[count:]
-        pool, pay, glob_pay, rim_pay, band, band_sum, glob_sum, sems, out_sems = rest
+        pool, pay, glob_pay, rim_pay, band, listed, band_sum, glob_sum, sems, out_sems = rest
         head = pl.program_id(0)
 
         @pl.when(head == 0)
@@ -338,39 +428,36 @@
 
         fill(k_ref, pool, band, head, heads, lanes, slots, blocks)
         band_sum[...] = jnp.zeros_like(band_sum)
-        cuts = pieces()
-        for block in range(blocks):
-            here = slice(block * BLOCK, (block + 1) * BLOCK)
-            near = slice(block * BLOCK, (block + SPAN) * BLOCK)
-            query = q_ref[here]
-            grad = g_ref[here]
-            window = dot(band[near], query, NT)
-            scores = [window[o * BLOCK : (o + 1) * BLOCK] for o in range(SPAN)]
+
+        def front(block):
+            lay_out(listed.at[block], pick, pool, band, head, block, heads, blocks)
+            query = q_ref[block * BLOCK : (block + 1) * BLOCK]
+            return dot(listed[block], query, NT)
+
+        def middle(block, scores):
+            ahead, behind = scores[:BLOCK], scores[(SPAN - 1) * BLOCK : SPAN * BLOCK]
             if block == 0:
-                scores[0] = jnp.where(ends[0] > 0, MASKED, scores[0])
+                ahead = jnp.where(ends[0] > 0, MASKED, ahead)
             if block == blocks - 1:
-                scores[-1] = jnp.where(ends[1] > 0, MASKED, scores[-1])
-            far = far_blocks(pick, pool, head, block, heads, blocks)
-            scores += [dot(item, query, NT) for item in far]
-            peak = scores[0]
-            for score in scores[1:]:
-                peak = jnp.maximum(peak, score)
-            peak = jnp.max(peak, axis=0, keepdims=True)
-            powers = [jnp.exp2((score - peak) * POWER) for score in scores]
-            total = powers[0]
-            for power in powers[1:]:
-                total = total + power
-            inverse = 1.0 / jnp.sum(total, axis=0, keepdims=True)
-            for number, power in enumerate(powers):
-                weights = (power * inverse).astype(jnp.bfloat16)
-                p_ref[0, block, number * BLOCK : (number + 1) * BLOCK] = weights
-            store_random(p_ref, grad, block, cuts, pay, pick, head, heads, blocks, 1.0)
-            add_terms(p_ref, grad, block, cuts, band_sum, glob_sum)
+                behind = jnp.where(ends[1] > 0, MASKED, behind)
+            inner = scores[BLOCK : (SPAN - 1) * BLOCK]
+            scores = jnp.concatenate([ahead, inner, behind, scores[SPAN * BLOCK :]], axis=0)
+            peak = jnp.max(scores, axis=0, keepdims=True)
+            powers = jnp.exp2((scores - peak) * POWER)
+            inverse = 1.0 / jnp.sum(powers, axis=0, keepdims=True)
+            return (powers * inverse).astype(jnp.bfloat16)
+
+        def back(block, weights):
+            p_ref[0, block] = weights
+            terms = dot(weights, g_ref[block * BLOCK : (block + 1) * BLOCK], NN)
+            share_terms(terms, block, band_sum, glob_sum, pay, pick, head, heads, blocks, 1.0)
+
+        in_turn(blocks, front, middle, back)
         store_sums(own_ref, band_sum, glob_sum, glob_pay, rim_pay, head, heads, blocks, 1.0)
 
         @pl.when(head == heads - 1)
         def _():
-            store_parts(pay_refs, pay, glob_pay, rim_pay, out_sems, *sizes)
+            store_parts(pay_refs, True, pick, pay, glob_pay, rim_pay, out_sems, sizes, blocks)
 
     return kernel
 
@@ -382,7 +469,7 @@
     def kernel(pick, q_ref, g_ref, p_ref, v_ref, *rest):
         vr_refs, (ds_ref, own_ref), rest = rest[:count], rest[count : count + 2], rest[count + 2 :]
         pay_refs, rest = rest[:count], rest[count:]
-        pool, pay, glob_pay, rim_pay, band, band_sum, glob_sum, sems, out_sems = rest
+        pool, pay, glob_pay, rim_pay, band, listed, band_sum, glob_sum, sems, out_sems = rest
         head = pl.program_id(0)
 
         @pl.when(head == 0)
@@ -391,27 +478,28 @@
 
         fill(v_ref, pool, band, head, heads, lanes, slots, blocks)
         band_sum[...] = jnp.zeros_like(band_sum)
-        cuts = pieces()
-        for block in range(blocks):
-            here = slice(block * BLOCK, (block + 1) * BLOCK)
-            near = slice(block * BLOCK, (block + SPAN) * BLOCK)
-            query = q_ref[here]
-            grad = g_ref[here]
-            listed = [band[near]] + far_blocks(pick, pool, head, block, heads, blocks)
-            slopes = [dot(value, grad, NT) for value in listed]
-            wide = [p_ref[0, block, a:b].astype(jnp.float32) for a, b in cuts]
-            delta = 0.0
-            for weight, slope in zip(wide, slopes):
-                delta = delta + jnp.sum(weight * slope, axis=0, keepdims=True)
-            for (a, b), weight, slope in zip(cuts, wide, slopes):
-                ds_ref[0, block, a:b] = (weight * (slope - delta)).astype(jnp.bfloat16)
-            store_random(ds_ref, query, block, cuts, pay, pick, head, heads, blocks, SCALE)
-            add_terms(ds_ref, query, block, cuts, band_sum, glob_sum)
+
+        def front(block):
+            lay_out(listed.at[block], pick, pool, band, head, block, heads, blocks)
+            grad = g_ref[block * BLOCK : (block + 1) * BLOCK]
+            return dot(listed[block], grad, NT)
+
+        def middle(block, slopes):
+            weights = p_ref[0, block].astype(jnp.float32)
+            delta = jnp.sum(weights * slopes, axis=0, keepdims=True)
+            return (weights * (slopes - delta)).astype(jnp.bfloat16)
+
+        def back(block, slopes):
+            ds_ref[0, block] = slopes
+            terms = dot(slopes, q_ref[block * BLOCK : (block + 1) * BLOCK], NN)
+            share_terms(terms, block, band_sum, glob_sum, pay, pick, head, heads, blocks, SCALE)
+
+        in_turn(blocks, front, middle, back)
         store_sums(own_ref, band_sum, glob_sum, glob_pay, rim_pay, head, heads, blocks, SCALE)
 
         @pl.when(head == heads - 1)
         def _():
-            store_parts(pay_refs, pay, glob_pay, rim_pay, out_sems, *sizes)
+            store_parts(pay_refs, False, pick, pay, glob_pay, rim_pay, out_sems, sizes, blocks)
 
     return kernel
 
@@ -422,7 +510,7 @@
 
     def kernel(pick, p_ref, ds_ref, k_ref, v_ref, *rest):
         kr_refs, vr_refs, rest = rest[:count], rest[count : 2 * count], rest[2 * count :]
-        out_ref, dq_ref, k_pool, v_pool, k_band, v_band, sems, more = rest
+        out_ref, dq_ref, k_pool, v_pool, k_band, v_band, listed, sems, more = rest
         head = pl.program_id(0)
 
         @pl.when(head == 0)
@@ -434,15 +522,15 @@
         fill(v_ref, v_pool, v_band, head, heads, lanes, slots, blocks)
         for block in range(blocks):
             here = slice(block * BLOCK, (block + 1) * BLOCK)
-            near = slice(block * BLOCK, (block + SPAN) * BLOCK)
-            for left, band, pool, scale, to_ref in (
-                (p_ref, v_band, v_pool, 1.0, out_ref),
-                (ds_ref, k_band, k_pool, SCALE, dq_ref),
+            for number, (left, band, pool, scale, to_ref) in enumerate(
+                (
+                    (p_ref, v_band, v_pool, 1.0, out_ref),
+                    (ds_ref, k_band, k_pool, SCALE, dq_ref),
+                )
             ):
-                listed = [band[near]] + far_blocks(pick, pool, head, block, heads, blocks)
-                result = 0.0
-                for (a, b), item in zip(pieces(), listed):
-                    result = result + dot(left[0, block, a:b], item, TN)
+                target = listed.at[2 * block + number]
+                lay_out(target, pick, pool, band, head, block, heads, blocks)
+                result = dot(left[0, block], target[...], TN)
                 to_ref[here] = (result * scale).astype(jnp.bfloat16)
 
     return kernel
@@ -494,6 +582,7 @@
             distance * stride + spot[lane],
             glob_distance * stride + slots + jnp.arange(GLOB, dtype=jnp.int32) * heads,
             distance * slots + spot[lane],
+            (lane - jnp.arange(lanes, dtype=jnp.int32) + lanes) % lanes * (GLOB * heads // lanes),
         ]
     )
     head_of = jnp.arange(entries, dtype=jnp.int32) // (blocks * RAND)
@@ -520,14 +609,16 @@
         axis=1,
     )
     info = jnp.concatenate([info.reshape(-1), jnp.stack(rims)]).astype(jnp.int32)
+    mine = jnp.where(glob_place == place, glob_ids % blocks, -1)
+    final_info = jnp.concatenate([mine, jnp.stack([plane, lane])]).astype(jnp.int32)
     ends = jnp.stack([place == 0, place == shards - 1]).astype(jnp.int32)
 
-    def cut(array, part):
-        return array.reshape(blocks, BLOCK, width)[:, part * ROWS : (part + 1) * ROWS]
+    def cut(array, cuts, part):
+        return array.reshape(blocks, BLOCK, width)[:, cuts[part] : cuts[part + 1]]
 
     def gather(piece):
         column = lax.all_gather(piece, "seq", axis_index_groups=columns)
-        return column.reshape(planes * blocks, ROWS, width)
+        return column.reshape(planes * blocks, piece.shape[1], width)
 
     def choose(column, table):
         return list(pick_blocks(column, table, info, *sizes))
@@ -538,8 +629,17 @@
     def requested(own, parts):
         return [array for k in range(lanes) for array in [own[k]] + [part[k] for part in parts]]
 
-    def dense(returned):
-        return sum_blocks(returned, table, info, planes * blocks, heads, slots, cap)
+    def dense(returned, part, shared):
+        return sum_blocks(returned, part, shared, table, info, planes, blocks, heads, slots, cap)
+
+    def spread(array):
+        thin = array[blocks * ROWS :]
+        column = [thin]
+        for step in range(1, planes):
+            moves = [(i, (i + step * lanes) % shards) for i in range(shards)]
+            column.append(lax.ppermute(thin, "seq", moves))
+        column = jnp.stack(column)
+        return jnp.concatenate([column] + [rotate(column, k) for k in range(1, lanes)], axis=1)
 
     def terms_of(outs, part):
         return [outs[2 + k * (PARTS + 1) + part] for k in range(lanes)]
@@ -549,9 +649,9 @@
             array, "seq", scatter_dimension=0, axis_index_groups=columns, tiled=True
         )
 
-    def finish(own, sums, returned):
+    def finish(own, sums, returned, thins):
         own = own.reshape(blocks, BLOCK, width)
-        total = final_sum(own, sums, returned, table, heads, slots, cap)
+        total = final_sum(own, sums, returned, thins, table, final_info, heads, slots, cap)
         return total.reshape(rows_here, width)
 
     head_block = pl.BlockSpec((rows_here, DH), lambda h: (0, h))
@@ -559,12 +659,16 @@
     like = jax.ShapeDtypeStruct((rows_here, width), jnp.bfloat16)
     wide_like = jax.ShapeDtypeStruct((rows_here, width), jnp.float32)
     weights_like = jax.ShapeDtypeStruct((heads, blocks, LISTED * BLOCK, BLOCK), jnp.bfloat16)
-    pay_like = []
-    for partner in range(lanes):
-        pay_like.append(jax.ShapeDtypeStruct((cap, BLOCK, DH), jnp.bfloat16))
-        length = part_slots(partner, *sizes)
-        pay_like += [jax.ShapeDtypeStruct((length, ROWS, DH), jnp.bfloat16)] * PARTS
-    count = len(pay_like)
+    def payloads(shared):
+        shapes = []
+        for partner in range(lanes):
+            shapes.append(jax.ShapeDtypeStruct((cap, BLOCK, DH), jnp.bfloat16))
+            for part in range(PARTS):
+                length = back_slots(partner, part, shared, *sizes)
+                shapes.append(jax.ShapeDtypeStruct((length, ROWS, DH), jnp.bfloat16))
+        return shapes
+
+    count = lanes * (PARTS + 1)
 
     def many(*shape):
         return pltpu.VMEM(shape + (BLOCK, DH), jnp.bfloat16)
@@ -578,11 +682,13 @@
         many(GLOB * heads),
         many(2 * heads),
         band,
+        pltpu.VMEM((blocks, LISTED * BLOCK, DH), jnp.bfloat16),
         pltpu.VMEM(((blocks + 2 * WMAX) * BLOCK, DH), jnp.float32),
         pltpu.VMEM((GLOB * BLOCK, DH), jnp.float32),
         sems,
         pltpu.SemaphoreType.DMA((out_copies(lanes),)),
     ]
+    listed = pltpu.VMEM((2 * blocks, LISTED * BLOCK, DH), jnp.bfloat16)
     anywhere = [any_spec()] * count
 
     def per_head(kernel, out_shape, in_specs, out_specs, scratch, micros):
@@ -597,20 +703,20 @@
             cost_estimate=cost(micros),
         )
 
-    column_0 = gather(cut(keys, 0))
-    piece, table = tie(cut(keys, 1), table)
+    column_0 = gather(cut(keys, KEY_CUTS, 0))
+    piece, table = tie(cut(keys, KEY_CUTS, 1), table)
     column_1 = gather(piece)
     blocks_of = (blocks, BLOCK, width)
     own = pick_own(keys.reshape(blocks_of), values.reshape(blocks_of), table, *sizes)
     own = out_to_partners(own)
     column_0, own = tie(column_0, own)
     chosen_0 = choose(column_0, table)
-    piece, chosen_0 = tie(cut(values, 0), chosen_0)
+    piece, chosen_0 = tie(cut(values, VALUE_CUTS, 0), chosen_0)
     column_2 = gather(piece)
     key_0 = exchange(chosen_0)
     column_1, key_0 = tie(column_1, key_0)
     chosen_1 = choose(column_1, table)
-    piece, chosen_1 = tie(cut(values, 1), chosen_1)
+    piece, chosen_1 = tie(cut(values, VALUE_CUTS, 1), chosen_1)
     column_3 = gather(piece)
     key_1 = exchange(chosen_1)
     column_2, key_1 = tie(column_2, key_1)
@@ -621,7 +727,7 @@
 
     outs = per_head(
         weights_kernel,
-        [weights_like, wide_like] + pay_like,
+        [weights_like, wide_like] + payloads(True),
         [smem_spec()] * 2 + [head_block] * 3 + anywhere,
         [weight_block, head_block] + anywhere,
         term_scratch,
@@ -635,7 +741,7 @@
     chosen_3 = choose(column_3, table)
     chosen_3[0], returned = tie(chosen_3[0], returned)
     value_1 = exchange(chosen_3)
-    total, weights = tie(dense(returned), weights)
+    total, weights = tie(dense(returned, 0, True), weights)
     value_sums = [scatter(total)]
     later, value_1[lanes // 2] = tie(outs, value_1[lanes // 2])
     returned = back_to_partners(terms_of(later, 2))
@@ -643,7 +749,7 @@
 
     outs = per_head(
         slope_kernel,
-        [weights_like, wide_like] + pay_like,
+        [weights_like, wide_like] + payloads(False),
         [smem_spec()] + [head_block] * 2 + [weight_block, head_block] + anywhere,
         [weight_block, head_block] + anywhere,
         term_scratch,
@@ -651,26 +757,30 @@
     )(pick, queries, out_grad, weights, values, *value_rand)
     slopes, key_own = outs[:2]
     returned, key_own = tie(returned, key_own)
-    value_sums.append(scatter(dense(returned)))
+    total, slopes = tie(dense(returned, 1, True), slopes)
+    total, value_sums[0] = tie(total, value_sums[0])
+    value_sums.append(scatter(total))
+    value_thin = spread(value_sums[0])
     returned = back_to_partners(terms_of(outs, 1))
     more, returned[lanes // 2] = tie(outs, returned[lanes // 2])
-    key_sums = [scatter(dense(returned))]
-    returned = back_to_partners(terms_of(more, 2))
-    value_mine, key_mine, returned = tie(terms_of(later, 0), terms_of(more, 0), returned)
-    total, slopes = tie(dense(returned), slopes)
-    key_sums.append(scatter(total))
-    value_mine, key_mine = back_to_partners(value_mine), back_to_partners(key_mine)
-
     out, query_grad = per_head(
         output_kernel,
         [like, like],
         [smem_spec()] + [weight_block] * 2 + [head_block] * 2 + anywhere * 2,
         [head_block] * 2,
-        [pool, pool, band, band, sems, sems],
+        [pool, pool, band, band, listed, sems, sems],
         15,
     )(pick, weights, slopes, keys, values, *key_rand, *value_rand)
-    value_grad = finish(value_own, value_sums, value_mine)
-    key_grad = finish(key_own, key_sums, key_mine)
+    out, returned = tie(out, returned)
+    total, value_sums[1] = tie(dense(returned, 0, False), value_sums[1])
+    key_sums = [scatter(total)]
+    returned = back_to_partners(terms_of(more, 2))
+    value_mine, key_mine, returned = tie(terms_of(later, 0), terms_of(more, 0), returned)
+    total, key_sums[0] = tie(dense(returned, 1, False), key_sums[0])
+    key_sums.append(scatter(total))
+    value_mine, key_mine = back_to_partners(value_mine), back_to_partners(key_mine)
+    value_grad = finish(value_own, value_sums, value_mine, [value_thin])
+    key_grad = finish(key_own, key_sums, key_mine, [])
     return out, query_grad, key_grad, value_grad
 
 

time: 457 us -> 444 us (0.972)
  waiting for transfers between devices: 250 us -> 229 us
  starting transfers between devices: 40.8 us -> 49 us
    ppermute x33 -> x36, waiting for transfers between devices: 184 us -> 156 us  [rotate(): return lax.ppermute(array, 'seq', moves)]
    pallas_call x6, Pallas kernels: 65 us -> 56.5 us  [the longest x4 19.5 us: sum_blocks(): call(kernel, jax.ShapeDtypeStruct((planes * segment, heads * DH), jnp.bfl...]
    all_gather x4, waiting for transfers between devices: 56 us -> 62.5 us  [gather(): column = lax.all_gather(piece, 'seq', axis_index_groups=columns)]
    ppermute x33 -> x36, starting transfers between devices: 40.5 us -> 45.5 us  [rotate(): return lax.ppermute(array, 'seq', moves)]
    unnamed x155 -> x143, local copies, waits for them, and re-layouts: 43.3 us -> 40.9 us
  transfers between devices with their start and end apart: 41 -> 47, of which waited for: 22 -> 22; matrix products, arithmetic and copies ran while one was open for 1% -> 1% of each run, Pallas kernels for 20% -> 20%
where the time goes in v4:
time: 444 us; the launch traced here: 440 us
  waiting for transfers between devices  229 us (52%)
  Pallas kernels  97.5 us (22%)
  starting transfers between devices  49 us (11%)
  local copies, waits for them, and re-layouts  47 us (11%)
  between operations  14.7 us (3%)
    ppermute x36, waiting for transfers between devices, rotate(): return lax.ppermute(array, 'seq', moves)  156 us
    all_gather x4, waiting for transfers between devices, gather(): column = lax.all_gather(piece, 'seq', axis_index_groups=columns)  62.5 us
    ppermute x36, starting transfers between devices, rotate(): return lax.ppermute(array, 'seq', moves)  45.5 us
    unnamed x143, local copies, waits for them, and re-layouts  40.9 us
    pallas_call x4, Pallas kernels, sum_blocks(): call(kernel, jax.ShapeDtypeStruct((planes * segment, heads * DH), jnp.bfl...  19.5 us
    pallas_call x1, Pallas kernels, body(): per_head(slope_kernel, [weights_like, wide_like] + payloads(False), [smem...  19.4 us
    pallas_call x1, Pallas kernels, body(): per_head(output_kernel, [like, like], [smem_spec()] + [weight_block] * 2...  17.6 us
    pallas_call x1, Pallas kernels, body(): per_head(weights_kernel, [weights_like, wide_like] + payloads(True), [sme...  17.6 us
  transfers between devices with their start and end apart: 47, of which 22 were waited for; matrix products, arithmetic and copies ran while one was open for 1% of the time, Pallas kernels for 20%

profile of v4, /device:TPU:16, one launch (start us, length us, event | category | flops | bytes accessed | tf_op | source)
XLA Modules:
  0.0 439.7 jit_solution(16066596087071180571)
XLA Ops:
  7.3 2.4 fusion.23
  11.6 2.5 shard_map.93
  14.9 1.5 collective-permute-start
  16.4 1.5 collective-permute-start.1
  20.4 10.4 %collective-permute-done.rest_3_.rest_15_ = bf16[2,8,128,128]{3,2,1,0:T(8,128)(2,1)S(1)} collective-permute-done((bf16[2,8,128,128]{3,2,1,0:T(8,128)(2,1)}, bf16[2,8,128,128]{3,2,1,0:T(8,128)(2,1)S(1)}, u32[]{:S(2)}, u32[]{:S(2)}) %collective-permute-start) | collective-permute-done | bytes 524320 | tf_op jit(solution)/shard_map/ppermute | solution.py:558
  31.6 9.2 %collective-permute-done.1.rest_6_.rest_18_ = bf16[2,8,128,128]{3,2,1,0:T(8,128)(2,1)S(1)} collective-permute-done((bf16[2,8,128,128]{3,2,1,0:T(8,128)(2,1)}, bf16[2,8,128,128]{3,2,1,0:T(8,128)(2,1)S(1)}, u32[]{:S(2)}, u32[]{:S(2)}) %collective-permute-start.1) | collective-permute-done | bytes 524320 | tf_op jit(solution)/shard_map/ppermute | solution.py:558
  42.5 13.4 %all-gather.11.cloned.1.call-done.column_ref = bf16[16,64,1024]{2,1,0:T(8,128)(2,1)} async-done(((bf16[4,64,1024]{2,1,0:T(8,128)(2,1)}), bf16[16,64,1024]{2,1,0:T(8,128)(2,1)}) %all-gather.11.cloned.1.call-update) | async-done | bytes 2097168 | tf_op jit(solution)/shard_map/all_gather | solution.py:620
  55.9 1.6 copy-done.5
  57.5 2.3 shard_map.94
  60.6 1.5 collective-permute-start.3
  66.0 36.7 %all-gather.9.cloned.1.call-done.column_ref = bf16[16,64,1024]{2,1,0:T(8,128)(2,1)} async-done(((bf16[4,64,1024]{2,1,0:T(8,128)(2,1)}), bf16[16,64,1024]{2,1,0:T(8,128)(2,1)}) %all-gather.9.cloned.1.call-update) | async-done | bytes 2097168 | tf_op jit(solution)/shard_map/all_gather | solution.py:620
  102.7 1.6 copy-done.6
  104.3 2.3 shard_map.95
  107.5 1.5 collective-permute-start.6
  110.5 1.5 collective-permute-start.7
  112.2 29.5 %collective-permute-done.7.rest_8_ = bf16[40,64,128]{2,1,0:T(8,128)(2,1)S(1)} collective-permute-done((bf16[40,64,128]{2,1,0:T(8,128)(2,1)S(1)}, bf16[40,64,128]{2,1,0:T(8,128)(2,1)S(1)}, u32[]{:S(2)}, u32[]{:S(2)}) %collective-permute-start.7) | collective-permute-done | bytes 655392 | tf_op jit(solution)/shard_map/ppermute | solution.py:558
  142.6 2.1 collective-permute-done.8.rest_11_
  146.2 2.2 shard_map.96
  151.1 1.5 collective-permute-start.11
  152.6 17.6 %shard_map.97 = (bf16[8,4,1024,128]{3,2,1,0:T(8,128)(2,1)}, f32[512,1024]{1,0:T(8,128)}, bf16[8,128,128]{2,1,0:T(8,128)(2,1)S(1)}, bf16[32,64,128]{2,1,0:T(8,128...) custom-call(s32[198]{0:T(256)S(1)} %pad_add_fusion.pick, ...), custom_call_target="tpu_custom_call" | custom-call | flops 24000000000 | bytes 84000000 | tf_op jit(solution)/shard_map/pallas_call | solution.py:728
  181.5 1.5 collective-permute-start.13
  183.0 12.4 %all-gather.13.cloned.1.call-done.column_ref = bf16[16,80,1024]{2,1,0:T(8,128)(2,1)} async-done(((bf16[4,80,1024]{2,1,0:T(8,128)(2,1)}), bf16[16,80,1024]{2,1,0:T(8,128)(2,1)}) %all-gather.13.cloned.1.call-update) | async-done | bytes 2621456 | tf_op jit(solution)/shard_map/all_gather | solution.py:620
  195.4 3.7 shard_map.98
  200.0 9.6 %collective-permute-done.14.rest_3_ = bf16[40,64,128]{2,1,0:T(8,128)(2,1)} collective-permute-done((bf16[40,64,128]{2,1,0:T(8,128)(2,1)}, bf16[40,64,128]{2,1,0:T(8,128)(2,1)}, u32[]{:S(2)}, u32[]{:S(2)}) %collective-permute-start.14) | collective-permute-done | bytes 655392 | tf_op jit(solution)/shard_map/ppermute | solution.py:558
  210.6 5.6 %shard_map.99 = bf16[1088,1024]{1,0:T(8,128)(2,1)} custom-call(s32[128]{0:T(128)S(1)} %reshape.301.table_ref, s32[8]{0:T(128)S(1)} %concatenate.13.info_ref, bf16[32,64,128]{2,1,0:T(8,128)(2,1)S(1)} %copy-done.54, bf16[40,64,128]{2,1,0:T(8,128)(2,1)} %collective-permute-done.12.rest_1_, bf16[32,64,128]{2,1,0:T(8,128)(2,1)} %collective-permute-done.13.rest_2_, ...), custom_call_target="tpu_custom_call" | custom-call | flops 6000000000 | bytes 21000000 | tf_op jit(solution)/shard_map/pallas_call | solution.py:221
  217.0 2.3 collective-permute-start.20
  220.1 35.6 %collective-permute-done.15.rest_8_.rest_20_ = bf16[40,80,128]{2,1,0:T(8,128)(2,1)S(1)} collective-permute-done((bf16[40,80,128]{2,1,0:T(8,128)(2,1)S(1)}, bf16[40,80,128]{2,1,0:T(8,128)(2,1)S(1)}, u32[]{:S(2)}, u32[]{:S(2)}) %collective-permute-start.15) | collective-permute-done | bytes 819232 | tf_op jit(solution)/shard_map/ppermute | solution.py:558
  256.8 2.0 collective-permute-start.18
  268.1 19.4 %shard_map.100 = (bf16[8,4,1024,128]{3,2,1,0:T(8,128)(2,1)}, f32[512,1024]{1,0:T(8,128)}, bf16[8,128,128]{2,1,0:T(8,128)(2,1)S(1)}, bf16[40,64,128]{2,1,0:T(8,12...) custom-call(s32[198]{0:T(256)S(1)} %pad_add_fusion.pick, ...), custom_call_target="tpu_custom_call" | custom-call | flops 20000000000 | bytes 70000000 | tf_op jit(solution)/shard_map/pallas_call | solution.py:750
  289.0 4.7 %shard_map.101 = bf16[1024,1024]{1,0:T(8,128)(2,1)} custom-call(s32[128]{0:T(128)S(1)} %reshape.301.table_ref, s32[8]{0:T(128)S(1)} %concatenate.13.info_ref, bf16[24,64,128]{2,1,0:T(8,128)(2,1)S(1)} %copy-done.58, bf16[32,64,128]{2,1,0:T(8,128)(2,1)S(1)} %collective-permute-done.16.rest_1_, bf16[24,64,128]{2,1,0:T(8,128)(2,1)S(1)} %collective-permute-done.17.rest_2_, ...), custom_call_target="tpu_custom_call" | custom-call | flops 6000000000 | bytes 21000000 | tf_op jit(solution)/shard_map/pallas_call | solution.py:221
  303.3 17.6 %shard_map.102 = (bf16[512,1024]{1,0:T(8,128)(2,1)}, bf16[512,1024]{1,0:T(8,128)(2,1)}) custom-call(s32[198]{0:T(256)S(1)} %pad_add_fusion.pick, bf16[8,4,1024,128]{3,2,1,0:T(8,128)(2,1)} %get-tuple-element.241.p_ref, bf16[8,4,1024,128]{3,2,1,0:T(8,128)(2,1)} %get-tuple-element.269.ds_ref, bf16[512,1024]{1,0:T(8,128)(2,1)} %k_ref.3, ...), custom_call_target="tpu_custom_call" | custom-call | flops 15000000512 | bytes 52500000 | tf_op jit(solution)/shard_map/pallas_call | solution.py:766
  320.9 9.8 %collective-permute-done.23.rest_3_ = bf16[48,64,128]{2,1,0:T(8,128)(2,1)S(1)} collective-permute-done((bf16[48,64,128]{2,1,0:T(8,128)(2,1)}, bf16[48,64,128]{2,1,0:T(8,128)(2,1)S(1)}, u32[]{:S(2)}, u32[]{:S(2)}) %collective-permute-start.23) | collective-permute-done | bytes 786464 | tf_op jit(solution)/shard_map/ppermute | solution.py:558
  330.8 4.6 %shard_map.104 = bf16[1024,1024]{1,0:T(8,128)(2,1)} custom-call(s32[128]{0:T(128)S(1)} %reshape.301.table_ref, s32[8]{0:T(128)S(1)} %concatenate.13.info_ref, bf16[40,64,128]{2,1,0:T(8,128)(2,1)S(1)} %copy-done.52, bf16[48,64,128]{2,1,0:T(8,128)(2,1)S(1)} %collective-permute-done.21.rest_1_, bf16[40,64,128]{2,1,0:T(8,128)(2,1)S(1)} %collective-permute-done.22.rest_2_, ...), custom_call_target="tpu_custom_call" | custom-call | flops 6000000000 | bytes 21000000 | tf_op jit(solution)/shard_map/pallas_call | solution.py:221
  336.6 2.4 collective-permute-start.24
  340.1 15.2 %collective-permute-done.25.rest_2_ = bf16[40,64,128]{2,1,0:T(8,128)(2,1)S(1)} collective-permute-done((bf16[40,64,128]{2,1,0:T(8,128)(2,1)S(1)}, bf16[40,64,128]{2,1,0:T(8,128)(2,1)S(1)}, u32[]{:S(2)}, u32[]{:S(2)}) %collective-permute-start.25) | collective-permute-done | bytes 655392 | tf_op jit(solution)/shard_map/ppermute | solution.py:558
  355.4 2.0 collective-permute-done.24.rest_1_
  357.3 16.6 %collective-permute-done.26.rest_3_ = bf16[48,64,128]{2,1,0:T(8,128)(2,1)S(1)} collective-permute-done((bf16[48,64,128]{2,1,0:T(8,128)(2,1)S(1)}, bf16[48,64,128]{2,1,0:T(8,128)(2,1)S(1)}, u32[]{:S(2)}, u32[]{:S(2)}) %collective-permute-start.26) | collective-permute-done | bytes 786464 | tf_op jit(solution)/shard_map/ppermute | solution.py:558
  374.0 4.6 %shard_map.103 = bf16[1024,1024]{1,0:T(8,128)(2,1)} custom-call(s32[128]{0:T(128)S(1)} %reshape.301.table_ref, s32[8]{0:T(128)S(1)} %concatenate.13.info_ref, bf16[40,64,128]{2,1,0:T(8,128)(2,1)S(1)} %copy-done.50, bf16[48,64,128]{2,1,0:T(8,128)(2,1)S(1)} %collective-permute-done.24.rest_1_, bf16[40,64,128]{2,1,0:T(8,128)(2,1)S(1)} %collective-permute-done.25.rest_2_, ...), custom_call_target="tpu_custom_call" | custom-call | flops 6000000000 | bytes 21000000 | tf_op jit(solution)/shard_map/pallas_call | solution.py:221
  378.6 3.6 reduce-scatter.9.cloned.1.call-done.rest_1_
  384.1 2.0 collective-permute-start.35
  386.1 1.6 collective-permute-done.34
  389.6 2.4 collective-permute-start.38
  396.1 2.4 collective-permute-start.36
  399.1 11.0 %collective-permute-done.37 = bf16[4,16,1024]{2,1,0:T(8,128)(2,1)S(1)} collective-permute-done((bf16[4,16,1024]{2,1,0:T(8,128)(2,1)S(1)}, bf16[4,16,1024]{2,1,0:T(8,128)(2,1)S(1)}, u32[]{:S(2)}, u32[]{:S(2)}) %collective-permute-start.37) | collective-permute-done | bytes 131104 | tf_op jit(solution)/shard_map/ppermute | solution.py:558
  414.9 5.3 %shard_map.106 = bf16[4,128,1024]{2,1,0:T(8,128)(2,1)} custom-call(s32[128]{0:T(128)} %copy-done.4, s32[4]{0:T(128)} %pad_add_fusion.2.info_ref, f32[4,128,1024]{2,1,0:T(8,128)} %bitcast.49, bf16[272,1024]{1,0:T(8,128)(2,1)} %reduce-scatter.5.cloned.1.call-done.rest_1_, bf16[256,1024]{1,0:T(8,128)(2,1)} %reduce-scatter.7.cloned.1.call-done.rest_2_, ...), custom_call_target="tpu_custom_call" | custom-call | flops 5000000000 | bytes 17500000 | tf_op jit(solution)/shard_map/pallas_call | solution.py:291
  420.2 4.6 %collective-permute-done.28.rest_5_ = bf16[8,128,128]{2,1,0:T(8,128)(2,1)} collective-permute-done((bf16[8,128,128]{2,1,0:T(8,128)(2,1)S(1)}, bf16[8,128,128]{2,1,0:T(8,128)(2,1)}, u32[]{:S(2)}, u32[]{:S(2)}) %collective-permute-start.28) | collective-permute-done | bytes 262176 | tf_op jit(solution)/shard_map/ppermute | solution.py:558
  424.8 2.9 reduce-scatter.11.cloned.1.call-done.rest_2_
  427.7 5.2 %shard_map.105 = bf16[4,128,1024]{2,1,0:T(8,128)(2,1)} custom-call(s32[128]{0:T(128)} %copy-done.4, s32[4]{0:T(128)} %pad_add_fusion.2.info_ref, f32[4,128,1024]{2,1,0:T(8,128)} %bitcast.50, bf16[256,1024]{1,0:T(8,128)(2,1)} %reduce-scatter.9.cloned.1.call-done.rest_1_, bf16[256,1024]{1,0:T(8,128)(2,1)} %reduce-scatter.11.cloned.1.call-done.rest_2_, ...), custom_call_target="tpu_custom_call" | custom-call | flops 5000000000 | bytes 17500000 | tf_op jit(solution)/shard_map/pallas_call | solution.py:291
  (246 shorter events, 71.6 us)
Async XLA Ops:
  7.2 48.7 %all-gather.11.cloned.1.call-start = ((), (), s32[]{:S(2)}) async-start(), calls=%async_computation.9 | async-start | bytes 2621440 | tf_op jit(solution)/shard_map/all_gather | solution.py:620
  9.7 93.0 %all-gather.9.cloned.1.call-start = ((), (), s32[]{:S(2)}) async-start(), calls=%async_computation.8 | async-start | bytes 2621440 | tf_op jit(solution)/shard_map/all_gather | solution.py:620
  11.4 362.5 %copy-start.4 = (s32[128]{0:T(128)}, s32[128]{0:T(128)S(1)}, u32[]{:S(2)}) copy-start(s32[128]{0:T(128)S(1)} %reshape.301.table_ref) | copy-start | bytes 1540
  11.5 133.3 %all-gather.15.cloned.1.call-start = ((), (), s32[]{:S(2)}) async-start(), calls=%async_computation.11 | async-start | bytes 1966080 | tf_op jit(solution)/shard_map/all_gather | solution.py:620
  14.9 16.0 %collective-permute-start = (bf16[2,8,128,128]{3,2,1,0:T(8,128)(2,1)}, bf16[2,8,128,128]{3,2,1,0:T(8,128)(2,1)S(1)}, u32[]{:S(2)}, u32[]{:S(2)}) collective-permute-start(bf16[2,8,128,128]{3,2,1,0:T(8,128)(2,1)} %get-tuple-element.167), channel_id=1, source_target_pairs={{0,2},{2,4},{4,6},{6,0},{8,10},{10,12},{12,14},{14,8},{16,18},{18,... | collective-permute-start | bytes 1572872 | tf_op jit(solution)/shard_map/ppermute | solution.py:558
  16.4 24.5 %collective-permute-start.1 = (bf16[2,8,128,128]{3,2,1,0:T(8,128)(2,1)}, bf16[2,8,128,128]{3,2,1,0:T(8,128)(2,1)S(1)}, u32[]{:S(2)}, u32[]{:S(2)}) collective-permute-start(bf16[2,8,128,128]{3,2,1,0:T(8,128)(2,1)} %get-tuple-element.168), channel_id=1, source_target_pairs={{0,4},{2,6},{4,0},{6,2},{8,12},{10,14},{12,8},{14,10},{16,20},{18,... | collective-permute-start | bytes 1572872 | tf_op jit(solution)/shard_map/ppermute | solution.py:558
  17.9 23.8 %collective-permute-start.2 = (bf16[2,8,128,128]{3,2,1,0:T(8,128)(2,1)S(1)}, bf16[2,8,128,128]{3,2,1,0:T(8,128)(2,1)S(1)}, u32[]{:S(2)}, u32[]{:S(2)}) collective-permute-start(bf16[2,8,128,128]{3,2,1,0:T(8,128)(2,1)S(1)} %get-tuple-element.169), channel_id=1, source_target_pairs={{0,6},{2,0},{4,2},{6,4},{8,14},{10,8},{12,10},{14,12},{16,22},{18,... | collective-permute-start | bytes 1572872 | tf_op jit(solution)/shard_map/ppermute | solution.py:558
  60.6 134.8 %all-gather.13.cloned.1.call-start = ((), (), s32[]{:S(2)}) async-start(), calls=%async_computation.10 | async-start | bytes 3276800 | tf_op jit(solution)/shard_map/all_gather | solution.py:620
  60.6 42.1 %collective-permute-start.3 = (bf16[48,64,128]{2,1,0:T(8,128)(2,1)S(1)}, bf16[48,64,128]{2,1,0:T(8,128)(2,1)}, u32[]{:S(2)}, u32[]{:S(2)}) collective-permute-start(bf16[48,64,128]{2,1,0:T(8,128)(2,1)S(1)} %get-tuple-element.176), channel_id=1, source_target_pairs={{0,2},{2,4},{4,6},{6,0},{8,10},{10,12},{12,14},{14,8},{16,18},{18,... | collective-permute-start | bytes 2359304 | tf_op jit(solution)/shard_map/ppermute | solution.py:558
  62.2 40.5 %collective-permute-start.5 = (bf16[48,64,128]{2,1,0:T(8,128)(2,1)S(1)}, bf16[48,64,128]{2,1,0:T(8,128)(2,1)}, u32[]{:S(2)}, u32[]{:S(2)}) collective-permute-start(bf16[48,64,128]{2,1,0:T(8,128)(2,1)S(1)} %get-tuple-element.178), channel_id=1, source_target_pairs={{0,6},{2,0},{4,2},{6,4},{8,14},{10,8},{12,10},{14,12},{16,22},{18,... | collective-permute-start | bytes 2359304 | tf_op jit(solution)/shard_map/ppermute | solution.py:558
  63.6 39.1 %collective-permute-start.4 = (bf16[40,64,128]{2,1,0:T(8,128)(2,1)S(1)}, bf16[40,64,128]{2,1,0:T(8,128)(2,1)}, u32[]{:S(2)}, u32[]{:S(2)}) collective-permute-start(bf16[40,64,128]{2,1,0:T(8,128)(2,1)S(1)} %get-tuple-element.177), channel_id=1, source_target_pairs={{0,4},{2,6},{4,0},{6,2},{8,12},{10,14},{12,8},{14,10},{16,20},{18,... | collective-permute-start | bytes 1966088 | tf_op jit(solution)/shard_map/ppermute | solution.py:558
  107.4 186.3 %reduce-scatter.5.cloned.1.call-start = ((), (), s32[]{:S(2)}) async-start(), calls=%async_computation.4 | async-start | bytes 2785280 | tf_op jit(solution)/shard_map/reduce_scatter | solution.py:648
  107.5 34.3 %collective-permute-start.6 = (bf16[48,64,128]{2,1,0:T(8,128)(2,1)S(1)}, bf16[48,64,128]{2,1,0:T(8,128)(2,1)S(1)}, u32[]{:S(2)}, u32[]{:S(2)}) collective-permute-start(bf16[48,64,128]{2,1,0:T(8,128)(2,1)S(1)} %get-tuple-element.189), channel_id=1, source_target_pairs={{0,2},{2,4},{4,6},{6,0},{8,10},{10,12},{12,14},{14,8},{16,18},{18,... | collective-permute-start | bytes 2359304 | tf_op jit(solution)/shard_map/ppermute | solution.py:558
  109.0 35.7 %collective-permute-start.8 = (bf16[48,64,128]{2,1,0:T(8,128)(2,1)S(1)}, bf16[48,64,128]{2,1,0:T(8,128)(2,1)}, u32[]{:S(2)}, u32[]{:S(2)}) collective-permute-start(bf16[48,64,128]{2,1,0:T(8,128)(2,1)S(1)} %get-tuple-element.191), channel_id=1, source_target_pairs={{0,6},{2,0},{4,2},{6,4},{8,14},{10,8},{12,10},{14,12},{16,22},{18,... | collective-permute-start | bytes 2359304 | tf_op jit(solution)/shard_map/ppermute | solution.py:558
  110.5 31.2 %collective-permute-start.7 = (bf16[40,64,128]{2,1,0:T(8,128)(2,1)S(1)}, bf16[40,64,128]{2,1,0:T(8,128)(2,1)S(1)}, u32[]{:S(2)}, u32[]{:S(2)}) collective-permute-start(bf16[40,64,128]{2,1,0:T(8,128)(2,1)S(1)} %get-tuple-element.190), channel_id=1, source_target_pairs={{0,4},{2,6},{4,0},{6,2},{8,12},{10,14},{12,8},{14,10},{16,20},{18,... | collective-permute-start | bytes 1966088 | tf_op jit(solution)/shard_map/ppermute | solution.py:558
  149.1 27.8 %collective-permute-start.10 = (bf16[40,48,128]{2,1,0:T(8,128)(2,1)S(1)}, bf16[40,48,128]{2,1,0:T(8,128)(2,1)S(1)}, u32[]{:S(2)}, u32[]{:S(2)}) collective-permute-start(bf16[40,48,128]{2,1,0:T(8,128)(2,1)S(1)} %get-tuple-element.227), channel_id=1, source_target_pairs={{0,4},{2,6},{4,0},{6,2},{8,12},{10,14},{12,8},{14,10},{16,20},{18,... | collective-permute-start | bytes 1474568 | tf_op jit(solution)/shard_map/ppermute | solution.py:558
  149.7 28.1 %collective-permute-start.9 = (bf16[48,48,128]{2,1,0:T(8,128)(2,1)S(1)}, bf16[48,48,128]{2,1,0:T(8,128)(2,1)S(1)}, u32[]{:S(2)}, u32[]{:S(2)}) collective-permute-start(bf16[48,48,128]{2,1,0:T(8,128)(2,1)S(1)} %get-tuple-element.226), channel_id=1, source_target_pairs={{0,2},{2,4},{4,6},{6,0},{8,10},{10,12},{12,14},{14,8},{16,18},{18,... | collective-permute-start | bytes 1769480 | tf_op jit(solution)/shard_map/ppermute | solution.py:558
  151.1 27.5 %collective-permute-start.11 = (bf16[48,48,128]{2,1,0:T(8,128)(2,1)S(1)}, bf16[48,48,128]{2,1,0:T(8,128)(2,1)S(1)}, u32[]{:S(2)}, u32[]{:S(2)}) collective-permute-start(bf16[48,48,128]{2,1,0:T(8,128)(2,1)S(1)} %get-tuple-element.228), channel_id=1, source_target_pairs={{0,6},{2,0},{4,2},{6,4},{8,14},{10,8},{12,10},{14,12},{16,22},{18,... | collective-permute-start | bytes 1769480 | tf_op jit(solution)/shard_map/ppermute | solution.py:558
  179.4 20.5 %collective-permute-start.12 = (bf16[40,64,128]{2,1,0:T(8,128)(2,1)}, bf16[40,64,128]{2,1,0:T(8,128)(2,1)}, u32[]{:S(2)}, u32[]{:S(2)}) collective-permute-start(bf16[40,64,128]{2,1,0:T(8,128)(2,1)} %get-tuple-element.233), channel_id=1, source_target_pairs={{0,6},{2,0},{4,2},{6,4},{8,14},{10,8},{12,10},{14,12},{16,22},{18,... | collective-permute-start | bytes 1966088 | tf_op jit(solution)/shard_map/ppermute | solution.py:558
  180.9 28.6 %collective-permute-start.14 = (bf16[40,64,128]{2,1,0:T(8,128)(2,1)}, bf16[40,64,128]{2,1,0:T(8,128)(2,1)}, u32[]{:S(2)}, u32[]{:S(2)}) collective-permute-start(bf16[40,64,128]{2,1,0:T(8,128)(2,1)} %get-tuple-element.235), channel_id=1, source_target_pairs={{0,2},{2,4},{4,6},{6,0},{8,10},{10,12},{12,14},{14,8},{16,18},{18,... | collective-permute-start | bytes 1966088 | tf_op jit(solution)/shard_map/ppermute | solution.py:558
  181.5 18.5 %collective-permute-start.13 = (bf16[32,64,128]{2,1,0:T(8,128)(2,1)S(1)}, bf16[32,64,128]{2,1,0:T(8,128)(2,1)}, u32[]{:S(2)}, u32[]{:S(2)}) collective-permute-start(bf16[32,64,128]{2,1,0:T(8,128)(2,1)S(1)} %get-tuple-element.234), channel_id=1, source_target_pairs={{0,4},{2,6},{4,0},{6,2},{8,12},{10,14},{12,8},{14,10},{16,20},{18,... | collective-permute-start | bytes 1572872 | tf_op jit(solution)/shard_map/ppermute | solution.py:558
  216.3 120.2 %reduce-scatter.7.cloned.1.call-start = ((), (), s32[]{:S(2)}) async-start(), calls=%async_computation.5 | async-start | bytes 2621440 | tf_op jit(solution)/shard_map/reduce_scatter | solution.py:648
  216.3 42.5 %collective-permute-start.19 = (bf16[48,80,128]{2,1,0:T(8,128)(2,1)S(1)}, bf16[48,80,128]{2,1,0:T(8,128)(2,1)S(1)}, u32[]{:S(2)}, u32[]{:S(2)}) collective-permute-start(bf16[48,80,128]{2,1,0:T(8,128)(2,1)S(1)} %get-tuple-element.258), channel_id=1, source_target_pairs={{0,2},{2,4},{4,6},{6,0},{8,10},{10,12},{12,14},{14,8},{16,18},{18,... | collective-permute-start | bytes 2949128 | tf_op jit(solution)/shard_map/ppermute | solution.py:558
  217.0 41.9 %collective-permute-start.20 = (bf16[48,80,128]{2,1,0:T(8,128)(2,1)S(1)}, bf16[48,80,128]{2,1,0:T(8,128)(2,1)S(1)}, u32[]{:S(2)}, u32[]{:S(2)}) collective-permute-start(bf16[48,80,128]{2,1,0:T(8,128)(2,1)S(1)} %get-tuple-element.262), channel_id=1, source_target_pairs={{0,6},{2,0},{4,2},{6,4},{8,14},{10,8},{12,10},{14,12},{16,22},{18,... | collective-permute-start | bytes 2949128 | tf_op jit(solution)/shard_map/ppermute | solution.py:558
  219.3 36.4 %collective-permute-start.15 = (bf16[40,80,128]{2,1,0:T(8,128)(2,1)S(1)}, bf16[40,80,128]{2,1,0:T(8,128)(2,1)S(1)}, u32[]{:S(2)}, u32[]{:S(2)}) collective-permute-start(bf16[40,80,128]{2,1,0:T(8,128)(2,1)S(1)} %get-tuple-element.250), channel_id=1, source_target_pairs={{0,4},{2,6},{4,0},{6,2},{8,12},{10,14},{12,8},{14,10},{16,20},{18,... | collective-permute-start | bytes 2457608 | tf_op jit(solution)/shard_map/ppermute | solution.py:558
  255.7 33.3 %collective-permute-start.17 = (bf16[24,64,128]{2,1,0:T(8,128)(2,1)}, bf16[24,64,128]{2,1,0:T(8,128)(2,1)S(1)}, u32[]{:S(2)}, u32[]{:S(2)}) collective-permute-start(bf16[24,64,128]{2,1,0:T(8,128)(2,1)} %copy-done.31), channel_id=1, source_target_pairs={{0,4},{2,6},{4,0},{6,2},{8,12},{10,14},{12,8},{14,10},{16,20},{18,... | collective-permute-start | bytes 1179656 | tf_op jit(solution)/shard_map/ppermute | solution.py:558
  256.8 32.2 %collective-permute-start.16 = (bf16[32,64,128]{2,1,0:T(8,128)(2,1)}, bf16[32,64,128]{2,1,0:T(8,128)(2,1)S(1)}, u32[]{:S(2)}, u32[]{:S(2)}) collective-permute-start(bf16[32,64,128]{2,1,0:T(8,128)(2,1)} %copy-done.27), channel_id=1, source_target_pairs={{0,6},{2,0},{4,2},{6,4},{8,14},{10,8},{12,10},{14,12},{16,22},{18,... | collective-permute-start | bytes 1572872 | tf_op jit(solution)/shard_map/ppermute | solution.py:558
  256.8 32.2 %collective-permute-start.18 = (bf16[32,64,128]{2,1,0:T(8,128)(2,1)}, bf16[32,64,128]{2,1,0:T(8,128)(2,1)S(1)}, u32[]{:S(2)}, u32[]{:S(2)}) collective-permute-start(bf16[32,64,128]{2,1,0:T(8,128)(2,1)} %copy-done.26), channel_id=1, source_target_pairs={{0,2},{2,4},{4,6},{6,0},{8,10},{10,12},{12,14},{14,8},{16,18},{18,... | collective-permute-start | bytes 1572872 | tf_op jit(solution)/shard_map/ppermute | solution.py:558
  293.7 88.4 %reduce-scatter.9.cloned.1.call-start = ((), (), s32[]{:S(2)}) async-start(), calls=%async_computation.6 | async-start | bytes 2621440 | tf_op jit(solution)/shard_map/reduce_scatter | solution.py:648
  293.8 27.1 %collective-permute-start.22 = (bf16[40,64,128]{2,1,0:T(8,128)(2,1)}, bf16[40,64,128]{2,1,0:T(8,128)(2,1)S(1)}, u32[]{:S(2)}, u32[]{:S(2)}) collective-permute-start(bf16[40,64,128]{2,1,0:T(8,128)(2,1)} %get-tuple-element.278), channel_id=1, source_target_pairs={{0,4},{2,6},{4,0},{6,2},{8,12},{10,14},{12,8},{14,10},{16,20},{18,... | collective-permute-start | bytes 1966088 | tf_op jit(solution)/shard_map/ppermute | solution.py:558
  294.8 26.2 %collective-permute-start.21 = (bf16[48,64,128]{2,1,0:T(8,128)(2,1)}, bf16[48,64,128]{2,1,0:T(8,128)(2,1)S(1)}, u32[]{:S(2)}, u32[]{:S(2)}) collective-permute-start(bf16[48,64,128]{2,1,0:T(8,128)(2,1)} %get-tuple-element.272), channel_id=1, source_target_pairs={{0,6},{2,0},{4,2},{6,4},{8,14},{10,8},{12,10},{14,12},{16,22},{18,... | collective-permute-start | bytes 2359304 | tf_op jit(solution)/shard_map/ppermute | solution.py:558
  295.7 35.1 %collective-permute-start.23 = (bf16[48,64,128]{2,1,0:T(8,128)(2,1)}, bf16[48,64,128]{2,1,0:T(8,128)(2,1)S(1)}, u32[]{:S(2)}, u32[]{:S(2)}) collective-permute-start(bf16[48,64,128]{2,1,0:T(8,128)(2,1)} %get-tuple-element.281), channel_id=1, source_target_pairs={{0,2},{2,4},{4,6},{6,0},{8,10},{10,12},{12,14},{14,8},{16,18},{18,... | collective-permute-start | bytes 2359304 | tf_op jit(solution)/shard_map/ppermute | solution.py:558
  336.5 91.1 %reduce-scatter.11.cloned.1.call-start = ((), (), s32[]{:S(2)}) async-start(), calls=%async_computation.7 | async-start | bytes 2621440 | tf_op jit(solution)/shard_map/reduce_scatter | solution.py:648
  336.6 20.7 %collective-permute-start.24 = (bf16[48,64,128]{2,1,0:T(8,128)(2,1)}, bf16[48,64,128]{2,1,0:T(8,128)(2,1)S(1)}, u32[]{:S(2)}, u32[]{:S(2)}) collective-permute-start(bf16[48,64,128]{2,1,0:T(8,128)(2,1)} %get-tuple-element.296), channel_id=1, source_target_pairs={{0,6},{2,0},{4,2},{6,4},{8,14},{10,8},{12,10},{14,12},{16,22},{18,... | collective-permute-start | bytes 2359304 | tf_op jit(solution)/shard_map/ppermute | solution.py:558
  339.0 34.9 %collective-permute-start.26 = (bf16[48,64,128]{2,1,0:T(8,128)(2,1)S(1)}, bf16[48,64,128]{2,1,0:T(8,128)(2,1)S(1)}, u32[]{:S(2)}, u32[]{:S(2)}) collective-permute-start(bf16[48,64,128]{2,1,0:T(8,128)(2,1)S(1)} %copy-done.64), channel_id=1, source_target_pairs={{0,2},{2,4},{4,6},{6,0},{8,10},{10,12},{12,14},{14,8},{16,18},{18,... | collective-permute-start | bytes 2359304 | tf_op jit(solution)/shard_map/ppermute | solution.py:558
  339.0 16.3 %collective-permute-start.25 = (bf16[40,64,128]{2,1,0:T(8,128)(2,1)S(1)}, bf16[40,64,128]{2,1,0:T(8,128)(2,1)S(1)}, u32[]{:S(2)}, u32[]{:S(2)}) collective-permute-start(bf16[40,64,128]{2,1,0:T(8,128)(2,1)S(1)} %copy-done.66), channel_id=1, source_target_pairs={{0,4},{2,6},{4,0},{6,2},{8,12},{10,14},{12,8},{14,10},{16,20},{18,... | collective-permute-start | bytes 1966088 | tf_op jit(solution)/shard_map/ppermute | solution.py:558
  382.9 4.8 %collective-permute-start.34 = (bf16[16,1024]{1,0:T(8,128)(2,1)S(1)}, bf16[16,1024]{1,0:T(8,128)(2,1)S(1)}, u32[]{:S(2)}, u32[]{:S(2)}) collective-permute-start(bf16[16,1024]{1,0:T(8,128)(2,1)S(1)} %get-tuple-element.337), channel_id=1, source_target_pairs={{0,16},{2,18},{4,20},{6,22},{8,24},{10,26},{12,28},{14,30},{16,0},... | collective-permute-start | bytes 98312 | tf_op jit(solution)/shard_map/ppermute | solution.py:640
  384.1 4.0 collective-permute-start.33
  384.1 5.4 %collective-permute-start.35 = (bf16[16,1024]{1,0:T(8,128)(2,1)S(1)}, bf16[16,1024]{1,0:T(8,128)(2,1)S(1)}, u32[]{:S(2)}, u32[]{:S(2)}) collective-permute-start(bf16[16,1024]{1,0:T(8,128)(2,1)S(1)} %get-tuple-element.337), channel_id=1, source_target_pairs={{0,24},{2,26},{4,28},{6,30},{8,0},{10,2},{12,4},{14,6},{16,8},{18,... | collective-permute-start | bytes 98312 | tf_op jit(solution)/shard_map/ppermute | solution.py:640
  389.6 6.5 %collective-permute-start.38 = (bf16[4,16,1024]{2,1,0:T(8,128)(2,1)S(1)}, bf16[4,16,1024]{2,1,0:T(8,128)(2,1)S(1)}, u32[]{:S(2)}, u32[]{:S(2)}) collective-permute-start(bf16[4,16,1024]{2,1,0:T(8,128)(2,1)S(1)} %pad_maximum_fusion.1), channel_id=1, source_target_pairs={{0,6},{2,0},{4,2},{6,4},{8,14},{10,8},{12,10},{14,12},{16,22},{18,... | collective-permute-start | bytes 393224 | tf_op jit(solution)/shard_map/ppermute | solution.py:558
  392.0 20.4 %collective-permute-start.30 = (bf16[8,128,128]{2,1,0:T(8,128)(2,1)S(1)}, bf16[8,128,128]{2,1,0:T(8,128)(2,1)S(1)}, u32[]{:S(2)}, u32[]{:S(2)}) collective-permute-start(bf16[8,128,128]{2,1,0:T(8,128)(2,1)S(1)} %copy-done.37), channel_id=1, source_target_pairs={{0,6},{2,0},{4,2},{6,4},{8,14},{10,8},{12,10},{14,12},{16,22},{18,... | collective-permute-start | bytes 786440 | tf_op jit(solution)/shard_map/ppermute | solution.py:558
  392.6 21.0 %collective-permute-start.31 = (bf16[8,128,128]{2,1,0:T(8,128)(2,1)S(1)}, bf16[8,128,128]{2,1,0:T(8,128)(2,1)S(1)}, u32[]{:S(2)}, u32[]{:S(2)}) collective-permute-start(bf16[8,128,128]{2,1,0:T(8,128)(2,1)S(1)} %copy-done.35), channel_id=1, source_target_pairs={{0,4},{2,6},{4,0},{6,2},{8,12},{10,14},{12,8},{14,10},{16,20},{18,... | collective-permute-start | bytes 786440 | tf_op jit(solution)/shard_map/ppermute | solution.py:558
  393.1 20.4 %collective-permute-start.32 = (bf16[8,128,128]{2,1,0:T(8,128)(2,1)S(1)}, bf16[8,128,128]{2,1,0:T(8,128)(2,1)S(1)}, u32[]{:S(2)}, u32[]{:S(2)}) collective-permute-start(bf16[8,128,128]{2,1,0:T(8,128)(2,1)S(1)} %copy-done.33), channel_id=1, source_target_pairs={{0,2},{2,4},{4,6},{6,0},{8,10},{10,12},{12,14},{14,8},{16,18},{18,... | collective-permute-start | bytes 786440 | tf_op jit(solution)/shard_map/ppermute | solution.py:558
  394.6 15.5 %collective-permute-start.37 = (bf16[4,16,1024]{2,1,0:T(8,128)(2,1)S(1)}, bf16[4,16,1024]{2,1,0:T(8,128)(2,1)S(1)}, u32[]{:S(2)}, u32[]{:S(2)}) collective-permute-start(bf16[4,16,1024]{2,1,0:T(8,128)(2,1)S(1)} %pad_maximum_fusion.1), channel_id=1, source_target_pairs={{0,4},{2,6},{4,0},{6,2},{8,12},{10,14},{12,8},{14,10},{16,20},{18,... | collective-permute-start | bytes 393224 | tf_op jit(solution)/shard_map/ppermute | solution.py:558
  396.1 14.9 %collective-permute-start.36 = (bf16[4,16,1024]{2,1,0:T(8,128)(2,1)S(1)}, bf16[4,16,1024]{2,1,0:T(8,128)(2,1)S(1)}, u32[]{:S(2)}, u32[]{:S(2)}) collective-permute-start(bf16[4,16,1024]{2,1,0:T(8,128)(2,1)S(1)} %pad_maximum_fusion.1), channel_id=1, source_target_pairs={{0,2},{2,4},{4,6},{6,0},{8,10},{10,12},{12,14},{14,8},{16,18},{18,... | collective-permute-start | bytes 393224 | tf_op jit(solution)/shard_map/ppermute | solution.py:558
  410.1 10.1 %collective-permute-start.27 = (bf16[8,128,128]{2,1,0:T(8,128)(2,1)S(1)}, bf16[8,128,128]{2,1,0:T(8,128)(2,1)}, u32[]{:S(2)}, u32[]{:S(2)}) collective-permute-start(bf16[8,128,128]{2,1,0:T(8,128)(2,1)S(1)} %get-tuple-element.314), channel_id=1, source_target_pairs={{0,6},{2,0},{4,2},{6,4},{8,14},{10,8},{12,10},{14,12},{16,22},{18,... | collective-permute-start | bytes 786440 | tf_op jit(solution)/shard_map/ppermute | solution.py:558
  411.0 13.8 %collective-permute-start.28 = (bf16[8,128,128]{2,1,0:T(8,128)(2,1)S(1)}, bf16[8,128,128]{2,1,0:T(8,128)(2,1)}, u32[]{:S(2)}, u32[]{:S(2)}) collective-permute-start(bf16[8,128,128]{2,1,0:T(8,128)(2,1)S(1)} %get-tuple-element.315), channel_id=1, source_target_pairs={{0,4},{2,6},{4,0},{6,2},{8,12},{10,14},{12,8},{14,10},{16,20},{18,... | collective-permute-start | bytes 786440 | tf_op jit(solution)/shard_map/ppermute | solution.py:558
  412.4 12.4 %collective-permute-start.29 = (bf16[8,128,128]{2,1,0:T(8,128)(2,1)S(1)}, bf16[8,128,128]{2,1,0:T(8,128)(2,1)S(1)}, u32[]{:S(2)}, u32[]{:S(2)}) collective-permute-start(bf16[8,128,128]{2,1,0:T(8,128)(2,1)S(1)} %get-tuple-element.316), channel_id=1, source_target_pairs={{0,2},{2,4},{4,6},{6,0},{8,10},{10,12},{12,14},{14,8},{16,18},{18,... | collective-permute-start | bytes 786440 | tf_op jit(solution)/shard_map/ppermute | solution.py:558
  (70 other events, 304.1 us)
Sparse Core Ops, SparseCore 0:
  10.2 45.6 all-gather.10
  58.0 44.6 all-gather.8
  104.3 36.0 all-gather.14
  141.8 53.5 all-gather.12
  216.4 44.2 reduce-scatter.4
  293.9 42.6 reduce-scatter.6
  338.9 43.1 reduce-scatter.8
  384.4 43.1 reduce-scatter.10

commit v5 on v4

--- a/solution.py
+++ b/solution.py
@@ -753,7 +753,7 @@
         [smem_spec()] + [head_block] * 2 + [weight_block, head_block] + anywhere,
         [weight_block, head_block] + anywhere,
         term_scratch,
-        20,
+        50,
     )(pick, queries, out_grad, weights, values, *value_rand)
     slopes, key_own = outs[:2]
     returned, key_own = tie(returned, key_own)

time: 444 us -> 436 us (0.982)
  waiting for transfers between devices: 229 us -> 223 us
    ppermute x36, waiting for transfers between devices: 156 us -> 147 us  [rotate(): return lax.ppermute(array, 'seq', moves)]
    unnamed x143 -> x137, local copies, waits for them, and re-layouts: 40.9 us -> 38.5 us
  transfers between devices with their start and end apart: 47 -> 47, of which waited for: 22 -> 22; matrix products, arithmetic and copies ran while one was open for 1% -> 1% of each run, Pallas kernels for 20% -> 21%
where the time goes in v5:
time: 436 us; the launch traced here: 432 us
  waiting for transfers between devices  223 us (51%)
  Pallas kernels  97.8 us (22%)
  starting transfers between devices  50.3 us (12%)
  local copies, waits for them, and re-layouts  44.6 us (10%)
  between operations  14.7 us (3%)
    ppermute x36, waiting for transfers between devices, rotate(): return lax.ppermute(array, 'seq', moves)  147 us
    all_gather x4, waiting for transfers between devices, gather(): column = lax.all_gather(piece, 'seq', axis_index_groups=columns)  62.9 us
    ppermute x36, starting transfers between devices, rotate(): return lax.ppermute(array, 'seq', moves)  46.8 us
    unnamed x137, local copies, waits for them, and re-layouts  38.5 us
    pallas_call x4, Pallas kernels, sum_blocks(): call(kernel, jax.ShapeDtypeStruct((planes * segment, heads * DH), jnp.bfl...  19.7 us
    pallas_call x1, Pallas kernels, body(): per_head(slope_kernel, [weights_like, wide_like] + payloads(False), [smem...  19.5 us
    pallas_call x1, Pallas kernels, body(): per_head(weights_kernel, [weights_like, wide_like] + payloads(True), [sme...  17.7 us
    pallas_call x1, Pallas kernels, body(): per_head(output_kernel, [like, like], [smem_spec()] + [weight_block] * 2...  17.7 us
  transfers between devices with their start and end apart: 47, of which 22 were waited for; matrix products, arithmetic and copies ran while one was open for 1% of the time, Pallas kernels for 21%

profile of v5, /device:TPU:16, one launch (start us, length us, event | category | flops | bytes accessed | tf_op | source)
XLA Modules:
  0.0 432.4 jit_solution(876324941177114408)
XLA Ops:
  7.3 2.4 fusion.23
  11.6 2.5 shard_map.93
  16.4 1.5 collective-permute-start.1
  20.4 10.4 %collective-permute-done.rest_3_.rest_15_ = bf16[2,8,128,128]{3,2,1,0:T(8,128)(2,1)S(1)} collective-permute-done((bf16[2,8,128,128]{3,2,1,0:T(8,128)(2,1)}, bf16[2,8,128,128]{3,2,1,0:T(8,128)(2,1)S(1)}, u32[]{:S(2)}, u32[]{:S(2)}) %collective-permute-start) | collective-permute-done | bytes 524320 | tf_op jit(solution)/shard_map/ppermute | solution.py:558
  31.7 9.2 %collective-permute-done.1.rest_6_.rest_18_ = bf16[2,8,128,128]{3,2,1,0:T(8,128)(2,1)S(1)} collective-permute-done((bf16[2,8,128,128]{3,2,1,0:T(8,128)(2,1)}, bf16[2,8,128,128]{3,2,1,0:T(8,128)(2,1)S(1)}, u32[]{:S(2)}, u32[]{:S(2)}) %collective-permute-start.1) | collective-permute-done | bytes 524320 | tf_op jit(solution)/shard_map/ppermute | solution.py:558
  42.5 13.4 %all-gather.11.cloned.1.call-done.column_ref = bf16[16,64,1024]{2,1,0:T(8,128)(2,1)} async-done(((bf16[4,64,1024]{2,1,0:T(8,128)(2,1)}), bf16[16,64,1024]{2,1,0:T(8,128)(2,1)}) %all-gather.11.cloned.1.call-update) | async-done | bytes 2097168 | tf_op jit(solution)/shard_map/all_gather | solution.py:620
  55.9 1.6 copy-done.5
  57.5 2.3 shard_map.94
  60.6 1.5 collective-permute-start.3
  66.0 36.7 %all-gather.9.cloned.1.call-done.column_ref = bf16[16,64,1024]{2,1,0:T(8,128)(2,1)} async-done(((bf16[4,64,1024]{2,1,0:T(8,128)(2,1)}), bf16[16,64,1024]{2,1,0:T(8,128)(2,1)}) %all-gather.9.cloned.1.call-update) | async-done | bytes 2097168 | tf_op jit(solution)/shard_map/all_gather | solution.py:620
  102.7 1.6 copy-done.6
  104.3 2.3 shard_map.95
  107.5 1.5 collective-permute-start.6
  110.5 1.5 collective-permute-start.7
  112.2 29.5 %collective-permute-done.7.rest_8_ = bf16[40,64,128]{2,1,0:T(8,128)(2,1)S(1)} collective-permute-done((bf16[40,64,128]{2,1,0:T(8,128)(2,1)S(1)}, bf16[40,64,128]{2,1,0:T(8,128)(2,1)S(1)}, u32[]{:S(2)}, u32[]{:S(2)}) %collective-permute-start.7) | collective-permute-done | bytes 655392 | tf_op jit(solution)/shard_map/ppermute | solution.py:558
  142.6 2.1 collective-permute-done.8.rest_11_
  146.2 2.2 shard_map.96
  151.1 1.5 collective-permute-start.11
  152.6 17.7 %shard_map.97 = (bf16[8,4,1024,128]{3,2,1,0:T(8,128)(2,1)}, f32[512,1024]{1,0:T(8,128)}, bf16[8,128,128]{2,1,0:T(8,128)(2,1)S(1)}, bf16[32,64,128]{2,1,0:T(8,128...) custom-call(s32[198]{0:T(256)S(1)} %pad_add_fusion.pick, ...), custom_call_target="tpu_custom_call" | custom-call | flops 24000000000 | bytes 84000000 | tf_op jit(solution)/shard_map/pallas_call | solution.py:728
  181.6 1.5 collective-permute-start.14
  183.1 12.8 %all-gather.13.cloned.1.call-done.column_ref = bf16[16,80,1024]{2,1,0:T(8,128)(2,1)} async-done(((bf16[4,80,1024]{2,1,0:T(8,128)(2,1)}), bf16[16,80,1024]{2,1,0:T(8,128)(2,1)}) %all-gather.13.cloned.1.call-update) | async-done | bytes 2621456 | tf_op jit(solution)/shard_map/all_gather | solution.py:620
  196.0 3.7 shard_map.98
  204.9 8.3 %collective-permute-done.14.rest_3_ = bf16[40,64,128]{2,1,0:T(8,128)(2,1)} collective-permute-done((bf16[40,64,128]{2,1,0:T(8,128)(2,1)}, bf16[40,64,128]{2,1,0:T(8,128)(2,1)}, u32[]{:S(2)}, u32[]{:S(2)}) %collective-permute-start.14) | collective-permute-done | bytes 655392 | tf_op jit(solution)/shard_map/ppermute | solution.py:558
  214.3 5.7 %shard_map.99 = bf16[1088,1024]{1,0:T(8,128)(2,1)} custom-call(s32[128]{0:T(128)S(1)} %reshape.301.table_ref, s32[8]{0:T(128)S(1)} %concatenate.13.info_ref, bf16[32,64,128]{2,1,0:T(8,128)(2,1)S(1)} %copy-done.54, bf16[40,64,128]{2,1,0:T(8,128)(2,1)} %collective-permute-done.12.rest_1_, bf16[32,64,128]{2,1,0:T(8,128)(2,1)} %collective-permute-done.13.rest_2_, ...), custom_call_target="tpu_custom_call" | custom-call | flops 6000000000 | bytes 21000000 | tf_op jit(solution)/shard_map/pallas_call | solution.py:221
  220.0 28.9 %collective-permute-done.15.rest_8_.rest_20_ = bf16[40,80,128]{2,1,0:T(8,128)(2,1)} collective-permute-done((bf16[40,80,128]{2,1,0:T(8,128)(2,1)S(1)}, bf16[40,80,128]{2,1,0:T(8,128)(2,1)}, u32[]{:S(2)}, u32[]{:S(2)}) %collective-permute-start.15) | collective-permute-done | bytes 819232 | tf_op jit(solution)/shard_map/ppermute | solution.py:558
  250.0 2.0 collective-permute-start.18
  259.5 19.5 %shard_map.100 = (bf16[8,4,1024,128]{3,2,1,0:T(8,128)(2,1)}, f32[512,1024]{1,0:T(8,128)}, bf16[8,128,128]{2,1,0:T(8,128)(2,1)S(1)}, bf16[40,64,128]{2,1,0:T(8,12...) custom-call(s32[198]{0:T(256)S(1)} %pad_add_fusion.pick, ...), custom_call_target="tpu_custom_call" | custom-call | flops 49999998976 | bytes 175000000 | tf_op jit(solution)/shard_map/pallas_call | solution.py:750
  280.5 4.7 %shard_map.101 = bf16[1024,1024]{1,0:T(8,128)(2,1)} custom-call(s32[128]{0:T(128)S(1)} %reshape.301.table_ref, s32[8]{0:T(128)S(1)} %concatenate.13.info_ref, bf16[24,64,128]{2,1,0:T(8,128)(2,1)S(1)} %copy-done.58, bf16[32,64,128]{2,1,0:T(8,128)(2,1)S(1)} %collective-permute-done.16.rest_1_, bf16[24,64,128]{2,1,0:T(8,128)(2,1)S(1)} %collective-permute-done.17.rest_2_, ...), custom_call_target="tpu_custom_call" | custom-call | flops 6000000000 | bytes 21000000 | tf_op jit(solution)/shard_map/pallas_call | solution.py:221
  286.1 2.9 collective-permute-start.21
  295.4 17.7 %shard_map.102 = (bf16[512,1024]{1,0:T(8,128)(2,1)}, bf16[512,1024]{1,0:T(8,128)(2,1)}) custom-call(s32[198]{0:T(256)S(1)} %pad_add_fusion.pick, bf16[8,4,1024,128]{3,2,1,0:T(8,128)(2,1)} %get-tuple-element.241.p_ref, bf16[8,4,1024,128]{3,2,1,0:T(8,128)(2,1)} %get-tuple-element.269.ds_ref, bf16[512,1024]{1,0:T(8,128)(2,1)} %k_ref.3, ...), custom_call_target="tpu_custom_call" | custom-call | flops 15000000512 | bytes 52500000 | tf_op jit(solution)/shard_map/pallas_call | solution.py:766
  313.1 9.0 %collective-permute-done.23.rest_3_ = bf16[48,64,128]{2,1,0:T(8,128)(2,1)S(1)} collective-permute-done((bf16[48,64,128]{2,1,0:T(8,128)(2,1)}, bf16[48,64,128]{2,1,0:T(8,128)(2,1)S(1)}, u32[]{:S(2)}, u32[]{:S(2)}) %collective-permute-start.23) | collective-permute-done | bytes 786464 | tf_op jit(solution)/shard_map/ppermute | solution.py:558
  322.1 4.7 %shard_map.104 = bf16[1024,1024]{1,0:T(8,128)(2,1)} custom-call(s32[128]{0:T(128)S(1)} %reshape.301.table_ref, s32[8]{0:T(128)S(1)} %concatenate.13.info_ref, bf16[40,64,128]{2,1,0:T(8,128)(2,1)S(1)} %copy-done.52, bf16[48,64,128]{2,1,0:T(8,128)(2,1)S(1)} %collective-permute-done.21.rest_1_, bf16[40,64,128]{2,1,0:T(8,128)(2,1)S(1)} %collective-permute-done.22.rest_2_, ...), custom_call_target="tpu_custom_call" | custom-call | flops 6000000000 | bytes 21000000 | tf_op jit(solution)/shard_map/pallas_call | solution.py:221
  326.7 2.5 reduce-scatter.7.cloned.1.call-done.rest_2_
  329.3 2.5 collective-permute-start.24
  332.9 15.3 %collective-permute-done.25.rest_2_ = bf16[40,64,128]{2,1,0:T(8,128)(2,1)S(1)} collective-permute-done((bf16[40,64,128]{2,1,0:T(8,128)(2,1)}, bf16[40,64,128]{2,1,0:T(8,128)(2,1)S(1)}, u32[]{:S(2)}, u32[]{:S(2)}) %collective-permute-start.25) | collective-permute-done | bytes 655392 | tf_op jit(solution)/shard_map/ppermute | solution.py:558
  348.2 1.6 collective-permute-done.24.rest_1_
  349.8 16.7 %collective-permute-done.26.rest_3_ = bf16[48,64,128]{2,1,0:T(8,128)(2,1)S(1)} collective-permute-done((bf16[48,64,128]{2,1,0:T(8,128)(2,1)S(1)}, bf16[48,64,128]{2,1,0:T(8,128)(2,1)S(1)}, u32[]{:S(2)}, u32[]{:S(2)}) %collective-permute-start.26) | collective-permute-done | bytes 786464 | tf_op jit(solution)/shard_map/ppermute | solution.py:558
  366.5 4.6 %shard_map.103 = bf16[1024,1024]{1,0:T(8,128)(2,1)} custom-call(s32[128]{0:T(128)S(1)} %reshape.301.table_ref, s32[8]{0:T(128)S(1)} %concatenate.13.info_ref, bf16[40,64,128]{2,1,0:T(8,128)(2,1)S(1)} %copy-done.50, bf16[48,64,128]{2,1,0:T(8,128)(2,1)S(1)} %collective-permute-done.24.rest_1_, bf16[40,64,128]{2,1,0:T(8,128)(2,1)S(1)} %collective-permute-done.25.rest_2_, ...), custom_call_target="tpu_custom_call" | custom-call | flops 6000000000 | bytes 21000000 | tf_op jit(solution)/shard_map/pallas_call | solution.py:221
  371.1 3.7 reduce-scatter.9.cloned.1.call-done.rest_1_
  376.8 2.0 collective-permute-start.35
  378.9 1.6 collective-permute-done.34
  382.3 2.4 collective-permute-start.38
  388.8 2.5 collective-permute-start.36
  391.8 11.0 %collective-permute-done.37 = bf16[4,16,1024]{2,1,0:T(8,128)(2,1)S(1)} collective-permute-done((bf16[4,16,1024]{2,1,0:T(8,128)(2,1)S(1)}, bf16[4,16,1024]{2,1,0:T(8,128)(2,1)S(1)}, u32[]{:S(2)}, u32[]{:S(2)}) %collective-permute-start.37) | collective-permute-done | bytes 131104 | tf_op jit(solution)/shard_map/ppermute | solution.py:558
  407.1 5.2 %shard_map.106 = bf16[4,128,1024]{2,1,0:T(8,128)(2,1)} custom-call(s32[128]{0:T(128)} %copy-done.4, s32[4]{0:T(128)} %pad_add_fusion.2.info_ref, f32[4,128,1024]{2,1,0:T(8,128)} %bitcast.49, bf16[272,1024]{1,0:T(8,128)(2,1)} %reduce-scatter.5.cloned.1.call-done.rest_1_, bf16[256,1024]{1,0:T(8,128)(2,1)} %reduce-scatter.7.cloned.1.call-done.rest_2_, ...), custom_call_target="tpu_custom_call" | custom-call | flops 5000000000 | bytes 17500000 | tf_op jit(solution)/shard_map/pallas_call | solution.py:291
  412.3 5.2 %collective-permute-done.28.rest_5_ = bf16[8,128,128]{2,1,0:T(8,128)(2,1)} collective-permute-done((bf16[8,128,128]{2,1,0:T(8,128)(2,1)S(1)}, bf16[8,128,128]{2,1,0:T(8,128)(2,1)}, u32[]{:S(2)}, u32[]{:S(2)}) %collective-permute-start.28) | collective-permute-done | bytes 262176 | tf_op jit(solution)/shard_map/ppermute | solution.py:558
  417.5 2.9 reduce-scatter.11.cloned.1.call-done.rest_2_
  420.4 5.2 %shard_map.105 = bf16[4,128,1024]{2,1,0:T(8,128)(2,1)} custom-call(s32[128]{0:T(128)} %copy-done.4, s32[4]{0:T(128)} %pad_add_fusion.2.info_ref, f32[4,128,1024]{2,1,0:T(8,128)} %bitcast.50, bf16[256,1024]{1,0:T(8,128)(2,1)} %reduce-scatter.9.cloned.1.call-done.rest_1_, bf16[256,1024]{1,0:T(8,128)(2,1)} %reduce-scatter.11.cloned.1.call-done.rest_2_, ...), custom_call_target="tpu_custom_call" | custom-call | flops 5000000000 | bytes 17500000 | tf_op jit(solution)/shard_map/pallas_call | solution.py:291
  (240 shorter events, 70.2 us)
Async XLA Ops:
  7.2 48.7 %all-gather.11.cloned.1.call-start = ((), (), s32[]{:S(2)}) async-start(), calls=%async_computation.9 | async-start | bytes 2621440 | tf_op jit(solution)/shard_map/all_gather | solution.py:620
  9.7 93.0 %all-gather.9.cloned.1.call-start = ((), (), s32[]{:S(2)}) async-start(), calls=%async_computation.8 | async-start | bytes 2621440 | tf_op jit(solution)/shard_map/all_gather | solution.py:620
  11.4 355.0 %copy-start.4 = (s32[128]{0:T(128)}, s32[128]{0:T(128)S(1)}, u32[]{:S(2)}) copy-start(s32[128]{0:T(128)S(1)} %reshape.301.table_ref) | copy-start | bytes 1540
  11.5 133.3 %all-gather.15.cloned.1.call-start = ((), (), s32[]{:S(2)}) async-start(), calls=%async_computation.11 | async-start | bytes 1966080 | tf_op jit(solution)/shard_map/all_gather | solution.py:620
  14.9 16.0 %collective-permute-start = (bf16[2,8,128,128]{3,2,1,0:T(8,128)(2,1)}, bf16[2,8,128,128]{3,2,1,0:T(8,128)(2,1)S(1)}, u32[]{:S(2)}, u32[]{:S(2)}) collective-permute-start(bf16[2,8,128,128]{3,2,1,0:T(8,128)(2,1)} %get-tuple-element.167), channel_id=1, source_target_pairs={{0,2},{2,4},{4,6},{6,0},{8,10},{10,12},{12,14},{14,8},{16,18},{18,... | collective-permute-start | bytes 1572872 | tf_op jit(solution)/shard_map/ppermute | solution.py:558
  16.4 24.5 %collective-permute-start.1 = (bf16[2,8,128,128]{3,2,1,0:T(8,128)(2,1)}, bf16[2,8,128,128]{3,2,1,0:T(8,128)(2,1)S(1)}, u32[]{:S(2)}, u32[]{:S(2)}) collective-permute-start(bf16[2,8,128,128]{3,2,1,0:T(8,128)(2,1)} %get-tuple-element.168), channel_id=1, source_target_pairs={{0,4},{2,6},{4,0},{6,2},{8,12},{10,14},{12,8},{14,10},{16,20},{18,... | collective-permute-start | bytes 1572872 | tf_op jit(solution)/shard_map/ppermute | solution.py:558
  17.9 23.8 %collective-permute-start.2 = (bf16[2,8,128,128]{3,2,1,0:T(8,128)(2,1)S(1)}, bf16[2,8,128,128]{3,2,1,0:T(8,128)(2,1)S(1)}, u32[]{:S(2)}, u32[]{:S(2)}) collective-permute-start(bf16[2,8,128,128]{3,2,1,0:T(8,128)(2,1)S(1)} %get-tuple-element.169), channel_id=1, source_target_pairs={{0,6},{2,0},{4,2},{6,4},{8,14},{10,8},{12,10},{14,12},{16,22},{18,... | collective-permute-start | bytes 1572872 | tf_op jit(solution)/shard_map/ppermute | solution.py:558
  60.6 135.4 %all-gather.13.cloned.1.call-start = ((), (), s32[]{:S(2)}) async-start(), calls=%async_computation.10 | async-start | bytes 3276800 | tf_op jit(solution)/shard_map/all_gather | solution.py:620
  60.6 42.1 %collective-permute-start.3 = (bf16[48,64,128]{2,1,0:T(8,128)(2,1)S(1)}, bf16[48,64,128]{2,1,0:T(8,128)(2,1)}, u32[]{:S(2)}, u32[]{:S(2)}) collective-permute-start(bf16[48,64,128]{2,1,0:T(8,128)(2,1)S(1)} %get-tuple-element.176), channel_id=1, source_target_pairs={{0,2},{2,4},{4,6},{6,0},{8,10},{10,12},{12,14},{14,8},{16,18},{18,... | collective-permute-start | bytes 2359304 | tf_op jit(solution)/shard_map/ppermute | solution.py:558
  62.2 40.5 %collective-permute-start.5 = (bf16[48,64,128]{2,1,0:T(8,128)(2,1)S(1)}, bf16[48,64,128]{2,1,0:T(8,128)(2,1)}, u32[]{:S(2)}, u32[]{:S(2)}) collective-permute-start(bf16[48,64,128]{2,1,0:T(8,128)(2,1)S(1)} %get-tuple-element.178), channel_id=1, source_target_pairs={{0,6},{2,0},{4,2},{6,4},{8,14},{10,8},{12,10},{14,12},{16,22},{18,... | collective-permute-start | bytes 2359304 | tf_op jit(solution)/shard_map/ppermute | solution.py:558
  63.6 39.1 %collective-permute-start.4 = (bf16[40,64,128]{2,1,0:T(8,128)(2,1)S(1)}, bf16[40,64,128]{2,1,0:T(8,128)(2,1)}, u32[]{:S(2)}, u32[]{:S(2)}) collective-permute-start(bf16[40,64,128]{2,1,0:T(8,128)(2,1)S(1)} %get-tuple-element.177), channel_id=1, source_target_pairs={{0,4},{2,6},{4,0},{6,2},{8,12},{10,14},{12,8},{14,10},{16,20},{18,... | collective-permute-start | bytes 1966088 | tf_op jit(solution)/shard_map/ppermute | solution.py:558
  107.4 177.8 %reduce-scatter.5.cloned.1.call-start = ((), (), s32[]{:S(2)}) async-start(), calls=%async_computation.4 | async-start | bytes 2785280 | tf_op jit(solution)/shard_map/reduce_scatter | solution.py:648
  107.5 34.3 %collective-permute-start.6 = (bf16[48,64,128]{2,1,0:T(8,128)(2,1)S(1)}, bf16[48,64,128]{2,1,0:T(8,128)(2,1)S(1)}, u32[]{:S(2)}, u32[]{:S(2)}) collective-permute-start(bf16[48,64,128]{2,1,0:T(8,128)(2,1)S(1)} %get-tuple-element.189), channel_id=1, source_target_pairs={{0,2},{2,4},{4,6},{6,0},{8,10},{10,12},{12,14},{14,8},{16,18},{18,... | collective-permute-start | bytes 2359304 | tf_op jit(solution)/shard_map/ppermute | solution.py:558
  109.0 35.7 %collective-permute-start.8 = (bf16[48,64,128]{2,1,0:T(8,128)(2,1)S(1)}, bf16[48,64,128]{2,1,0:T(8,128)(2,1)}, u32[]{:S(2)}, u32[]{:S(2)}) collective-permute-start(bf16[48,64,128]{2,1,0:T(8,128)(2,1)S(1)} %get-tuple-element.191), channel_id=1, source_target_pairs={{0,6},{2,0},{4,2},{6,4},{8,14},{10,8},{12,10},{14,12},{16,22},{18,... | collective-permute-start | bytes 2359304 | tf_op jit(solution)/shard_map/ppermute | solution.py:558
  110.5 31.2 %collective-permute-start.7 = (bf16[40,64,128]{2,1,0:T(8,128)(2,1)S(1)}, bf16[40,64,128]{2,1,0:T(8,128)(2,1)S(1)}, u32[]{:S(2)}, u32[]{:S(2)}) collective-permute-start(bf16[40,64,128]{2,1,0:T(8,128)(2,1)S(1)} %get-tuple-element.190), channel_id=1, source_target_pairs={{0,4},{2,6},{4,0},{6,2},{8,12},{10,14},{12,8},{14,10},{16,20},{18,... | collective-permute-start | bytes 1966088 | tf_op jit(solution)/shard_map/ppermute | solution.py:558
  149.1 28.0 %collective-permute-start.10 = (bf16[40,48,128]{2,1,0:T(8,128)(2,1)S(1)}, bf16[40,48,128]{2,1,0:T(8,128)(2,1)S(1)}, u32[]{:S(2)}, u32[]{:S(2)}) collective-permute-start(bf16[40,48,128]{2,1,0:T(8,128)(2,1)S(1)} %get-tuple-element.227), channel_id=1, source_target_pairs={{0,4},{2,6},{4,0},{6,2},{8,12},{10,14},{12,8},{14,10},{16,20},{18,... | collective-permute-start | bytes 1474568 | tf_op jit(solution)/shard_map/ppermute | solution.py:558
  149.7 28.2 %collective-permute-start.9 = (bf16[48,48,128]{2,1,0:T(8,128)(2,1)S(1)}, bf16[48,48,128]{2,1,0:T(8,128)(2,1)S(1)}, u32[]{:S(2)}, u32[]{:S(2)}) collective-permute-start(bf16[48,48,128]{2,1,0:T(8,128)(2,1)S(1)} %get-tuple-element.226), channel_id=1, source_target_pairs={{0,2},{2,4},{4,6},{6,0},{8,10},{10,12},{12,14},{14,8},{16,18},{18,... | collective-permute-start | bytes 1769480 | tf_op jit(solution)/shard_map/ppermute | solution.py:558
  151.1 27.7 %collective-permute-start.11 = (bf16[48,48,128]{2,1,0:T(8,128)(2,1)S(1)}, bf16[48,48,128]{2,1,0:T(8,128)(2,1)S(1)}, u32[]{:S(2)}, u32[]{:S(2)}) collective-permute-start(bf16[48,48,128]{2,1,0:T(8,128)(2,1)S(1)} %get-tuple-element.228), channel_id=1, source_target_pairs={{0,6},{2,0},{4,2},{6,4},{8,14},{10,8},{12,10},{14,12},{16,22},{18,... | collective-permute-start | bytes 1769480 | tf_op jit(solution)/shard_map/ppermute | solution.py:558
  179.6 23.8 %collective-permute-start.13 = (bf16[32,64,128]{2,1,0:T(8,128)(2,1)S(1)}, bf16[32,64,128]{2,1,0:T(8,128)(2,1)}, u32[]{:S(2)}, u32[]{:S(2)}) collective-permute-start(bf16[32,64,128]{2,1,0:T(8,128)(2,1)S(1)} %get-tuple-element.234), channel_id=1, source_target_pairs={{0,4},{2,6},{4,0},{6,2},{8,12},{10,14},{12,8},{14,10},{16,20},{18,... | collective-permute-start | bytes 1572872 | tf_op jit(solution)/shard_map/ppermute | solution.py:558
  181.1 23.8 %collective-permute-start.12 = (bf16[40,64,128]{2,1,0:T(8,128)(2,1)}, bf16[40,64,128]{2,1,0:T(8,128)(2,1)}, u32[]{:S(2)}, u32[]{:S(2)}) collective-permute-start(bf16[40,64,128]{2,1,0:T(8,128)(2,1)} %get-tuple-element.233), channel_id=1, source_target_pairs={{0,6},{2,0},{4,2},{6,4},{8,14},{10,8},{12,10},{14,12},{16,22},{18,... | collective-permute-start | bytes 1966088 | tf_op jit(solution)/shard_map/ppermute | solution.py:558
  181.6 31.6 %collective-permute-start.14 = (bf16[40,64,128]{2,1,0:T(8,128)(2,1)}, bf16[40,64,128]{2,1,0:T(8,128)(2,1)}, u32[]{:S(2)}, u32[]{:S(2)}) collective-permute-start(bf16[40,64,128]{2,1,0:T(8,128)(2,1)} %get-tuple-element.235), channel_id=1, source_target_pairs={{0,2},{2,4},{4,6},{6,0},{8,10},{10,12},{12,14},{14,8},{16,18},{18,... | collective-permute-start | bytes 1966088 | tf_op jit(solution)/shard_map/ppermute | solution.py:558
  200.5 51.5 %collective-permute-start.19 = (bf16[48,80,128]{2,1,0:T(8,128)(2,1)S(1)}, bf16[48,80,128]{2,1,0:T(8,128)(2,1)}, u32[]{:S(2)}, u32[]{:S(2)}) collective-permute-start(bf16[48,80,128]{2,1,0:T(8,128)(2,1)S(1)} %get-tuple-element.258), channel_id=1, source_target_pairs={{0,2},{2,4},{4,6},{6,0},{8,10},{10,12},{12,14},{14,8},{16,18},{18,... | collective-permute-start | bytes 2949128 | tf_op jit(solution)/shard_map/ppermute | solution.py:558
  202.0 50.1 %collective-permute-start.20 = (bf16[48,80,128]{2,1,0:T(8,128)(2,1)S(1)}, bf16[48,80,128]{2,1,0:T(8,128)(2,1)}, u32[]{:S(2)}, u32[]{:S(2)}) collective-permute-start(bf16[48,80,128]{2,1,0:T(8,128)(2,1)S(1)} %get-tuple-element.262), channel_id=1, source_target_pairs={{0,6},{2,0},{4,2},{6,4},{8,14},{10,8},{12,10},{14,12},{16,22},{18,... | collective-permute-start | bytes 2949128 | tf_op jit(solution)/shard_map/ppermute | solution.py:558
  203.5 45.4 %collective-permute-start.15 = (bf16[40,80,128]{2,1,0:T(8,128)(2,1)S(1)}, bf16[40,80,128]{2,1,0:T(8,128)(2,1)}, u32[]{:S(2)}, u32[]{:S(2)}) collective-permute-start(bf16[40,80,128]{2,1,0:T(8,128)(2,1)S(1)} %get-tuple-element.250), channel_id=1, source_target_pairs={{0,4},{2,6},{4,0},{6,2},{8,12},{10,14},{12,8},{14,10},{16,20},{18,... | collective-permute-start | bytes 2457608 | tf_op jit(solution)/shard_map/ppermute | solution.py:558
  219.9 109.3 %reduce-scatter.7.cloned.1.call-start = ((), (), s32[]{:S(2)}) async-start(), calls=%async_computation.5 | async-start | bytes 2621440 | tf_op jit(solution)/shard_map/reduce_scatter | solution.py:648
  248.9 31.6 %collective-permute-start.17 = (bf16[24,64,128]{2,1,0:T(8,128)(2,1)}, bf16[24,64,128]{2,1,0:T(8,128)(2,1)S(1)}, u32[]{:S(2)}, u32[]{:S(2)}) collective-permute-start(bf16[24,64,128]{2,1,0:T(8,128)(2,1)} %copy-done.31), channel_id=1, source_target_pairs={{0,4},{2,6},{4,0},{6,2},{8,12},{10,14},{12,8},{14,10},{16,20},{18,... | collective-permute-start | bytes 1179656 | tf_op jit(solution)/shard_map/ppermute | solution.py:558
  250.0 30.5 %collective-permute-start.16 = (bf16[32,64,128]{2,1,0:T(8,128)(2,1)}, bf16[32,64,128]{2,1,0:T(8,128)(2,1)S(1)}, u32[]{:S(2)}, u32[]{:S(2)}) collective-permute-start(bf16[32,64,128]{2,1,0:T(8,128)(2,1)} %copy-done.27), channel_id=1, source_target_pairs={{0,6},{2,0},{4,2},{6,4},{8,14},{10,8},{12,10},{14,12},{16,22},{18,... | collective-permute-start | bytes 1572872 | tf_op jit(solution)/shard_map/ppermute | solution.py:558
  250.0 30.5 %collective-permute-start.18 = (bf16[32,64,128]{2,1,0:T(8,128)(2,1)}, bf16[32,64,128]{2,1,0:T(8,128)(2,1)S(1)}, u32[]{:S(2)}, u32[]{:S(2)}) collective-permute-start(bf16[32,64,128]{2,1,0:T(8,128)(2,1)} %copy-done.26), channel_id=1, source_target_pairs={{0,2},{2,4},{4,6},{6,0},{8,10},{10,12},{12,14},{14,8},{16,18},{18,... | collective-permute-start | bytes 1572872 | tf_op jit(solution)/shard_map/ppermute | solution.py:558
  285.3 89.6 %reduce-scatter.9.cloned.1.call-start = ((), (), s32[]{:S(2)}) async-start(), calls=%async_computation.6 | async-start | bytes 2621440 | tf_op jit(solution)/shard_map/reduce_scatter | solution.py:648
  285.3 27.7 %collective-permute-start.22 = (bf16[40,64,128]{2,1,0:T(8,128)(2,1)}, bf16[40,64,128]{2,1,0:T(8,128)(2,1)S(1)}, u32[]{:S(2)}, u32[]{:S(2)}) collective-permute-start(bf16[40,64,128]{2,1,0:T(8,128)(2,1)} %get-tuple-element.278), channel_id=1, source_target_pairs={{0,4},{2,6},{4,0},{6,2},{8,12},{10,14},{12,8},{14,10},{16,20},{18,... | collective-permute-start | bytes 1966088 | tf_op jit(solution)/shard_map/ppermute | solution.py:558
  286.1 27.0 %collective-permute-start.21 = (bf16[48,64,128]{2,1,0:T(8,128)(2,1)}, bf16[48,64,128]{2,1,0:T(8,128)(2,1)S(1)}, u32[]{:S(2)}, u32[]{:S(2)}) collective-permute-start(bf16[48,64,128]{2,1,0:T(8,128)(2,1)} %get-tuple-element.272), channel_id=1, source_target_pairs={{0,6},{2,0},{4,2},{6,4},{8,14},{10,8},{12,10},{14,12},{16,22},{18,... | collective-permute-start | bytes 2359304 | tf_op jit(solution)/shard_map/ppermute | solution.py:558
  289.0 33.1 %collective-permute-start.23 = (bf16[48,64,128]{2,1,0:T(8,128)(2,1)}, bf16[48,64,128]{2,1,0:T(8,128)(2,1)S(1)}, u32[]{:S(2)}, u32[]{:S(2)}) collective-permute-start(bf16[48,64,128]{2,1,0:T(8,128)(2,1)} %get-tuple-element.281), channel_id=1, source_target_pairs={{0,2},{2,4},{4,6},{6,0},{8,10},{10,12},{12,14},{14,8},{16,18},{18,... | collective-permute-start | bytes 2359304 | tf_op jit(solution)/shard_map/ppermute | solution.py:558
  329.2 91.1 %reduce-scatter.11.cloned.1.call-start = ((), (), s32[]{:S(2)}) async-start(), calls=%async_computation.7 | async-start | bytes 2621440 | tf_op jit(solution)/shard_map/reduce_scatter | solution.py:648
  329.3 20.5 %collective-permute-start.24 = (bf16[48,64,128]{2,1,0:T(8,128)(2,1)S(1)}, bf16[48,64,128]{2,1,0:T(8,128)(2,1)S(1)}, u32[]{:S(2)}, u32[]{:S(2)}) collective-permute-start(bf16[48,64,128]{2,1,0:T(8,128)(2,1)S(1)} %copy-done.62), channel_id=1, source_target_pairs={{0,6},{2,0},{4,2},{6,4},{8,14},{10,8},{12,10},{14,12},{16,22},{18,... | collective-permute-start | bytes 2359304 | tf_op jit(solution)/shard_map/ppermute | solution.py:558
  331.7 34.7 %collective-permute-start.26 = (bf16[48,64,128]{2,1,0:T(8,128)(2,1)S(1)}, bf16[48,64,128]{2,1,0:T(8,128)(2,1)S(1)}, u32[]{:S(2)}, u32[]{:S(2)}) collective-permute-start(bf16[48,64,128]{2,1,0:T(8,128)(2,1)S(1)} %copy-done.61), channel_id=1, source_target_pairs={{0,2},{2,4},{4,6},{6,0},{8,10},{10,12},{12,14},{14,8},{16,18},{18,... | collective-permute-start | bytes 2359304 | tf_op jit(solution)/shard_map/ppermute | solution.py:558
  331.8 16.4 %collective-permute-start.25 = (bf16[40,64,128]{2,1,0:T(8,128)(2,1)}, bf16[40,64,128]{2,1,0:T(8,128)(2,1)S(1)}, u32[]{:S(2)}, u32[]{:S(2)}) collective-permute-start(bf16[40,64,128]{2,1,0:T(8,128)(2,1)} %get-tuple-element.297), channel_id=1, source_target_pairs={{0,4},{2,6},{4,0},{6,2},{8,12},{10,14},{12,8},{14,10},{16,20},{18,... | collective-permute-start | bytes 1966088 | tf_op jit(solution)/shard_map/ppermute | solution.py:558
  375.6 4.8 %collective-permute-start.34 = (bf16[16,1024]{1,0:T(8,128)(2,1)S(1)}, bf16[16,1024]{1,0:T(8,128)(2,1)S(1)}, u32[]{:S(2)}, u32[]{:S(2)}) collective-permute-start(bf16[16,1024]{1,0:T(8,128)(2,1)S(1)} %get-tuple-element.337), channel_id=1, source_target_pairs={{0,16},{2,18},{4,20},{6,22},{8,24},{10,26},{12,28},{14,30},{16,0},... | collective-permute-start | bytes 98312 | tf_op jit(solution)/shard_map/ppermute | solution.py:640
  376.8 4.0 collective-permute-start.33
  376.8 5.4 %collective-permute-start.35 = (bf16[16,1024]{1,0:T(8,128)(2,1)S(1)}, bf16[16,1024]{1,0:T(8,128)(2,1)S(1)}, u32[]{:S(2)}, u32[]{:S(2)}) collective-permute-start(bf16[16,1024]{1,0:T(8,128)(2,1)S(1)} %get-tuple-element.337), channel_id=1, source_target_pairs={{0,24},{2,26},{4,28},{6,30},{8,0},{10,2},{12,4},{14,6},{16,8},{18,... | collective-permute-start | bytes 98312 | tf_op jit(solution)/shard_map/ppermute | solution.py:640
  382.3 6.5 %collective-permute-start.38 = (bf16[4,16,1024]{2,1,0:T(8,128)(2,1)S(1)}, bf16[4,16,1024]{2,1,0:T(8,128)(2,1)S(1)}, u32[]{:S(2)}, u32[]{:S(2)}) collective-permute-start(bf16[4,16,1024]{2,1,0:T(8,128)(2,1)S(1)} %pad_maximum_fusion.1), channel_id=1, source_target_pairs={{0,6},{2,0},{4,2},{6,4},{8,14},{10,8},{12,10},{14,12},{16,22},{18,... | collective-permute-start | bytes 393224 | tf_op jit(solution)/shard_map/ppermute | solution.py:558
  384.7 20.4 %collective-permute-start.30 = (bf16[8,128,128]{2,1,0:T(8,128)(2,1)S(1)}, bf16[8,128,128]{2,1,0:T(8,128)(2,1)S(1)}, u32[]{:S(2)}, u32[]{:S(2)}) collective-permute-start(bf16[8,128,128]{2,1,0:T(8,128)(2,1)S(1)} %copy-done.37), channel_id=1, source_target_pairs={{0,6},{2,0},{4,2},{6,4},{8,14},{10,8},{12,10},{14,12},{16,22},{18,... | collective-permute-start | bytes 786440 | tf_op jit(solution)/shard_map/ppermute | solution.py:558
  385.3 21.0 %collective-permute-start.31 = (bf16[8,128,128]{2,1,0:T(8,128)(2,1)S(1)}, bf16[8,128,128]{2,1,0:T(8,128)(2,1)S(1)}, u32[]{:S(2)}, u32[]{:S(2)}) collective-permute-start(bf16[8,128,128]{2,1,0:T(8,128)(2,1)S(1)} %copy-done.35), channel_id=1, source_target_pairs={{0,4},{2,6},{4,0},{6,2},{8,12},{10,14},{12,8},{14,10},{16,20},{18,... | collective-permute-start | bytes 786440 | tf_op jit(solution)/shard_map/ppermute | solution.py:558
  385.8 20.4 %collective-permute-start.32 = (bf16[8,128,128]{2,1,0:T(8,128)(2,1)S(1)}, bf16[8,128,128]{2,1,0:T(8,128)(2,1)S(1)}, u32[]{:S(2)}, u32[]{:S(2)}) collective-permute-start(bf16[8,128,128]{2,1,0:T(8,128)(2,1)S(1)} %copy-done.33), channel_id=1, source_target_pairs={{0,2},{2,4},{4,6},{6,0},{8,10},{10,12},{12,14},{14,8},{16,18},{18,... | collective-permute-start | bytes 786440 | tf_op jit(solution)/shard_map/ppermute | solution.py:558
  387.3 15.5 %collective-permute-start.37 = (bf16[4,16,1024]{2,1,0:T(8,128)(2,1)S(1)}, bf16[4,16,1024]{2,1,0:T(8,128)(2,1)S(1)}, u32[]{:S(2)}, u32[]{:S(2)}) collective-permute-start(bf16[4,16,1024]{2,1,0:T(8,128)(2,1)S(1)} %pad_maximum_fusion.1), channel_id=1, source_target_pairs={{0,4},{2,6},{4,0},{6,2},{8,12},{10,14},{12,8},{14,10},{16,20},{18,... | collective-permute-start | bytes 393224 | tf_op jit(solution)/shard_map/ppermute | solution.py:558
  388.8 14.9 %collective-permute-start.36 = (bf16[4,16,1024]{2,1,0:T(8,128)(2,1)S(1)}, bf16[4,16,1024]{2,1,0:T(8,128)(2,1)S(1)}, u32[]{:S(2)}, u32[]{:S(2)}) collective-permute-start(bf16[4,16,1024]{2,1,0:T(8,128)(2,1)S(1)} %pad_maximum_fusion.1), channel_id=1, source_target_pairs={{0,2},{2,4},{4,6},{6,0},{8,10},{10,12},{12,14},{14,8},{16,18},{18,... | collective-permute-start | bytes 393224 | tf_op jit(solution)/shard_map/ppermute | solution.py:558
  402.8 9.5 %collective-permute-start.27 = (bf16[8,128,128]{2,1,0:T(8,128)(2,1)S(1)}, bf16[8,128,128]{2,1,0:T(8,128)(2,1)S(1)}, u32[]{:S(2)}, u32[]{:S(2)}) collective-permute-start(bf16[8,128,128]{2,1,0:T(8,128)(2,1)S(1)} %get-tuple-element.314), channel_id=1, source_target_pairs={{0,6},{2,0},{4,2},{6,4},{8,14},{10,8},{12,10},{14,12},{16,22},{18,... | collective-permute-start | bytes 786440 | tf_op jit(solution)/shard_map/ppermute | solution.py:558
  403.7 13.8 %collective-permute-start.28 = (bf16[8,128,128]{2,1,0:T(8,128)(2,1)S(1)}, bf16[8,128,128]{2,1,0:T(8,128)(2,1)}, u32[]{:S(2)}, u32[]{:S(2)}) collective-permute-start(bf16[8,128,128]{2,1,0:T(8,128)(2,1)S(1)} %get-tuple-element.315), channel_id=1, source_target_pairs={{0,4},{2,6},{4,0},{6,2},{8,12},{10,14},{12,8},{14,10},{16,20},{18,... | collective-permute-start | bytes 786440 | tf_op jit(solution)/shard_map/ppermute | solution.py:558
  405.1 12.4 %collective-permute-start.29 = (bf16[8,128,128]{2,1,0:T(8,128)(2,1)S(1)}, bf16[8,128,128]{2,1,0:T(8,128)(2,1)}, u32[]{:S(2)}, u32[]{:S(2)}) collective-permute-start(bf16[8,128,128]{2,1,0:T(8,128)(2,1)S(1)} %get-tuple-element.316), channel_id=1, source_target_pairs={{0,2},{2,4},{4,6},{6,0},{8,10},{10,12},{12,14},{14,8},{16,18},{18,... | collective-permute-start | bytes 786440 | tf_op jit(solution)/shard_map/ppermute | solution.py:558
  (67 other events, 299.2 us)
Sparse Core Ops, SparseCore 0:
  10.2 45.6 all-gather.10
  58.0 44.6 all-gather.8
  104.3 36.0 all-gather.14
  142.3 53.5 all-gather.12
  220.1 44.8 reduce-scatter.4
  285.4 43.7 reduce-scatter.6
  331.6 43.1 reduce-scatter.8
  377.1 43.1 reduce-scatter.10

commit v6 on v5

--- a/solution.py
+++ b/solution.py
@@ -228,6 +228,7 @@
 
 
 def final_sum(own, sums, returned, thins, table, final_info, heads, slots, cap):
+    partial = len(sums) < PARTS
     blocks, _, width = own.shape
     lanes = len(returned)
     pairs = GLOB * heads // lanes
@@ -236,15 +237,19 @@
     number = len(arrays)
 
     def kernel(table_ref, info_ref, *rest):
-        far, out_ref, total = rest[:number], rest[number], rest[number + 1]
-        near, sems = rest[number + 2 : 2 * number + 2], rest[2 * number + 2]
+        far, rest = rest[:number], rest[number:]
+        out_refs, rest = rest[: 1 + partial], rest[1 + partial :]
+        total, near, sems = rest[0], rest[1 : number + 1], rest[number + 1]
         copies = [pltpu.make_async_copy(*pair, sems.at[n]) for n, pair in enumerate(zip(far, near))]
         for copy in copies:
             copy.start()
         for copy in copies:
             copy.wait()
         own_ref, rest = near[0], near[1:]
-        sum_refs, refs, thin_refs = rest[:PARTS], rest[PARTS : PARTS + lanes], rest[PARTS + lanes :]
+        count = len(sums)
+        sum_refs, refs, thin_refs = rest[:count], rest[count : count + lanes], rest[count + lanes :]
+        if partial:
+            total[:, ROWS:] = own_ref[:, ROWS:]
         for part, sum_ref in enumerate(sum_refs):
             here = slice(part * ROWS, (part + 1) * ROWS)
             for block in range(blocks):
@@ -285,12 +290,20 @@
                         columns = slice(head * DH, (head + 1) * DH)
                         total[row, here, columns] += value.astype(jnp.float32)
 
-        out_ref[...] = total[...].astype(out_ref.dtype)
+        if partial:
+            out_refs[0][...] = total[:, :ROWS].astype(jnp.bfloat16)
+            out_refs[1][...] = total[:, ROWS:]
+        else:
+            out_refs[0][...] = total[...].astype(jnp.bfloat16)
 
     specs = [smem_spec()] * 2 + [any_spec()] * number
+    shapes = [jax.ShapeDtypeStruct(own.shape, jnp.bfloat16)]
+    if partial:
+        half = (blocks, ROWS, width)
+        shapes = [jax.ShapeDtypeStruct(half, kind) for kind in (jnp.bfloat16, jnp.float32)]
     return call(
         kernel,
-        jax.ShapeDtypeStruct(own.shape, jnp.bfloat16),
+        shapes,
         specs,
         5,
         [pltpu.VMEM(own.shape, jnp.float32)]
@@ -651,7 +664,12 @@
 
     def finish(own, sums, returned, thins):
         own = own.reshape(blocks, BLOCK, width)
-        total = final_sum(own, sums, returned, thins, table, final_info, heads, slots, cap)
+        parts = final_sum(own, sums[: PARTS - 1 if not thins else PARTS], returned, thins, table,
+                          final_info, heads, slots, cap)
+        if thins:
+            return parts[0].reshape(rows_here, width)
+        rest = parts[1] + sums[1].reshape(parts[1].shape).astype(jnp.float32)
+        total = jnp.concatenate([parts[0], rest.astype(jnp.bfloat16)], axis=1)
         return total.reshape(rows_here, width)
 
     head_block = pl.BlockSpec((rows_here, DH), lambda h: (0, h))

time: 436 us -> 437 us (level)
    unnamed x137 -> x143, local copies, waits for them, and re-layouts: 38.5 us -> 36.9 us
  transfers between devices with their start and end apart: 47 -> 47, of which waited for: 22 -> 21; matrix products, arithmetic and copies ran while one was open for 1% -> 1% of each run, Pallas kernels for 21% -> 23%
where the time goes in v6:
time: 437 us; the launch traced here: 432 us
  waiting for transfers between devices  223 us (51%)
  Pallas kernels  97.3 us (22%)
  starting transfers between devices  49.9 us (11%)
  local copies, waits for them, and re-layouts  43 us (10%)
  between operations  14.8 us (3%)
  other arithmetic  4.8 us (1%)
    ppermute x36, waiting for transfers between devices, rotate(): return lax.ppermute(array, 'seq', moves)  149 us
    all_gather x4, waiting for transfers between devices, gather(): column = lax.all_gather(piece, 'seq', axis_index_groups=columns)  64.1 us
    ppermute x36, starting transfers between devices, rotate(): return lax.ppermute(array, 'seq', moves)  46.3 us
    unnamed x143, local copies, waits for them, and re-layouts  36.9 us
    pallas_call x4, Pallas kernels, sum_blocks(): call(kernel, jax.ShapeDtypeStruct((planes * segment, heads * DH), jnp.bfl...  19.5 us
    pallas_call x1, Pallas kernels, body(): per_head(slope_kernel, [weights_like, wide_like] + payloads(False), [smem...  19.4 us
    pallas_call x1, Pallas kernels, body(): per_head(weights_kernel, [weights_like, wide_like] + payloads(True), [sme...  17.8 us
    pallas_call x1, Pallas kernels, body(): per_head(output_kernel, [like, like], [smem_spec()] + [weight_block] * 2...  17.6 us
  transfers between devices with their start and end apart: 47, of which 21 were waited for; matrix products, arithmetic and copies ran while one was open for 1% of the time, Pallas kernels for 23%

profile of v6, /device:TPU:16, one launch (start us, length us, event | category | flops | bytes accessed | tf_op | source)
XLA Modules:
  0.0 432.5 jit_solution(6375210819156860726)
XLA Ops:
  7.3 2.4 fusion.24
  11.6 2.5 shard_map.93
  16.4 1.5 collective-permute-start.1
  20.4 10.4 %collective-permute-done.rest_3_.rest_15_ = bf16[2,8,128,128]{3,2,1,0:T(8,128)(2,1)S(1)} collective-permute-done((bf16[2,8,128,128]{3,2,1,0:T(8,128)(2,1)}, bf16[2,8,128,128]{3,2,1,0:T(8,128)(2,1)S(1)}, u32[]{:S(2)}, u32[]{:S(2)}) %collective-permute-start) | collective-permute-done | bytes 524320 | tf_op jit(solution)/shard_map/ppermute | solution.py:571
  31.6 9.2 %collective-permute-done.1.rest_6_.rest_18_ = bf16[2,8,128,128]{3,2,1,0:T(8,128)(2,1)S(1)} collective-permute-done((bf16[2,8,128,128]{3,2,1,0:T(8,128)(2,1)}, bf16[2,8,128,128]{3,2,1,0:T(8,128)(2,1)S(1)}, u32[]{:S(2)}, u32[]{:S(2)}) %collective-permute-start.1) | collective-permute-done | bytes 524320 | tf_op jit(solution)/shard_map/ppermute | solution.py:571
  42.5 13.9 %all-gather.11.cloned.1.call-done.column_ref = bf16[16,64,1024]{2,1,0:T(8,128)(2,1)} async-done(((bf16[4,64,1024]{2,1,0:T(8,128)(2,1)}), bf16[16,64,1024]{2,1,0:T(8,128)(2,1)}) %all-gather.11.cloned.1.call-update) | async-done | bytes 2097168 | tf_op jit(solution)/shard_map/all_gather | solution.py:633
  56.4 1.6 copy-done.5
  58.0 2.3 shard_map.94
  62.2 2.0 collective-permute-start.5
  66.0 36.7 %all-gather.9.cloned.1.call-done.column_ref = bf16[16,64,1024]{2,1,0:T(8,128)(2,1)} async-done(((bf16[4,64,1024]{2,1,0:T(8,128)(2,1)}), bf16[16,64,1024]{2,1,0:T(8,128)(2,1)}) %all-gather.9.cloned.1.call-update) | async-done | bytes 2097168 | tf_op jit(solution)/shard_map/all_gather | solution.py:633
  102.7 1.6 copy-done.6
  104.3 2.3 shard_map.95
  107.5 1.5 collective-permute-start.6
  110.5 1.5 collective-permute-start.7
  112.2 29.5 %collective-permute-done.7.rest_8_ = bf16[40,64,128]{2,1,0:T(8,128)(2,1)S(1)} collective-permute-done((bf16[40,64,128]{2,1,0:T(8,128)(2,1)S(1)}, bf16[40,64,128]{2,1,0:T(8,128)(2,1)S(1)}, u32[]{:S(2)}, u32[]{:S(2)}) %collective-permute-start.7) | collective-permute-done | bytes 655392 | tf_op jit(solution)/shard_map/ppermute | solution.py:571
  142.6 2.1 collective-permute-done.8.rest_11_
  146.2 2.2 shard_map.96
  151.1 1.5 collective-permute-start.11
  152.6 17.8 %shard_map.97 = (bf16[8,4,1024,128]{3,2,1,0:T(8,128)(2,1)}, f32[512,1024]{1,0:T(8,128)}, bf16[8,128,128]{2,1,0:T(8,128)(2,1)S(1)}, bf16[32,64,128]{2,1,0:T(8,128...) custom-call(s32[198]{0:T(256)S(1)} %pad_add_fusion.pick, ...), custom_call_target="tpu_custom_call" | custom-call | flops 24000000000 | bytes 84000000 | tf_op jit(solution)/shard_map/pallas_call | solution.py:746
  180.9 1.5 collective-permute-start.14
  182.4 13.6 %all-gather.13.cloned.1.call-done.column_ref = bf16[16,80,1024]{2,1,0:T(8,128)(2,1)} async-done(((bf16[4,80,1024]{2,1,0:T(8,128)(2,1)}), bf16[16,80,1024]{2,1,0:T(8,128)(2,1)}) %all-gather.13.cloned.1.call-update) | async-done | bytes 2621456 | tf_op jit(solution)/shard_map/all_gather | solution.py:633
  196.0 3.7 shard_map.98
  204.9 7.5 %collective-permute-done.14.rest_3_ = bf16[40,64,128]{2,1,0:T(8,128)(2,1)} collective-permute-done((bf16[40,64,128]{2,1,0:T(8,128)(2,1)}, bf16[40,64,128]{2,1,0:T(8,128)(2,1)}, u32[]{:S(2)}, u32[]{:S(2)}) %collective-permute-start.14) | collective-permute-done | bytes 655392 | tf_op jit(solution)/shard_map/ppermute | solution.py:571
  213.5 5.6 %shard_map.99 = bf16[1088,1024]{1,0:T(8,128)(2,1)} custom-call(s32[128]{0:T(128)S(1)} %reshape.304.table_ref, s32[8]{0:T(128)S(1)} %concatenate.16.info_ref, bf16[32,64,128]{2,1,0:T(8,128)(2,1)S(1)} %copy-done.55, bf16[40,64,128]{2,1,0:T(8,128)(2,1)} %collective-permute-done.12.rest_1_, bf16[32,64,128]{2,1,0:T(8,128)(2,1)} %collective-permute-done.13.rest_2_, ...), custom_call_target="tpu_custom_call" | custom-call | flops 6000000000 | bytes 21000000 | tf_op jit(solution)/shard_map/pallas_call | solution.py:221
  219.2 28.9 %collective-permute-done.15.rest_8_.rest_20_ = bf16[40,80,128]{2,1,0:T(8,128)(2,1)} collective-permute-done((bf16[40,80,128]{2,1,0:T(8,128)(2,1)S(1)}, bf16[40,80,128]{2,1,0:T(8,128)(2,1)}, u32[]{:S(2)}, u32[]{:S(2)}) %collective-permute-start.15) | collective-permute-done | bytes 819232 | tf_op jit(solution)/shard_map/ppermute | solution.py:571
  249.3 2.0 collective-permute-start.18
  258.7 19.4 %shard_map.100 = (bf16[8,4,1024,128]{3,2,1,0:T(8,128)(2,1)}, f32[512,1024]{1,0:T(8,128)}, bf16[8,128,128]{2,1,0:T(8,128)(2,1)S(1)}, bf16[40,64,128]{2,1,0:T(8,12...) custom-call(s32[198]{0:T(256)S(1)} %pad_add_fusion.pick, ...), custom_call_target="tpu_custom_call" | custom-call | flops 49999998976 | bytes 175000000 | tf_op jit(solution)/shard_map/pallas_call | solution.py:768
  281.1 4.6 %shard_map.101 = bf16[1024,1024]{1,0:T(8,128)(2,1)} custom-call(s32[128]{0:T(128)S(1)} %reshape.304.table_ref, s32[8]{0:T(128)S(1)} %concatenate.16.info_ref, bf16[24,64,128]{2,1,0:T(8,128)(2,1)S(1)} %copy-done.59, bf16[32,64,128]{2,1,0:T(8,128)(2,1)S(1)} %collective-permute-done.16.rest_1_, bf16[24,64,128]{2,1,0:T(8,128)(2,1)S(1)} %collective-permute-done.17.rest_2_, ...), custom_call_target="tpu_custom_call" | custom-call | flops 6000000000 | bytes 21000000 | tf_op jit(solution)/shard_map/pallas_call | solution.py:221
  286.7 2.9 collective-permute-start.21
  294.0 17.6 %shard_map.102 = (bf16[512,1024]{1,0:T(8,128)(2,1)}, bf16[512,1024]{1,0:T(8,128)(2,1)}) custom-call(s32[198]{0:T(256)S(1)} %pad_add_fusion.pick, bf16[8,4,1024,128]{3,2,1,0:T(8,128)(2,1)} %get-tuple-element.243.p_ref, bf16[8,4,1024,128]{3,2,1,0:T(8,128)(2,1)} %get-tuple-element.271.ds_ref, bf16[512,1024]{1,0:T(8,128)(2,1)} %k_ref.3, ...), custom_call_target="tpu_custom_call" | custom-call | flops 15000000512 | bytes 52500000 | tf_op jit(solution)/shard_map/pallas_call | solution.py:784
  311.6 11.1 %collective-permute-done.23.rest_3_ = bf16[48,64,128]{2,1,0:T(8,128)(2,1)S(1)} collective-permute-done((bf16[48,64,128]{2,1,0:T(8,128)(2,1)}, bf16[48,64,128]{2,1,0:T(8,128)(2,1)S(1)}, u32[]{:S(2)}, u32[]{:S(2)}) %collective-permute-start.23) | collective-permute-done | bytes 786464 | tf_op jit(solution)/shard_map/ppermute | solution.py:571
  322.7 4.7 %shard_map.104 = bf16[1024,1024]{1,0:T(8,128)(2,1)} custom-call(s32[128]{0:T(128)S(1)} %reshape.304.table_ref, s32[8]{0:T(128)S(1)} %concatenate.16.info_ref, bf16[40,64,128]{2,1,0:T(8,128)(2,1)S(1)} %copy-done.53, bf16[48,64,128]{2,1,0:T(8,128)(2,1)S(1)} %collective-permute-done.21.rest_1_, bf16[40,64,128]{2,1,0:T(8,128)(2,1)S(1)} %collective-permute-done.22.rest_2_, ...), custom_call_target="tpu_custom_call" | custom-call | flops 6000000000 | bytes 21000000 | tf_op jit(solution)/shard_map/pallas_call | solution.py:221
  327.4 2.4 reduce-scatter.7.cloned.1.call-done.rest_2_
  329.9 2.4 collective-permute-start.24
  333.5 15.2 %collective-permute-done.25.rest_2_ = bf16[40,64,128]{2,1,0:T(8,128)(2,1)S(1)} collective-permute-done((bf16[40,64,128]{2,1,0:T(8,128)(2,1)S(1)}, bf16[40,64,128]{2,1,0:T(8,128)(2,1)S(1)}, u32[]{:S(2)}, u32[]{:S(2)}) %collective-permute-start.25) | collective-permute-done | bytes 655392 | tf_op jit(solution)/shard_map/ppermute | solution.py:571
  348.6 1.7 collective-permute-done.24.rest_1_
  350.4 16.7 %collective-permute-done.26.rest_3_ = bf16[48,64,128]{2,1,0:T(8,128)(2,1)S(1)} collective-permute-done((bf16[48,64,128]{2,1,0:T(8,128)(2,1)S(1)}, bf16[48,64,128]{2,1,0:T(8,128)(2,1)S(1)}, u32[]{:S(2)}, u32[]{:S(2)}) %collective-permute-start.26) | collective-permute-done | bytes 786464 | tf_op jit(solution)/shard_map/ppermute | solution.py:571
  367.1 4.6 %shard_map.103 = bf16[1024,1024]{1,0:T(8,128)(2,1)} custom-call(s32[128]{0:T(128)S(1)} %reshape.304.table_ref, s32[8]{0:T(128)S(1)} %concatenate.16.info_ref, bf16[40,64,128]{2,1,0:T(8,128)(2,1)S(1)} %copy-done.51, bf16[48,64,128]{2,1,0:T(8,128)(2,1)S(1)} %collective-permute-done.24.rest_1_, bf16[40,64,128]{2,1,0:T(8,128)(2,1)S(1)} %collective-permute-done.25.rest_2_, ...), custom_call_target="tpu_custom_call" | custom-call | flops 6000000000 | bytes 21000000 | tf_op jit(solution)/shard_map/pallas_call | solution.py:221
  371.7 3.7 reduce-scatter.9.cloned.1.call-done.rest_1_
  377.4 2.0 collective-permute-start.35
  379.4 1.6 collective-permute-done.34
  382.9 2.4 collective-permute-start.38
  389.4 2.5 collective-permute-start.36
  392.4 11.0 %collective-permute-done.37 = bf16[4,16,1024]{2,1,0:T(8,128)(2,1)S(1)} collective-permute-done((bf16[4,16,1024]{2,1,0:T(8,128)(2,1)S(1)}, bf16[4,16,1024]{2,1,0:T(8,128)(2,1)S(1)}, u32[]{:S(2)}, u32[]{:S(2)}) %collective-permute-start.37) | collective-permute-done | bytes 131104 | tf_op jit(solution)/shard_map/ppermute | solution.py:571
  407.6 5.2 %shard_map.106 = bf16[4,128,1024]{2,1,0:T(8,128)(2,1)} custom-call(s32[128]{0:T(128)} %copy-done.4, s32[4]{0:T(128)} %pad_add_fusion.2.info_ref, f32[4,128,1024]{2,1,0:T(8,128)} %bitcast.53, bf16[272,1024]{1,0:T(8,128)(2,1)} %reduce-scatter.5.cloned.1.call-done.rest_1_, bf16[256,1024]{1,0:T(8,128)(2,1)} %reduce-scatter.7.cloned.1.call-done.rest_2_, ...), custom_call_target="tpu_custom_call" | custom-call | flops 5000000000 | bytes 17500000 | tf_op jit(solution)/shard_map/pallas_call | solution.py:304
  412.8 5.3 %collective-permute-done.28.rest_4_ = bf16[8,128,128]{2,1,0:T(8,128)(2,1)} collective-permute-done((bf16[8,128,128]{2,1,0:T(8,128)(2,1)S(1)}, bf16[8,128,128]{2,1,0:T(8,128)(2,1)}, u32[]{:S(2)}, u32[]{:S(2)}) %collective-permute-start.28) | collective-permute-done | bytes 262176 | tf_op jit(solution)/shard_map/ppermute | solution.py:571
  418.1 4.9 %shard_map.105 = (bf16[4,64,1024]{2,1,0:T(8,128)(2,1)}, f32[4,64,1024]{2,1,0:T(8,128)}) custom-call(s32[128]{0:T(128)} %copy-done.4, s32[4]{0:T(128)} %pad_add_fusion.2.info_ref, f32[4,128,1024]{2,1,0:T(8,128)} %bitcast.54, bf16[256,1024]{1,0:T(8,128)(2,1)} %reduce-scatter.9.cloned.1.call-done.rest_1_, bf16[8,128,128]{2,1,0:T(8,128)(2,1)} %copy-done.57, ...), custom_call_target="tpu_custom_call" | custom-call | flops 5000000000 | bytes 17500000 | tf_op jit(solution)/shard_map/pallas_call | solution.py:304
  423.0 1.6 fusion
  (248 shorter events, 68.8 us)
Async XLA Ops:
  7.2 49.2 %all-gather.11.cloned.1.call-start = ((), (), s32[]{:S(2)}) async-start(), calls=%async_computation.9 | async-start | bytes 2621440 | tf_op jit(solution)/shard_map/all_gather | solution.py:633
  9.7 93.0 %all-gather.9.cloned.1.call-start = ((), (), s32[]{:S(2)}) async-start(), calls=%async_computation.8 | async-start | bytes 2621440 | tf_op jit(solution)/shard_map/all_gather | solution.py:633
  11.4 355.6 %copy-start.4 = (s32[128]{0:T(128)}, s32[128]{0:T(128)S(1)}, u32[]{:S(2)}) copy-start(s32[128]{0:T(128)S(1)} %reshape.304.table_ref) | copy-start | bytes 1540
  11.5 133.3 %all-gather.15.cloned.1.call-start = ((), (), s32[]{:S(2)}) async-start(), calls=%async_computation.11 | async-start | bytes 1966080 | tf_op jit(solution)/shard_map/all_gather | solution.py:633
  14.9 16.0 %collective-permute-start = (bf16[2,8,128,128]{3,2,1,0:T(8,128)(2,1)}, bf16[2,8,128,128]{3,2,1,0:T(8,128)(2,1)S(1)}, u32[]{:S(2)}, u32[]{:S(2)}) collective-permute-start(bf16[2,8,128,128]{3,2,1,0:T(8,128)(2,1)} %get-tuple-element.169), channel_id=1, source_target_pairs={{0,2},{2,4},{4,6},{6,0},{8,10},{10,12},{12,14},{14,8},{16,18},{18,... | collective-permute-start | bytes 1572872 | tf_op jit(solution)/shard_map/ppermute | solution.py:571
  16.4 24.5 %collective-permute-start.1 = (bf16[2,8,128,128]{3,2,1,0:T(8,128)(2,1)}, bf16[2,8,128,128]{3,2,1,0:T(8,128)(2,1)S(1)}, u32[]{:S(2)}, u32[]{:S(2)}) collective-permute-start(bf16[2,8,128,128]{3,2,1,0:T(8,128)(2,1)} %get-tuple-element.170), channel_id=1, source_target_pairs={{0,4},{2,6},{4,0},{6,2},{8,12},{10,14},{12,8},{14,10},{16,20},{18,... | collective-permute-start | bytes 1572872 | tf_op jit(solution)/shard_map/ppermute | solution.py:571
  17.9 23.8 %collective-permute-start.2 = (bf16[2,8,128,128]{3,2,1,0:T(8,128)(2,1)S(1)}, bf16[2,8,128,128]{3,2,1,0:T(8,128)(2,1)S(1)}, u32[]{:S(2)}, u32[]{:S(2)}) collective-permute-start(bf16[2,8,128,128]{3,2,1,0:T(8,128)(2,1)S(1)} %get-tuple-element.171), channel_id=1, source_target_pairs={{0,6},{2,0},{4,2},{6,4},{8,14},{10,8},{12,10},{14,12},{16,22},{18,... | collective-permute-start | bytes 1572872 | tf_op jit(solution)/shard_map/ppermute | solution.py:571
  61.1 134.9 %all-gather.13.cloned.1.call-start = ((), (), s32[]{:S(2)}) async-start(), calls=%async_computation.10 | async-start | bytes 3276800 | tf_op jit(solution)/shard_map/all_gather | solution.py:633
  61.1 41.6 %collective-permute-start.3 = (bf16[48,64,128]{2,1,0:T(8,128)(2,1)S(1)}, bf16[48,64,128]{2,1,0:T(8,128)(2,1)}, u32[]{:S(2)}, u32[]{:S(2)}) collective-permute-start(bf16[48,64,128]{2,1,0:T(8,128)(2,1)S(1)} %get-tuple-element.178), channel_id=1, source_target_pairs={{0,2},{2,4},{4,6},{6,0},{8,10},{10,12},{12,14},{14,8},{16,18},{18,... | collective-permute-start | bytes 2359304 | tf_op jit(solution)/shard_map/ppermute | solution.py:571
  62.2 40.5 %collective-permute-start.5 = (bf16[48,64,128]{2,1,0:T(8,128)(2,1)S(1)}, bf16[48,64,128]{2,1,0:T(8,128)(2,1)}, u32[]{:S(2)}, u32[]{:S(2)}) collective-permute-start(bf16[48,64,128]{2,1,0:T(8,128)(2,1)S(1)} %get-tuple-element.180), channel_id=1, source_target_pairs={{0,6},{2,0},{4,2},{6,4},{8,14},{10,8},{12,10},{14,12},{16,22},{18,... | collective-permute-start | bytes 2359304 | tf_op jit(solution)/shard_map/ppermute | solution.py:571
  64.1 38.6 %collective-permute-start.4 = (bf16[40,64,128]{2,1,0:T(8,128)(2,1)S(1)}, bf16[40,64,128]{2,1,0:T(8,128)(2,1)}, u32[]{:S(2)}, u32[]{:S(2)}) collective-permute-start(bf16[40,64,128]{2,1,0:T(8,128)(2,1)S(1)} %get-tuple-element.179), channel_id=1, source_target_pairs={{0,4},{2,6},{4,0},{6,2},{8,12},{10,14},{12,8},{14,10},{16,20},{18,... | collective-permute-start | bytes 1966088 | tf_op jit(solution)/shard_map/ppermute | solution.py:571
  107.4 178.3 %reduce-scatter.5.cloned.1.call-start = ((), (), s32[]{:S(2)}) async-start(), calls=%async_computation.4 | async-start | bytes 2785280 | tf_op jit(solution)/shard_map/reduce_scatter | solution.py:661
  107.5 34.3 %collective-permute-start.6 = (bf16[48,64,128]{2,1,0:T(8,128)(2,1)S(1)}, bf16[48,64,128]{2,1,0:T(8,128)(2,1)S(1)}, u32[]{:S(2)}, u32[]{:S(2)}) collective-permute-start(bf16[48,64,128]{2,1,0:T(8,128)(2,1)S(1)} %get-tuple-element.191), channel_id=1, source_target_pairs={{0,2},{2,4},{4,6},{6,0},{8,10},{10,12},{12,14},{14,8},{16,18},{18,... | collective-permute-start | bytes 2359304 | tf_op jit(solution)/shard_map/ppermute | solution.py:571
  109.0 35.7 %collective-permute-start.8 = (bf16[48,64,128]{2,1,0:T(8,128)(2,1)S(1)}, bf16[48,64,128]{2,1,0:T(8,128)(2,1)}, u32[]{:S(2)}, u32[]{:S(2)}) collective-permute-start(bf16[48,64,128]{2,1,0:T(8,128)(2,1)S(1)} %get-tuple-element.193), channel_id=1, source_target_pairs={{0,6},{2,0},{4,2},{6,4},{8,14},{10,8},{12,10},{14,12},{16,22},{18,... | collective-permute-start | bytes 2359304 | tf_op jit(solution)/shard_map/ppermute | solution.py:571
  110.5 31.2 %collective-permute-start.7 = (bf16[40,64,128]{2,1,0:T(8,128)(2,1)S(1)}, bf16[40,64,128]{2,1,0:T(8,128)(2,1)S(1)}, u32[]{:S(2)}, u32[]{:S(2)}) collective-permute-start(bf16[40,64,128]{2,1,0:T(8,128)(2,1)S(1)} %get-tuple-element.192), channel_id=1, source_target_pairs={{0,4},{2,6},{4,0},{6,2},{8,12},{10,14},{12,8},{14,10},{16,20},{18,... | collective-permute-start | bytes 1966088 | tf_op jit(solution)/shard_map/ppermute | solution.py:571
  149.1 28.1 %collective-permute-start.10 = (bf16[40,48,128]{2,1,0:T(8,128)(2,1)S(1)}, bf16[40,48,128]{2,1,0:T(8,128)(2,1)S(1)}, u32[]{:S(2)}, u32[]{:S(2)}) collective-permute-start(bf16[40,48,128]{2,1,0:T(8,128)(2,1)S(1)} %get-tuple-element.229), channel_id=1, source_target_pairs={{0,4},{2,6},{4,0},{6,2},{8,12},{10,14},{12,8},{14,10},{16,20},{18,... | collective-permute-start | bytes 1474568 | tf_op jit(solution)/shard_map/ppermute | solution.py:571
  149.7 28.4 %collective-permute-start.9 = (bf16[48,48,128]{2,1,0:T(8,128)(2,1)S(1)}, bf16[48,48,128]{2,1,0:T(8,128)(2,1)S(1)}, u32[]{:S(2)}, u32[]{:S(2)}) collective-permute-start(bf16[48,48,128]{2,1,0:T(8,128)(2,1)S(1)} %get-tuple-element.228), channel_id=1, source_target_pairs={{0,2},{2,4},{4,6},{6,0},{8,10},{10,12},{12,14},{14,8},{16,18},{18,... | collective-permute-start | bytes 1769480 | tf_op jit(solution)/shard_map/ppermute | solution.py:571
  151.1 26.9 %collective-permute-start.11 = (bf16[48,48,128]{2,1,0:T(8,128)(2,1)S(1)}, bf16[48,48,128]{2,1,0:T(8,128)(2,1)S(1)}, u32[]{:S(2)}, u32[]{:S(2)}) collective-permute-start(bf16[48,48,128]{2,1,0:T(8,128)(2,1)S(1)} %get-tuple-element.230), channel_id=1, source_target_pairs={{0,6},{2,0},{4,2},{6,4},{8,14},{10,8},{12,10},{14,12},{16,22},{18,... | collective-permute-start | bytes 1769480 | tf_op jit(solution)/shard_map/ppermute | solution.py:571
  178.9 24.6 %collective-permute-start.13 = (bf16[32,64,128]{2,1,0:T(8,128)(2,1)}, bf16[32,64,128]{2,1,0:T(8,128)(2,1)}, u32[]{:S(2)}, u32[]{:S(2)}) collective-permute-start(bf16[32,64,128]{2,1,0:T(8,128)(2,1)} %get-tuple-element.236), channel_id=1, source_target_pairs={{0,4},{2,6},{4,0},{6,2},{8,12},{10,14},{12,8},{14,10},{16,20},{18,... | collective-permute-start | bytes 1572872 | tf_op jit(solution)/shard_map/ppermute | solution.py:571
  180.4 24.6 %collective-permute-start.12 = (bf16[40,64,128]{2,1,0:T(8,128)(2,1)}, bf16[40,64,128]{2,1,0:T(8,128)(2,1)}, u32[]{:S(2)}, u32[]{:S(2)}) collective-permute-start(bf16[40,64,128]{2,1,0:T(8,128)(2,1)} %get-tuple-element.235), channel_id=1, source_target_pairs={{0,6},{2,0},{4,2},{6,4},{8,14},{10,8},{12,10},{14,12},{16,22},{18,... | collective-permute-start | bytes 1966088 | tf_op jit(solution)/shard_map/ppermute | solution.py:571
  180.9 31.6 %collective-permute-start.14 = (bf16[40,64,128]{2,1,0:T(8,128)(2,1)}, bf16[40,64,128]{2,1,0:T(8,128)(2,1)}, u32[]{:S(2)}, u32[]{:S(2)}) collective-permute-start(bf16[40,64,128]{2,1,0:T(8,128)(2,1)} %get-tuple-element.237), channel_id=1, source_target_pairs={{0,2},{2,4},{4,6},{6,0},{8,10},{10,12},{12,14},{14,8},{16,18},{18,... | collective-permute-start | bytes 1966088 | tf_op jit(solution)/shard_map/ppermute | solution.py:571
  200.5 50.8 %collective-permute-start.19 = (bf16[48,80,128]{2,1,0:T(8,128)(2,1)S(1)}, bf16[48,80,128]{2,1,0:T(8,128)(2,1)}, u32[]{:S(2)}, u32[]{:S(2)}) collective-permute-start(bf16[48,80,128]{2,1,0:T(8,128)(2,1)S(1)} %get-tuple-element.260), channel_id=1, source_target_pairs={{0,2},{2,4},{4,6},{6,0},{8,10},{10,12},{12,14},{14,8},{16,18},{18,... | collective-permute-start | bytes 2949128 | tf_op jit(solution)/shard_map/ppermute | solution.py:571
  202.0 49.4 %collective-permute-start.20 = (bf16[48,80,128]{2,1,0:T(8,128)(2,1)S(1)}, bf16[48,80,128]{2,1,0:T(8,128)(2,1)}, u32[]{:S(2)}, u32[]{:S(2)}) collective-permute-start(bf16[48,80,128]{2,1,0:T(8,128)(2,1)S(1)} %get-tuple-element.264), channel_id=1, source_target_pairs={{0,6},{2,0},{4,2},{6,4},{8,14},{10,8},{12,10},{14,12},{16,22},{18,... | collective-permute-start | bytes 2949128 | tf_op jit(solution)/shard_map/ppermute | solution.py:571
  203.5 44.6 %collective-permute-start.15 = (bf16[40,80,128]{2,1,0:T(8,128)(2,1)S(1)}, bf16[40,80,128]{2,1,0:T(8,128)(2,1)}, u32[]{:S(2)}, u32[]{:S(2)}) collective-permute-start(bf16[40,80,128]{2,1,0:T(8,128)(2,1)S(1)} %get-tuple-element.252), channel_id=1, source_target_pairs={{0,4},{2,6},{4,0},{6,2},{8,12},{10,14},{12,8},{14,10},{16,20},{18,... | collective-permute-start | bytes 2457608 | tf_op jit(solution)/shard_map/ppermute | solution.py:571
  219.1 110.7 %reduce-scatter.7.cloned.1.call-start = ((), (), s32[]{:S(2)}) async-start(), calls=%async_computation.5 | async-start | bytes 2621440 | tf_op jit(solution)/shard_map/reduce_scatter | solution.py:661
  248.1 33.0 %collective-permute-start.17 = (bf16[24,64,128]{2,1,0:T(8,128)(2,1)}, bf16[24,64,128]{2,1,0:T(8,128)(2,1)S(1)}, u32[]{:S(2)}, u32[]{:S(2)}) collective-permute-start(bf16[24,64,128]{2,1,0:T(8,128)(2,1)} %copy-done.28), channel_id=1, source_target_pairs={{0,4},{2,6},{4,0},{6,2},{8,12},{10,14},{12,8},{14,10},{16,20},{18,... | collective-permute-start | bytes 1179656 | tf_op jit(solution)/shard_map/ppermute | solution.py:571
  249.3 31.8 %collective-permute-start.16 = (bf16[32,64,128]{2,1,0:T(8,128)(2,1)}, bf16[32,64,128]{2,1,0:T(8,128)(2,1)S(1)}, u32[]{:S(2)}, u32[]{:S(2)}) collective-permute-start(bf16[32,64,128]{2,1,0:T(8,128)(2,1)} %copy-done.24), channel_id=1, source_target_pairs={{0,6},{2,0},{4,2},{6,4},{8,14},{10,8},{12,10},{14,12},{16,22},{18,... | collective-permute-start | bytes 1572872 | tf_op jit(solution)/shard_map/ppermute | solution.py:571
  249.3 31.8 %collective-permute-start.18 = (bf16[32,64,128]{2,1,0:T(8,128)(2,1)}, bf16[32,64,128]{2,1,0:T(8,128)(2,1)S(1)}, u32[]{:S(2)}, u32[]{:S(2)}) collective-permute-start(bf16[32,64,128]{2,1,0:T(8,128)(2,1)} %copy-done.23), channel_id=1, source_target_pairs={{0,2},{2,4},{4,6},{6,0},{8,10},{10,12},{12,14},{14,8},{16,18},{18,... | collective-permute-start | bytes 1572872 | tf_op jit(solution)/shard_map/ppermute | solution.py:571
  285.8 89.6 %reduce-scatter.9.cloned.1.call-start = ((), (), s32[]{:S(2)}) async-start(), calls=%async_computation.6 | async-start | bytes 2621440 | tf_op jit(solution)/shard_map/reduce_scatter | solution.py:661
  285.8 25.7 %collective-permute-start.22 = (bf16[40,64,128]{2,1,0:T(8,128)(2,1)}, bf16[40,64,128]{2,1,0:T(8,128)(2,1)S(1)}, u32[]{:S(2)}, u32[]{:S(2)}) collective-permute-start(bf16[40,64,128]{2,1,0:T(8,128)(2,1)} %get-tuple-element.280), channel_id=1, source_target_pairs={{0,4},{2,6},{4,0},{6,2},{8,12},{10,14},{12,8},{14,10},{16,20},{18,... | collective-permute-start | bytes 1966088 | tf_op jit(solution)/shard_map/ppermute | solution.py:571
  286.7 24.9 %collective-permute-start.21 = (bf16[48,64,128]{2,1,0:T(8,128)(2,1)}, bf16[48,64,128]{2,1,0:T(8,128)(2,1)S(1)}, u32[]{:S(2)}, u32[]{:S(2)}) collective-permute-start(bf16[48,64,128]{2,1,0:T(8,128)(2,1)} %get-tuple-element.274), channel_id=1, source_target_pairs={{0,6},{2,0},{4,2},{6,4},{8,14},{10,8},{12,10},{14,12},{16,22},{18,... | collective-permute-start | bytes 2359304 | tf_op jit(solution)/shard_map/ppermute | solution.py:571
  289.6 33.1 %collective-permute-start.23 = (bf16[48,64,128]{2,1,0:T(8,128)(2,1)}, bf16[48,64,128]{2,1,0:T(8,128)(2,1)S(1)}, u32[]{:S(2)}, u32[]{:S(2)}) collective-permute-start(bf16[48,64,128]{2,1,0:T(8,128)(2,1)} %get-tuple-element.283), channel_id=1, source_target_pairs={{0,2},{2,4},{4,6},{6,0},{8,10},{10,12},{12,14},{14,8},{16,18},{18,... | collective-permute-start | bytes 2359304 | tf_op jit(solution)/shard_map/ppermute | solution.py:571
  329.8 93.2 %reduce-scatter.11.cloned.1.call-start = ((), (), s32[]{:S(2)}) async-start(), calls=%async_computation.7 | async-start | bytes 2621440 | tf_op jit(solution)/shard_map/reduce_scatter | solution.py:661
  329.9 20.5 %collective-permute-start.24 = (bf16[48,64,128]{2,1,0:T(8,128)(2,1)S(1)}, bf16[48,64,128]{2,1,0:T(8,128)(2,1)S(1)}, u32[]{:S(2)}, u32[]{:S(2)}) collective-permute-start(bf16[48,64,128]{2,1,0:T(8,128)(2,1)S(1)} %copy-done.64), channel_id=1, source_target_pairs={{0,6},{2,0},{4,2},{6,4},{8,14},{10,8},{12,10},{14,12},{16,22},{18,... | collective-permute-start | bytes 2359304 | tf_op jit(solution)/shard_map/ppermute | solution.py:571
  332.3 34.7 %collective-permute-start.26 = (bf16[48,64,128]{2,1,0:T(8,128)(2,1)S(1)}, bf16[48,64,128]{2,1,0:T(8,128)(2,1)S(1)}, u32[]{:S(2)}, u32[]{:S(2)}) collective-permute-start(bf16[48,64,128]{2,1,0:T(8,128)(2,1)S(1)} %copy-done.63), channel_id=1, source_target_pairs={{0,2},{2,4},{4,6},{6,0},{8,10},{10,12},{12,14},{14,8},{16,18},{18,... | collective-permute-start | bytes 2359304 | tf_op jit(solution)/shard_map/ppermute | solution.py:571
  332.3 16.3 %collective-permute-start.25 = (bf16[40,64,128]{2,1,0:T(8,128)(2,1)S(1)}, bf16[40,64,128]{2,1,0:T(8,128)(2,1)S(1)}, u32[]{:S(2)}, u32[]{:S(2)}) collective-permute-start(bf16[40,64,128]{2,1,0:T(8,128)(2,1)S(1)} %copy-done.66), channel_id=1, source_target_pairs={{0,4},{2,6},{4,0},{6,2},{8,12},{10,14},{12,8},{14,10},{16,20},{18,... | collective-permute-start | bytes 1966088 | tf_op jit(solution)/shard_map/ppermute | solution.py:571
  376.2 4.8 %collective-permute-start.34 = (bf16[16,1024]{1,0:T(8,128)(2,1)S(1)}, bf16[16,1024]{1,0:T(8,128)(2,1)S(1)}, u32[]{:S(2)}, u32[]{:S(2)}) collective-permute-start(bf16[16,1024]{1,0:T(8,128)(2,1)S(1)} %get-tuple-element.341), channel_id=1, source_target_pairs={{0,16},{2,18},{4,20},{6,22},{8,24},{10,26},{12,28},{14,30},{16,0},... | collective-permute-start | bytes 98312 | tf_op jit(solution)/shard_map/ppermute | solution.py:653
  377.4 4.0 collective-permute-start.33
  377.4 5.4 %collective-permute-start.35 = (bf16[16,1024]{1,0:T(8,128)(2,1)S(1)}, bf16[16,1024]{1,0:T(8,128)(2,1)S(1)}, u32[]{:S(2)}, u32[]{:S(2)}) collective-permute-start(bf16[16,1024]{1,0:T(8,128)(2,1)S(1)} %get-tuple-element.341), channel_id=1, source_target_pairs={{0,24},{2,26},{4,28},{6,30},{8,0},{10,2},{12,4},{14,6},{16,8},{18,... | collective-permute-start | bytes 98312 | tf_op jit(solution)/shard_map/ppermute | solution.py:653
  382.9 6.5 %collective-permute-start.38 = (bf16[4,16,1024]{2,1,0:T(8,128)(2,1)S(1)}, bf16[4,16,1024]{2,1,0:T(8,128)(2,1)S(1)}, u32[]{:S(2)}, u32[]{:S(2)}) collective-permute-start(bf16[4,16,1024]{2,1,0:T(8,128)(2,1)S(1)} %pad_maximum_fusion.2), channel_id=1, source_target_pairs={{0,6},{2,0},{4,2},{6,4},{8,14},{10,8},{12,10},{14,12},{16,22},{18,... | collective-permute-start | bytes 393224 | tf_op jit(solution)/shard_map/ppermute | solution.py:571
  385.3 20.4 %collective-permute-start.30 = (bf16[8,128,128]{2,1,0:T(8,128)(2,1)S(1)}, bf16[8,128,128]{2,1,0:T(8,128)(2,1)S(1)}, u32[]{:S(2)}, u32[]{:S(2)}) collective-permute-start(bf16[8,128,128]{2,1,0:T(8,128)(2,1)S(1)} %copy-done.34), channel_id=1, source_target_pairs={{0,6},{2,0},{4,2},{6,4},{8,14},{10,8},{12,10},{14,12},{16,22},{18,... | collective-permute-start | bytes 786440 | tf_op jit(solution)/shard_map/ppermute | solution.py:571
  385.9 20.9 %collective-permute-start.31 = (bf16[8,128,128]{2,1,0:T(8,128)(2,1)S(1)}, bf16[8,128,128]{2,1,0:T(8,128)(2,1)S(1)}, u32[]{:S(2)}, u32[]{:S(2)}) collective-permute-start(bf16[8,128,128]{2,1,0:T(8,128)(2,1)S(1)} %copy-done.32), channel_id=1, source_target_pairs={{0,4},{2,6},{4,0},{6,2},{8,12},{10,14},{12,8},{14,10},{16,20},{18,... | collective-permute-start | bytes 786440 | tf_op jit(solution)/shard_map/ppermute | solution.py:571
  386.4 20.4 %collective-permute-start.32 = (bf16[8,128,128]{2,1,0:T(8,128)(2,1)S(1)}, bf16[8,128,128]{2,1,0:T(8,128)(2,1)S(1)}, u32[]{:S(2)}, u32[]{:S(2)}) collective-permute-start(bf16[8,128,128]{2,1,0:T(8,128)(2,1)S(1)} %copy-done.30), channel_id=1, source_target_pairs={{0,2},{2,4},{4,6},{6,0},{8,10},{10,12},{12,14},{14,8},{16,18},{18,... | collective-permute-start | bytes 786440 | tf_op jit(solution)/shard_map/ppermute | solution.py:571
  387.9 15.5 %collective-permute-start.37 = (bf16[4,16,1024]{2,1,0:T(8,128)(2,1)S(1)}, bf16[4,16,1024]{2,1,0:T(8,128)(2,1)S(1)}, u32[]{:S(2)}, u32[]{:S(2)}) collective-permute-start(bf16[4,16,1024]{2,1,0:T(8,128)(2,1)S(1)} %pad_maximum_fusion.2), channel_id=1, source_target_pairs={{0,4},{2,6},{4,0},{6,2},{8,12},{10,14},{12,8},{14,10},{16,20},{18,... | collective-permute-start | bytes 393224 | tf_op jit(solution)/shard_map/ppermute | solution.py:571
  389.4 14.9 %collective-permute-start.36 = (bf16[4,16,1024]{2,1,0:T(8,128)(2,1)S(1)}, bf16[4,16,1024]{2,1,0:T(8,128)(2,1)S(1)}, u32[]{:S(2)}, u32[]{:S(2)}) collective-permute-start(bf16[4,16,1024]{2,1,0:T(8,128)(2,1)S(1)} %pad_maximum_fusion.2), channel_id=1, source_target_pairs={{0,2},{2,4},{4,6},{6,0},{8,10},{10,12},{12,14},{14,8},{16,18},{18,... | collective-permute-start | bytes 393224 | tf_op jit(solution)/shard_map/ppermute | solution.py:571
  403.4 9.4 %collective-permute-start.27 = (bf16[8,128,128]{2,1,0:T(8,128)(2,1)S(1)}, bf16[8,128,128]{2,1,0:T(8,128)(2,1)S(1)}, u32[]{:S(2)}, u32[]{:S(2)}) collective-permute-start(bf16[8,128,128]{2,1,0:T(8,128)(2,1)S(1)} %copy-done.38), channel_id=1, source_target_pairs={{0,6},{2,0},{4,2},{6,4},{8,14},{10,8},{12,10},{14,12},{16,22},{18,... | collective-permute-start | bytes 786440 | tf_op jit(solution)/shard_map/ppermute | solution.py:571
  404.3 13.8 %collective-permute-start.28 = (bf16[8,128,128]{2,1,0:T(8,128)(2,1)S(1)}, bf16[8,128,128]{2,1,0:T(8,128)(2,1)}, u32[]{:S(2)}, u32[]{:S(2)}) collective-permute-start(bf16[8,128,128]{2,1,0:T(8,128)(2,1)S(1)} %copy-done.36), channel_id=1, source_target_pairs={{0,4},{2,6},{4,0},{6,2},{8,12},{10,14},{12,8},{14,10},{16,20},{18,... | collective-permute-start | bytes 786440 | tf_op jit(solution)/shard_map/ppermute | solution.py:571
  405.7 12.4 %collective-permute-start.29 = (bf16[8,128,128]{2,1,0:T(8,128)(2,1)S(1)}, bf16[8,128,128]{2,1,0:T(8,128)(2,1)}, u32[]{:S(2)}, u32[]{:S(2)}) collective-permute-start(bf16[8,128,128]{2,1,0:T(8,128)(2,1)S(1)} %get-tuple-element.317), channel_id=1, source_target_pairs={{0,2},{2,4},{4,6},{6,0},{8,10},{10,12},{12,14},{14,8},{16,18},{18,... | collective-permute-start | bytes 786440 | tf_op jit(solution)/shard_map/ppermute | solution.py:571
  (70 other events, 343.1 us)
Sparse Core Ops, SparseCore 0:
  10.2 46.1 all-gather.10
  58.5 44.1 all-gather.8
  104.3 36.0 all-gather.14
  142.3 53.5 all-gather.12
  219.3 44.8 reduce-scatter.4
  285.9 43.8 reduce-scatter.6
  332.2 43.1 reduce-scatter.8
  377.7 43.1 reduce-scatter.10
